TPU v7x, 32 devices: a whole 2x2x4 slice. The times are simulated.
32 devices in a mesh: dp: 16 (over z, y, x), tensor: 2 (over core).
Axes of the slice: x: 2, y: 2, z: 4, core: 2. Of those that a mesh axis runs over, the one named last changes fastest.
Arguments:
- latents: float32 [256, 256, 16], P('dp'), may hold values from -6 to 6
- gauss_noise: float32 [256, 256, 16], P('dp'), may hold values from -6 to 6
- time_steps: float32 [256], P('dp'), may hold values from 0.05 to 0.95
- labels: int32 [256], replicated, may hold values from 0 to 999
- targets: float32 [256, 256, 16], P('dp'), may hold values from -12 to 12, as said below
- w_col: float32 [2, 384, 2688], P(None, 'dp', 'tensor'), may hold values from -0.3125 to 0.3125
- w_row: float32 [2, 1920, 384], P(None, 'tensor', 'dp'), may hold values from -0.3125 to 0.3125
- w_cond: float32 [384, 5376], P('dp'), may hold values from -0.3125 to 0.3125
- w_time: float32 [640, 384], P('dp'), may hold values from -0.375 to 0.375
- w_io: float32 [2, 384, 16], P(None, 'dp'), may hold values from -0.75 to 0.75
- class_table: float32 [1000, 384], P(None, 'dp'), may hold values from -0.3125 to 0.3125
- b_col: float32 [2, 2688], P(None, 'tensor'), may hold values from -1.75 to 1.75
- b_rep: float32 [8080], replicated, may hold values from -1.75 to 1.75
- mom_col: float32 [2, 384, 2688], P(None, 'dp', 'tensor'), may hold values from -0.01953125 to 0.01953125
- mom_row: float32 [2, 1920, 384], P(None, 'tensor', 'dp'), may hold values from -0.01953125 to 0.01953125
- mom_cond: float32 [384, 5376], P('dp'), may hold values from -0.01953125 to 0.01953125
- mom_time: float32 [640, 384], P('dp'), may hold values from -0.01953125 to 0.01953125
- mom_io: float32 [2, 384, 16], P(None, 'dp'), may hold values from -0.0625 to 0.0625
- mom_table: float32 [1000, 384], P(None, 'dp'), may hold values from -0.0012207031 to 0.0012207031
- mom_bcol: float32 [2, 2688], P(None, 'tensor'), may hold values from -0.0625 to 0.0625
- mom_brep: float32 [8080], replicated, may hold values from -0.0625 to 0.0625
- err_col: float32 [32, 384, 2688], P('dp', None, 'tensor'), may hold values from -6144 to 6144
- err_row: float32 [32, 1920, 384], P('dp', 'tensor'), may hold values from -6144 to 6144
- err_io: float32 [32, 384, 16], P('dp'), may hold values from -65536 to 65536
- fac_col: float32 [2, 2688, 8], P(None, 'tensor'), may hold values from -6 to 6
- fac_row: float32 [2, 768, 8], P(None, 'tensor'), may hold values from -6 to 6
- fac_io: float32 [2, 16, 8], replicated, may hold values from -6 to 6
Outputs:
- loss_sum: float32 [], replicated
- clip_norm: float32 [], replicated
- next_w_col: float32 [2, 384, 2688], P(None, 'dp', 'tensor')
- next_w_row: float32 [2, 1920, 384], P(None, 'tensor', 'dp')
- next_w_cond: float32 [384, 5376], P('dp')
- next_w_time: float32 [640, 384], P('dp')
- next_w_io: float32 [2, 384, 16], P(None, 'dp')
- next_table: float32 [1000, 384], P(None, 'dp')
- next_b_col: float32 [2, 2688], P(None, 'tensor')
- next_b_rep: float32 [8080], replicated
- next_mom_col: float32 [2, 384, 2688], P(None, 'dp', 'tensor')
- next_mom_row: float32 [2, 1920, 384], P(None, 'tensor', 'dp')
- next_mom_cond: float32 [384, 5376], P('dp')
- next_mom_time: float32 [640, 384], P('dp')
- next_mom_io: float32 [2, 384, 16], P(None, 'dp')
- next_mom_table: float32 [1000, 384], P(None, 'dp')
- next_mom_bcol: float32 [2, 2688], P(None, 'tensor')
- next_mom_brep: float32 [8080], replicated
- next_err_col: float32 [32, 384, 2688], P('dp', None, 'tensor')
- next_err_row: float32 [32, 1920, 384], P('dp', 'tensor')
- next_err_io: float32 [32, 384, 16], P('dp')
- next_fac_col: float32 [2, 2688, 8], P(None, 'tensor')
- next_fac_row: float32 [2, 768, 8], P(None, 'tensor')
- next_fac_io: float32 [2, 16, 8], replicated
Inputs may be any that keep to these rules, and one draw needn't show every extreme that they name: `targets`: rows of velocity grow in size along the latents.
All inputs are finite; a program needn't handle non-finite values.
Results may differ from a plain program's by a relative error of at most 0.00045.
The roundings to bfloat16 on the way count: a program that leaves them out, or rounds other values in their place, can miss the bound.
Values may be sent and summed in bfloat16 or wider, within the bound.
No kernel may reach another device: no remote copies, remote signals or barrier semaphores. Data moves between devices by JAX's collectives and lax.ppermute only.
A program may use at most 320 MiB of HBM per device.

v0:
```python
import jax
import jax.numpy as jnp
from jax import lax
from jax.sharding import PartitionSpec as P

D = 384
HEADS = 6
HD = 64
CLASSES = 1000
FREQ = 256
PV = 16
GRID = 16
L = 2
MB = 2
TOK = 256


highest = lax.Precision.HIGHEST
norm_eps = 1e-06
ortho_eps = 1e-06
clip_limit = 1.0
momentum_decay = 0.9
learn_rate = 4.0


def position_table():
    quarter = D // 4
    omega = 1.0 / 10000.0 ** (jnp.arange(quarter, dtype=jnp.float32) / quarter)
    index = jnp.arange(TOK, dtype=jnp.int32)
    across = (index % GRID).astype(jnp.float32)[:, None] * omega[None, :]
    down = (index // GRID).astype(jnp.float32)[:, None] * omega[None, :]
    return jnp.concatenate([jnp.sin(across), jnp.cos(across), jnp.sin(down), jnp.cos(down)], 1)


def frequency_features(steps):
    half = FREQ // 2
    rates = jnp.exp(-jnp.log(10000.0) * jnp.arange(half, dtype=jnp.float32) / half)
    angles = steps[:, None] * rates[None, :]
    return jnp.concatenate([jnp.cos(angles), jnp.sin(angles)], 1)


def layer_norm(values):
    centered = values - jnp.mean(values, -1, keepdims=True)
    inv_std = lax.rsqrt(jnp.mean(centered * centered, -1, keepdims=True) + norm_eps)
    return (centered * inv_std, inv_std)


def norm_back(grad_normed, normed, inv_std):
    mean_grad = jnp.mean(grad_normed, -1, keepdims=True)
    mean_mixed = jnp.mean(grad_normed * normed, -1, keepdims=True)
    return inv_std * (grad_normed - mean_grad - normed * mean_mixed)


def token_matmul(left, right):
    return jnp.einsum("ntd,df->ntf", left, right, preferred_element_type=jnp.float32)


def token_back(grad, right):
    return jnp.einsum("ntf,df->ntd", grad, right, preferred_element_type=jnp.float32)


def weight_grad(left, grad):
    return jnp.einsum("ntd,ntf->df", left, grad, preferred_element_type=jnp.float32)


def token_total(values):
    return jnp.sum(values.astype(jnp.float32), (0, 1))


def row_sum(partial_value):
    return lax.psum(partial_value, "tensor")


def input_sum(partial_value):
    return lax.psum(partial_value.astype(jnp.bfloat16), "tensor").astype(jnp.float32)


def modulated(values, shift, scale):
    normed, inv_std = layer_norm(values)
    return (
        normed,
        inv_std,
        (normed * (1.0 + scale[:, None, :]) + shift[:, None, :]).astype(jnp.bfloat16),
    )


def modulate_back(grad_input, normed, inv_std, scale):
    grad_shift = jnp.sum(grad_input, 1)
    grad_scale = jnp.sum(grad_input * normed, 1)
    grad_values = norm_back(grad_input * (1.0 + scale[:, None, :]), normed, inv_std)
    return (grad_values, grad_shift, grad_scale)


def attention_scores(qkv_bf, heads_local):
    count, tokens = (qkv_bf.shape[0], qkv_bf.shape[1])
    split = qkv_bf.reshape(count, tokens, heads_local, 3, HD)
    query, keyed, valued = (split[:, :, :, 0], split[:, :, :, 1], split[:, :, :, 2])
    scores = jnp.einsum(
        "nqhd,nkhd->nhqk", query, keyed, preferred_element_type=jnp.float32
    ) * HD ** (-0.5)
    return (query, keyed, valued, scores)


def attention(qkv_bf, heads_local):
    query, keyed, valued, scores = attention_scores(qkv_bf, heads_local)
    peak = jnp.max(scores, -1, keepdims=True)
    expo = jnp.exp(scores - peak)
    total = jnp.sum(expo, -1, keepdims=True)
    probs = (expo / total).astype(jnp.bfloat16)
    mixed = jnp.einsum("nhqk,nkhd->nqhd", probs, valued, preferred_element_type=jnp.float32)
    return (
        mixed.reshape(qkv_bf.shape[0], qkv_bf.shape[1], heads_local * HD),
        peak + jnp.log(total),
    )


def attention_back(qkv_bf, log_total, grad_mixed, heads_local):
    query, keyed, valued, scores = attention_scores(qkv_bf, heads_local)
    count, tokens = (qkv_bf.shape[0], qkv_bf.shape[1])
    probs = jnp.exp(scores - log_total)
    grad_heads = grad_mixed.reshape(count, tokens, heads_local, HD)
    grad_probs = jnp.einsum(
        "nqhd,nkhd->nhqk", grad_heads, valued, preferred_element_type=jnp.float32
    )
    grad_value = jnp.einsum(
        "nhqk,nqhd->nkhd",
        probs.astype(jnp.bfloat16),
        grad_heads,
        preferred_element_type=jnp.float32,
    )
    row_dot = jnp.sum(grad_probs * probs, -1, keepdims=True)
    grad_scores = (probs * (grad_probs - row_dot)).astype(jnp.bfloat16)
    grad_query = jnp.einsum(
        "nhqk,nkhd->nqhd", grad_scores, keyed, preferred_element_type=jnp.float32
    ) * HD ** (-0.5)
    grad_key = jnp.einsum(
        "nhqk,nqhd->nkhd", grad_scores, query, preferred_element_type=jnp.float32
    ) * HD ** (-0.5)
    stacked = jnp.stack([grad_query, grad_key, grad_value], 3)
    return stacked.reshape(count, tokens, heads_local * 3 * HD).astype(jnp.bfloat16)


def layer_forward(hidden, col_block, row_block, col_bias, proj_bias, fc2_bias, mods, heads_local):
    qkv_width = 3 * HD * heads_local
    attn_rows = HD * heads_local
    normed_a, inv_a, input_a = modulated(hidden, mods[0], mods[1])
    qkv = (token_matmul(input_a, col_block[:, :qkv_width]) + col_bias[:qkv_width]).astype(
        jnp.bfloat16
    )
    mixed, log_total = attention(qkv, heads_local)
    mixed_bf = mixed.astype(jnp.bfloat16)
    branch_a = row_sum(token_matmul(mixed_bf, row_block[:attn_rows])) + proj_bias
    middle = hidden + mods[2][:, None, :] * branch_a
    normed_m, inv_m, input_m = modulated(middle, mods[3], mods[4])
    pre_act = token_matmul(input_m, col_block[:, qkv_width:]) + col_bias[qkv_width:]
    acted = jax.nn.gelu(pre_act, approximate=True).astype(jnp.bfloat16)
    branch_m = row_sum(token_matmul(acted, row_block[attn_rows:])) + fc2_bias
    output = middle + mods[5][:, None, :] * branch_m
    return (output, (hidden, middle, qkv, log_total, mixed_bf, pre_act, branch_a, branch_m))


def layer_backward(grad_output, saved, col_block, row_block, mods, heads_local):
    hidden, middle, qkv, log_total, mixed_bf, pre_act, branch_a, branch_m = saved
    qkv_width = 3 * HD * heads_local
    attn_rows = HD * heads_local
    grad_gate_m = jnp.sum(grad_output * branch_m, 1)
    grad_branch_m = (grad_output * mods[5][:, None, :]).astype(jnp.bfloat16)
    acted, gelu_pull = jax.vjp(lambda values: jax.nn.gelu(values, approximate=True), pre_act)
    acted = acted.astype(jnp.bfloat16)
    grad_fc2 = weight_grad(acted, grad_branch_m)
    grad_acted = token_back(grad_branch_m, row_block[attn_rows:])
    grad_pre = gelu_pull(grad_acted)[0].astype(jnp.bfloat16)
    normed_m, inv_m, input_m = modulated(middle, mods[3], mods[4])
    grad_fc1 = weight_grad(input_m, grad_pre)
    grad_input_m = input_sum(token_back(grad_pre, col_block[:, qkv_width:]))
    grad_norm_m, grad_shift_m, grad_scale_m = modulate_back(grad_input_m, normed_m, inv_m, mods[4])
    grad_middle = grad_output + grad_norm_m
    grad_gate_a = jnp.sum(grad_middle * branch_a, 1)
    grad_branch_a = (grad_middle * mods[2][:, None, :]).astype(jnp.bfloat16)
    grad_proj = weight_grad(mixed_bf, grad_branch_a)
    grad_mixed = token_back(grad_branch_a, row_block[:attn_rows]).astype(jnp.bfloat16)
    grad_qkv = attention_back(qkv, log_total, grad_mixed, heads_local)
    normed_a, inv_a, input_a = modulated(hidden, mods[0], mods[1])
    grad_qkv_weight = weight_grad(input_a, grad_qkv)
    grad_input_a = input_sum(token_back(grad_qkv, col_block[:, :qkv_width]))
    grad_norm_a, grad_shift_a, grad_scale_a = modulate_back(grad_input_a, normed_a, inv_a, mods[1])
    grad_hidden = grad_middle + grad_norm_a
    grad_mods = jnp.concatenate(
        [grad_shift_a, grad_scale_a, grad_gate_a, grad_shift_m, grad_scale_m, grad_gate_m], -1
    )
    grad_col = jnp.concatenate([grad_qkv_weight, grad_fc1], 1)
    grad_row = jnp.concatenate([grad_proj, grad_fc2], 0)
    grad_col_bias = jnp.concatenate([token_total(grad_qkv), token_total(grad_pre)], 0)
    return (
        grad_hidden,
        grad_col,
        grad_row,
        grad_col_bias,
        token_total(grad_branch_a),
        token_total(grad_branch_m),
        grad_mods,
    )


def project(matrix, factor):
    return jnp.einsum("...nm,...mr->...nr", matrix, factor, precision=highest)


def project_back(matrix, basis):
    return jnp.einsum("...nm,...nr->...mr", matrix, basis, precision=highest)


def expand(basis, fresh):
    return jnp.einsum("...nr,...mr->...nm", basis, fresh, precision=highest)


def orthonormal(basis):
    columns = []
    for index in range(basis.shape[-1]):
        column = basis[..., index]
        for earlier in columns:
            column = column - jnp.sum(earlier * column, -1, keepdims=True) * earlier
        column = column * lax.rsqrt(jnp.sum(column * column, -1, keepdims=True) + ortho_eps)
        columns.append(column)
    return jnp.stack(columns, -1)


def squares(values):
    return jnp.sum(values * values)


def on_device(
    latents,
    gauss_noise,
    time_steps,
    labels,
    targets,
    w_col,
    w_row,
    w_cond,
    w_time,
    w_io,
    class_table,
    b_col,
    b_rep,
    mom_col,
    mom_row,
    mom_cond,
    mom_time,
    mom_io,
    mom_table,
    mom_bcol,
    mom_brep,
    err_col,
    err_row,
    err_io,
    fac_col,
    fac_row,
    fac_io,
):
    tensor_count = lax.axis_size("tensor")
    heads_local = HEADS // tensor_count
    start_fc2 = L * D
    start_cond = 2 * L * D
    start_first = start_cond + (6 * L + 2) * D
    start_second = start_first + D
    start_patch = start_first + 2 * D
    start_head = start_first + 3 * D
    full_col, full_row, full_cond, full_time, full_io, full_table = (
        lax.all_gather(w_col.astype(jnp.bfloat16), "dp", axis=1, tiled=True),
        lax.all_gather(w_row.astype(jnp.bfloat16), "dp", axis=2, tiled=True),
        lax.all_gather(w_cond.astype(jnp.bfloat16), "dp", axis=0, tiled=True),
        lax.all_gather(w_time.astype(jnp.bfloat16), "dp", axis=0, tiled=True),
        lax.all_gather(w_io.astype(jnp.bfloat16), "dp", axis=1, tiled=True),
        lax.all_gather(class_table.astype(jnp.bfloat16), "dp", axis=1, tiled=True),
    )
    local_count = latents.shape[0]
    per_micro = local_count // MB
    label_local = lax.dynamic_slice_in_dim(
        labels, lax.axis_index("dp") * local_count, local_count, 0
    )
    positions = position_table()
    classes = jnp.arange(CLASSES, dtype=jnp.int32)
    acc_col = [jnp.zeros(full_col.shape[1:], jnp.float32) for layer in range(L)]
    acc_row = [jnp.zeros(full_row.shape[1:], jnp.float32) for layer in range(L)]
    acc_bcol = [jnp.zeros(b_col.shape[1:], jnp.float32) for layer in range(L)]
    acc_proj = [jnp.zeros((D,), jnp.float32) for layer in range(L)]
    acc_fc2 = [jnp.zeros((D,), jnp.float32) for layer in range(L)]
    acc_cond = jnp.zeros(full_cond.shape, jnp.float32)
    acc_cond_bias = jnp.zeros((full_cond.shape[1],), jnp.float32)
    acc_first = jnp.zeros((FREQ, D), jnp.float32)
    acc_second = jnp.zeros((D, D), jnp.float32)
    acc_patch = jnp.zeros((D, PV), jnp.float32)
    acc_head = jnp.zeros((D, PV), jnp.float32)
    acc_small = jnp.zeros((3 * D + PV,), jnp.float32)
    acc_table = jnp.zeros((CLASSES, D), jnp.float32)
    loss_local = jnp.zeros((), jnp.float32)
    for micro in range(MB):
        lower = micro * per_micro
        steps = time_steps[lower : lower + per_micro]
        label_now = label_local[lower : lower + per_micro]
        steps_col = steps[:, None, None]
        mixed_in = (
            (1.0 - steps_col) * latents[lower : lower + per_micro]
            + steps_col * gauss_noise[lower : lower + per_micro]
        ).astype(jnp.bfloat16)
        features = frequency_features(steps).astype(jnp.bfloat16)
        first = (
            jnp.dot(features, full_time[:FREQ], preferred_element_type=jnp.float32)
            + b_rep[start_first:start_second]
        )
        first_act, first_pull = jax.vjp(jax.nn.silu, first)
        first_act = first_act.astype(jnp.bfloat16)
        second = (
            jnp.dot(first_act, full_time[FREQ:], preferred_element_type=jnp.float32)
            + b_rep[start_second:start_patch]
        )
        onehot = (label_now[:, None] == classes[None, :]).astype(jnp.float32)
        looked = jnp.dot(
            onehot.astype(jnp.bfloat16), full_table, preferred_element_type=jnp.float32
        )
        cond_act, cond_pull = jax.vjp(jax.nn.silu, second + looked)
        cond_act = cond_act.astype(jnp.bfloat16)
        mods_all = (
            jnp.dot(cond_act, full_cond, preferred_element_type=jnp.float32)
            + b_rep[start_cond:start_first]
        )
        hidden = (
            token_matmul(mixed_in, full_io[0].T) + b_rep[start_patch:start_head] + positions[None]
        )
        saved_list = []
        for layer in range(L):
            mods = [mods_all[:, (6 * layer + j) * D : (6 * layer + j + 1) * D] for j in range(6)]
            hidden, saved = layer_forward(
                hidden,
                full_col[layer],
                full_row[layer],
                b_col[layer],
                b_rep[layer * D : (layer + 1) * D],
                b_rep[start_fc2 + layer * D : start_fc2 + (layer + 1) * D],
                mods,
                heads_local,
            )
            saved_list.append(saved)
        base = 6 * L * D
        shift_final, scale_final = (
            mods_all[:, base : base + D],
            mods_all[:, base + D : base + 2 * D],
        )
        normed_f, inv_f, input_f = modulated(hidden, shift_final, scale_final)
        predicted = token_matmul(input_f, full_io[1]) + b_rep[start_head : start_head + PV]
        miss = predicted - targets[lower : lower + per_micro]
        loss_local = loss_local + jnp.sum(miss * miss)
        grad_pred = (2.0 * miss).astype(jnp.bfloat16)
        acc_head = acc_head + weight_grad(input_f, grad_pred)
        head_bias = token_total(grad_pred)
        grad_hidden, grad_shift_f, grad_scale_f = modulate_back(
            token_back(grad_pred, full_io[1]), normed_f, inv_f, scale_final
        )
        grad_mods_list = [None] * L
        for layer in reversed(range(L)):
            mods = [mods_all[:, (6 * layer + j) * D : (6 * layer + j + 1) * D] for j in range(6)]
            (
                grad_hidden,
                grad_col,
                grad_row,
                grad_col_bias,
                grad_proj_bias,
                grad_fc2_bias,
                grad_mods,
            ) = layer_backward(
                grad_hidden, saved_list[layer], full_col[layer], full_row[layer], mods, heads_local
            )
            acc_col[layer] = acc_col[layer] + grad_col
            acc_row[layer] = acc_row[layer] + grad_row
            acc_bcol[layer] = acc_bcol[layer] + grad_col_bias
            acc_proj[layer] = acc_proj[layer] + grad_proj_bias
            acc_fc2[layer] = acc_fc2[layer] + grad_fc2_bias
            grad_mods_list[layer] = grad_mods
        grad_embedded = grad_hidden.astype(jnp.bfloat16)
        acc_patch = acc_patch + weight_grad(grad_embedded, mixed_in)
        grad_mods_all = jnp.concatenate(grad_mods_list + [grad_shift_f, grad_scale_f], -1).astype(
            jnp.bfloat16
        )
        acc_cond = acc_cond + jnp.dot(cond_act.T, grad_mods_all, preferred_element_type=jnp.float32)
        acc_cond_bias = acc_cond_bias + jnp.sum(grad_mods_all.astype(jnp.float32), 0)
        grad_cond = cond_pull(
            jnp.dot(grad_mods_all, full_cond.T, preferred_element_type=jnp.float32)
        )[0]
        acc_table = acc_table + jnp.dot(onehot.T, grad_cond, precision=highest)
        grad_second = grad_cond.astype(jnp.bfloat16)
        acc_second = acc_second + jnp.dot(
            first_act.T, grad_second, preferred_element_type=jnp.float32
        )
        grad_first = first_pull(
            jnp.dot(grad_second, full_time[FREQ:].T, preferred_element_type=jnp.float32)
        )[0].astype(jnp.bfloat16)
        acc_first = acc_first + jnp.dot(features.T, grad_first, preferred_element_type=jnp.float32)
        acc_small = acc_small + jnp.concatenate(
            [
                jnp.sum(grad_first.astype(jnp.float32), 0),
                jnp.sum(grad_second.astype(jnp.float32), 0),
                token_total(grad_embedded),
                head_bias,
            ],
            0,
        )
    matrix_io = jnp.stack([acc_patch, acc_head], 0) + err_io
    matrix_col = jnp.stack(acc_col, 0) + err_col
    matrix_row = jnp.stack(acc_row, 0) + err_row
    left_col, left_row, left_io = lax.psum(
        (project(matrix_col, fac_col), project(matrix_row, fac_row), project(matrix_io, fac_io)),
        "dp",
    )
    left_col = orthonormal(left_col)
    left_row = orthonormal(left_row)
    left_io = orthonormal(left_io)
    right_col, right_row, right_io = lax.psum(
        (
            project_back(matrix_col, left_col),
            project_back(matrix_row, left_row),
            project_back(matrix_io, left_io),
        ),
        "dp",
    )
    approx_col = expand(left_col, right_col)
    approx_row = expand(left_row, right_row)
    approx_io = expand(left_io, right_io)
    brep_local = jnp.concatenate(
        [jnp.concatenate(acc_proj, 0), jnp.concatenate(acc_fc2, 0), acc_cond_bias, acc_small], 0
    )
    time_local = jnp.concatenate([acc_first, acc_second], 0)
    position = lax.axis_index("dp")
    loss_total, bcol_grad, brep_grad, table_grad, cond_grad, time_grad = lax.psum(
        (loss_local, jnp.stack(acc_bcol, 0), brep_local, acc_table, acc_cond, time_local), "dp"
    )
    shared_squares = squares(cond_grad) + squares(time_grad) + squares(table_grad)
    cond_share = lax.dynamic_slice_in_dim(cond_grad, position * w_cond.shape[0], w_cond.shape[0], 0)
    time_share = lax.dynamic_slice_in_dim(time_grad, position * w_time.shape[0], w_time.shape[0], 0)
    table_share = lax.dynamic_slice_in_dim(
        table_grad, position * class_table.shape[1], class_table.shape[1], 1
    )
    split_part = squares(approx_col) + squares(approx_row) + squares(bcol_grad)
    whole_part = shared_squares + squares(approx_io) + squares(brep_grad)
    clip_norm = jnp.sqrt(lax.psum(split_part, "tensor") + whole_part)
    scaling = jnp.minimum(1.0, clip_limit / clip_norm)

    def advance(weight, momentum, gradient):
        moved = momentum_decay * momentum + scaling * gradient
        return (weight - learn_rate * moved, moved)

    next_w_col, next_mom_col = advance(
        w_col,
        mom_col,
        lax.dynamic_slice_in_dim(approx_col, position * w_col.shape[1], w_col.shape[1], 1),
    )
    next_w_row, next_mom_row = advance(
        w_row,
        mom_row,
        lax.dynamic_slice_in_dim(approx_row, position * w_row.shape[2], w_row.shape[2], 2),
    )
    next_w_cond, next_mom_cond = advance(w_cond, mom_cond, cond_share)
    next_w_time, next_mom_time = advance(w_time, mom_time, time_share)
    next_w_io, next_mom_io = advance(
        w_io,
        mom_io,
        lax.dynamic_slice_in_dim(approx_io, position * w_io.shape[1], w_io.shape[1], 1),
    )
    next_table, next_mom_table = advance(class_table, mom_table, table_share)
    next_b_col, next_mom_bcol = advance(b_col, mom_bcol, bcol_grad)
    next_b_rep, next_mom_brep = advance(b_rep, mom_brep, brep_grad)
    next_err_col = matrix_col - approx_col
    next_err_row = matrix_row - approx_row
    next_err_io = matrix_io - approx_io
    return (
        loss_total,
        clip_norm,
        next_w_col,
        next_w_row,
        next_w_cond,
        next_w_time,
        next_w_io,
        next_table,
        next_b_col,
        next_b_rep,
        next_mom_col,
        next_mom_row,
        next_mom_cond,
        next_mom_time,
        next_mom_io,
        next_mom_table,
        next_mom_bcol,
        next_mom_brep,
        next_err_col,
        next_err_row,
        next_err_io,
        right_col,
        right_row,
        right_io,
    )


def solution(mesh):
    placed = (
        P("dp", None, None),
        P("dp", None, None),
        P("dp"),
        P(),
        P("dp", None, None),
        P(None, "dp", "tensor"),
        P(None, "tensor", "dp"),
        P("dp", None),
        P("dp", None),
        P(None, "dp", None),
        P(None, "dp"),
        P(None, "tensor"),
        P(),
        P(None, "dp", "tensor"),
        P(None, "tensor", "dp"),
        P("dp", None),
        P("dp", None),
        P(None, "dp", None),
        P(None, "dp"),
        P(None, "tensor"),
        P(),
        P("dp", None, "tensor"),
        P("dp", "tensor", None),
        P("dp", None, None),
        P(None, "tensor", None),
        P(None, "tensor", None),
        P(),
    )
    return jax.shard_map(
        on_device,
        mesh=mesh,
        in_specs=placed,
        out_specs=(
            P(),
            P(),
            P(None, "dp", "tensor"),
            P(None, "tensor", "dp"),
            P("dp", None),
            P("dp", None),
            P(None, "dp", None),
            P(None, "dp"),
            P(None, "tensor"),
            P(),
            P(None, "dp", "tensor"),
            P(None, "tensor", "dp"),
            P("dp", None),
            P("dp", None),
            P(None, "dp", None),
            P(None, "dp"),
            P(None, "tensor"),
            P(),
            P("dp", None, "tensor"),
            P("dp", "tensor", None),
            P("dp", None, None),
            P(None, "tensor", None),
            P(None, "tensor", None),
            P(),
        ),
        check_vma=False,
    )
```

profile of v0, /device:TPU:1, one launch (start us, length us, event | category | flops | bytes accessed | tf_op | source)
XLA Modules:
  0.0 1422.8 jit_solution(10580160241936548010)
XLA Ops:
  13.7 36.1 %all_gather.18 = bf16[2,384,16]{2,0,1:T(2,128)(2,1)S(1)} all-gather(bf16[2,24,16]{2,0,1:T(2,128)(2,1)S(1)} %copy.767), channel_id=1, replica_groups=mesh['dp'=16,'tensor'=2] {'dp'}, dimensions={1}, use_global_device_ids=true | all-gather | bytes 26112 | tf_op jit(solution)/shard_map/all_gather | solution.py:274
  58.6 32.7 %all_gather.19 = bf16[640,384]{1,0:T(8,128)(2,1)S(1)} all-gather(bf16[40,384]{1,0:T(8,128)(2,1)S(1)} %convert_element_type.450), channel_id=1, replica_groups=mesh['dp'=16,'tensor'=2] {'dp'}, dimensions={0}, use_global_device_ids=true | all-gather | bytes 522240 | tf_op jit(solution)/shard_map/all_gather | solution.py:273
  92.2 38.5 %all_gather.20 = bf16[1000,384]{0,1:T(8,128)(2,1)S(1)} all-gather(bf16[1000,24]{0,1:T(8,128)(2,1)S(1)} %convert_element_type.454), channel_id=1, replica_groups=mesh['dp'=16,'tensor'=2] {'dp'}, dimensions={1}, use_global_device_ids=true | all-gather | bytes 816000 | tf_op jit(solution)/shard_map/all_gather | solution.py:275
  135.4 4.6 all-gather.6.cloned.1.call-done
  140.0 7.0 fusion.302
  147.0 6.5 copy.909
  153.5 62.9 %all-gather.4.cloned.1.call-done = bf16[384,5376]{1,0:T(8,128)(2,1)} async-done(((bf16[24,5376]{1,0:T(8,128)(2,1)}), bf16[384,5376]{1,0:T(8,128)(2,1)}) %all-gather.4.cloned.1.call-update) | async-done | bytes 4128784 | tf_op jit(solution)/shard_map/all_gather | solution.py:272
  243.3 6.1 fusion.303
  252.3 22.0 %all-reduce.33.cloned.1.call-done = (f32[8,256,384]{2,1,0:T(8,128)}, f32[8,256,384]{2,1,0:T(8,128)}) async-done(((f32[8,256,384]{2,1,0:T(8,128)}, f32[8,256,384]{2,1,0:T(8,128)}), (f32[8,256,384]{2,1,0:T(8,128)}, f32[8,256,384]{2,1,0:T(8,128)})) %all-reduce.33.cloned.1.call-update) | async-done | bytes 6291472 | tf_op jit(solution)/shard_map/psum | solution.py:71
  274.3 5.7 fusion.300
  284.0 6.7 multiply_convert_fusion.5
  299.9 6.5 copy.915
  306.4 25.0 %all-reduce.31.cloned.1.call-done = (f32[8,256,384]{2,1,0:T(8,128)}, f32[8,256,384]{2,1,0:T(8,128)}) async-done(((f32[8,256,384]{2,1,0:T(8,128)}, f32[8,256,384]{2,1,0:T(8,128)}), (f32[8,256,384]{2,1,0:T(8,128)}, f32[8,256,384]{2,1,0:T(8,128)})) %all-reduce.31.cloned.1.call-update) | async-done | bytes 6291472 | tf_op jit(solution)/shard_map/psum | solution.py:71
  331.5 4.9 fusion.298
  362.7 29.0 %all-reduce.29.cloned.1.call-done = (f32[8,256,384]{2,1,0:T(8,128)}, f32[8,256,384]{2,1,0:T(8,128)}) async-done(((f32[8,256,384]{2,1,0:T(8,128)}, f32[8,256,384]{2,1,0:T(8,128)}), (f32[8,256,384]{2,1,0:T(8,128)}, f32[8,256,384]{2,1,0:T(8,128)})) %all-reduce.29.cloned.1.call-update) | async-done | bytes 6291472 | tf_op jit(solution)/shard_map/psum | solution.py:71
  391.7 5.6 fusion.296
  401.4 6.6 multiply_convert_fusion.4
  418.0 30.6 %all-reduce.27.cloned.1.call-done = (f32[8,256,384]{2,1,0:T(8,128)}, f32[8,256,384]{2,1,0:T(8,128)}) async-done(((f32[8,256,384]{2,1,0:T(8,128)}, f32[8,256,384]{2,1,0:T(8,128)}), (f32[8,256,384]{2,1,0:T(8,128)}, f32[8,256,384]{2,1,0:T(8,128)})) %all-reduce.27.cloned.1.call-update) | async-done | bytes 6291472 | tf_op jit(solution)/shard_map/psum | solution.py:71
  448.6 4.9 fusion.294
  470.4 6.0 convert_reduce_fusion
  480.5 6.0 convert_reduce_fusion.1
  491.3 5.7 copy.826
  504.3 11.5 all-reduce.41.cloned.1.call-done
  523.6 8.7 multiply_reduce_fusion.12
  539.9 4.4 multiply_convert_fusion.1
  560.5 4.5 multiply_convert_fusion.3
  584.4 6.3 convolution_bitcast_fusion
  609.9 5.1 convolution_bitcast_fusion.9
  622.9 6.8 multiply_reduce_fusion.13
  631.1 9.2 convert_reduce_fusion.2
  644.5 6.0 convert_reduce_fusion.3
  664.5 5.7 convolution_bitcast_fusion.2
  687.7 9.0 multiply_reduce_fusion.14
  703.8 4.4 multiply_convert_fusion
  721.2 4.4 multiply_convert_fusion.2
  750.8 5.0 convolution_bitcast_fusion.11
  787.5 5.2 convolution_add_fusion
  799.8 102.3 %all-reduce.23.cloned.1.call-done = (f32[2,960,8]{1,0,2:T(2,128)}, f32[2,384,8]{1,0,2:T(2,128)}) async-done(((f32[2,960,8]{1,0,2:T(2,128)}, f32[2,384,8]{1,0,2:T(2,128)}), (f32[2,960,8]{1,0,2:T(2,128)}, f32[2,384,8]{1,0,2:T(2,128)})) %all-reduce.23.cloned.1.call-update) | async-done | bytes 86032 | tf_op jit(solution)/shard_map/psum | solution.py:411
  927.3 4.6 fusion.188
  933.0 63.7 %all-reduce.42 = (f32[]{:T(128)}, f32[2,384,8]{1,0,2:T(2,128)S(1)}, f32[2,384,8]{1,2,0:T(8,128)}, f32[2,1344]{1,0:T(2,128)}, f32[2,16,8]{1,2,0:T(8,128)}, /*index=5*/f32[8080]{0:T(1024)}) all-reduce(f32[]{:T(128)S(6)} %add.1148, f32[2,384,8]{1,0,2:T(2,128)S(1)} %copy-done.234, ...), channel_id=1, replica_groups=mesh['dp'=16,'tensor'=2] {'dp'}, use_global_device_ids=true, to_apply=%region_38.39 | all-reduce | flops 23313 | bytes 186504 | tf_op jit(solution)/shard_map/psum | solution.py:434
  1000.6 6.2 fusion.197
  1019.2 7.7 fusion.280
  1027.0 315.8 %all-reduce.25.cloned.1.call-done = (f32[2,1344,8]{1,2,0:T(8,128)}, f32[384,5376]{1,0:T(8,128)}, f32[640,384]{1,0:T(8,128)}, f32[1000,384]{1,0:T(8,128)}) async-done(((f32[2,1344,8]{1,2,0:T(8,128)}, f32[384,5376]{1,0:T(8,128)}, f32[640,384]{1,0:T(8,128)}, f32[1000,384]{1,0:T(8,128)}), (f32[2,1344,8]{1,2,0:T(8,128)}, f32[384,5376]{1,0:T(8,128)}, f32[640,384]{1,0:T(8,128)}, ...) | async-done | bytes 10862608 | tf_op jit(solution)/shard_map/psum | solution.py:418
  1342.7 7.0 multiply_reduce_fusion.9
  1349.8 5.9 copy.852
  1355.7 7.0 fusion.282
  1362.7 6.2 multiply_reduce_fusion
  1372.8 5.7 copy.859
  (1170 shorter events, 408.0 us)
Async XLA Ops:
  7.2 751.5 %copy-start = (f32[2,1344,8]{1,2,0:T(8,128)S(1)}, f32[2,1344,8]{1,2,0:T(8,128)}, u32[]{:S(2)}) copy-start(f32[2,1344,8]{1,2,0:T(8,128)} %param.51) | copy-start | bytes 258052
  7.2 43.7 %copy-start.169 = (f32[40,384]{1,0:T(8,128)S(1)}, f32[40,384]{1,0:T(8,128)}, u32[]{:S(2)}) copy-start(f32[40,384]{1,0:T(8,128)} %param.35) | copy-start | bytes 184324
  7.2 43.7 %copy-start.154 = (f32[1000,24]{0,1:T(8,128)S(1)}, f32[1000,24]{0,1:T(8,128)}, u32[]{:S(2)}) copy-start(f32[1000,24]{0,1:T(8,128)} %param.37) | copy-start | bytes 288004
  7.2 43.8 %copy-start.179 = (f32[8080]{0:T(1024)S(1)}, f32[8080]{0:T(1024)}, u32[]{:S(2)}) copy-start(f32[8080]{0:T(1024)} %param.39) | copy-start | bytes 96964
  7.2 43.8 %copy-start.348 = (s32[256]{0:T(256)S(1)}, s32[256]{0:T(256)}, u32[]{:S(2)}) copy-start(s32[256]{0:T(256)} %param.30) | copy-start | bytes 3076
  7.3 46.6 %copy-start.343 = (f32[16]{0:T(128)S(1)}, f32[16]{0:T(128)}, u32[]{:S(2)}) copy-start(f32[16]{0:T(128)} %param.29) | copy-start | bytes 196
  7.3 47.4 %copy-start.168 = (f32[16,256,16]{1,2,0:T(8,128)S(1)}, f32[16,256,16]{1,2,0:T(8,128)}, u32[]{:S(2)}) copy-start(f32[16,256,16]{1,2,0:T(8,128)} %param.27) | copy-start | bytes 786436
  7.3 47.4 %copy-start.167 = (f32[16,256,16]{1,2,0:T(8,128)S(1)}, f32[16,256,16]{1,2,0:T(8,128)}, u32[]{:S(2)}) copy-start(f32[16,256,16]{1,2,0:T(8,128)} %param.28) | copy-start | bytes 786436
  7.3 124.0 %all-gather.8.cloned.1.call-start = ((), (), s32[]{:S(2)}) async-start(), calls=%async_computation.2 | async-start | bytes 1671168 | tf_op jit(solution)/shard_map/all_gather | solution.py:271
  9.2 130.8 %all-gather.6.cloned.1.call-start = ((), (), s32[]{:S(2)}) async-start(), calls=%async_computation.1 | async-start | bytes 2297856 | tf_op jit(solution)/shard_map/all_gather | solution.py:270
  11.0 205.3 %all-gather.4.cloned.1.call-start = ((), (), s32[]{:S(2)}) async-start(), calls=%async_computation | async-start | bytes 4386816 | tf_op jit(solution)/shard_map/all_gather | solution.py:272
  12.9 261.4 %all-reduce.33.cloned.1.call-start = ((), (), s32[]{:S(2)}) async-start(), calls=%async_computation.8 | async-start | bytes 12582912 | tf_op jit(solution)/shard_map/psum | solution.py:71
  52.5 167.6 %copy-start.341 = (f32[576]{0:T(1024)}, f32[576]{0:T(1024)S(1)}, u32[]{:S(2)}) copy-start(f32[576]{0:T(1024)S(1)} %get-tuple-element.236) | copy-start | bytes 6916
  53.8 76.9 %copy-start.328 = (s32[8]{0:T(128)}, s32[8]{0:T(128)S(1)}, u32[]{:S(2)}) copy-start(s32[8]{0:T(128)S(1)} %get-tuple-element.590) | copy-start | bytes 100
  53.8 77.2 %copy-start.330 = (s32[8]{0:T(128)}, s32[8]{0:T(128)S(1)}, u32[]{:S(2)}) copy-start(s32[8]{0:T(128)S(1)} %get-tuple-element.591) | copy-start | bytes 100
  54.1 37.4 %copy-start.300 = (bf16[8,128]{1,0:T(8,128)(2,1)}, bf16[8,128]{1,0:T(8,128)(2,1)S(1)}, u32[]{:S(2)}) copy-start(bf16[8,128]{1,0:T(8,128)(2,1)S(1)} %get-tuple-element.593) | copy-start | bytes 6148
  56.3 163.8 %copy-start.198 = (f32[8,256]{1,0:T(8,128)}, f32[8,256]{1,0:T(8,128)S(1)}, u32[]{:S(2)}) copy-start(f32[8,256]{1,0:T(8,128)S(1)} %broadcast_multiply_fusion.29) | copy-start | bytes 24580
  57.0 163.1 %copy-start.245 = (f32[8,256]{1,0:T(8,128)}, f32[8,256]{1,0:T(8,128)S(1)}, u32[]{:S(2)}) copy-start(f32[8,256]{1,0:T(8,128)S(1)} %add_rsqrt_fusion.4) | copy-start | bytes 24580
  57.9 171.6 %copy-start.17 = (f32[8,256,384]{2,1,0:T(8,128)}, f32[8,256,384]{2,1,0:T(8,128)S(1)}, u32[]{:S(2)}) copy-start(f32[8,256,384]{2,1,0:T(8,128)S(1)} %get-tuple-element.601) | copy-start | bytes 9437188
  57.9 171.6 %copy-start.196 = (f32[8,256]{1,0:T(8,128)}, f32[8,256]{1,0:T(8,128)S(1)}, u32[]{:S(2)}) copy-start(f32[8,256]{1,0:T(8,128)S(1)} %broadcast_multiply_fusion.34) | copy-start | bytes 24580
  58.6 170.9 %copy-start.243 = (f32[8,256]{1,0:T(8,128)}, f32[8,256]{1,0:T(8,128)S(1)}, u32[]{:S(2)}) copy-start(f32[8,256]{1,0:T(8,128)S(1)} %add_rsqrt_fusion.9) | copy-start | bytes 24580
  91.5 55.6 %copy-start.256 = (f32[8,384]{1,0:T(8,128)}, f32[8,384]{1,0:T(8,128)S(1)}, u32[]{:S(2)}) copy-start(f32[8,384]{1,0:T(8,128)S(1)} %convolution_add_fusion.10) | copy-start | bytes 36868
  91.6 39.1 %copy-start.258 = (f32[8,384]{1,0:T(8,128)}, f32[8,384]{1,0:T(8,128)S(1)}, u32[]{:S(2)}) copy-start(f32[8,384]{1,0:T(8,128)S(1)} %convolution_add_fusion.13) | copy-start | bytes 36868
  131.0 85.4 %copy-start.177 = (f32[8,384]{1,0:T(8,128)}, f32[8,384]{1,0:T(8,128)S(1)}, u32[]{:S(2)}) copy-start(f32[8,384]{1,0:T(8,128)S(1)} %convolution_add_fusion.8) | copy-start | bytes 36868
  131.3 96.0 %copy-start.171 = (f32[8,384]{1,0:T(8,128)}, f32[8,384]{1,0:T(8,128)S(1)}, u32[]{:S(2)}) copy-start(f32[8,384]{1,0:T(8,128)S(1)} %convolution_add_fusion.11) | copy-start | bytes 36868
  135.4 104.1 %copy-start.85 = (bf16[1,192,384]{2,1,0:T(8,128)(2,1)}, bf16[1,192,384]{2,1,0:T(8,128)(2,1)S(1)}, u32[]{:S(2)}) copy-start(bf16[1,192,384]{2,1,0:T(8,128)(2,1)S(1)} %copy.913) | copy-start | bytes 442372
  220.0 54.3 %copy-start.209 = (f32[8,384]{1,0:T(8,128)}, f32[8,384]{1,0:T(8,128)S(1)}, u32[]{:S(2)}) copy-start(f32[8,384]{1,0:T(8,128)S(1)} %get-tuple-element.546) | copy-start | bytes 36868
  220.0 63.9 %copy-start.173 = (f32[8,384]{1,0:T(8,128)}, f32[8,384]{1,0:T(8,128)S(1)}, u32[]{:S(2)}) copy-start(f32[8,384]{1,0:T(8,128)S(1)} %get-tuple-element.542) | copy-start | bytes 36868
  220.1 117.0 %copy-start.207 = (f32[8,384]{1,0:T(8,128)}, f32[8,384]{1,0:T(8,128)S(1)}, u32[]{:S(2)}) copy-start(f32[8,384]{1,0:T(8,128)S(1)} %get-tuple-element.539) | copy-start | bytes 36868
  229.5 44.8 %copy-start.211 = (f32[8,384]{1,0:T(8,128)}, f32[8,384]{1,0:T(8,128)S(1)}, u32[]{:S(2)}) copy-start(f32[8,384]{1,0:T(8,128)S(1)} %get-tuple-element.560) | copy-start | bytes 36868
  229.5 51.9 %copy-start.157 = (f32[8,384]{1,0:T(8,128)}, f32[8,384]{1,0:T(8,128)S(1)}, u32[]{:S(2)}) copy-start(f32[8,384]{1,0:T(8,128)S(1)} %get-tuple-element.556) | copy-start | bytes 36868
  229.5 51.9 %copy-start.213 = (f32[8,384]{1,0:T(8,128)}, f32[8,384]{1,0:T(8,128)S(1)}, u32[]{:S(2)}) copy-start(f32[8,384]{1,0:T(8,128)S(1)} %get-tuple-element.555) | copy-start | bytes 36868
  229.5 116.7 %copy-start.204 = (f32[8,384]{1,0:T(8,128)}, f32[8,384]{1,0:T(8,128)S(1)}, u32[]{:S(2)}) copy-start(f32[8,384]{1,0:T(8,128)S(1)} %get-tuple-element.553) | copy-start | bytes 36868
  241.9 89.6 %all-reduce.31.cloned.1.call-start = ((), (), s32[]{:S(2)}) async-start(), calls=%async_computation.7 | async-start | bytes 12582912 | tf_op jit(solution)/shard_map/psum | solution.py:71
  243.3 40.7 %copy-start.332 = (f32[768]{0:T(1024)}, f32[768]{0:T(1024)S(1)}, u32[]{:S(2)}) copy-start(f32[768]{0:T(1024)S(1)} %get-tuple-element.234) | copy-start | bytes 9220
  243.3 158.0 %copy-start.334 = (f32[768]{0:T(1024)}, f32[768]{0:T(1024)S(1)}, u32[]{:S(2)}) copy-start(f32[768]{0:T(1024)S(1)} %get-tuple-element.233) | copy-start | bytes 9220
  280.0 51.5 %copy-start.5 = (f32[8,256,384]{2,1,0:T(8,128)}, f32[8,256,384]{2,1,0:T(8,128)S(1)}, u32[]{:S(2)}) copy-start(f32[8,256,384]{2,1,0:T(8,128)S(1)} %get-tuple-element.581) | copy-start | bytes 9437188
  298.1 93.6 %all-reduce.29.cloned.1.call-start = ((), (), s32[]{:S(2)}) async-start(), calls=%async_computation.6 | async-start | bytes 12582912 | tf_op jit(solution)/shard_map/psum | solution.py:71
  358.3 90.3 %all-reduce.27.cloned.1.call-start = ((), (), s32[]{:S(2)}) async-start(), calls=%async_computation.5 | async-start | bytes 12582912 | tf_op jit(solution)/shard_map/psum | solution.py:71
  415.1 100.7 %all-reduce.41.cloned.1.call-start = ((), (), s32[]{:S(2)}) async-start(), calls=%async_computation.12 | async-start | bytes 6291456 | tf_op jit(solution)/shard_map/psum | solution.py:75
  491.2 123.8 %all-reduce.39.cloned.1.call-start = ((), (), s32[]{:S(2)}) async-start(), calls=%async_computation.11 | async-start | bytes 6291456 | tf_op jit(solution)/shard_map/psum | solution.py:75
  578.0 101.9 %all-reduce.37.cloned.1.call-start = ((), (), s32[]{:S(2)}) async-start(), calls=%async_computation.10 | async-start | bytes 6291456 | tf_op jit(solution)/shard_map/psum | solution.py:75
  655.3 109.5 %all-reduce.35.cloned.1.call-start = ((), (), s32[]{:S(2)}) async-start(), calls=%async_computation.9 | async-start | bytes 6291456 | tf_op jit(solution)/shard_map/psum | solution.py:75
  740.1 162.0 %all-reduce.23.cloned.1.call-start = ((), (), s32[]{:S(2)}) async-start(), calls=%async_computation.3 | async-start | bytes 180224 | tf_op jit(solution)/shard_map/psum | solution.py:411
  799.6 543.1 %all-reduce.25.cloned.1.call-start = ((), (), s32[]{:S(2)}) async-start(), calls=%async_computation.4 | async-start | bytes 21733376 | tf_op jit(solution)/shard_map/psum | solution.py:418
  799.8 105.7 %copy-start.265 = (f32[8080]{0:T(1024)}, f32[8080]{0:T(1024)S(1)}, u32[]{:S(2)}) copy-start(f32[8080]{0:T(1024)S(1)} %fusion.227) | copy-start | bytes 96964
  927.3 73.3 %copy-start.27 = (f32[1,384,1344]{2,1,0:T(8,128)S(1)}, f32[1,384,1344]{2,1,0:T(8,128)}, u32[]{:S(2)}) copy-start(f32[1,384,1344]{2,1,0:T(8,128)} %maximum_add_fusion.3) | copy-start | bytes 6193156
  1019.2 323.5 %copy-start.203 = (f32[2,384,8]{1,0,2:T(2,128)S(1)}, f32[2,384,8]{1,0,2:T(2,128)}, u32[]{:S(2)}) copy-start(f32[2,384,8]{1,0,2:T(2,128)} %copy-done.202) | copy-start | bytes 73732
  (331 other events, 1834.4 us)
Sparse Core Ops, SparseCore 0:
  11.5 60.0 all-gather.7
  74.9 65.0 all-gather.5
  143.4 72.9 all-gather.3
  242.0 32.2 all-reduce.32
  298.2 33.2 all-reduce.30
  358.4 33.2 all-reduce.28
  415.2 33.3 all-reduce.26
  491.3 24.4 all-reduce.40
  578.1 24.4 all-reduce.38
  655.4 24.4 all-reduce.36
  740.2 24.4 all-reduce.34
  799.8 102.2 all-reduce.22
  1007.0 335.7 all-reduce.24
where the time goes:
time: 1430 us; the launch traced here: 1420 us
  waiting for transfers between devices  604 us (42%)
  matrix products  274 us (19%)
  other arithmetic  214 us (15%)
  blocking collectives  174 us (12%)
  local copies, waits for them, and re-layouts  129 us (9%)
  between operations  26.7 us (2%)
    psum x1, waiting for transfers between devices, on_device(): lax.psum((project_back(matrix_col, left_col), project_back(matrix_row, le...  316 us
    psum x4, waiting for transfers between devices, row_sum(): return lax.psum(partial_value, 'tensor')  107 us
    psum x1, waiting for transfers between devices, on_device(): lax.psum((project(matrix_col, fac_col), project(matrix_row, fac_row), pro...  102 us
    unnamed x783, local copies, waits for them, and re-layouts  96.9 us
    psum x1, blocking collectives, on_device(): lax.psum((loss_local, jnp.stack(acc_bcol, 0), brep_local, acc_table, acc_...  63.7 us
    all_gather x1, waiting for transfers between devices, on_device(): lax.all_gather(w_cond.astype(jnp.bfloat16), 'dp', axis=0, tiled=True)  62.9 us
    dot_general x18, matrix products, token_back(): jnp.einsum('ntf,df->ntd', grad, right, preferred_element_type=jnp.float32)  60.1 us
    dot_general x20, matrix products, weight_grad(): jnp.einsum('ntd,ntf->df', left, grad, preferred_element_type=jnp.float32)  56.1 us
  transfers between devices with their start and end apart: 13, of which 10 were waited for; matrix products, arithmetic and copies ran while one was open for 12% of the time, Pallas kernels for 0%

commit v1 on v0

v1 whole, which is shorter than its diff:
```python
import jax
import jax.numpy as jnp
import numpy as np
from jax import lax
from jax.experimental import pallas as pl
from jax.experimental.pallas import tpu as pltpu
from jax.sharding import PartitionSpec as P

D = 384
HEADS = 6
HD = 64
MLP = 1536
CLASSES = 1000
FREQ = 256
PV = 16
GRID = 16
L = 2
TOK = 256
RANK = 8

norm_eps = 1e-06
ortho_eps = 1e-06
clip_limit = 1.0
momentum_decay = 0.9
learn_rate = 4.0

HALF = D // 2
HMLP = MLP // 2
QKV_S = 3 * HALF
COL_S = QKV_S + HMLP
ROW_S = HALF + HMLP
OFF_W2 = HMLP
OFF_Q = 2 * HMLP
GATH = 2 * HMLP + 4 * HALF

f32 = jnp.float32
bf16 = jnp.bfloat16
highest = lax.Precision.HIGHEST
NN = (((1,), (0,)), ((), ()))
NT = (((1,), (1,)), ((), ()))
TN = (((0,), (0,)), ((), ()))


def dot(left, right, dims=NN):
    return lax.dot_general(left, right, dims, preferred_element_type=f32)


def dot_full(left, right, dims=NN):
    return lax.dot_general(left, right, dims, precision=highest, preferred_element_type=f32)


def position_table():
    quarter = D // 4
    omega = 1.0 / 10000.0 ** (np.arange(quarter, dtype=np.float32) / quarter)
    index = np.arange(TOK)
    across = (index % GRID).astype(np.float32)[:, None] * omega[None, :].astype(np.float32)
    down = (index // GRID).astype(np.float32)[:, None] * omega[None, :].astype(np.float32)
    table = np.concatenate([np.sin(across), np.cos(across), np.sin(down), np.cos(down)], 1)
    return table.astype(np.float32)


def frequency_features(steps):
    half = FREQ // 2
    rates = jnp.exp(-jnp.log(10000.0) * jnp.arange(half, dtype=f32) / half)
    angles = steps[:, None] * rates[None, :]
    return jnp.concatenate([jnp.cos(angles), jnp.sin(angles)], 1)


def normalize(values):
    centered = values - jnp.mean(values, -1, keepdims=True)
    inv_std = lax.rsqrt(jnp.mean(centered * centered, -1, keepdims=True) + norm_eps)
    return centered * inv_std, inv_std


def norm_back(grad, normed, inv_std):
    mean_grad = jnp.mean(grad, -1, keepdims=True)
    mean_mixed = jnp.mean(grad * normed, -1, keepdims=True)
    return inv_std * (grad - mean_grad - normed * mean_mixed)


def token_sum(values):
    return jnp.sum(values, 0, keepdims=True)


def assemble(own, other, wqkv, wo):
    for part in range(3):
        start = OFF_Q + part * HALF
        wqkv[:, part * D : part * D + HALF] = own[:, start : start + HALF]
        wqkv[:, part * D + HALF : (part + 1) * D] = other[:, start : start + HALF]
    start = OFF_Q + 3 * HALF
    wo[:, :HALF] = own[:, start : start + HALF]
    wo[:, HALF:] = other[:, start : start + HALF]


def head_mask(which):
    lane = lax.broadcasted_iota(jnp.int32, (1, 2 * HD), 1)
    return (lane < HD) if which == 0 else (lane >= HD)


def keep(values, mask):
    return jnp.where(mask, values, jnp.zeros_like(values))


def layer_forward(x, mod, own, other, wqkv, wo, bqkv, bfc1, bproj, bfc2, put):
    normed, inv_a = normalize(x)
    input_a = (normed * (1.0 + mod(1)) + mod(0)).astype(bf16)
    qkv = (dot(input_a, wqkv[...]) + bqkv).astype(bf16)
    query = qkv[:, :D] * jnp.asarray(HD**-0.5, bf16)
    keyed = qkv[:, D : 2 * D]
    valued = qkv[:, 2 * D :]
    put("input_a", input_a)
    put("query", query)
    put("keyed", keyed)
    put("valued", valued)
    pieces = []
    for pair in range(HEADS // 2):
        span = slice(pair * 2 * HD, (pair + 1) * 2 * HD)
        q_pair, k_pair, v_pair = query[:, span], keyed[:, span], valued[:, span]
        total = None
        for which in range(2):
            mask = head_mask(which)
            scores = dot(keep(q_pair, mask), k_pair, NT)
            expo = jnp.exp(scores - jnp.max(scores, -1, keepdims=True))
            probs = expo * (1.0 / jnp.sum(expo, -1, keepdims=True))
            put("probs", probs, 2 * pair + which)
            mixed = dot(probs.astype(bf16), keep(v_pair, mask))
            total = mixed if total is None else total + mixed
        pieces.append(total.astype(bf16))
    mixed = jnp.concatenate(pieces, 1)
    put("mixed", mixed)
    branch_a = dot(mixed, wo[...], NT) + bproj
    put("branch_a", branch_a)
    middle = x + mod(2) * branch_a
    put("middle", middle)
    normed_m, inv_m = normalize(middle)
    input_m = (normed_m * (1.0 + mod(4)) + mod(3)).astype(bf16)
    put("input_m", input_m)
    branch_m = bfc2
    for side, weights in enumerate((own, other)):
        pre = dot(input_m, weights[:, :HMLP]) + bfc1[:, side * HMLP : (side + 1) * HMLP]
        squared = pre * pre
        coef = np.float32(np.sqrt(2.0 / np.pi))
        tanh = jnp.tanh(pre * (coef + np.float32(coef * 0.044715) * squared))
        half = 0.5 * (1.0 + tanh)
        acted = (pre * half).astype(bf16)
        slope = half + (0.5 * pre) * (1.0 - tanh * tanh) * (
            coef + np.float32(3.0 * 0.044715 * coef) * squared
        )
        put("acted", acted, side)
        put("slope", slope, side)
        branch_m = branch_m + dot(acted, weights[:, OFF_W2 : OFF_W2 + HMLP], NT)
    put("branch_m", branch_m)
    return middle + mod(5) * branch_m


def layer_backward(grad, x, mod, own, other, wqkv, wo, take, rows, stash, mods_out, bias):
    branch_m = take("branch_m")
    mods_out(5, token_sum(grad * branch_m))
    grad_branch_m = (grad * mod(5)).astype(bf16)
    bias("fc2", 0, grad_branch_m)
    stash["dym"][rows, :] = grad_branch_m
    middle = take("middle")
    normed_m, inv_m = normalize(middle)
    grad_input = None
    for side, weights in enumerate((own, other)):
        span = slice(side * HMLP, (side + 1) * HMLP)
        grad_acted = dot(grad_branch_m, weights[:, OFF_W2 : OFF_W2 + HMLP])
        grad_pre = (grad_acted * take("slope", side)).astype(bf16)
        stash["dg"][rows, span] = grad_pre
        bias("fc1", side * HMLP, grad_pre)
        part = dot(grad_pre, weights[:, :HMLP], NT)
        grad_input = part if grad_input is None else grad_input + part
    mods_out(3, token_sum(grad_input))
    mods_out(4, token_sum(grad_input * normed_m))
    grad_middle = grad + norm_back(grad_input * (1.0 + mod(4)), normed_m, inv_m)
    branch_a = take("branch_a")
    mods_out(2, token_sum(grad_middle * branch_a))
    grad_branch_a = (grad_middle * mod(2)).astype(bf16)
    bias("proj", 0, grad_branch_a)
    stash["dya"][rows, :] = grad_branch_a
    grad_mixed = dot(grad_branch_a, wo[...]).astype(bf16)
    query, keyed, valued = take("query"), take("keyed"), take("valued")
    grads_q, grads_k, grads_v = [], [], []
    for pair in range(HEADS // 2):
        span = slice(pair * 2 * HD, (pair + 1) * 2 * HD)
        q_pair, k_pair, v_pair = query[:, span], keyed[:, span], valued[:, span]
        g_pair = grad_mixed[:, span]
        grad_q = grad_k = grad_v = None
        for which in range(2):
            mask = head_mask(which)
            probs = take("probs", 2 * pair + which)
            g_head = keep(g_pair, mask)
            grad_probs = dot(g_head, v_pair, NT)
            row_dot = jnp.sum(grad_probs * probs, -1, keepdims=True)
            grad_scores = (probs * (grad_probs - row_dot)).astype(bf16)
            part_q = dot(grad_scores, keep(k_pair, mask))
            part_k = dot(grad_scores, keep(q_pair, mask), TN)
            part_v = dot(probs.astype(bf16), g_head, TN)
            grad_q = part_q if grad_q is None else grad_q + part_q
            grad_k = part_k if grad_k is None else grad_k + part_k
            grad_v = part_v if grad_v is None else grad_v + part_v
        grads_q.append((grad_q * HD**-0.5).astype(bf16))
        grads_k.append(grad_k.astype(bf16))
        grads_v.append(grad_v.astype(bf16))
    grad_qkv = jnp.concatenate(grads_q + grads_k + grads_v, 1)
    stash["dqkv"][rows, :] = grad_qkv
    bias("qkv", 0, grad_qkv)
    grad_input_a = dot(grad_qkv, wqkv[...], NT)
    normed, inv_a = normalize(x)
    mods_out(0, token_sum(grad_input_a))
    mods_out(1, token_sum(grad_input_a * normed))
    return grad_middle + norm_back(grad_input_a * (1.0 + mod(1)), normed, inv_a)


def weight_grads(input_a, input_m, mixed, acted, stash, col_own, col_other, row_own, row_other):
    for part in range(3):
        piece = dot(input_a[...], stash["dqkv"][:, part * D : (part + 1) * D], TN)
        for side, out in enumerate((col_own, col_other)):
            for head in range(HEADS // 2):
                start = side * HALF + head * HD
                place = (3 * head + part) * HD
                out[:, place : place + HD] = piece[:, start : start + HD]
    for side, out in enumerate((col_own, col_other)):
        out[:, QKV_S:] = dot(input_m[...], stash["dg"][:, side * HMLP : (side + 1) * HMLP], TN)
    piece = dot(mixed[...], stash["dya"][...], TN)
    for side, out in enumerate((row_own, row_other)):
        out[:HALF, :] = piece[side * HALF : (side + 1) * HALF, :]
        out[HALF:, :] = dot(acted[:, side * HMLP : (side + 1) * HMLP], stash["dym"][...], TN)


BIAS = {"qkv": 0, "fc1": 3 * D, "proj": 3 * D + MLP, "fc2": 4 * D + MLP}
BIAS_WIDTH = 5 * D + MLP


def forward_kernel(xt, mods, wpatch, posbias, own, other, bqkv, bfc1, bproj, bfc2,
                   x0, query, keyed, valued, probs, branch_a, middle, slope, branch_m, mixed, acted,
                   input_a, input_m, x2, wqkv, wo):
    @pl.when(pl.program_id(0) == 0)
    def _():
        assemble(own, other, wqkv, wo)

    named = dict(query=query, keyed=keyed, valued=valued, mixed=mixed, branch_a=branch_a,
                 middle=middle, branch_m=branch_m, input_a=input_a, input_m=input_m)

    def put(name, value, index=None):
        if name == "probs":
            probs[0, index] = value
        elif name == "acted":
            acted[0, :, index * HMLP : (index + 1) * HMLP] = value
        elif name == "slope":
            slope[0, :, index * HMLP : (index + 1) * HMLP] = value
        else:
            named[name][0] = value

    x = dot(xt[0], wpatch[...], NT) + posbias[...]
    x0[0] = x
    x2[0] = layer_forward(x, lambda j: mods[0, j : j + 1, :], own, other, wqkv, wo, bqkv[...],
                          bfc1[...], bproj[...], bfc2[...], put)


def middle_kernel(x2, mods, own, other, bqkv, bfc1, bproj, bfc2, whead, bhead, targets,
                  dx, dmods, col_own, col_other, row_own, row_other, dbias, dhead, dbhead, loss,
                  wqkv, wo, query, keyed, valued, probs, mixed, branch_a, middle, acted, slope,
                  branch_m, input_a, input_m, s_dqkv, s_dg, s_dya, s_dym):
    step = pl.program_id(0)

    @pl.when(step == 0)
    def _():
        assemble(own, other, wqkv, wo)
        dbias[...] = jnp.zeros_like(dbias)
        dhead[...] = jnp.zeros_like(dhead)
        dbhead[...] = jnp.zeros_like(dbhead)
        loss[...] = jnp.zeros_like(loss)

    rows = pl.ds(pl.multiple_of(step * TOK, TOK), TOK)
    stacked = dict(mixed=mixed, input_a=input_a, input_m=input_m)
    single = dict(query=query, keyed=keyed, valued=valued, branch_a=branch_a, middle=middle,
                  branch_m=branch_m)

    def put(name, value, index=None):
        if name == "probs":
            probs[index] = value
        elif name == "acted":
            acted[rows, index * HMLP : (index + 1) * HMLP] = value
        elif name == "slope":
            slope[:, index * HMLP : (index + 1) * HMLP] = value
        elif name in stacked:
            stacked[name][rows, :] = value
        else:
            single[name][...] = value

    def take(name, index=None):
        if name == "probs":
            return probs[index]
        if name == "slope":
            return slope[:, index * HMLP : (index + 1) * HMLP]
        return single[name][...]

    def mod(j):
        return mods[0, 6 + j : 7 + j, :]

    x = x2[0]
    x = layer_forward(x, mod, own, other, wqkv, wo, bqkv[...], bfc1[...], bproj[...], bfc2[...], put)
    normed, inv_std = normalize(x)
    input_f = (normed * (1.0 + mod(7)) + mod(6)).astype(bf16)
    miss = dot(input_f, whead[...]) + bhead[...] - targets[0]
    loss[...] += jnp.sum(miss * miss).reshape(1, 1)
    grad_pred = (2.0 * miss).astype(bf16)
    dhead[...] += dot(grad_pred, input_f, TN)
    dbhead[...] += token_sum(grad_pred.astype(f32))
    grad_input = dot(grad_pred, whead[...], NT)
    dmods[0, 6:7, :] = token_sum(grad_input)
    dmods[0, 7:8, :] = token_sum(grad_input * normed)
    grad = norm_back(grad_input * (1.0 + mod(7)), normed, inv_std)

    def mods_out(j, value):
        dmods[0, j : j + 1, :] = value

    def bias(name, start, value):
        at = BIAS[name] + start
        dbias[:, at : at + value.shape[1]] += token_sum(value.astype(f32))

    stash = dict(dqkv=s_dqkv, dg=s_dg, dya=s_dya, dym=s_dym)
    dx[0] = layer_backward(grad, x2[0], mod, own, other, wqkv, wo, take, rows, stash, mods_out, bias)

    @pl.when(step == pl.num_programs(0) - 1)
    def _():
        weight_grads(input_a, input_m, mixed, acted, stash, col_own, col_other, row_own, row_other)


def last_kernel(dx, x0, mods, own, other, xt, query, keyed, valued, probs, branch_a, middle,
                slope, branch_m, mixed, acted, input_a, input_m,
                dmods, col_own, col_other, row_own, row_other, dbias, dpatch, dbpatch,
                wqkv, wo, a_input_a, a_input_m, a_mixed, a_acted, s_dqkv, s_dg, s_dya, s_dym, sems):
    step = pl.program_id(0)
    pairs = ((input_a, a_input_a), (input_m, a_input_m), (mixed, a_mixed), (acted, a_acted))
    copies = [pltpu.make_async_copy(src, dst, sems.at[i]) for i, (src, dst) in enumerate(pairs)]

    @pl.when(step == 0)
    def _():
        assemble(own, other, wqkv, wo)
        dbias[...] = jnp.zeros_like(dbias)
        dpatch[...] = jnp.zeros_like(dpatch)
        dbpatch[...] = jnp.zeros_like(dbpatch)
        for copy in copies:
            copy.start()

    rows = pl.ds(pl.multiple_of(step * TOK, TOK), TOK)
    single = dict(query=query, keyed=keyed, valued=valued, branch_a=branch_a, middle=middle,
                  branch_m=branch_m)

    def take(name, index=None):
        if name == "probs":
            return probs[0, index]
        if name == "slope":
            return slope[0, :, index * HMLP : (index + 1) * HMLP]
        return single[name][0]

    def mods_out(j, value):
        dmods[0, j : j + 1, :] = value

    def bias(name, start, value):
        at = BIAS[name] + start
        dbias[:, at : at + value.shape[1]] += token_sum(value.astype(f32))

    stash = dict(dqkv=s_dqkv, dg=s_dg, dya=s_dya, dym=s_dym)
    grad = layer_backward(dx[0], x0[0], lambda j: mods[0, j : j + 1, :], own, other, wqkv, wo,
                          take, rows, stash, mods_out, bias)
    grad = grad.astype(bf16)
    dpatch[...] += dot(xt[0], grad, TN)
    dbpatch[...] += token_sum(grad.astype(f32))

    @pl.when(step == pl.num_programs(0) - 1)
    def _():
        for copy in copies:
            copy.wait()
        weight_grads(a_input_a, a_input_m, a_mixed, a_acted, stash,
                     col_own, col_other, row_own, row_other)


def per_latent(*shape):
    zeros = (0,) * len(shape)
    return pl.BlockSpec((1,) + shape, lambda n: (n,) + zeros)


def fixed(*shape):
    zeros = (0,) * len(shape)
    return pl.BlockSpec(shape, lambda n: zeros, pipeline_mode=pl.Buffered(1))


def params():
    return pltpu.CompilerParams(dimension_semantics=("arbitrary",), vmem_limit_bytes=62 * 2**20)


SAVED = [
    ("query", (TOK, D), bf16), ("keyed", (TOK, D), bf16), ("valued", (TOK, D), bf16),
    ("probs", (HEADS, TOK, TOK), f32), ("branch_a", (TOK, D), f32), ("middle", (TOK, D), f32),
    ("slope", (TOK, MLP), f32), ("branch_m", (TOK, D), f32), ("mixed", (TOK, D), bf16),
    ("acted", (TOK, MLP), bf16), ("input_a", (TOK, D), bf16), ("input_m", (TOK, D), bf16),
]
WEIGHT_SPECS = [fixed(D, GATH), fixed(D, GATH)]
BIAS_SPECS = [fixed(1, 3 * D), fixed(1, MLP), fixed(1, D), fixed(1, D)]
GRAD_SHAPES = [(D, COL_S), (D, COL_S), (ROW_S, D), (ROW_S, D)]
WEIGHT_SCRATCH = [pltpu.VMEM((D, 3 * D), bf16), pltpu.VMEM((D, D), bf16)]


def stash_scratch(count):
    rows = count * TOK
    return [pltpu.VMEM((rows, 3 * D), bf16), pltpu.VMEM((rows, MLP), bf16),
            pltpu.VMEM((rows, D), bf16), pltpu.VMEM((rows, D), bf16)]


def cost(flops, nbytes, count):
    return pl.CostEstimate(flops=int(flops * count), bytes_accessed=int(nbytes * count),
                           transcendentals=int(2e6 * count))


def run_forward(xt, mods, wpatch, posbias, own, other, biases):
    count = xt.shape[0]
    outs = [("x0", (TOK, D), f32)] + SAVED + [("x2", (TOK, D), f32)]
    return pl.pallas_call(
        forward_kernel,
        grid=(count,),
        in_specs=[per_latent(TOK, PV), per_latent(14, D), fixed(D, PV), fixed(TOK, D)]
        + WEIGHT_SPECS + BIAS_SPECS,
        out_specs=[per_latent(*shape) for _, shape, _ in outs],
        out_shape=[jax.ShapeDtypeStruct((count,) + shape, kind) for _, shape, kind in outs],
        scratch_shapes=WEIGHT_SCRATCH,
        compiler_params=params(),
        cost_estimate=cost(1.0e9, 6e6, count),
        name="forward_first",
    )(xt, mods, wpatch, posbias, own, other, *biases)


def run_middle(x2, mods, own, other, biases, whead, bhead, targets):
    count = x2.shape[0]
    rows = count * TOK
    outs = [((count, TOK, D), per_latent(TOK, D)), ((count, 8, D), per_latent(8, D))]
    outs += [(shape, fixed(*shape)) for shape in GRAD_SHAPES]
    outs += [((1, BIAS_WIDTH), fixed(1, BIAS_WIDTH)), ((PV, D), fixed(PV, D)),
             ((1, PV), fixed(1, PV)), ((1, 1), fixed(1, 1))]
    return pl.pallas_call(
        middle_kernel,
        grid=(count,),
        in_specs=[per_latent(TOK, D), per_latent(14, D)] + WEIGHT_SPECS + BIAS_SPECS
        + [fixed(D, PV), fixed(1, PV), per_latent(TOK, PV)],
        out_specs=[spec for _, spec in outs],
        out_shape=[jax.ShapeDtypeStruct(shape, f32) for shape, _ in outs],
        scratch_shapes=WEIGHT_SCRATCH
        + [pltpu.VMEM((TOK, D), bf16)] * 3
        + [pltpu.VMEM((HEADS, TOK, TOK), f32), pltpu.VMEM((rows, D), bf16),
           pltpu.VMEM((TOK, D), f32), pltpu.VMEM((TOK, D), f32), pltpu.VMEM((rows, MLP), bf16),
           pltpu.VMEM((TOK, MLP), f32), pltpu.VMEM((TOK, D), f32),
           pltpu.VMEM((rows, D), bf16), pltpu.VMEM((rows, D), bf16)]
        + stash_scratch(count),
        compiler_params=params(),
        cost_estimate=cost(3.2e9, 3e6, count),
        name="layer_second",
    )(x2, mods, own, other, *biases, whead, bhead, targets)


def run_last(dx, x0, mods, own, other, xt, saved):
    count = dx.shape[0]
    rows = count * TOK
    outs = [((count, 6, D), per_latent(6, D))]
    outs += [(shape, fixed(*shape)) for shape in GRAD_SHAPES]
    outs += [((1, BIAS_WIDTH), fixed(1, BIAS_WIDTH)), ((PV, D), fixed(PV, D)), ((1, D), fixed(1, D))]
    return pl.pallas_call(
        last_kernel,
        grid=(count,),
        in_specs=[per_latent(TOK, D), per_latent(TOK, D), per_latent(14, D)] + WEIGHT_SPECS
        + [per_latent(TOK, PV)] + [per_latent(*shape) for _, shape, _ in SAVED[:-4]]
        + [pl.BlockSpec(memory_space=pl.ANY)] * 4,
        out_specs=[spec for _, spec in outs],
        out_shape=[jax.ShapeDtypeStruct(shape, f32) for shape, _ in outs],
        scratch_shapes=WEIGHT_SCRATCH
        + [pltpu.VMEM((rows, D), bf16)] * 3 + [pltpu.VMEM((rows, MLP), bf16)]
        + stash_scratch(count) + [pltpu.SemaphoreType.DMA((4,))],
        compiler_params=params(),
        cost_estimate=cost(2.2e9, 8e6, count),
        name="backward_first",
    )(dx, x0, mods, own, other, xt, *saved[:-4], *[v.reshape(rows, -1) for v in saved[-4:]])


def project_kernel(err_col, own_col, got_col, err_row, own_row, got_row, fac_col, fac_row,
                   mat_col, mat_row, left_col, left_row):
    matrix = err_col[0] + (own_col[...] + got_col[...])
    mat_col[...] = matrix
    left_col[...] = dot_full(fac_col[...], matrix, NT)
    matrix = err_row[0] + (own_row[...] + got_row[...])
    mat_row[...] = matrix
    left_row[...] = dot_full(fac_row[...], matrix, NT)


def run_project(layer, err_col, own_col, got_col, err_row, own_row, got_row, fac_col, fac_row):
    whole = [fixed(D, COL_S), fixed(D, COL_S)]
    tall = [fixed(ROW_S, D), fixed(ROW_S, D)]
    shapes = [(D, COL_S), (ROW_S, D), (RANK, D), (RANK, ROW_S)]
    return pl.pallas_call(
        project_kernel,
        grid=(1,),
        in_specs=[pl.BlockSpec((1, D, COL_S), lambda n: (layer, 0, 0))] + whole
        + [pl.BlockSpec((1, ROW_S, D), lambda n: (layer, 0, 0))] + tall
        + [fixed(RANK, COL_S), fixed(RANK, D)],
        out_specs=[fixed(*shape) for shape in shapes],
        out_shape=[jax.ShapeDtypeStruct(shape, f32) for shape in shapes],
        compiler_params=params(),
        name="left_factors",
    )(err_col, own_col, got_col, err_row, own_row, got_row, fac_col, fac_row)


def ortho_kernel(basis, out):
    columns = []
    for index in range(RANK):
        column = basis[index]
        for earlier in columns:
            column = column - jnp.sum(earlier * column, -1, keepdims=True) * earlier
        column = column * lax.rsqrt(jnp.sum(column * column, -1, keepdims=True) + ortho_eps)
        out[index] = column
        columns.append(column)


def run_ortho(basis):
    return pl.pallas_call(
        ortho_kernel,
        out_shape=jax.ShapeDtypeStruct(basis.shape, f32),
        name="orthonormal",
    )(basis)


def right_kernel(mat_col0, mat_row0, mat_col1, mat_row1, left_col, left_row, right_col, right_row):
    for layer, (col, row) in enumerate(((mat_col0, mat_row0), (mat_col1, mat_row1))):
        right_col[layer] = dot_full(left_col[layer], col[...])
        right_row[layer] = dot_full(left_row[layer], row[...])


def run_right(mats, left_col, left_row):
    return pl.pallas_call(
        right_kernel,
        out_shape=[jax.ShapeDtypeStruct((L, RANK, COL_S), f32),
                   jax.ShapeDtypeStruct((L, RANK, D), f32)],
        compiler_params=pltpu.CompilerParams(vmem_limit_bytes=62 * 2**20),
        name="right_factors",
    )(*mats, left_col, left_row)


def error_kernel(mat_col0, mat_row0, mat_col1, mat_row1, left_col, left_row, right_col, right_row,
                 err_col, err_row):
    for layer, (col, row) in enumerate(((mat_col0, mat_row0), (mat_col1, mat_row1))):
        err_col[layer] = col[...] - dot_full(left_col[layer], right_col[layer], TN)
        err_row[layer] = row[...] - dot_full(left_row[layer], right_row[layer], TN)


def run_error(mats, left_col, left_row, right_col, right_row):
    return pl.pallas_call(
        error_kernel,
        out_shape=[jax.ShapeDtypeStruct((L, D, COL_S), f32),
                   jax.ShapeDtypeStruct((L, ROW_S, D), f32)],
        compiler_params=pltpu.CompilerParams(vmem_limit_bytes=62 * 2**20),
        name="next_errors",
    )(*mats, left_col, left_row, right_col, right_row)


def swap(values):
    return lax.ppermute(values, "tensor", [(0, 1), (1, 0)])


def spread(values, axes):
    count = lax.axis_size(axes)
    sent = jnp.broadcast_to(values[None], (count,) + values.shape)
    return lax.all_to_all(sent, axes, 0, 0, tiled=True)


def flat_sum(parts):
    count = lax.axis_size("dp")
    sizes = [int(np.prod(part.shape)) for part in parts]
    total = sum(sizes)
    unit = count * 128
    padded = -(-total // unit) * unit
    flat = jnp.concatenate([part.reshape(-1) for part in parts] + [jnp.zeros((padded - total,), f32)])
    got = lax.all_to_all(flat.reshape(count, padded // unit, 128), "dp", 0, 0, tiled=True)
    share = jnp.sum(got, 0)
    flat = spread(share, "dp").reshape(-1)
    outs, at = [], 0
    for part, size in zip(parts, sizes):
        outs.append(flat[at : at + size].reshape(part.shape))
        at += size
    return outs


def squares(values):
    return jnp.sum(values * values)


def on_device(
    latents, gauss_noise, time_steps, labels, targets,
    w_col, w_row, w_cond, w_time, w_io, class_table, b_col, b_rep,
    mom_col, mom_row, mom_cond, mom_time, mom_io, mom_table, mom_bcol, mom_brep,
    err_col, err_row, err_io, fac_col, fac_row, fac_io,
):
    both = ("dp", "tensor")
    n_dp = lax.axis_size("dp")
    index_dp = lax.axis_index("dp")
    index_t = lax.axis_index("tensor")
    n_all = labels.shape[0]
    count = latents.shape[0] // 2
    rows = w_col.shape[1]
    start_fc2 = L * D
    start_cond = 2 * L * D
    n_mods = (6 * L + 2) * D
    start_first = start_cond + n_mods
    start_second = start_first + D
    start_patch = start_first + 2 * D
    start_head = start_first + 3 * D

    heads = HEADS // 2
    qkv_sh = w_col[:, :, :QKV_S].reshape(L, rows, heads, 3, HD).transpose(0, 1, 3, 2, 4)
    row_sh = w_row.transpose(0, 2, 1)
    shard = jnp.concatenate(
        [w_col[:, :, QKV_S:], row_sh[:, :, HALF:], qkv_sh.reshape(L, rows, QKV_S), row_sh[:, :, :HALF]],
        2,
    ).astype(bf16)
    own = [lax.all_gather(shard[layer], "dp", axis=0, tiled=True) for layer in range(L)]
    other = [swap(own[layer]) for layer in range(L)]
    bcol_other = swap(b_col)

    steps_all = spread(time_steps, "dp").reshape(n_all)
    classes = jnp.arange(CLASSES, dtype=jnp.int32)
    onehot = labels[:, None] == classes[None, :]
    looked = dot(onehot.astype(bf16), class_table.astype(bf16)).astype(bf16)
    looked = spread(looked, "dp").transpose(1, 0, 2).reshape(n_all, D)
    full_time = spread(w_time.astype(bf16), "dp").reshape(FREQ + D, D)
    full_io = spread(w_io.astype(bf16), "dp").transpose(1, 0, 2, 3).reshape(2, D, PV)
    half_cols = n_mods // 2
    block = half_cols // n_dp
    cond_half = lax.dynamic_slice_in_dim(w_cond, index_t * half_cols, half_cols, 1).astype(bf16)
    cond_cols = lax.all_to_all(
        cond_half.reshape(rows, n_dp, block).transpose(1, 0, 2), "dp", 0, 0, tiled=True
    ).reshape(D, block)
    features = frequency_features(steps_all).astype(bf16)
    first = dot(features, full_time[:FREQ]) + b_rep[start_first:start_second]
    first_act, first_pull = jax.vjp(jax.nn.silu, first)
    first_act = first_act.astype(bf16)
    second = dot(first_act, full_time[FREQ:]) + b_rep[start_second:start_patch]
    cond = second + looked.astype(f32)
    cond_act, cond_pull = jax.vjp(jax.nn.silu, cond)
    cond_act = cond_act.astype(bf16)
    mods_cols = dot(cond_act, cond_cols)
    mods = lax.all_to_all(mods_cols.reshape(2 * n_dp, count, block), both, 0, 0, tiled=True)
    mods = mods.reshape(n_dp, 2, count, block).transpose(2, 1, 0, 3).reshape(count, n_mods)
    mods = (mods + b_rep[start_cond:start_first]).reshape(count, 6 * L + 2, D)
    full_cond = lax.all_gather(w_cond.astype(bf16), "dp", axis=0, tiled=True)

    begin = index_t * count
    steps_own = lax.dynamic_slice_in_dim(time_steps, begin, count, 0)[:, None, None]
    xt = (
        (1.0 - steps_own) * lax.dynamic_slice_in_dim(latents, begin, count, 0)
        + steps_own * lax.dynamic_slice_in_dim(gauss_noise, begin, count, 0)
    ).astype(bf16)
    targets_own = lax.dynamic_slice_in_dim(targets, begin, count, 0)
    posbias = jnp.asarray(position_table()) + b_rep[start_patch:start_head]

    def layer_biases(layer):
        pair = []
        for values in (b_col[layer], bcol_other[layer]):
            pair.append(values[:QKV_S].reshape(heads, 3, HD).transpose(1, 0, 2).reshape(3, HALF))
        bqkv = jnp.concatenate(pair, 1).reshape(1, 3 * D)
        bfc1 = jnp.concatenate([b_col[layer, QKV_S:], bcol_other[layer, QKV_S:]])[None]
        bproj = b_rep[layer * D : (layer + 1) * D][None]
        bfc2 = b_rep[start_fc2 + layer * D : start_fc2 + (layer + 1) * D][None]
        return [bqkv, bfc1, bproj, bfc2]

    x0, *saved, x2 = run_forward(xt, mods, full_io[0], posbias, own[0], other[0], layer_biases(0))
    dx, dmods1, col_own1, col_oth1, row_own1, row_oth1, dbias1, dhead, dbhead, loss = run_middle(
        x2, mods, own[1], other[1], layer_biases(1), full_io[1],
        b_rep[start_head : start_head + PV][None], targets_own,
    )
    dmods0, col_own0, col_oth0, row_own0, row_oth0, dbias0, dpatch, dbpatch = run_last(
        dx, x0, mods, own[0], other[0], xt, saved
    )

    dmods = jnp.concatenate([dmods0, dmods1], 1).reshape(count, n_mods).astype(bf16)
    grad_cond_act = dot(dmods, full_cond, NT)
    mine = (index_dp * 2 + index_t) * count
    cond_own = lax.dynamic_slice_in_dim(cond, mine, count, 0)
    grad_cond = jax.vjp(jax.nn.silu, cond_own)[1](grad_cond_act)[0]
    grad_cond = spread(grad_cond, both).reshape(n_all, D)
    dmods_cols = lax.all_to_all(
        dmods.reshape(count, 2, n_dp, block).transpose(2, 1, 0, 3).reshape(2 * n_dp, count, block),
        both, 0, 0, tiled=True,
    ).reshape(n_all, block)
    cond_grad = dot(cond_act, dmods_cols, TN)
    cond_bias = jnp.sum(dmods_cols.astype(f32), 0)
    cond_part = lax.all_to_all(cond_grad.reshape(n_dp, rows, block), "dp", 0, 0, tiled=True)
    cond_part = cond_part.transpose(1, 0, 2).reshape(rows, half_cols)

    def both_halves(mine_half, axis):
        theirs = swap(mine_half)
        return jnp.where(
            index_t == 0,
            jnp.concatenate([mine_half, theirs], axis),
            jnp.concatenate([theirs, mine_half], axis),
        )

    cond_share = both_halves(cond_part, 1)
    table_share = dot_full(
        onehot.astype(f32), lax.dynamic_slice_in_dim(grad_cond, index_dp * rows, rows, 1), TN
    )
    grad_second = grad_cond.astype(bf16)
    grad_first = first_pull(dot(grad_second, full_time[FREQ:], NT))[0].astype(bf16)
    time_grad = jnp.concatenate([dot(features, grad_first, TN), dot(first_act, grad_second, TN)], 0)
    first_bias = jnp.sum(grad_first.astype(f32), 0)
    second_bias = jnp.sum(grad_second.astype(f32), 0)

    def side_bias(dbias, side):
        qkv = dbias[0, : 3 * D].reshape(3, 2, heads, HD)[:, side].transpose(1, 0, 2).reshape(QKV_S)
        return jnp.concatenate([qkv, dbias[0, 3 * D + side * HMLP : 3 * D + (side + 1) * HMLP]])

    small = jnp.concatenate(
        [dbias0[0, BIAS["proj"] :][:D], dbias1[0, BIAS["proj"] :][:D],
         dbias0[0, BIAS["fc2"] :], dbias1[0, BIAS["fc2"] :], dbpatch[0], dbhead[0], loss[0]]
    )
    io_t = jnp.stack([dpatch, dhead], 0)
    small_got, io_got, bias_got, col_got1, row_got1, col_got0, row_got0 = (
        swap(small), swap(io_t), swap(jnp.stack([side_bias(dbias0, 1), side_bias(dbias1, 1)])),
        swap(col_oth1), swap(row_oth1), swap(col_oth0), swap(row_oth0),
    )
    small = small + small_got
    bcol_part = jnp.stack([side_bias(dbias0, 0), side_bias(dbias1, 0)]) + bias_got
    fac_col_t = fac_col.transpose(0, 2, 1)
    fac_row_t = fac_row.transpose(0, 2, 1)
    fac_io_t = fac_io.transpose(0, 2, 1)
    mat_col1, mat_row1, left_col1, left_row1 = run_project(
        1, err_col, col_own1, col_got1, err_row, row_own1, row_got1, fac_col_t[1], fac_row_t[1]
    )
    mat_col0, mat_row0, left_col0, left_row0 = run_project(
        0, err_col, col_own0, col_got0, err_row, row_own0, row_got0, fac_col_t[0], fac_row_t[0]
    )
    mats = (mat_col0, mat_row0, mat_col1, mat_row1)
    mat_io = (io_t + io_got) + err_io.transpose(0, 2, 1)
    left_io = jnp.einsum("lrp,lpd->lrd", fac_io_t, mat_io, precision=highest)
    left_col, left_row, left_io, bcol_grad, small = flat_sum(
        [jnp.stack([left_col0, left_col1]), jnp.stack([left_row0, left_row1]), left_io, bcol_part, small]
    )
    pad = ((0, 0), (0, 0), (0, ROW_S - D))
    basis = jnp.concatenate([jnp.pad(left_col, pad), left_row, jnp.pad(left_io, pad)], 0)
    basis = run_ortho(basis.transpose(1, 0, 2)).transpose(1, 0, 2)
    left_col, left_row, left_io = basis[:2, :, :D], basis[2:4], basis[4:, :, :D]
    right_col, right_row = run_right(mats, left_col, left_row)
    right_io = jnp.einsum("lrd,lpd->lrp", left_io, mat_io, precision=highest)
    part_squares = jnp.stack([squares(cond_grad), squares(table_share)])
    right_col, right_row, right_io, part_squares = flat_sum(
        [right_col, right_row, right_io, part_squares]
    )
    next_err_col, next_err_row = run_error(mats, left_col, left_row, right_col, right_row)
    approx_io = jnp.einsum("lrd,lrp->ldp", left_io, right_io, precision=highest)
    next_err_io = mat_io.transpose(0, 2, 1) - approx_io

    def gram_squares(left, right):
        gram_left = jnp.einsum("lrn,lsn->lrs", left, left, precision=highest)
        gram_right = jnp.einsum("lrn,lsn->lrs", right, right, precision=highest)
        return jnp.sum(gram_left * gram_right)

    cond_bias = spread(cond_bias, both).reshape(n_dp, 2, block).transpose(1, 0, 2).reshape(n_mods)
    loss_total = small[5 * D + PV]
    brep_grad = jnp.concatenate(
        [small[: 4 * D], cond_bias, first_bias, second_bias, small[4 * D : 5 * D + PV]]
    )
    split_part = (
        gram_squares(left_col, right_col) + gram_squares(left_row, right_row)
        + squares(bcol_grad) + part_squares[0]
    )
    whole_part = squares(approx_io) + squares(brep_grad) + squares(time_grad) + part_squares[1]
    clip_norm = jnp.sqrt(split_part + swap(split_part) + whole_part)
    scaling = jnp.minimum(1.0, clip_limit / clip_norm)

    def advance(weight, momentum, gradient):
        moved = momentum_decay * momentum + scaling * gradient
        return (weight - learn_rate * moved, moved)

    at = index_dp * rows
    grad_col = jnp.einsum(
        "lrn,lrm->lnm", lax.dynamic_slice_in_dim(left_col, at, rows, 2), right_col, precision=highest
    )
    grad_row = jnp.einsum(
        "lrn,lrm->lnm", left_row, lax.dynamic_slice_in_dim(right_row, at, rows, 2), precision=highest
    )
    next_w_col, next_mom_col = advance(w_col, mom_col, grad_col)
    next_w_row, next_mom_row = advance(w_row, mom_row, grad_row)
    next_w_cond, next_mom_cond = advance(w_cond, mom_cond, cond_share)
    time_rows = w_time.shape[0]
    next_w_time, next_mom_time = advance(
        w_time, mom_time, lax.dynamic_slice_in_dim(time_grad, index_dp * time_rows, time_rows, 0)
    )
    next_w_io, next_mom_io = advance(
        w_io, mom_io, lax.dynamic_slice_in_dim(approx_io, at, rows, 1)
    )
    next_table, next_mom_table = advance(class_table, mom_table, table_share)
    next_b_col, next_mom_bcol = advance(b_col, mom_bcol, bcol_grad)
    next_b_rep, next_mom_brep = advance(b_rep, mom_brep, brep_grad)
    return (
        loss_total, clip_norm,
        next_w_col, next_w_row, next_w_cond, next_w_time, next_w_io, next_table, next_b_col, next_b_rep,
        next_mom_col, next_mom_row, next_mom_cond, next_mom_time, next_mom_io, next_mom_table,
        next_mom_bcol, next_mom_brep,
        next_err_col, next_err_row, next_err_io,
        right_col.transpose(0, 2, 1), right_row.transpose(0, 2, 1), right_io.transpose(0, 2, 1),
    )


def solution(mesh):
    weights = (
        P(None, "dp", "tensor"), P(None, "tensor", "dp"), P("dp", None), P("dp", None),
        P(None, "dp", None), P(None, "dp"), P(None, "tensor"), P(),
    )
    errors = (P("dp", None, "tensor"), P("dp", "tensor", None), P("dp", None, None))
    factors = (P(None, "tensor", None), P(None, "tensor", None), P())
    rows = P("dp", None, None)
    return jax.shard_map(
        on_device,
        mesh=mesh,
        in_specs=(rows, rows, P("dp"), P(), rows) + weights + weights + errors + factors,
        out_specs=(P(), P()) + weights + weights + errors + factors,
        check_vma=False,
    )
```

time: 1430 us -> 543 us (0.38)
  waiting for transfers between devices: 604 us -> 112 us
  matrix products: 274 us -> 19.3 us
  Pallas kernels: 0 us -> 207 us
  other arithmetic: 214 us -> 25.4 us
  blocking collectives: 174 us -> 0 us
  starting transfers between devices: 0.76 us -> 82.3 us
  local copies, waits for them, and re-layouts: 129 us -> 63.9 us
    psum x10 -> x0, waiting for transfers between devices: 537 us -> none  [the longest x1 316 us: on_device(): lax.psum((project_back(matrix_col, left_col), project_back(matrix_row, le...]
    dot_general x111 -> x19, matrix products: 274 us -> 19.3 us  [the longest x9 8.92 us: dot(): return lax.dot_general(left, right, dims, preferred_element_type=f32)]
    pallas_call x0 -> x8, Pallas kernels: none -> 207 us  [the longest x1 85.9 us: run_middle(): pl.pallas_call(middle_kernel, grid=(count,), in_specs=[per_latent(TOK, D)...]
    reduce_sum x99 -> x4, other arithmetic: 132 us -> 0.14 us  [the longest x1 0.05 us: on_device(): second_bias = jnp.sum(grad_second.astype(f32), 0)]
    all_gather x3 -> x0, blocking collectives: 107 us -> none  [the longest x1 38.5 us: on_device(): lax.all_gather(class_table.astype(jnp.bfloat16), 'dp', axis=1, tiled=True)]
    unnamed x783 -> x119, local copies, waits for them, and re-layouts: 96.9 us -> 18.7 us
    all_to_all x0 -> x14, starting transfers between devices: none -> 70.8 us  [the longest x8 43 us: spread(): return lax.all_to_all(sent, axes, 0, 0, tiled=True)]
    psum x2 -> x0, blocking collectives: 67.2 us -> none  [the longest x1 63.7 us: on_device(): lax.psum((loss_local, jnp.stack(acc_bcol, 0), brep_local, acc_table, acc_...]
  transfers between devices with their start and end apart: 13 -> 29, of which waited for: 10 -> 12; matrix products, arithmetic and copies ran while one was open for 12% -> 19% of each run, Pallas kernels for 0% -> 39%
where the time goes in v1:
time: 543 us; the launch traced here: 532 us
  Pallas kernels  207 us (38%)
  waiting for transfers between devices  112 us (21%)
  starting transfers between devices  82.3 us (15%)
  local copies, waits for them, and re-layouts  63.9 us (12%)
  other arithmetic  25.4 us (5%)
  between operations  22.6 us (4%)
  matrix products  19.3 us (4%)
    pallas_call x1, Pallas kernels, run_middle(): pl.pallas_call(middle_kernel, grid=(count,), in_specs=[per_latent(TOK, D)...  85.9 us
    all_gather x2, waiting for transfers between devices, on_device(): lax.all_gather(shard[layer], 'dp', axis=0, tiled=True)  57.5 us
    pallas_call x1, Pallas kernels, run_last(): pl.pallas_call(last_kernel, grid=(count,), in_specs=[per_latent(TOK, D),...  46.6 us
    all_to_all x8, starting transfers between devices, spread(): return lax.all_to_all(sent, axes, 0, 0, tiled=True)  43 us
    pallas_call x1, Pallas kernels, run_forward(): pl.pallas_call(forward_kernel, grid=(count,), in_specs=[per_latent(TOK, P...  37.4 us
    all_to_all x8, waiting for transfers between devices, spread(): return lax.all_to_all(sent, axes, 0, 0, tiled=True)  20.9 us
    unnamed x119, local copies, waits for them, and re-layouts  18.7 us
    pallas_call x2, Pallas kernels, run_project(): pl.pallas_call(project_kernel, grid=(1,), in_specs=[pl.BlockSpec((1, D, C...  16.1 us
  transfers between devices with their start and end apart: 29, of which 12 were waited for; matrix products, arithmetic and copies ran while one was open for 19% of the time, Pallas kernels for 39%

profile of v1, /device:TPU:1, one launch (start us, length us, event | category | flops | bytes accessed | tf_op | source)
XLA Modules:
  0.0 532.3 jit_solution(13795104014825149740)
XLA Ops:
  12.1 7.4 %all-to-all-start = ((f32[16,1,16]{2,1,0:T(1,128)}), f32[16,1,16]{2,1,0:T(1,128)S(1)}, u32[]{:S(2)}, u32[]{:S(2)}) async-start(f32[16,1,16]{2,1,0:T(1,128)} %broadcast_in_dim.34), calls=%async_computation | async-start | bytes 16384 | tf_op jit(solution)/shard_map/all_to_all | solution.py:571
  28.0 1.7 add_convert_fusion.xt
  30.5 6.6 %all-to-all-start.5 = ((bf16[16,2,384]{2,1,0:T(2,128)(2,1)}), bf16[16,2,384]{2,1,0:T(2,128)(2,1)S(1)}, u32[]{:S(2)}, u32[]{:S(2)}) async-start(bf16[16,2,384]{2,1,0:T(2,128)(2,1)} %reshape.351), calls=%async_computation.5 | async-start | bytes 49152 | tf_op jit(solution)/shard_map/all_to_all | solution.py:571
  37.2 6.2 %all-to-all-done.5 = bf16[16,2,384]{2,1,0:T(2,128)(2,1)S(1)} async-done(((bf16[16,2,384]{2,1,0:T(2,128)(2,1)}), bf16[16,2,384]{2,1,0:T(2,128)(2,1)S(1)}, u32[]{:S(2)}, u32[]{:S(2)}) %all-to-all-start.5) | async-done | bytes 24608 | tf_op jit(solution)/shard_map/all_to_all | solution.py:571
  44.1 3.5 all-to-all-start.2
  47.7 6.9 %all-to-all-done.2 = bf16[16,256,24]{1,2,0:T(8,128)(2,1)S(1)} async-done(((bf16[16,256,24]{1,2,0:T(8,128)(2,1)}), bf16[16,256,24]{1,2,0:T(8,128)(2,1)S(1)}, u32[]{:S(2)}, u32[]{:S(2)}) %all-to-all-start.2) | async-done | bytes 196640 | tf_op jit(solution)/shard_map/all_to_all | solution.py:571
  55.4 4.6 all-to-all-start.1
  65.2 5.7 %copy.171.err_col = f32[2,384,1344]{2,1,0:T(8,128)} copy(f32[2,384,1344]{1,2,0:T(8,128)} %param.49) | data formatting | bytes 8257536 | tf_op args[21]
  73.8 5.2 all-gather.8.cloned.1.call-done
  82.4 4.2 all-to-all-start.3
  86.8 52.3 %all-gather.10.cloned.1.call-done = bf16[1,384,2304]{2,1,0:T(8,128)(2,1)} async-done(((bf16[1,24,2304]{2,1,0:T(8,128)(2,1)}), bf16[1,384,2304]{2,1,0:T(8,128)(2,1)}) %all-gather.10.cloned.1.call-update) | async-done | bytes 1769488 | tf_op jit(solution)/shard_map/all_gather | solution.py:623
  139.1 1.9 collective-permute-start.2
  142.3 3.2 all-to-all-start.4
  147.1 8.8 %all-to-all-done.4 = f32[32,8,168]{2,1,0:T(8,128)S(1)} async-done(((f32[32,8,168]{2,1,0:T(8,128)}), f32[32,8,168]{2,1,0:T(8,128)S(1)}, u32[]{:S(2)}, u32[]{:S(2)}) %all-to-all-start.4) | async-done | bytes 172064 | tf_op jit(solution)/shard_map/all_to_all | solution.py:649
  157.0 37.4 %forward_first.1 = (f32[8,256,384]{2,1,0:T(8,128)}, bf16[8,256,384]{2,1,0:T(8,128)(2,1)}, bf16[8,256,384]{2,1,0:T(8,128)(2,1)}, bf16[8,256,384]{2,1,0:T(8,128)(2...) custom-call(bf16[8,256,16]{2,1,0:T(8,128)(2,1)} %add_convert_fusion., ...), custom_call_target="tpu_custom_call" | custom-call | flops 8000000000 | bytes 48000000 | tf_op jit(solution)/shard_map/forward_first/pallas_call | solution.py:421
  194.4 85.9 %layer_second.1 = (f32[8,256,384]{2,1,0:T(8,128)}, f32[8,8,384]{2,1,0:T(8,128)}, f32[384,1344]{1,0:T(8,128)}, f32[384,1344]{1,0:T(8,128)}, f32[960,384]{1,0:T(8,...) custom-call(f32[8,256,384]{2,1,0:T(8,128)} %get-tuple-element.68.x2,, ...), custom_call_target="tpu_custom_call" | custom-call | flops 25600000000 | bytes 24000000 | tf_op jit(solution)/shard_map/layer_second/pallas_call | solution.py:442
  280.3 46.6 %backward_first.1 = (f32[8,6,384]{2,1,0:T(8,128)}, f32[384,1344]{1,0:T(8,128)}, f32[384,1344]{1,0:T(8,128)}, f32[960,384]{1,0:T(8,128)}, f32[960,384]{1,0:T(8,12...) custom-call(f32[8,256,384]{2,1,0:T(8,128)} %get-tuple-element.69.dx, ...), custom_call_target="tpu_custom_call" | custom-call | flops 17600000000 | bytes 64000000 | tf_op jit(solution)/shard_map/backward_first/pallas_call | solution.py:468
  329.0 3.6 all-to-all-start.8
  336.1 3.0 copy.170
  339.4 1.9 copy.173
  343.8 3.7 collective-permute-done.8
  350.2 5.7 %all-to-all-start.12 = ((f32[32,1,168]{2,1,0:T(1,128)}), f32[32,1,168]{2,1,0:T(1,128)S(1)}, u32[]{:S(2)}, u32[]{:S(2)}) async-start(f32[32,1,168]{2,1,0:T(1,128)} %broadcast_in_dim.99), calls=%async_computation.12 | async-start | bytes 65536 | tf_op jit(solution)/shard_map/all_to_all | solution.py:571
  356.0 3.1 copy.172.got_col
  359.0 1.9 copy.175.got_col
  361.0 8.0 %left_factors.2 = (f32[384,1344]{1,0:T(8,128)}, f32[960,384]{1,0:T(8,128)}, f32[8,384]{1,0:T(8,128)}, f32[8,960]{1,0:T(8,128)}) custom-call(f32[2,384,1344]{2,1,0:T(8,128)} %copy.171.err_col, f32[384,1344]{1,0:T(8,128)} %get-tuple-element.83.own_col, f32[384,1344]{1,0:T(8,128)} %copy.172.got_col, f32[2,960,384]{2,1,0:T(8,128)} %err_row.3, ...), custom_call_target="tpu_custom_call" | custom-call | tf_op jit(solution)/shard_map/left_factors/pallas_call | solution.py:499
  369.0 8.1 %left_factors.3 = (f32[384,1344]{1,0:T(8,128)}, f32[960,384]{1,0:T(8,128)}, f32[8,384]{1,0:T(8,128)}, f32[8,960]{1,0:T(8,128)}) custom-call(f32[2,384,1344]{2,1,0:T(8,128)} %copy.171.err_col, f32[384,1344]{1,0:T(8,128)} %get-tuple-element.88.own_col, f32[384,1344]{1,0:T(8,128)} %copy.175.got_col, f32[2,960,384]{2,1,0:T(8,128)} %err_row.3, ...), custom_call_target="tpu_custom_call" | custom-call | tf_op jit(solution)/shard_map/left_factors/pallas_call | solution.py:499
  379.4 6.6 %all-to-all-start.6 = ((f32[16,16,128]{2,1,0:T(8,128)}), f32[16,16,128]{2,1,0:T(8,128)S(1)}, u32[]{:S(2)}, u32[]{:S(2)}) async-start(f32[16,16,128]{2,1,0:T(8,128)} %bitcast.49), calls=%async_computation.6 | async-start | bytes 262144 | tf_op jit(solution)/shard_map/all_to_all | solution.py:581
  387.9 4.8 all-to-all-done.6
  392.7 3.6 all-to-all-start.13
  396.3 9.3 %all-to-all-done.13 = f32[16,24,168]{2,1,0:T(8,128)S(1)} async-done(((f32[16,24,168]{2,1,0:T(8,128)}), f32[16,24,168]{2,1,0:T(8,128)S(1)}, u32[]{:S(2)}, u32[]{:S(2)}) %all-to-all-start.13) | async-done | bytes 258080 | tf_op jit(solution)/shard_map/all_to_all | solution.py:694
  406.2 5.8 %all-to-all-start.7 = ((f32[16,16,128]{2,1,0:T(8,128)}), f32[16,16,128]{2,1,0:T(8,128)S(1)}, u32[]{:S(2)}, u32[]{:S(2)}) async-start(f32[16,16,128]{2,1,0:T(8,128)} %broadcast_in_dim.46), calls=%async_computation.7 | async-start | bytes 262144 | tf_op jit(solution)/shard_map/all_to_all | solution.py:571
  413.4 2.1 collective-permute-start.11
  415.5 3.2 all-to-all-done.7
  419.8 3.0 orthonormal.1
  423.9 3.3 fusion.40
  428.0 5.8 %all-to-all-start.9 = ((f32[32,8,384]{2,1,0:T(8,128)}), f32[32,8,384]{2,1,0:T(8,128)S(1)}, u32[]{:S(2)}, u32[]{:S(2)}) async-start(f32[32,8,384]{2,1,0:T(8,128)} %broadcast_in_dim.47), calls=%async_computation.9 | async-start | bytes 786432 | tf_op jit(solution)/shard_map/all_to_all | solution.py:571
  435.9 7.0 %right_factors.1 = (f32[2,8,1344]{2,1,0:T(8,128)}, f32[2,8,384]{2,1,0:T(8,128)}) custom-call(f32[384,1344]{1,0:T(8,128)} %get-tuple-element.102.mat_col0, f32[960,384]{1,0:T(8,128)} %get-tuple-element.103.mat_row0, f32[384,1344]{1,0:T(8,128)} %get-tuple-element.104.mat_col1, f32[960,384]{1,0:T(8,128)} %get-tuple-element.105.mat_row1, ...), custom_call_target="tpu_custom_call" | custom-call | tf_op jit(solution)/shard_map/right_factors/pallas_call | solution.py:538
  448.7 1.8 multiply_reduce_fusion.1
  452.5 6.6 %all-to-all-start.10 = ((f32[16,14,128]{2,1,0:T(8,128)}), f32[16,14,128]{2,1,0:T(8,128)S(1)}, u32[]{:S(2)}, u32[]{:S(2)}) async-start(f32[16,14,128]{2,1,0:T(8,128)} %reshape.310), calls=%async_computation.10 | async-start | bytes 262144 | tf_op jit(solution)/shard_map/all_to_all | solution.py:581
  461.3 4.5 all-to-all-done.10
  466.5 3.6 all-to-all-start.11
  472.2 4.6 all-to-all-done.11
  481.3 11.0 %next_errors.1 = (f32[2,384,1344]{2,1,0:T(8,128)}, f32[2,960,384]{2,1,0:T(8,128)}) custom-call(f32[384,1344]{1,0:T(8,128)} %get-tuple-element.102.mat_col0, f32[960,384]{1,0:T(8,128)} %get-tuple-element.103.mat_row0, f32[384,1344]{1,0:T(8,128)} %get-tuple-element.104.mat_col1, f32[960,384]{1,0:T(8,128)} %get-tuple-element.105.mat_row1, ...), custom_call_target="tpu_custom_call" | custom-call | tf_op jit(solution)/shard_map/next_errors/pallas_call | solution.py:555
  492.4 5.8 %copy.188 = f32[2,384,1344]{1,2,0:T(8,128)} copy(f32[2,384,1344]{2,1,0:T(8,128)} %get-tuple-element.226) | data formatting | bytes 8257536
  502.6 3.6 collective-permute-start.10
  511.8 2.1 multiply_subtract_fusion.2
  519.9 2.1 multiply_subtract_fusion.1
  522.0 2.2 multiply_subtract_fusion
  (335 shorter events, 80.1 us)
Async XLA Ops:
  7.2 22.5 %copy-start = (f32[16,256,16]{1,2,0:T(8,128)S(1)}, f32[16,256,16]{1,2,0:T(8,128)}, u32[]{:S(2)}) copy-start(f32[16,256,16]{1,2,0:T(8,128)} %param.32) | copy-start | bytes 786436
  7.3 71.7 %all-gather.8.cloned.1.call-start = ((), (), s32[]{:S(2)}) async-start(), calls=%async_computation.15 | async-start | bytes 1880064 | tf_op jit(solution)/shard_map/all_gather | solution.py:623
  10.7 128.4 %all-gather.10.cloned.1.call-start = ((), (), s32[]{:S(2)}) async-start(), calls=%async_computation.16 | async-start | bytes 1880064 | tf_op jit(solution)/shard_map/all_gather | solution.py:623
  12.1 18.4 %all-to-all-start = ((f32[16,1,16]{2,1,0:T(1,128)}), f32[16,1,16]{2,1,0:T(1,128)S(1)}, u32[]{:S(2)}, u32[]{:S(2)}) async-start(f32[16,1,16]{2,1,0:T(1,128)} %broadcast_in_dim.34), calls=%async_computation | async-start | bytes 16384 | tf_op jit(solution)/shard_map/all_to_all | solution.py:571
  19.5 404.3 %all-gather.6.cloned.1.call-start = ((), (), s32[]{:S(2)}) async-start(), calls=%async_computation.14 | async-start | bytes 4386816 | tf_op jit(solution)/shard_map/all_gather | solution.py:652
  19.6 53.2 %collective-permute-start.1 = (f32[2,1344]{1,0:T(2,128)S(1)}, f32[2,1344]{1,0:T(2,128)S(1)}, u32[]{:S(2)}, u32[]{:S(2)}) collective-permute-start(f32[2,1344]{1,0:T(2,128)S(1)} %copy-done.37), channel_id=1, source_target_pairs={{0,1},{1,0},{2,3},{3,2},{4,5},{5,4},{6,7},{7,6},{8,9},{9,8},{10,11... | collective-permute-start | bytes 32264 | tf_op jit(solution)/shard_map/ppermute | solution.py:565
  27.2 20.5 %copy-start.22 = (f32[40,384]{1,0:T(8,128)S(1)}, f32[40,384]{1,0:T(8,128)}, u32[]{:S(2)}) copy-start(f32[40,384]{1,0:T(8,128)} %param.36) | copy-start | bytes 184324
  29.7 31.6 %copy-start.44 = (f32[384]{0:T(512)S(1)}, f32[384]{0:T(512)}, u32[]{:S(2)}) copy-start(f32[384]{0:T(512)} %get-tuple-element.275) | copy-start | bytes 4612
  29.7 32.2 %copy-start.43 = (f32[384]{0:T(512)S(1)}, f32[384]{0:T(512)}, u32[]{:S(2)}) copy-start(f32[384]{0:T(512)} %get-tuple-element.274) | copy-start | bytes 4612
  30.5 12.9 %all-to-all-start.5 = ((bf16[16,2,384]{2,1,0:T(2,128)(2,1)}), bf16[16,2,384]{2,1,0:T(2,128)(2,1)S(1)}, u32[]{:S(2)}, u32[]{:S(2)}) async-start(bf16[16,2,384]{2,1,0:T(2,128)(2,1)} %reshape.351), calls=%async_computation.5 | async-start | bytes 49152 | tf_op jit(solution)/shard_map/all_to_all | solution.py:571
  44.1 10.5 %all-to-all-start.2 = ((bf16[16,256,24]{1,2,0:T(8,128)(2,1)}), bf16[16,256,24]{1,2,0:T(8,128)(2,1)S(1)}, u32[]{:S(2)}, u32[]{:S(2)}) async-start(bf16[16,256,24]{1,2,0:T(8,128)(2,1)} %broadcast_in_dim.36), calls=%async_computation.2 | async-start | bytes 393216 | tf_op jit(solution)/shard_map/all_to_all | solution.py:571
  55.4 26.9 %all-to-all-start.1 = ((bf16[16,40,384]{2,1,0:T(8,128)(2,1)}), bf16[16,40,384]{2,1,0:T(8,128)(2,1)S(1)}, u32[]{:S(2)}, u32[]{:S(2)}) async-start(bf16[16,40,384]{2,1,0:T(8,128)(2,1)} %broadcast_in_dim.35), calls=%async_computation.1 | async-start | bytes 983040 | tf_op jit(solution)/shard_map/all_to_all | solution.py:571
  71.0 70.1 %copy-start.46 = (f32[384]{0:T(512)S(1)}, f32[384]{0:T(512)}, u32[]{:S(2)}) copy-start(f32[384]{0:T(512)} %get-tuple-element.277) | copy-start | bytes 4612
  72.8 68.6 %copy-start.9 = (bf16[256,128]{1,0:T(8,128)(2,1)}, bf16[256,128]{1,0:T(8,128)(2,1)S(1)}, u32[]{:S(2)}) copy-start(bf16[256,128]{1,0:T(8,128)(2,1)S(1)} %get-tuple-element.285) | copy-start | bytes 196612
  72.8 68.6 %copy-start.11 = (bf16[256,128]{1,0:T(8,128)(2,1)}, bf16[256,128]{1,0:T(8,128)(2,1)S(1)}, u32[]{:S(2)}) copy-start(bf16[256,128]{1,0:T(8,128)(2,1)S(1)} %get-tuple-element.286) | copy-start | bytes 196612
  79.0 78.0 %collective-permute-start = (bf16[384,2304]{1,0:T(8,128)(2,1)}, bf16[384,2304]{1,0:T(8,128)(2,1)}, u32[]{:S(2)}, u32[]{:S(2)}) collective-permute-start(bf16[384,2304]{1,0:T(8,128)(2,1)} %bitcast.208), channel_id=1, source_target_pairs={{0,1},{1,0},{2,3},{3,2},{4,5},{5,4},{6,7},{7,6},{8,9},{9,8},{10,11... | collective-permute-start | bytes 5308424 | tf_op jit(solution)/shard_map/ppermute | solution.py:565
  82.4 60.0 %copy-start.6 = (bf16[16,40,384]{2,1,0:T(8,128)(2,1)}, bf16[16,40,384]{2,1,0:T(8,128)(2,1)S(1)}, u32[]{:S(2)}) copy-start(bf16[16,40,384]{2,1,0:T(8,128)(2,1)S(1)} %all-to-all-done.1) | copy-start | bytes 1474564
  82.4 59.0 %all-to-all-start.3 = ((bf16[16,24,168]{2,1,0:T(8,128)(2,1)}), bf16[16,24,168]{2,1,0:T(8,128)(2,1)S(1)}, u32[]{:S(2)}, u32[]{:S(2)}) async-start(bf16[16,24,168]{2,1,0:T(8,128)(2,1)} %bitcast.159), calls=%async_computation.3 | async-start | bytes 393216 | tf_op jit(solution)/shard_map/all_to_all | solution.py:637
  86.8 55.6 %copy-start.17 = (f32[256,384]{1,0:T(8,128)}, f32[256,384]{1,0:T(8,128)S(1)}, u32[]{:S(2)}) copy-start(f32[256,384]{1,0:T(8,128)S(1)} %convolution_add_fusion) | copy-start | bytes 1179652
  139.1 55.3 %collective-permute-start.2 = (bf16[384,2304]{1,0:T(8,128)(2,1)}, bf16[384,2304]{1,0:T(8,128)(2,1)}, u32[]{:S(2)}, u32[]{:S(2)}) collective-permute-start(bf16[384,2304]{1,0:T(8,128)(2,1)} %bitcast.211), channel_id=1, source_target_pairs={{0,1},{1,0},{2,3},{3,2},{4,5},{5,4},{6,7},{7,6},{8,9},{9,8},{10,11... | collective-permute-start | bytes 5308424 | tf_op jit(solution)/shard_map/ppermute | solution.py:565
  141.3 244.7 %copy-start.49 = (f32[256,384]{1,0:T(8,128)}, f32[256,384]{1,0:T(8,128)S(1)}, u32[]{:S(2)}) copy-start(f32[256,384]{1,0:T(8,128)S(1)} %fusion.1) | copy-start | bytes 1179652
  142.3 13.5 %all-to-all-start.4 = ((f32[32,8,168]{2,1,0:T(8,128)}), f32[32,8,168]{2,1,0:T(8,128)S(1)}, u32[]{:S(2)}, u32[]{:S(2)}) async-start(f32[32,8,168]{2,1,0:T(8,128)} %fusion.22), calls=%async_computation.4 | async-start | bytes 524288 | tf_op jit(solution)/shard_map/all_to_all | solution.py:649
  280.3 46.7 %copy-start.19 = (f32[8,8,384]{2,1,0:T(8,128)S(1)}, f32[8,8,384]{2,1,0:T(8,128)}, u32[]{:S(2)}) copy-start(f32[8,8,384]{2,1,0:T(8,128)} %get-tuple-element.109) | copy-start | bytes 294916
  280.3 53.7 %copy-start.41 = (f32[1,3456]{1,0:T(1,128)S(1)}, f32[1,3456]{1,0:T(1,128)}, u32[]{:S(2)}) copy-start(f32[1,3456]{1,0:T(1,128)} %get-tuple-element.98) | copy-start | bytes 41476
  280.3 53.8 %copy-start.48 = (f32[1,16]{1,0:T(1,128)S(1)}, f32[1,16]{1,0:T(1,128)}, u32[]{:S(2)}) copy-start(f32[1,16]{1,0:T(1,128)} %get-tuple-element.100) | copy-start | bytes 196
  329.0 20.5 %all-to-all-start.8 = ((bf16[32,8,168]{2,1,0:T(8,128)(2,1)}), bf16[32,8,168]{2,1,0:T(8,128)(2,1)S(1)}, u32[]{:S(2)}, u32[]{:S(2)}) async-start(bf16[32,8,168]{2,1,0:T(8,128)(2,1)} %bitcast.55), calls=%async_computation.8 | async-start | bytes 262144 | tf_op jit(solution)/shard_map/all_to_all | solution.py:688
  335.0 8.5 %collective-permute-start.9 = (f32[1937]{0:T(1024)S(1)}, f32[1937]{0:T(1024)S(1)}, u32[]{:S(2)}, u32[]{:S(2)}) collective-permute-start(f32[1937]{0:T(1024)S(1)} %concatenate.69), channel_id=1, source_target_pairs={{0,1},{1,0},{2,3},{3,2},{4,5},{5,4},{6,7},{7,6},{8,9},{9,8},{10,11... | collective-permute-start | bytes 23252 | tf_op jit(solution)/shard_map/ppermute | solution.py:565
  339.1 16.8 %collective-permute-start.3 = (f32[384,1344]{0,1:T(8,128)}, f32[384,1344]{0,1:T(8,128)}, u32[]{:S(2)}, u32[]{:S(2)}) collective-permute-start(f32[384,1344]{0,1:T(8,128)} %copy.170), channel_id=1, source_target_pairs={{0,1},{1,0},{2,3},{3,2},{4,5},{5,4},{6,7},{7,6},{8,9},{9,8},{10,11... | collective-permute-start | bytes 6193160 | tf_op jit(solution)/shard_map/ppermute | solution.py:565
  341.3 17.7 %collective-permute-start.5 = (f32[384,1344]{0,1:T(8,128)}, f32[384,1344]{0,1:T(8,128)S(1)}, u32[]{:S(2)}, u32[]{:S(2)}) collective-permute-start(f32[384,1344]{0,1:T(8,128)} %copy.173), channel_id=1, source_target_pairs={{0,1},{1,0},{2,3},{3,2},{4,5},{5,4},{6,7},{7,6},{8,9},{9,8},{10,11... | collective-permute-start | bytes 6193160 | tf_op jit(solution)/shard_map/ppermute | solution.py:565
  341.7 19.2 %collective-permute-start.4 = (f32[960,384]{1,0:T(8,128)}, f32[960,384]{1,0:T(8,128)}, u32[]{:S(2)}, u32[]{:S(2)}) collective-permute-start(f32[960,384]{1,0:T(8,128)} %get-tuple-element.86), channel_id=1, source_target_pairs={{0,1},{1,0},{2,3},{3,2},{4,5},{5,4},{6,7},{7,6},{8,9},{9,8},{10,11... | collective-permute-start | bytes 4423688 | tf_op jit(solution)/shard_map/ppermute | solution.py:565
  342.0 27.0 %collective-permute-start.6 = (f32[960,384]{1,0:T(8,128)}, f32[960,384]{1,0:T(8,128)}, u32[]{:S(2)}, u32[]{:S(2)}) collective-permute-start(f32[960,384]{1,0:T(8,128)} %get-tuple-element.91), channel_id=1, source_target_pairs={{0,1},{1,0},{2,3},{3,2},{4,5},{5,4},{6,7},{7,6},{8,9},{9,8},{10,11... | collective-permute-start | bytes 4423688 | tf_op jit(solution)/shard_map/ppermute | solution.py:565
  343.5 4.0 collective-permute-start.8
  347.5 1.8 collective-permute-start.7
  350.2 29.2 %all-to-all-start.12 = ((f32[32,1,168]{2,1,0:T(1,128)}), f32[32,1,168]{2,1,0:T(1,128)S(1)}, u32[]{:S(2)}, u32[]{:S(2)}) async-start(f32[32,1,168]{2,1,0:T(1,128)} %broadcast_in_dim.99), calls=%async_computation.12 | async-start | bytes 65536 | tf_op jit(solution)/shard_map/all_to_all | solution.py:571
  379.4 32.7 %copy-start.20 = (f32[8,6,384]{2,1,0:T(8,128)S(1)}, f32[8,6,384]{2,1,0:T(8,128)}, u32[]{:S(2)}) copy-start(f32[8,6,384]{2,1,0:T(8,128)} %get-tuple-element.108) | copy-start | bytes 221188
  379.4 13.3 %all-to-all-start.6 = ((f32[16,16,128]{2,1,0:T(8,128)}), f32[16,16,128]{2,1,0:T(8,128)S(1)}, u32[]{:S(2)}, u32[]{:S(2)}) async-start(f32[16,16,128]{2,1,0:T(8,128)} %bitcast.49), calls=%async_computation.6 | async-start | bytes 262144 | tf_op jit(solution)/shard_map/all_to_all | solution.py:581
  392.7 12.9 %all-to-all-start.13 = ((f32[16,24,168]{2,1,0:T(8,128)}), f32[16,24,168]{2,1,0:T(8,128)S(1)}, u32[]{:S(2)}, u32[]{:S(2)}) async-start(f32[16,24,168]{2,1,0:T(8,128)} %bitcast.63), calls=%async_computation.13 | async-start | bytes 786432 | tf_op jit(solution)/shard_map/all_to_all | solution.py:694
  406.2 12.5 %all-to-all-start.7 = ((f32[16,16,128]{2,1,0:T(8,128)}), f32[16,16,128]{2,1,0:T(8,128)S(1)}, u32[]{:S(2)}, u32[]{:S(2)}) async-start(f32[16,16,128]{2,1,0:T(8,128)} %broadcast_in_dim.46), calls=%async_computation.7 | async-start | bytes 262144 | tf_op jit(solution)/shard_map/all_to_all | solution.py:571
  413.4 108.6 %collective-permute-start.11 = (f32[24,2688]{1,0:T(8,128)S(1)}, f32[24,2688]{1,0:T(8,128)}, u32[]{:S(2)}, u32[]{:S(2)}) collective-permute-start(f32[24,2688]{1,0:T(8,128)S(1)} %reshape.317), channel_id=1, source_target_pairs={{0,1},{1,0},{2,3},{3,2},{4,5},{5,4},{6,7},{7,6},{8,9},{9,8},{10,11... | collective-permute-start | bytes 774152 | tf_op jit(solution)/shard_map/ppermute | solution.py:565
  428.0 20.7 %all-to-all-start.9 = ((f32[32,8,384]{2,1,0:T(8,128)}), f32[32,8,384]{2,1,0:T(8,128)S(1)}, u32[]{:S(2)}, u32[]{:S(2)}) async-start(f32[32,8,384]{2,1,0:T(8,128)} %broadcast_in_dim.47), calls=%async_computation.9 | async-start | bytes 786432 | tf_op jit(solution)/shard_map/all_to_all | solution.py:571
  435.9 23.3 %copy-start.7 = (bf16[16,40,384]{2,1,0:T(8,128)(2,1)S(1)}, bf16[16,40,384]{2,1,0:T(8,128)(2,1)}, u32[]{:S(2)}) copy-start(bf16[16,40,384]{2,1,0:T(8,128)(2,1)} %copy-done.6) | copy-start | bytes 1474564
  452.5 13.3 %all-to-all-start.10 = ((f32[16,14,128]{2,1,0:T(8,128)}), f32[16,14,128]{2,1,0:T(8,128)S(1)}, u32[]{:S(2)}, u32[]{:S(2)}) async-start(f32[16,14,128]{2,1,0:T(8,128)} %reshape.310), calls=%async_computation.10 | async-start | bytes 262144 | tf_op jit(solution)/shard_map/all_to_all | solution.py:581
  466.5 10.3 %all-to-all-start.11 = ((f32[16,14,128]{2,1,0:T(8,128)}), f32[16,14,128]{2,1,0:T(8,128)S(1)}, u32[]{:S(2)}, u32[]{:S(2)}) async-start(f32[16,14,128]{2,1,0:T(8,128)} %broadcast_in_dim.98), calls=%async_computation.11 | async-start | bytes 262144 | tf_op jit(solution)/shard_map/all_to_all | solution.py:571
  492.4 22.9 %copy-start.31 = (f32[1000,24]{0,1:T(8,128)S(1)}, f32[1000,24]{0,1:T(8,128)}, u32[]{:S(2)}) copy-start(f32[1000,24]{0,1:T(8,128)} %param.38) | copy-start | bytes 288004
  498.2 21.7 %copy-start.5 = (f32[2,24,1344]{2,1,0:T(8,128)S(1)}, f32[2,24,1344]{2,1,0:T(8,128)}, u32[]{:S(2)}) copy-start(f32[2,24,1344]{2,1,0:T(8,128)} %param.33) | copy-start | bytes 774148
  498.2 21.7 %copy-start.21 = (f32[2,24,1344]{2,1,0:T(8,128)S(1)}, f32[2,24,1344]{2,1,0:T(8,128)}, u32[]{:S(2)}) copy-start(f32[2,24,1344]{2,1,0:T(8,128)} %param.41) | copy-start | bytes 774148
  499.9 22.0 %copy-start.14 = (f32[24,5376]{1,0:T(8,128)S(1)}, f32[24,5376]{1,0:T(8,128)}, u32[]{:S(2)}) copy-start(f32[24,5376]{1,0:T(8,128)} %param.43) | copy-start | bytes 1548292
  502.6 6.2 %collective-permute-start.10 = (f32[]{:T(128)}, f32[]{:T(128)}, u32[]{:S(2)}, u32[]{:S(2)}) collective-permute-start(f32[]{:T(128)} %add.166), channel_id=1, source_target_pairs={{0,1},{1,0},{2,3},{3,2},{4,5},{5,4},{6,7},{7,6},{8,9},{9,8},{10,11... | collective-permute-start | bytes 20 | tf_op jit(solution)/shard_map/ppermute | solution.py:565
  (33 other events, 336.1 us)
Sparse Core Ops, SparseCore 0:
  11.5 67.4 all-gather.7
  82.3 56.7 all-gather.9
  141.9 74.2 all-gather.5

commit v2 on v1

v2 whole, which is shorter than its diff:
```python
import jax
import jax.numpy as jnp
import numpy as np
from jax import lax
from jax.experimental import pallas as pl
from jax.experimental.pallas import tpu as pltpu
from jax.sharding import PartitionSpec as P

D = 384
HEADS = 6
HD = 64
MLP = 1536
NBR = 8080
CLASSES = 1000
FREQ = 256
PV = 16
GRID = 16
L = 2
TOK = 256
RANK = 8

norm_eps = 1e-06
ortho_eps = 1e-06
clip_limit = 1.0
momentum_decay = 0.9
learn_rate = 4.0

HALF = D // 2
HMLP = MLP // 2
QKV_S = 3 * HALF
COL_S = QKV_S + HMLP
ROW_S = HALF + HMLP
OFF_W2 = HMLP
OFF_Q = 2 * HMLP
GATH = 2 * HMLP + 4 * HALF

f32 = jnp.float32
bf16 = jnp.bfloat16
highest = lax.Precision.HIGHEST
NN = (((1,), (0,)), ((), ()))
NT = (((1,), (1,)), ((), ()))
TN = (((0,), (0,)), ((), ()))


def dot(left, right, dims=NN):
    return lax.dot_general(left, right, dims, preferred_element_type=f32)


def dot_full(left, right, dims=NN):
    return lax.dot_general(left, right, dims, precision=highest, preferred_element_type=f32)


def position_table():
    quarter = D // 4
    omega = 1.0 / 10000.0 ** (np.arange(quarter, dtype=np.float32) / quarter)
    index = np.arange(TOK)
    across = (index % GRID).astype(np.float32)[:, None] * omega[None, :].astype(np.float32)
    down = (index // GRID).astype(np.float32)[:, None] * omega[None, :].astype(np.float32)
    table = np.concatenate([np.sin(across), np.cos(across), np.sin(down), np.cos(down)], 1)
    return table.astype(np.float32)


def frequency_features(steps):
    half = FREQ // 2
    rates = jnp.exp(-jnp.log(10000.0) * jnp.arange(half, dtype=f32) / half)
    angles = steps[:, None] * rates[None, :]
    return jnp.concatenate([jnp.cos(angles), jnp.sin(angles)], 1)


def normalize(values):
    centered = values - jnp.mean(values, -1, keepdims=True)
    inv_std = lax.rsqrt(jnp.mean(centered * centered, -1, keepdims=True) + norm_eps)
    return centered * inv_std, inv_std


def norm_back(grad, normed, inv_std):
    mean_grad = jnp.mean(grad, -1, keepdims=True)
    mean_mixed = jnp.mean(grad * normed, -1, keepdims=True)
    return inv_std * (grad - mean_grad - normed * mean_mixed)


def token_sum(values):
    return jnp.sum(values, 0, keepdims=True)


START_FC2 = L * D
START_COND = 2 * L * D
N_MODS = (6 * L + 2) * D
START_FIRST = START_COND + N_MODS
START_SECOND = START_FIRST + D
START_PATCH = START_FIRST + 2 * D
START_HEAD = START_FIRST + 3 * D


def assemble(layer, own, other, bcol_own, bcol_other, wqkv, wo, bqkv, bfc1):
    for side, (weights, bias) in enumerate(((own, bcol_own), (other, bcol_other))):
        for head in range(HEADS // 2):
            for part in range(3):
                at = (3 * head + part) * HD
                to = part * D + side * HALF + head * HD
                wqkv[:, to : to + HD] = weights[:, OFF_Q + at : OFF_Q + at + HD]
                bqkv[:, to : to + HD] = bias[layer : layer + 1, at : at + HD]
        wo[:, side * HALF : (side + 1) * HALF] = weights[:, OFF_Q + QKV_S :]
        bfc1[:, side * HMLP : (side + 1) * HMLP] = bias[layer : layer + 1, QKV_S:]


def vector(b_rep, at):
    return b_rep[:, at : at + D]


def head_mask(which):
    lane = lax.broadcasted_iota(jnp.int32, (1, 2 * HD), 1)
    return (lane < HD) if which == 0 else (lane >= HD)


def keep(values, mask):
    return jnp.where(mask, values, jnp.zeros_like(values))


def layer_forward(x, mod, own, other, wqkv, wo, bqkv, bfc1, bproj, bfc2, put):
    normed, inv_a = normalize(x)
    input_a = (normed * (1.0 + mod(1)) + mod(0)).astype(bf16)
    qkv = (dot(input_a, wqkv[...]) + bqkv).astype(bf16)
    query = qkv[:, :D] * jnp.asarray(HD**-0.5, bf16)
    keyed = qkv[:, D : 2 * D]
    valued = qkv[:, 2 * D :]
    put("input_a", input_a)
    put("query", query)
    put("keyed", keyed)
    put("valued", valued)
    pieces = []
    for pair in range(HEADS // 2):
        span = slice(pair * 2 * HD, (pair + 1) * 2 * HD)
        q_pair, k_pair, v_pair = query[:, span], keyed[:, span], valued[:, span]
        total = None
        for which in range(2):
            mask = head_mask(which)
            scores = dot(keep(q_pair, mask), k_pair, NT)
            expo = jnp.exp(scores - jnp.max(scores, -1, keepdims=True))
            probs = expo * (1.0 / jnp.sum(expo, -1, keepdims=True))
            put("probs", probs, 2 * pair + which)
            mixed = dot(probs.astype(bf16), keep(v_pair, mask))
            total = mixed if total is None else total + mixed
        pieces.append(total.astype(bf16))
    mixed = jnp.concatenate(pieces, 1)
    put("mixed", mixed)
    branch_a = dot(mixed, wo[...], NT) + bproj
    put("branch_a", branch_a)
    middle = x + mod(2) * branch_a
    put("middle", middle)
    normed_m, inv_m = normalize(middle)
    input_m = (normed_m * (1.0 + mod(4)) + mod(3)).astype(bf16)
    put("input_m", input_m)
    branch_m = bfc2
    for side, weights in enumerate((own, other)):
        pre = dot(input_m, weights[:, :HMLP]) + bfc1[:, side * HMLP : (side + 1) * HMLP]
        squared = pre * pre
        coef = np.float32(np.sqrt(2.0 / np.pi))
        tanh = jnp.tanh(pre * (coef + np.float32(coef * 0.044715) * squared))
        half = 0.5 * (1.0 + tanh)
        acted = (pre * half).astype(bf16)
        slope = half + (0.5 * pre) * (1.0 - tanh * tanh) * (
            coef + np.float32(3.0 * 0.044715 * coef) * squared
        )
        put("acted", acted, side)
        put("slope", slope, side)
        branch_m = branch_m + dot(acted, weights[:, OFF_W2 : OFF_W2 + HMLP], NT)
    put("branch_m", branch_m)
    return middle + mod(5) * branch_m


def layer_backward(grad, x, mod, own, other, wqkv, wo, take, rows, stash, mods_out, bias):
    branch_m = take("branch_m")
    mods_out(5, token_sum(grad * branch_m))
    grad_branch_m = (grad * mod(5)).astype(bf16)
    bias("fc2", 0, grad_branch_m)
    stash["dym"][rows, :] = grad_branch_m
    middle = take("middle")
    normed_m, inv_m = normalize(middle)
    grad_input = None
    for side, weights in enumerate((own, other)):
        span = slice(side * HMLP, (side + 1) * HMLP)
        grad_acted = dot(grad_branch_m, weights[:, OFF_W2 : OFF_W2 + HMLP])
        grad_pre = (grad_acted * take("slope", side)).astype(bf16)
        stash["dg"][rows, span] = grad_pre
        bias("fc1", side * HMLP, grad_pre)
        part = dot(grad_pre, weights[:, :HMLP], NT)
        grad_input = part if grad_input is None else grad_input + part
    mods_out(3, token_sum(grad_input))
    mods_out(4, token_sum(grad_input * normed_m))
    grad_middle = grad + norm_back(grad_input * (1.0 + mod(4)), normed_m, inv_m)
    branch_a = take("branch_a")
    mods_out(2, token_sum(grad_middle * branch_a))
    grad_branch_a = (grad_middle * mod(2)).astype(bf16)
    bias("proj", 0, grad_branch_a)
    stash["dya"][rows, :] = grad_branch_a
    grad_mixed = dot(grad_branch_a, wo[...]).astype(bf16)
    query, keyed, valued = take("query"), take("keyed"), take("valued")
    grads_q, grads_k, grads_v = [], [], []
    for pair in range(HEADS // 2):
        span = slice(pair * 2 * HD, (pair + 1) * 2 * HD)
        q_pair, k_pair, v_pair = query[:, span], keyed[:, span], valued[:, span]
        g_pair = grad_mixed[:, span]
        grad_q = grad_k = grad_v = None
        for which in range(2):
            mask = head_mask(which)
            probs = take("probs", 2 * pair + which)
            g_head = keep(g_pair, mask)
            grad_probs = dot(g_head, v_pair, NT)
            row_dot = jnp.sum(grad_probs * probs, -1, keepdims=True)
            grad_scores = (probs * (grad_probs - row_dot)).astype(bf16)
            part_q = dot(grad_scores, keep(k_pair, mask))
            part_k = dot(grad_scores, keep(q_pair, mask), TN)
            part_v = dot(probs.astype(bf16), g_head, TN)
            grad_q = part_q if grad_q is None else grad_q + part_q
            grad_k = part_k if grad_k is None else grad_k + part_k
            grad_v = part_v if grad_v is None else grad_v + part_v
        grads_q.append((grad_q * HD**-0.5).astype(bf16))
        grads_k.append(grad_k.astype(bf16))
        grads_v.append(grad_v.astype(bf16))
    grad_qkv = jnp.concatenate(grads_q + grads_k + grads_v, 1)
    stash["dqkv"][rows, :] = grad_qkv
    bias("qkv", 0, grad_qkv)
    grad_input_a = dot(grad_qkv, wqkv[...], NT)
    normed, inv_a = normalize(x)
    mods_out(0, token_sum(grad_input_a))
    mods_out(1, token_sum(grad_input_a * normed))
    return grad_middle + norm_back(grad_input_a * (1.0 + mod(1)), normed, inv_a)


def weight_grads(input_a, input_m, mixed, acted, stash, cols, rows_out):
    for part in range(3):
        piece = dot(stash["dqkv"][:, part * D : (part + 1) * D], input_a[...], TN)
        for side, out in enumerate(cols):
            for head in range(HEADS // 2):
                start = side * HALF + head * HD
                place = (3 * head + part) * HD
                out[place : place + HD, :] = piece[start : start + HD, :]
    for side, out in enumerate(cols):
        out[QKV_S:, :] = dot(stash["dg"][:, side * HMLP : (side + 1) * HMLP], input_m[...], TN)
    piece = dot(mixed[...], stash["dya"][...], TN)
    for side, out in enumerate(rows_out):
        out[:HALF, :] = piece[side * HALF : (side + 1) * HALF, :]
        out[HALF:, :] = dot(acted[:, side * HMLP : (side + 1) * HMLP], stash["dym"][...], TN)


BIAS = {"qkv": 0, "fc1": 3 * D, "proj": 3 * D + MLP, "fc2": 4 * D + MLP}
BIAS_WIDTH = 5 * D + MLP

PAY_PATCH, PAY_HEAD, PAY_PROJ, PAY_FC2, PAY_BPATCH, PAY_BHEAD, PAY_COND, PAY_BCOL = 0, 16, 32, 34, 36, 37, 38, 52
PAY_ROWS = 64
SMALL_ROWS = PAY_BCOL + 8 - PAY_PROJ


def forward_kernel(xt, mods, wpatch, pos, own, other, bcol_own, bcol_other, b_rep,
                   x0, query, keyed, valued, probs, branch_a, middle, slope, branch_m, mixed, acted,
                   input_a, input_m, x2, wqkv, wo, bqkv, bfc1):
    @pl.when(pl.program_id(0) == 0)
    def _():
        assemble(0, own, other, bcol_own, bcol_other, wqkv, wo, bqkv, bfc1)

    named = dict(query=query, keyed=keyed, valued=valued, mixed=mixed, branch_a=branch_a,
                 middle=middle, branch_m=branch_m, input_a=input_a, input_m=input_m)

    def put(name, value, index=None):
        if name == "probs":
            probs[0, index] = value
        elif name == "acted":
            acted[0, :, index * HMLP : (index + 1) * HMLP] = value
        elif name == "slope":
            slope[0, :, index * HMLP : (index + 1) * HMLP] = value
        else:
            named[name][0] = value

    x = dot(xt[0], wpatch[0], TN) + vector(b_rep, START_PATCH) + pos[...]
    x0[0] = x
    x2[0] = layer_forward(x, lambda j: mods[0, j : j + 1, :], own, other, wqkv, wo, bqkv[...],
                          bfc1[...], vector(b_rep, 0), vector(b_rep, START_FC2), put)


def diagonal(count):
    down = lax.broadcasted_iota(jnp.int32, (count, count), 0)
    across = lax.broadcasted_iota(jnp.int32, (count, count), 1)
    return down == across


def write_bcol(dbias, side, out, layer):
    pieces = []
    for head in range(HEADS // 2):
        for part in range(3):
            start = part * D + side * HALF + head * HD
            pieces.append(dbias[:, start : start + HD])
    start = 3 * D + side * HMLP
    pieces.append(dbias[:, start : start + HMLP])
    pieces.append(jnp.zeros((1, 4 * D - COL_S), f32))
    line = jnp.concatenate(pieces, 1)
    for row in range(4):
        at = PAY_BCOL + 4 * layer + row
        out[at : at + 1, :] = line[:, row * D : (row + 1) * D]


def middle_kernel(x2, mods, own, other, bcol_own, bcol_other, b_rep, whead, targets,
                  dx, dmods, col_own, col_other, row_own, row_other, dbias, dhead, dbhead, loss,
                  wqkv, wo, bqkv, bfc1, query, keyed, valued, probs, mixed, branch_a, middle, acted,
                  slope, branch_m, input_a, input_m, s_dqkv, s_dg, s_dya, s_dym):
    step = pl.program_id(0)

    @pl.when(step == 0)
    def _():
        assemble(1, own, other, bcol_own, bcol_other, wqkv, wo, bqkv, bfc1)
        dbias[...] = jnp.zeros_like(dbias)
        dhead[...] = jnp.zeros_like(dhead)
        dbhead[...] = jnp.zeros_like(dbhead)
        loss[...] = jnp.zeros_like(loss)

    rows = pl.ds(pl.multiple_of(step * TOK, TOK), TOK)
    stacked = dict(mixed=mixed, input_a=input_a, input_m=input_m)
    single = dict(query=query, keyed=keyed, valued=valued, branch_a=branch_a, middle=middle,
                  branch_m=branch_m)

    def put(name, value, index=None):
        if name == "probs":
            probs[index] = value
        elif name == "acted":
            acted[rows, index * HMLP : (index + 1) * HMLP] = value
        elif name == "slope":
            slope[:, index * HMLP : (index + 1) * HMLP] = value
        elif name in stacked:
            stacked[name][rows, :] = value
        else:
            single[name][...] = value

    def take(name, index=None):
        if name == "probs":
            return probs[index]
        if name == "slope":
            return slope[:, index * HMLP : (index + 1) * HMLP]
        return single[name][...]

    def mod(j):
        return mods[0, 6 + j : 7 + j, :]

    x = layer_forward(x2[0], mod, own, other, wqkv, wo, bqkv[...], bfc1[...], vector(b_rep, D),
                      vector(b_rep, START_FC2 + D), put)
    normed, inv_std = normalize(x)
    input_f = (normed * (1.0 + mod(7)) + mod(6)).astype(bf16)
    bhead = jnp.sum(
        jnp.where(diagonal(PV), b_rep[:, START_HEAD : START_HEAD + PV], 0.0), 1, keepdims=True
    )
    miss = dot(whead[0], input_f, NT) + bhead - targets[0]
    loss[...] += jnp.sum(miss * miss, 0, keepdims=True)
    grad_pred = (2.0 * miss).astype(bf16)
    dhead[...] += dot(grad_pred, input_f)
    dbhead[...] += jnp.sum(grad_pred.astype(f32), 1, keepdims=True)
    grad_input = dot(grad_pred, whead[0], TN)
    dmods[0, 6:7, :] = token_sum(grad_input)
    dmods[0, 7:8, :] = token_sum(grad_input * normed)
    grad = norm_back(grad_input * (1.0 + mod(7)), normed, inv_std)

    def mods_out(j, value):
        dmods[0, j : j + 1, :] = value

    def bias(name, start, value):
        at = BIAS[name] + start
        dbias[:, at : at + value.shape[1]] += token_sum(value.astype(f32))

    stash = dict(dqkv=s_dqkv, dg=s_dg, dya=s_dya, dym=s_dym)
    dx[0] = layer_backward(grad, x2[0], mod, own, other, wqkv, wo, take, rows, stash, mods_out, bias)

    @pl.when(step == pl.num_programs(0) - 1)
    def _():
        weight_grads(input_a, input_m, mixed, acted, stash, (col_own, col_other), (row_own, row_other))


def last_kernel(dx, x0, mods, own, other, bcol_own, bcol_other, b_rep, xt,
                dbias1, dhead, dbhead, loss, dmods1,
                query, keyed, valued, probs, branch_a, middle, slope, branch_m, mixed, acted, input_a, input_m,
                dmods, col_own, col_other, row_own, row_other, pay_own, pay_other,
                wqkv, wo, bqkv, bfc1, a_input_a, a_input_m, a_mixed, a_acted, s_dqkv, s_dg, s_dya, s_dym,
                dbias, sems):
    step = pl.program_id(0)
    pairs = ((input_a, a_input_a), (input_m, a_input_m), (mixed, a_mixed), (acted, a_acted))
    copies = [pltpu.make_async_copy(src, dst, sems.at[i]) for i, (src, dst) in enumerate(pairs)]

    @pl.when(step == 0)
    def _():
        assemble(0, own, other, bcol_own, bcol_other, wqkv, wo, bqkv, bfc1)
        dbias[...] = jnp.zeros_like(dbias)
        pay_own[...] = jnp.zeros_like(pay_own)
        for copy in copies:
            copy.start()

    rows = pl.ds(pl.multiple_of(step * TOK, TOK), TOK)
    single = dict(query=query, keyed=keyed, valued=valued, branch_a=branch_a, middle=middle,
                  branch_m=branch_m)

    def take(name, index=None):
        if name == "probs":
            return probs[0, index]
        if name == "slope":
            return slope[0, :, index * HMLP : (index + 1) * HMLP]
        return single[name][0]

    def mods_out(j, value):
        dmods[0, j : j + 1, :] = value

    def bias(name, start, value):
        at = BIAS[name] + start
        dbias[:, at : at + value.shape[1]] += token_sum(value.astype(f32))

    stash = dict(dqkv=s_dqkv, dg=s_dg, dya=s_dya, dym=s_dym)
    grad = layer_backward(dx[0], x0[0], lambda j: mods[0, j : j + 1, :], own, other, wqkv, wo,
                          take, rows, stash, mods_out, bias)
    grad = grad.astype(bf16)
    pay_own[PAY_PATCH : PAY_PATCH + PV, :] += dot(xt[0], grad)
    pay_own[PAY_BPATCH : PAY_BPATCH + 1, :] += token_sum(grad.astype(f32))
    dmods[0, 6 : 6 + 8, :] = dmods1[0]
    rounded = dmods[0].astype(bf16).astype(f32)
    dmods[0] = rounded
    pay_own[PAY_COND : PAY_COND + 14, :] += rounded

    @pl.when(step == pl.num_programs(0) - 1)
    def _():
        for copy in copies:
            copy.wait()
        weight_grads(a_input_a, a_input_m, a_mixed, a_acted, stash,
                     (col_own, col_other), (row_own, row_other))
        pay_own[PAY_HEAD : PAY_HEAD + PV, :] = dhead[...]
        for layer, values in enumerate((dbias, dbias1)):
            pay_own[PAY_PROJ + layer : PAY_PROJ + layer + 1, :] = values[:, BIAS["proj"] : BIAS["proj"] + D]
            pay_own[PAY_FC2 + layer : PAY_FC2 + layer + 1, :] = values[:, BIAS["fc2"] : BIAS["fc2"] + D]
        head_line = jnp.sum(jnp.where(diagonal(PV), dbhead[...], 0.0), 0, keepdims=True)
        pay_own[PAY_BHEAD : PAY_BHEAD + 1, :] = jnp.concatenate(
            [head_line, jnp.sum(loss[...], 1, keepdims=True), jnp.zeros((1, D - PV - 1), f32)], 1
        )
        pay_other[...] = pay_own[...]
        for side, out in enumerate((pay_own, pay_other)):
            for layer, values in enumerate((dbias, dbias1)):
                write_bcol(values, side, out, layer)
        for out in (pay_own, pay_other):
            out[PAY_BCOL + 8 :, :] = jnp.zeros((PAY_ROWS - PAY_BCOL - 8, D), f32)


def per_latent(*shape):
    zeros = (0,) * len(shape)
    return pl.BlockSpec((1,) + shape, lambda n: (n,) + zeros)


def fixed(*shape):
    zeros = (0,) * len(shape)
    return pl.BlockSpec(shape, lambda n: zeros, pipeline_mode=pl.Buffered(1))


def params():
    return pltpu.CompilerParams(dimension_semantics=("arbitrary",), vmem_limit_bytes=62 * 2**20)


SAVED = [
    ("query", (TOK, D), bf16), ("keyed", (TOK, D), bf16), ("valued", (TOK, D), bf16),
    ("probs", (HEADS, TOK, TOK), f32), ("branch_a", (TOK, D), f32), ("middle", (TOK, D), f32),
    ("slope", (TOK, MLP), f32), ("branch_m", (TOK, D), f32), ("mixed", (TOK, D), bf16),
    ("acted", (TOK, MLP), bf16), ("input_a", (TOK, D), bf16), ("input_m", (TOK, D), bf16),
]
GRAD_SHAPES = [(COL_S, D), (COL_S, D), (ROW_S, D), (ROW_S, D)]
WEIGHT_SCRATCH = [pltpu.VMEM((D, 3 * D), bf16), pltpu.VMEM((D, D), bf16),
                  pltpu.VMEM((1, 3 * D), f32), pltpu.VMEM((1, MLP), f32)]


def weight_specs(layer):
    half = pl.BlockSpec((D, GATH), lambda n: (0, layer), pipeline_mode=pl.Buffered(1))
    return [half, half, fixed(L, COL_S), fixed(L, COL_S), fixed(1, NBR)]


def stash_scratch(count):
    rows = count * TOK
    return [pltpu.VMEM((rows, 3 * D), bf16), pltpu.VMEM((rows, MLP), bf16),
            pltpu.VMEM((rows, D), bf16), pltpu.VMEM((rows, D), bf16)]


def cost(flops, nbytes, count):
    return pl.CostEstimate(flops=int(flops * count), bytes_accessed=int(nbytes * count),
                           transcendentals=int(2e6 * count))


def run_forward(xt, mods, full_io, pos, weights):
    count = xt.shape[0]
    outs = [("x0", (TOK, D), f32)] + SAVED + [("x2", (TOK, D), f32)]
    return pl.pallas_call(
        forward_kernel,
        grid=(count,),
        in_specs=[per_latent(PV, TOK), per_latent(14, D),
                  pl.BlockSpec((1, PV, D), lambda n: (0, 0, 0)), fixed(TOK, D)] + weight_specs(0),
        out_specs=[per_latent(*shape) for _, shape, _ in outs],
        out_shape=[jax.ShapeDtypeStruct((count,) + shape, kind) for _, shape, kind in outs],
        scratch_shapes=WEIGHT_SCRATCH,
        compiler_params=params(),
        cost_estimate=cost(1.0e9, 6e6, count),
        name="forward_first",
    )(xt, mods, full_io, pos, *weights)


def run_middle(x2, mods, weights, full_io, targets):
    count = x2.shape[0]
    rows = count * TOK
    outs = [((count, TOK, D), per_latent(TOK, D)), ((count, 8, D), per_latent(8, D))]
    outs += [(shape, fixed(*shape)) for shape in GRAD_SHAPES]
    outs += [(shape, fixed(*shape)) for shape in ((1, BIAS_WIDTH), (PV, D), (PV, 1), (1, TOK))]
    return pl.pallas_call(
        middle_kernel,
        grid=(count,),
        in_specs=[per_latent(TOK, D), per_latent(14, D)] + weight_specs(1)
        + [pl.BlockSpec((1, PV, D), lambda n: (1, 0, 0)), per_latent(PV, TOK)],
        out_specs=[spec for _, spec in outs],
        out_shape=[jax.ShapeDtypeStruct(shape, f32) for shape, _ in outs],
        scratch_shapes=WEIGHT_SCRATCH
        + [pltpu.VMEM((TOK, D), bf16)] * 3
        + [pltpu.VMEM((HEADS, TOK, TOK), f32), pltpu.VMEM((rows, D), bf16),
           pltpu.VMEM((TOK, D), f32), pltpu.VMEM((TOK, D), f32), pltpu.VMEM((rows, MLP), bf16),
           pltpu.VMEM((TOK, MLP), f32), pltpu.VMEM((TOK, D), f32),
           pltpu.VMEM((rows, D), bf16), pltpu.VMEM((rows, D), bf16)]
        + stash_scratch(count),
        compiler_params=params(),
        cost_estimate=cost(3.2e9, 3e6, count),
        name="layer_second",
    )(x2, mods, *weights, full_io, targets)


def run_last(dx, x0, mods, weights, xt, smalls, dmods1, saved):
    count = dx.shape[0]
    rows = count * TOK
    outs = [((count, 14, D), per_latent(14, D))]
    outs += [(shape, fixed(*shape)) for shape in GRAD_SHAPES]
    outs += [(shape, fixed(*shape)) for shape in ((PAY_ROWS, D), (PAY_ROWS, D))]
    return pl.pallas_call(
        last_kernel,
        grid=(count,),
        in_specs=[per_latent(TOK, D), per_latent(TOK, D), per_latent(14, D)] + weight_specs(0)
        + [per_latent(PV, TOK)]
        + [fixed(*shape) for shape in ((1, BIAS_WIDTH), (PV, D), (PV, 1), (1, TOK))] + [per_latent(8, D)]
        + [per_latent(*shape) for _, shape, _ in SAVED[:-4]] + [pl.BlockSpec(memory_space=pl.ANY)] * 4,
        out_specs=[spec for _, spec in outs],
        out_shape=[jax.ShapeDtypeStruct(shape, f32) for shape, _ in outs],
        scratch_shapes=WEIGHT_SCRATCH
        + [pltpu.VMEM((rows, D), bf16)] * 3 + [pltpu.VMEM((rows, MLP), bf16)]
        + stash_scratch(count) + [pltpu.VMEM((1, BIAS_WIDTH), f32), pltpu.SemaphoreType.DMA((4,))],
        compiler_params=params(),
        cost_estimate=cost(2.2e9, 8e6, count),
        name="backward_first",
    )(dx, x0, mods, *weights, xt, *smalls, dmods1, *saved[:-4], *[v.reshape(rows, -1) for v in saved[-4:]])


PACK = 128
WIDE = 3 * D


def split3(values):
    high = values.astype(bf16)
    rest = values - high.astype(f32)
    mid = rest.astype(bf16)
    low = (rest - mid.astype(f32)).astype(bf16)
    return high, mid, low


def narrow_dot(small, big, dims):
    parts = split3(small)
    high, mid, low = split3(big)
    first = dot(jnp.concatenate(parts, 0), high, dims)
    second = dot(jnp.concatenate(parts[:2], 0), mid, dims)
    third = dot(parts[0], low, dims)
    r = small.shape[0]
    return first[:r] + ((first[r : 2 * r] + second[:r]) + (first[2 * r :] + second[r:] + third))


def outer(left, right):
    l1, l2, l3 = split3(left)
    r1, r2, r3 = split3(right)
    return dot(
        jnp.concatenate([l1, l1, l2, l2, l1, l3], 0), jnp.concatenate([r1, r2, r1, r2, r3, r1], 0), TN
    )


PROJECT_STEPS = 2
WIDE_BLOCK = COL_S // PROJECT_STEPS
TALL_BLOCK = ROW_S // PROJECT_STEPS


def project_step(err_col, own_col, got_col, err_row, own_row, got_row, fac_col, fac_row,
                 mat_col, mat_row, left_col, left_row):
    step = pl.program_id(0)
    matrix = err_col[0] + (own_col[...] + got_col[...])
    mat_col[...] = matrix
    part = narrow_dot(fac_col[0], matrix, NN)
    matrix = err_row[0] + (own_row[...] + got_row[...])
    mat_row[...] = matrix
    side = narrow_dot(fac_row[0], matrix, NT)

    @pl.when(step == 0)
    def _():
        left_col[...] = part
        left_row[...] = jnp.zeros_like(left_row)
        left_row[:, :TALL_BLOCK] = side

    @pl.when(step == 1)
    def _():
        left_col[...] += part
        left_row[:, TALL_BLOCK:ROW_S] = side


def project_second_kernel(block, err_col, own_col, got_col, err_row, own_row, got_row, fac_col, fac_row,
                          dmods, full_cond, cond_own,
                          mat_col, mat_row, left_col, left_row, grad_cond, cols_sent):
    project_step(err_col, own_col, got_col, err_row, own_row, got_row, fac_col, fac_row,
                 mat_col, mat_row, left_col, left_row)

    @pl.when(pl.program_id(0) == 0)
    def _():
        n_dp, count = cols_sent.shape[0], cols_sent.shape[1]
        line = jnp.concatenate([dmods[:, j, :] for j in range(14)], 1)
        grad_act = dot(line.astype(bf16), full_cond[...], NT)
        cond = cond_own[...]
        gate = 1.0 / (1.0 + jnp.exp(-cond))
        grad_cond[...] = grad_act * (gate * (1.0 + cond * (1.0 - gate)))
        for j in range(n_dp):
            cols_sent[j] = jnp.concatenate(
                [line[:, j * block : (j + 1) * block], jnp.zeros((count, D - block), f32)], 1
            )


def packed_slots():
    return ["row0", "row1", "col0", "col1", "io0", "io1", "row0", "row1", "row0", "row1"]


def project_first_kernel(err_col, own_col, got_col, err_row, own_row, got_row, fac_col, fac_row,
                         left_col1, left_row1, grad_cond, cols_sent, pay_own, pay_got, err_io, fac_io,
                         mat_col, mat_row, mat_io, sent, left_col, left_row):
    project_step(err_col, own_col, got_col, err_row, own_row, got_row, fac_col, fac_row,
                 mat_col, mat_row, left_col, left_row)

    @pl.when(pl.program_id(0) == PROJECT_STEPS - 1)
    def _():
        n_dp, count = cols_sent.shape[0], cols_sent.shape[1]
        share = PACK // n_dp
        pay = pay_own[...] + pay_got[...]
        left_io = []
        for index in range(2):
            matrix = pay[index * PV : (index + 1) * PV] + err_io[index]
            mat_io[index] = matrix
            left_io.append(dot_full(fac_io[index], matrix))
        sent[:, :count, :] = jnp.broadcast_to(grad_cond[...][None], (n_dp, count, D))
        sent[:, count : 2 * count, :] = cols_sent[...]
        sent[:, 2 * count :, :] = jnp.zeros((n_dp, share, D), f32)
        tall = (left_row, left_row1)
        for column in range(RANK):
            pick = slice(column, column + 1)
            lines = [tall[i % 2][pick, (i // 2) * D : (i // 2 + 1) * D] for i in (0, 1)]
            lines += [left_col[pick, :], left_col1[pick, :], left_io[0][pick], left_io[1][pick]]
            lines += [tall[i % 2][pick, (i // 2) * D : (i // 2 + 1) * D] for i in (2, 3, 4, 5)]
            for extra in range(6):
                at = column * 6 + extra
                if at < SMALL_ROWS:
                    lines.append(pay[PAY_PROJ + at : PAY_PROJ + at + 1])
            for slot, line in enumerate(lines):
                at = column * 16 + slot
                place = 2 * count + at % share
                sent[at // share, place : place + 1, :] = line


def project_specs(layer):
    col_block = pl.BlockSpec((WIDE_BLOCK, D), lambda n: (n, 0))
    row_block = pl.BlockSpec((TALL_BLOCK, D), lambda n: (n, 0))
    ins = [pl.BlockSpec((1, WIDE_BLOCK, D), lambda n: (layer, n, 0)), col_block, col_block,
           pl.BlockSpec((1, TALL_BLOCK, D), lambda n: (layer, n, 0)), row_block, row_block,
           pl.BlockSpec((1, RANK, WIDE_BLOCK), lambda n: (n, 0, 0)),
           pl.BlockSpec((1, RANK, D), lambda n: (layer, 0, 0))]
    return ins, [col_block, row_block]


def steps_of(fac_col):
    return fac_col.reshape(RANK, PROJECT_STEPS, WIDE_BLOCK).transpose(1, 0, 2)


def run_project_second(err_col, grads, err_row, fac_col, fac_row, dmods, full_cond, cond_own, n_dp):
    own_col, got_col, own_row, got_row = grads
    count = dmods.shape[0]
    ins, outs = project_specs(1)
    extra = [(RANK, D), (RANK, WIDE), (count, D), (n_dp, count, D)]
    return pl.pallas_call(
        lambda *refs: project_second_kernel(N_MODS // n_dp, *refs),
        grid=(PROJECT_STEPS,),
        in_specs=ins + [fixed(count, 14, D), fixed(D, N_MODS), fixed(count, D)],
        out_specs=outs + [fixed(*shape) for shape in extra],
        out_shape=[jax.ShapeDtypeStruct(shape, f32) for shape in [(COL_S, D), (ROW_S, D)] + extra],
        compiler_params=params(),
        name="left_second",
    )(err_col, own_col, got_col, err_row, own_row, got_row, steps_of(fac_col[1]), fac_row,
      dmods, full_cond, cond_own)


def run_project_first(err_col, grads, err_row, fac_col, fac_row, left_col1, left_row1, grad_cond, cols_sent,
                      pay_own, pay_got, err_io, fac_io):
    own_col, got_col, own_row, got_row = grads
    n_dp, count = cols_sent.shape[:2]
    ins, outs = project_specs(0)
    extra = [(2, PV, D), (n_dp, 2 * count + PACK // n_dp, D)]
    return pl.pallas_call(
        project_first_kernel,
        grid=(PROJECT_STEPS,),
        in_specs=ins + [fixed(RANK, D), fixed(RANK, WIDE), fixed(count, D), fixed(n_dp, count, D),
                        fixed(PAY_ROWS, D), fixed(PAY_ROWS, D), fixed(2, PV, D), fixed(2, RANK, PV)],
        out_specs=outs + [fixed(*shape) for shape in extra],
        out_shape=[jax.ShapeDtypeStruct(shape, f32) for shape in [(COL_S, D), (ROW_S, D)] + extra],
        scratch_shapes=[pltpu.VMEM((RANK, D), f32), pltpu.VMEM((RANK, WIDE), f32)],
        compiler_params=params(),
        name="left_first",
    )(err_col, own_col, got_col, err_row, own_row, got_row, steps_of(fac_col[0]), fac_row,
      left_col1, left_row1, grad_cond, cols_sent, pay_own, pay_got, err_io, fac_io)


TIME_ROWS = FREQ + D + 8


def modulation_kernel(block, core, got, act_half, features, first, first_act, full_time, labels,
                      cond_mine, cond_their, time_part, table_part):
    n_dp = got.shape[0]
    count = (got.shape[1] - PACK // n_dp) // 2
    half = block // 2
    grad_cond = got[:, :count, :].reshape(n_dp * count, D)
    cols = got[:, count : 2 * count, :].reshape(n_dp * count, D)
    left, right = cols[:, :half].astype(bf16), cols[:, half:block].astype(bf16)
    is_first = core[0] == 0
    grad_left = dot(act_half[...], left, TN)
    grad_right = dot(act_half[...], right, TN)
    cond_mine[...] = jnp.where(is_first, grad_left, grad_right)
    cond_their[...] = jnp.where(is_first, grad_right, grad_left)
    grad_second = grad_cond.astype(bf16)
    gate = 1.0 / (1.0 + jnp.exp(-first[...]))
    slope = gate * (1.0 + first[...] * (1.0 - gate))
    grad_first = (dot(grad_second, full_time[FREQ:, :], NT) * slope).astype(bf16)
    time_part[:FREQ, :] = dot(features[...], grad_first, TN)
    time_part[FREQ : FREQ + D, :] = dot(first_act[...], grad_second, TN)
    time_part[FREQ + D :, :] = jnp.concatenate(
        [token_sum(grad_first.astype(f32)), token_sum(grad_second.astype(f32)), jnp.zeros((6, D), f32)], 0
    )
    onehot = (labels[...] == lax.broadcasted_iota(jnp.int32, (n_dp * count, CLASSES), 1)).astype(f32).astype(bf16)
    high, mid, low = split3(grad_cond)
    table_part[...] = dot(high, onehot, TN) + (dot(mid, onehot, TN) + dot(low, onehot, TN))


def run_modulation(core, got, act_half, features, first, first_act, full_time, labels):
    half = N_MODS // got.shape[0] // 2
    shapes = [(D, half), (D, half), (TIME_ROWS, D), (D, CLASSES)]
    vmem = pl.BlockSpec(memory_space=pltpu.VMEM)
    return pl.pallas_call(
        lambda *refs: modulation_kernel(2 * half, *refs),
        in_specs=[pl.BlockSpec(memory_space=pltpu.SMEM)] + [vmem] * 7,
        out_shape=[jax.ShapeDtypeStruct(shape, f32) for shape in shapes],
        compiler_params=pltpu.CompilerParams(vmem_limit_bytes=62 * 2**20),
        name="modulation_gradients",
    )(core, got, act_half, features, first, first_act, full_time, labels)


COL_ROWS = 4 * RANK
ROW_AT = L * COL_ROWS
IO_AT = ROW_AT + L * RANK
EXTRA_AT = IO_AT + 2 * RANK


def cond_top(rows):
    return -(-((rows + 1) // 2) // 8) * 8


def ortho(packed, left_col, left_row, left_io):
    columns = []
    blank = jnp.zeros((4, D), f32)
    for index in range(RANK):
        block = packed[index]
        column = jnp.concatenate(
            [block[0:6], jnp.concatenate([block[6:8], blank], 0), jnp.concatenate([block[8:10], blank], 0)], 1
        )
        for earlier in columns:
            column = column - jnp.sum(earlier * column, -1, keepdims=True) * earlier
        column = column * lax.rsqrt(jnp.sum(column * column, -1, keepdims=True) + ortho_eps)
        for layer in range(L):
            left_row[layer, index : index + 1, :] = column[layer : layer + 1]
            left_col[layer, index : index + 1, :] = column[2 + layer : 3 + layer, :D]
            left_io[layer, index : index + 1, :] = column[4 + layer : 5 + layer, :D]
        columns.append(column)


def total_squares(values):
    return jnp.sum(values * values, keepdims=True)


def right_kernel(packed, mat_col0, mat_row0, mat_col1, mat_row1, mat_io, cond_own, cond_got, table_own, table_got,
                 sent, left_col, left_row, left_io, table_share, flat):
    ortho(packed, left_col, left_row, left_io)
    for layer, (col, row) in enumerate(((mat_col0, mat_row0), (mat_col1, mat_row1))):
        right = narrow_dot(left_col[layer], col[...], NT)
        for piece in range(4):
            wide = min(D, COL_S - piece * D)
            at = layer * COL_ROWS + piece * RANK
            if wide < D:
                flat[at : at + RANK, :] = jnp.zeros((RANK, D), f32)
            flat[at : at + RANK, :wide] = right[:, piece * D : piece * D + wide]
        at = ROW_AT + layer * RANK
        flat[at : at + RANK, :] = narrow_dot(left_row[layer][:, :ROW_S], row[...], NN)
        at = IO_AT + layer * RANK
        flat[at : at + RANK, :] = jnp.zeros((RANK, D), f32)
        flat[at : at + RANK, :PV] = dot_full(left_io[layer], mat_io[layer], NT)
    cond_grad = cond_own[...] + cond_got[...]
    table = table_own[...] + table_got[...]
    table_share[...] = table
    flat[EXTRA_AT:, :] = jnp.zeros((PACK - EXTRA_AT, D), f32)
    flat[EXTRA_AT : EXTRA_AT + 1, :] = jnp.concatenate(
        [total_squares(cond_grad), total_squares(table), jnp.zeros((1, D - 2), f32)], 1
    )
    n_dp = sent.shape[0]
    share = PACK // n_dp
    rows, half = D // n_dp, cond_grad.shape[1]
    top = cond_top(rows)
    sent[:, :share, :] = flat[...].reshape(n_dp, share, D)
    for j in range(n_dp):
        piece = cond_grad[j * rows : (j + 1) * rows]
        sent[j, share : share + min(top, rows), :half] = piece[:top]
        if rows > top:
            sent[j, share : share + rows - top, half : 2 * half] = piece[top:]


def run_right(n_dp, packed, mats, mat_io, cond_own, cond_got, table_own, table_got):
    shapes = [(n_dp, PACK // n_dp + cond_top(D // n_dp), D), (L, RANK, D), (L, RANK, WIDE), (2, RANK, D),
              table_own.shape]
    return pl.pallas_call(
        right_kernel,
        out_shape=[jax.ShapeDtypeStruct(shape, f32) for shape in shapes],
        scratch_shapes=[pltpu.VMEM((PACK, D), f32)],
        compiler_params=pltpu.CompilerParams(vmem_limit_bytes=62 * 2**20),
        name="right_factors",
    )(packed, *mats, mat_io, cond_own, cond_got, table_own, table_got)


def norm_kernel(packed, left_packed, left_col, left_row, left_io, time_own, time_got,
                right_col, right_row, right_io, parts, brep_grad, bcol_grad):
    for layer in range(L):
        for piece in range(4):
            wide = min(D, COL_S - piece * D)
            at = layer * COL_ROWS + piece * RANK
            right_col[layer, :, piece * D : piece * D + wide] = packed[at : at + RANK, :wide]
        at = ROW_AT + layer * RANK
        right_row[layer] = packed[at : at + RANK, :]
        at = IO_AT + layer * RANK
        right_io[layer] = packed[at : at + RANK, :PV]

    def small(at):
        row = at - PAY_PROJ
        return left_packed[row // 6, 10 + row % 6 : 11 + row % 6, :]

    time_bias = time_own[FREQ + D :, :] + time_got[FREQ + D :, :]
    lines = [small(PAY_PROJ + row) for row in range(4)] + [small(PAY_COND + row) for row in range(14)]
    lines += [time_bias[0:1], time_bias[1:2], small(PAY_BPATCH), small(PAY_BHEAD)[:, :PV]]
    whole = jnp.zeros((1, 1), f32)
    for row, line in enumerate(lines):
        brep_grad[:, row * D : row * D + line.shape[1]] = line
        whole = whole + total_squares(line)
    split = jnp.zeros((1, 1), f32)
    for layer in range(L):
        line = jnp.concatenate([small(PAY_BCOL + 4 * layer + row) for row in range(4)], 1)[:, :COL_S]
        bcol_grad[layer : layer + 1, :] = line
        split = split + total_squares(line)
    whole = whole + total_squares(time_own[: FREQ + D, :] + time_got[: FREQ + D, :])

    def gram(left, right):
        return jnp.sum(dot_full(left, left, NT) * dot_full(right, right, NT), keepdims=True)

    for layer in range(L):
        split = split + gram(left_col[layer], right_col[layer]) + gram(left_row[layer], right_row[layer])
        whole = whole + gram(left_io[layer], right_io[layer])
    sums = packed[EXTRA_AT : EXTRA_AT + 1, :]
    split = split + sums[:, 0:1]
    whole = whole + sums[:, 1:2]
    loss = small(PAY_BHEAD)[:, PV : PV + 1]
    parts[...] = jnp.concatenate([split, whole, loss, jnp.zeros((1, 125), f32)], 1)


def run_norm(packed, left_packed, lefts, time_own, time_got):
    shapes = [(L, RANK, COL_S), (L, RANK, D), (2, RANK, PV), (1, 128), (1, NBR), (L, COL_S)]
    return pl.pallas_call(
        norm_kernel,
        out_shape=[jax.ShapeDtypeStruct(shape, f32) for shape in shapes],
        compiler_params=pltpu.CompilerParams(vmem_limit_bytes=62 * 2**20),
        name="gradient_norm",
    )(packed, left_packed, *lefts, time_own, time_got)


def error_kernel(mat_col0, mat_row0, mat_col1, mat_row1, mat_io, left_col, left_row, left_io,
                 right_col, right_row, right_io, err_col, err_row, err_io):
    for layer, (col, row) in enumerate(((mat_col0, mat_row0), (mat_col1, mat_row1))):
        @pl.when(pl.program_id(0) == layer)
        def _():
            err_col[0] = col[...] - outer(right_col[layer], left_col[layer])
            err_row[0] = row[...] - outer(left_row[layer][:, :ROW_S], right_row[layer])
            err_io[layer] = mat_io[layer] - outer(right_io[layer], left_io[layer])


def run_error(mats, mat_io, lefts, rights):
    return pl.pallas_call(
        error_kernel,
        grid=(L,),
        in_specs=[fixed(*v.shape) for v in (*mats, mat_io, *lefts, *rights)],
        out_specs=[pl.BlockSpec((1, COL_S, D), lambda n: (n, 0, 0)),
                   pl.BlockSpec((1, ROW_S, D), lambda n: (n, 0, 0)), fixed(2, PV, D)],
        out_shape=[jax.ShapeDtypeStruct((L, COL_S, D), f32), jax.ShapeDtypeStruct((L, ROW_S, D), f32),
                   jax.ShapeDtypeStruct((2, PV, D), f32)],
        compiler_params=params(),
        name="next_errors",
    )(*mats, mat_io, *lefts, *rights)


def update_kernel(core, parts, parts_got, left_col, right_col, right_row, left_row, right_io, left_io,
                  cond_own, cond_got, time_grad, table_grad, bcol_grad, brep_grad,
                  w_col, w_row, w_cond, w_time, w_io, w_table, b_col, b_rep,
                  m_col, m_row, m_cond, m_time, m_io, m_table, m_bcol, m_brep,
                  scalars, n_col, n_row, n_cond, n_time, n_io, n_table, n_bcol, n_brep,
                  v_col, v_row, v_cond, v_time, v_io, v_table, v_bcol, v_brep):
    clip_norm = jnp.sqrt(parts[:, 0:1] + parts_got[:, 0:1] + parts[:, 1:2])
    scaling = jnp.minimum(1.0, clip_limit / clip_norm)
    scalars[...] = jnp.concatenate([parts[:, 2:3], clip_norm, jnp.zeros((1, 126), f32)], 1)

    def advance(weight, momentum, gradient):
        moved = momentum_decay * momentum + scaling * gradient
        return weight - learn_rate * moved, moved

    for layer in range(L):
        n_col[layer], v_col[layer] = advance(
            w_col[layer], m_col[layer], outer(left_col[layer], right_col[layer]))
        n_row[layer], v_row[layer] = advance(
            w_row[layer], m_row[layer], outer(right_row[layer], left_row[layer][:, :ROW_S]))
        n_io[layer], v_io[layer] = advance(
            w_io[layer], m_io[layer], outer(right_io[layer], left_io[layer]))
    n_dp = cond_own.shape[0]
    rows = w_cond.shape[0]
    half = N_MODS // n_dp // 2
    top = cond_top(rows)
    share = cond_own.shape[1] - top
    is_first = core[0] == 0
    pieces = []
    for j in range(n_dp):
        mine, theirs = cond_own[j, share:, :], cond_got[j]
        for pair in ((mine, theirs), (theirs, mine)):
            block = jnp.where(is_first, pair[0], pair[1])
            if rows > top:
                block = jnp.concatenate([block[:top, :half], block[: rows - top, half : 2 * half]], 0)
            else:
                block = block[:rows, :half]
            pieces.append(block)
    n_cond[...], v_cond[...] = advance(w_cond[...], m_cond[...], jnp.concatenate(pieces, 1))
    n_time[...], v_time[...] = advance(w_time[...], m_time[...], time_grad[...])
    n_table[...], v_table[...] = advance(w_table[...], m_table[...], table_grad[...])
    n_bcol[...], v_bcol[...] = advance(b_col[...], m_bcol[...], bcol_grad[...])
    n_brep[...], v_brep[...] = advance(b_rep[...], m_brep[...], brep_grad[...])


def run_update(core, grads, weights, momenta):
    vmem = pl.BlockSpec(memory_space=pltpu.VMEM)
    shapes = [(1, 128)] + [v.shape for v in weights] * 2
    return pl.pallas_call(
        update_kernel,
        in_specs=[pl.BlockSpec(memory_space=pltpu.SMEM)] + [vmem] * (len(grads) + 2 * len(weights)),
        out_shape=[jax.ShapeDtypeStruct(shape, f32) for shape in shapes],
        compiler_params=pltpu.CompilerParams(vmem_limit_bytes=62 * 2**20),
        name="weight_update",
    )(core, *grads, *weights, *momenta)


def swap(values):
    return lax.ppermute(values, "tensor", [(0, 1), (1, 0)])


def trade(chunks):
    return lax.all_to_all(chunks, "dp", 0, 0, tiled=True)


def spread(values):
    return trade(jnp.broadcast_to(values[None], (lax.axis_size("dp"),) + values.shape))


def exact_parts(values):
    high = lax.reduce_precision(values, 8, 7)
    mid = lax.reduce_precision(values - high, 8, 7)
    return [part.astype(bf16) for part in (high, mid, (values - high) - mid)]


def on_device(
    latents, gauss_noise, time_steps, labels, targets,
    w_col, w_row, w_cond, w_time, w_io, class_table, b_col, b_rep,
    mom_col, mom_row, mom_cond, mom_time, mom_io, mom_table, mom_bcol, mom_brep,
    err_col, err_row, err_io, fac_col, fac_row, fac_io,
):
    n_dp = lax.axis_size("dp")
    index_dp = lax.axis_index("dp")
    index_t = lax.axis_index("tensor")
    core = index_t.astype(jnp.int32).reshape(1)
    first_core = index_t == 0
    n_all = labels.shape[0]
    per_dp = latents.shape[0]
    count = per_dp // 2
    rows = w_col.shape[1]

    def flip(values):
        return values.transpose(0, 2, 1)

    def halves(mine, theirs, axis):
        pair = jnp.stack([mine, theirs], axis)
        return jnp.where(first_core, pair, jnp.flip(pair, axis))

    row_sh = flip(w_row)
    shard = jnp.concatenate(
        [piece[layer] for layer in range(L)
         for piece in (w_col[:, :, QKV_S:], row_sh[:, :, HALF:], w_col[:, :, :QKV_S], row_sh[:, :, :HALF])], 1
    ).astype(bf16)
    full = lax.all_gather(shard, ("dp", "tensor"))

    block = N_MODS // n_dp
    half_block = block // 2
    classes = jnp.arange(CLASSES, dtype=jnp.int32)
    onehot_t = classes[:, None] == labels[None, :]
    looked = dot(class_table.astype(bf16), onehot_t.astype(bf16), TN).astype(bf16)
    time_rows = w_time.shape[0]
    sizes = [rows * n_all, time_rows * D, 2 * PV * rows, 3 * per_dp]
    wide = -(-sum(sizes) // 256) * 128
    common = jnp.concatenate(
        [part.reshape(-1) for part in
         (looked, w_time.astype(bf16), flip(w_io).astype(bf16), *exact_parts(time_steps))]
    )
    common = jnp.pad(common, (0, 2 * wide - common.shape[0]))
    common = lax.dynamic_slice_in_dim(common.reshape(2, wide), index_t, 1, 0)
    cond_bf = w_cond.astype(bf16).reshape(rows, n_dp, 2, half_block)
    cond_mine = lax.dynamic_slice_in_dim(cond_bf, index_t, 1, 2)[:, :, 0].transpose(1, 0, 2)
    sent = jnp.concatenate(
        [jnp.broadcast_to(common, (n_dp, wide)), cond_mine.reshape(n_dp, rows * half_block)], 1
    )
    got = trade(sent)
    cond_cols = got[:, wide:].reshape(D, half_block)
    mine = got[:, :wide]
    common = halves(mine, swap(mine), 1).reshape(n_dp, 2 * wide)
    ends = np.cumsum([0] + sizes)
    looked = common[:, : ends[1]].reshape(D, n_all).T
    full_time = common[:, ends[1] : ends[2]].reshape(FREQ + D, D)
    full_io = flip(common[:, ends[2] : ends[3]].reshape(n_dp, 2 * PV, rows).transpose(1, 0, 2).reshape(2, PV, D).transpose(0, 2, 1))
    steps_all = jnp.sum(common[:, ends[3] : ends[4]].reshape(n_dp, 3, per_dp).astype(f32), 1).reshape(n_all)

    features = frequency_features(steps_all).astype(bf16)
    first = dot(features, full_time[:FREQ]) + b_rep[START_FIRST:START_SECOND]
    first_act = jax.nn.silu(first).astype(bf16)
    second = dot(first_act, full_time[FREQ:]) + b_rep[START_SECOND:START_PATCH]
    cond = second + looked.astype(f32)
    cond_act = jax.nn.silu(cond).astype(bf16)
    mods = dot(cond_act, cond_cols).reshape(n_dp * 2, count, half_block)
    mods = lax.all_to_all(mods, ("dp", "tensor"), 0, 0, tiled=True)
    mods = mods.transpose(1, 0, 2).reshape(count, N_MODS)
    mods = (mods + b_rep[START_COND:START_FIRST]).reshape(count, 14, D)
    full, mods = lax.optimization_barrier((full, mods))
    full = full.reshape(n_dp, 2, rows, L * GATH)

    def half_of(values):
        split = values.reshape((n_dp, 2, count) + values.shape[1:])
        return lax.dynamic_slice_in_dim(split, index_t, 1, 1).reshape((n_dp * count,) + values.shape[1:])

    halves_of = [half_of(v) for v in (cond_act, features, first, first_act)]
    labels_half = half_of(labels)[:, None]
    cond_own = lax.dynamic_slice_in_dim(cond, (index_dp * 2 + index_t) * count, count, 0)

    def mine_of(values):
        return lax.dynamic_slice_in_dim(values, index_t * count, count, 0)

    steps_own = mine_of(time_steps)[:, None, None]
    xt = (
        (1.0 - steps_own) * flip(mine_of(latents)) + steps_own * flip(mine_of(gauss_noise))
    ).astype(bf16)
    b_line = b_rep[None]
    own = lax.dynamic_slice_in_dim(full, index_t, 1, 1).reshape(D, L * GATH)
    other = lax.dynamic_slice_in_dim(full, 1 - index_t, 1, 1).reshape(D, L * GATH)
    weights = (own, other, b_col, swap(b_col), b_line)
    x0, *saved, x2 = run_forward(xt, mods, full_io, jnp.asarray(position_table()), weights)
    x2, late_cond = lax.optimization_barrier((x2, w_cond))
    full_cond = lax.all_gather(late_cond.astype(bf16), "dp", axis=0, tiled=True)
    dx, dmods1, col_own1, col_oth1, row_own1, row_oth1, *smalls = run_middle(
        x2, mods, weights, full_io, flip(mine_of(targets))
    )
    grads1 = (col_own1, swap(col_oth1), row_own1, swap(row_oth1))
    dmods, col_own0, col_oth0, row_own0, row_oth0, pay_own, pay_oth = run_last(
        dx, x0, mods, weights, xt, smalls, dmods1, saved
    )
    grads0 = (col_own0, swap(col_oth0), row_own0, swap(row_oth0))
    pay_got = swap(pay_oth)

    err_col_t, err_io_t = flip(err_col), flip(err_io)
    fac_col_t, fac_row_t, fac_io_t = flip(fac_col), flip(fac_row), flip(fac_io)
    mat_col1, mat_row1, left_col1, left_row1, grad_cond, cols_sent = run_project_second(
        err_col_t, grads1, err_row, fac_col_t, fac_row_t, dmods, full_cond, cond_own, n_dp
    )
    mat_col0, mat_row0, mat_io, sent = run_project_first(
        err_col_t, grads0, err_row, fac_col_t, fac_row_t, left_col1, left_row1, grad_cond, cols_sent,
        pay_own, pay_got, err_io_t, fac_io_t
    )
    mats = (mat_col0, mat_row0, mat_col1, mat_row1)
    got = trade(sent)
    left_packed = spread(jnp.sum(got[:, 2 * count :], 0)).reshape(RANK, 16, D)

    cond_mine, cond_their, time_own, table_part = run_modulation(core, got, *halves_of, full_time, labels_half)
    cond_got, time_got = swap(cond_their), swap(time_own)
    table_own = lax.dynamic_slice_in_dim(table_part, index_dp * rows, rows, 0)
    table_got = swap(table_own)

    sent, left_col, left_row, left_io, table_share = run_right(
        n_dp, left_packed, mats, mat_io, cond_mine, cond_got, table_own, table_got
    )
    share = PACK // n_dp
    got = trade(sent)
    packed = spread(jnp.sum(got[:, :share], 0)).reshape(PACK, D)
    cond_rows_got = swap(got[:, share:])
    lefts = (left_col, left_row, left_io)
    right_col, right_row, right_io, parts, brep_grad, bcol_grad = run_norm(
        packed, left_packed, lefts, time_own, time_got
    )
    parts_got = swap(parts)
    next_err_col, next_err_row, next_err_io = run_error(mats, mat_io, lefts, (right_col, right_row, right_io))

    def mine_cols(values):
        return lax.dynamic_slice_in_dim(values, index_dp * rows, rows, 2)

    time_at = index_dp * time_rows
    time_grad = (
        lax.dynamic_slice_in_dim(time_own, time_at, time_rows, 0)
        + lax.dynamic_slice_in_dim(time_got, time_at, time_rows, 0)
    )
    olds = (w_col, flip(w_row), w_cond, w_time, flip(w_io), class_table.T, b_col, b_line)
    momenta = (mom_col, flip(mom_row), mom_cond, mom_time, flip(mom_io), mom_table.T, mom_bcol, mom_brep[None])
    scalars, *new = run_update(
        core,
        (parts, parts_got, mine_cols(left_col), right_col, mine_cols(right_row), left_row, right_io,
         mine_cols(left_io), got, cond_rows_got, time_grad, table_share, bcol_grad, brep_grad),
        olds, momenta,
    )

    def outward(col, row, cond, time, io, table, bcol, brep):
        return (col, flip(row), cond, time, flip(io), table.T, bcol, brep[0])

    return (
        scalars[0, 0], scalars[0, 1], *outward(*new[:8]), *outward(*new[8:]),
        flip(next_err_col), next_err_row, flip(next_err_io), flip(right_col), flip(right_row), flip(right_io),
    )


def solution(mesh):
    weights = (
        P(None, "dp", "tensor"), P(None, "tensor", "dp"), P("dp", None), P("dp", None),
        P(None, "dp", None), P(None, "dp"), P(None, "tensor"), P(),
    )
    errors = (P("dp", None, "tensor"), P("dp", "tensor", None), P("dp", None, None))
    factors = (P(None, "tensor", None), P(None, "tensor", None), P())
    rows = P("dp", None, None)
    return jax.shard_map(
        on_device,
        mesh=mesh,
        in_specs=(rows, rows, P("dp"), P(), rows) + weights + weights + errors + factors,
        out_specs=(P(), P()) + weights + weights + errors + factors,
        check_vma=False,
    )
```

time: 543 us -> 399 us (0.73)
  waiting for transfers between devices: 112 us -> 65.4 us
  starting transfers between devices: 82.3 us -> 36.4 us
  local copies, waits for them, and re-layouts: 63.9 us -> 32.9 us
  blocking collectives: 0 us -> 23.6 us
  matrix products: 19.3 us -> 4.18 us
  other arithmetic: 25.4 us -> 10.3 us
  between operations: 22.6 us -> 14.9 us
    all_to_all x14 -> x5, starting transfers between devices: 70.8 us -> 25.2 us  [the longest x4 22.1 us: trade(): return lax.all_to_all(chunks, 'dp', 0, 0, tiled=True)]
    all_gather x3 -> x2, waiting for transfers between devices: 57.5 us -> 26.5 us  [the longest x1 26.5 us: on_device(): full = lax.all_gather(shard, ('dp', 'tensor'))]
    all_to_all x0 -> x1, blocking collectives: none -> 23.6 us  [trade(): return lax.all_to_all(chunks, 'dp', 0, 0, tiled=True)]
    all_to_all x14 -> x5, waiting for transfers between devices: 48.2 us -> 31.9 us  [the longest x4 24 us: trade(): return lax.all_to_all(chunks, 'dp', 0, 0, tiled=True)]
    dynamic_slice x2 -> x9, local copies, waits for them, and re-layouts: 0.03 us -> 13.5 us  [the longest x1 6.48 us: on_device(): lax.dynamic_slice_in_dim(full, 1 - index_t, 1, 1).reshape(D, L * GATH)]
    unnamed x119 -> x48, local copies, waits for them, and re-layouts: 18.7 us -> 5.46 us
    dot_general x10 -> x0, matrix products: 10.4 us -> none  [the longest x1 2.15 us: on_device(): jnp.einsum('lrn,lrm->lnm', left_row, lax.dynamic_slice_in_dim(right_row,...]
    sub x6 -> x0, other arithmetic: 9.54 us -> none  [advance(): return (weight - learn_rate * moved, moved)]
  transfers between devices with their start and end apart: 29 -> 19, of which waited for: 12 -> 8; matrix products, arithmetic and copies ran while one was open for 19% -> 10% of each run, Pallas kernels for 39% -> 38%
where the time goes in v2:
time: 399 us; the launch traced here: 393 us
  Pallas kernels  206 us (52%)
  waiting for transfers between devices  65.4 us (16%)
  starting transfers between devices  36.4 us (9%)
  local copies, waits for them, and re-layouts  32.9 us (8%)
  blocking collectives  23.6 us (6%)
  between operations  14.9 us (4%)
  other arithmetic  10.3 us (3%)
  matrix products  4.18 us (1%)
    pallas_call x1, Pallas kernels, run_middle(): pl.pallas_call(middle_kernel, grid=(count,), in_specs=[per_latent(TOK, D)...  78.6 us
    pallas_call x1, Pallas kernels, run_last(): pl.pallas_call(last_kernel, grid=(count,), in_specs=[per_latent(TOK, D),...  47 us
    pallas_call x1, Pallas kernels, run_forward(): pl.pallas_call(forward_kernel, grid=(count,), in_specs=[per_latent(PV, TO...  38.2 us
    all_gather x1, waiting for transfers between devices, on_device(): full = lax.all_gather(shard, ('dp', 'tensor'))  26.5 us
    all_to_all x4, waiting for transfers between devices, trade(): return lax.all_to_all(chunks, 'dp', 0, 0, tiled=True)  24 us
    all_to_all x1, blocking collectives, trade(): return lax.all_to_all(chunks, 'dp', 0, 0, tiled=True)  23.6 us
    all_to_all x4, starting transfers between devices, trade(): return lax.all_to_all(chunks, 'dp', 0, 0, tiled=True)  22.1 us
    ppermute x12, starting transfers between devices, swap(): return lax.ppermute(values, 'tensor', [(0, 1), (1, 0)])  10.7 us
  transfers between devices with their start and end apart: 19, of which 8 were waited for; matrix products, arithmetic and copies ran while one was open for 10% of the time, Pallas kernels for 38%

profile of v2, /device:TPU:1, one launch (start us, length us, event | category | flops | bytes accessed | tf_op | source)
XLA Modules:
  0.0 393.2 jit_solution(2059885897216408239)
XLA Ops:
  7.3 1.0 convert.35
  8.3 0.9 bitcast_convert_fusion.1
  9.4 0.8 concatenate.25
  10.8 0.8 convert_element_type.74
  11.7 1.2 fusion.1
  13.2 1.1 reshape.287
  16.0 0.9 reduce.6
  17.4 23.6 %all_to_all.37 = bf16[16,2,7648]{2,1,0:T(2,128)(2,1)S(1)} all-to-all(bf16[16,2,7648]{2,1,0:T(2,128)(2,1)S(1)} %reshape.324), channel_id=1, replica_groups=mesh['dp'=16,'tensor'=2] {'dp'}, dimensions={0} | all-to-all | bytes 978944 | tf_op jit(solution)/shard_map/all_to_all | solution.py:979
  41.9 2.1 collective-permute-start
  44.5 0.8 collective-permute-done
  46.9 1.0 multiply_convert_fusion.1
  47.9 1.1 multiply_convert_fusion
  49.0 0.9 fusion.6
  49.9 3.1 all-to-all-start.1
  53.6 1.7 dynamic-slice_bitcast_fusion.1
  55.6 0.8 reshape.294.wpatch.whead
  56.4 7.9 %all-to-all-done.1 = f32[32,8,168]{2,1,0:T(8,128)S(1)} async-done(((f32[32,8,168]{2,1,0:T(8,128)}), f32[32,8,168]{2,1,0:T(8,128)S(1)}, u32[]{:S(2)}, u32[]{:S(2)}) %all-to-all-start.1) | async-done | bytes 172064 | tf_op jit(solution)/shard_map/all_to_all | solution.py:1058
  65.3 26.5 %all-gather.3.cloned.1.call-done = bf16[32,24,4608]{2,1,0:T(8,128)(2,1)} async-done(((bf16[1,24,4608]{2,1,0:T(8,128)(2,1)}), bf16[32,24,4608]{2,1,0:T(8,128)(2,1)}) %all-gather.3.cloned.1.call-update) | async-done | bytes 7077904 | tf_op jit(solution)/shard_map/all_gather | solution.py:1020
  91.9 6.5 %constant_dynamic-slice_fusion.5 = (bf16[16,1,24,4608]{3,2,1,0:T(8,128)(2,1)}, bf16[16,1,24,4608]{3,2,1,0:T(8,128)(2,1)}) fusion(bf16[16,2,24,4608]{3,2,1,0:T(8,128)(2,1)} %bitcast.106, s32[]{:T(128)S(6)} %select_n.44, s32[]{:T(128)S(6)} %select_n.22), kind=kLoop, calls=%fused_computation.56 | loop fusion | bytes 14155784 | tf_op jit(solution)/shard_map/dynamic_slice | solution.py:1081
  98.9 38.2 %forward_first.1 = (f32[8,256,384]{2,1,0:T(8,128)}, bf16[8,256,384]{2,1,0:T(8,128)(2,1)}, bf16[8,256,384]{2,1,0:T(8,128)(2,1)}, bf16[8,256,384]{2,1,0:T(8,128)(2...) custom-call(bf16[8,16,256]{2,1,0:T(8,128)(2,1)} %get-tuple-element.2, ...), custom_call_target="tpu_custom_call" | custom-call | flops 8000000000 | bytes 48000000 | tf_op jit(solution)/shard_map/forward_first/pallas_call | solution.py:488
  137.9 78.6 %layer_second.1 = (f32[8,256,384]{2,1,0:T(8,128)}, f32[8,8,384]{2,1,0:T(8,128)}, f32[1344,384]{1,0:T(8,128)}, f32[1344,384]{1,0:T(8,128)}, f32[960,384]{1,0:T(8,...) custom-call(f32[8,256,384]{2,1,0:T(8,128)} %get-tuple-element.107.x2, ...), custom_call_target="tpu_custom_call" | custom-call | flops 25600000000 | bytes 24000000 | tf_op jit(solution)/shard_map/layer_second/pallas_call | solution.py:508
  216.8 47.0 %backward_first.1 = (f32[8,14,384]{2,1,0:T(8,128)}, f32[1344,384]{1,0:T(8,128)}, f32[1344,384]{1,0:T(8,128)}, f32[960,384]{1,0:T(8,128)}, f32[960,384]{1,0:T(8,1...) custom-call(f32[8,256,384]{2,1,0:T(8,128)} %get-tuple-element.108.dx, f32[8,256,384]{2,1,0:T(8,128)} %get-tuple-element.109.x0, ...), custom_call_target="tpu_custom_call" | custom-call | flops 17600000000 | bytes 64000000 | tf_op jit(solution)/shard_map/backward_first/pallas_call | solution.py:534
  266.4 1.3 constant_dynamic-slice_fusion.4.refs_10_
  267.7 4.9 %collective-permute-done.5.refs_5_ = f32[960,384]{1,0:T(8,128)} collective-permute-done((f32[960,384]{1,0:T(8,128)}, f32[960,384]{1,0:T(8,128)}, u32[]{:S(2)}, u32[]{:S(2)}) %collective-permute-start.5) | collective-permute-done | bytes 1474592 | tf_op jit(solution)/shard_map/ppermute | solution.py:975
  272.5 9.0 %left_second.1 = (f32[1344,384]{1,0:T(8,128)}, f32[960,384]{1,0:T(8,128)}, f32[8,384]{1,0:T(8,128)}, f32[8,1152]{1,0:T(8,128)}, f32[8,384]{1,0:T(8,128)}, /*index=5*/f32[16,8,384]{2,1,0:T(8,128)}) custom-call(f32[2,1344,384]{2,1,0:T(8,128)} %bitcast.104, f32[1344,384]{1,0:T(8,128)} %get-tuple-element.131.refs_1_, ...), custom_call_target="tpu_custom_call" | custom-call | tf_op jit(solution)/shard_map/left_second/pallas_call | solution.py:687
  282.7 6.7 %left_first.1 = (f32[1344,384]{1,0:T(8,128)}, f32[960,384]{1,0:T(8,128)}, f32[2,16,384]{2,1,0:T(8,128)}, f32[16,24,384]{2,1,0:T(8,128)}) custom-call(f32[2,1344,384]{2,1,0:T(8,128)} %bitcast.105, f32[1344,384]{1,0:T(8,128)} %get-tuple-element.127.own_col, f32[1344,384]{1,0:T(8,128)} %collective-permute-done.2.got_col, f32[2,960,384]{2,1,0:T(8,128)} %err_row.1, ...), custom_call_target="tpu_custom_call" | custom-call | tf_op jit(solution)/shard_map/left_first/pallas_call | solution.py:705
  289.4 3.9 all-to-all-start.2
  294.3 1.6 dynamic-slice_bitcast_fusion.refs_4_
  297.2 9.9 %all-to-all-done.2.refs_1_ = f32[16,24,384]{2,1,0:T(8,128)S(1)} async-done(((f32[16,24,384]{2,1,0:T(8,128)}), f32[16,24,384]{2,1,0:T(8,128)S(1)}, u32[]{:S(2)}, u32[]{:S(2)}) %all-to-all-start.2) | async-done | bytes 589856 | tf_op jit(solution)/shard_map/all_to_all | solution.py:979
  307.9 5.8 %all-to-all-start.3 = ((f32[16,8,384]{2,1,0:T(8,128)}), f32[16,8,384]{2,1,0:T(8,128)S(1)}, u32[]{:S(2)}, u32[]{:S(2)}) async-start(f32[16,8,384]{2,1,0:T(8,128)} %broadcast_in_dim.15), calls=%async_computation.3 | async-start | bytes 393216 | tf_op jit(solution)/shard_map/all_to_all | solution.py:979
  314.4 3.8 modulation_gradients.1
  318.2 1.8 collective-permute-start.7
  320.0 0.9 constant_dynamic-slice_fusion.3.table_own
  320.9 1.3 collective-permute-done.8.table_got
  323.1 8.4 %right_factors.1 = (f32[16,24,384]{2,1,0:T(8,128)}, f32[2,8,384]{2,1,0:T(8,128)}, f32[2,8,1152]{2,1,0:T(8,128)}, f32[2,8,384]{2,1,0:T(8,128)}, f32[24,1000]{1,0:T(8,128)}) custom-call(f32[8,16,384]{2,1,0:T(8,128)} %bitcast.119, f32[1344,384]{1,0:T(8,128)} %get-tuple-element.144.mat_col0, f32[960,384]{1,0:T(8,128)} %get-tuple-element.145.mat_row0, ...), custom_call_target="tpu_custom_call" | custom-call | tf_op jit(solution)/shard_map/right_factors/pallas_call | solution.py:832
  331.4 6.6 %all-to-all-start.4 = ((f32[16,24,384]{2,1,0:T(8,128)}), f32[16,24,384]{2,1,0:T(8,128)S(1)}, u32[]{:S(2)}, u32[]{:S(2)}) async-start(f32[16,24,384]{2,1,0:T(8,128)} %get-tuple-element.152), calls=%async_computation.4 | async-start | bytes 1179648 | tf_op jit(solution)/shard_map/all_to_all | solution.py:979
  338.6 13.3 %all-to-all-done.4.cond_own = f32[16,24,384]{2,1,0:T(8,128)S(1)} async-done(((f32[16,24,384]{2,1,0:T(8,128)}), f32[16,24,384]{2,1,0:T(8,128)S(1)}, u32[]{:S(2)}, u32[]{:S(2)}) %all-to-all-start.4) | async-done | bytes 589856 | tf_op jit(solution)/shard_map/all_to_all | solution.py:979
  352.7 5.8 %all-to-all-start.5 = ((f32[16,8,384]{2,1,0:T(8,128)}), f32[16,8,384]{2,1,0:T(8,128)S(1)}, u32[]{:S(2)}, u32[]{:S(2)}) async-start(f32[16,8,384]{2,1,0:T(8,128)} %broadcast_in_dim.16), calls=%async_computation.5 | async-start | bytes 393216 | tf_op jit(solution)/shard_map/all_to_all | solution.py:979
  358.5 0.8 slice.148
  359.2 1.8 collective-permute-start.11
  361.0 1.4 constant_dynamic-slice_fusion.left_io
  362.4 1.4 constant_dynamic-slice_fusion.2.left_col
  366.1 3.2 gradient_norm.1
  369.4 2.8 collective-permute-start.10
  372.2 1.4 constant_dynamic-slice_fusion.1.right_row
  373.6 6.8 %next_errors.1 = (f32[2,1344,384]{2,1,0:T(8,128)}, f32[2,960,384]{2,1,0:T(8,128)}, f32[2,16,384]{2,1,0:T(8,128)}) custom-call(f32[1344,384]{1,0:T(8,128)} %get-tuple-element.144.mat_col0, f32[960,384]{1,0:T(8,128)} %get-tuple-element.145.mat_row0, f32[1344,384]{1,0:T(8,128)} %get-tuple-element.146.mat_col1, f32[960,384]{1,0:T(8,128)} %get-tuple-element.147.mat_row1, ...), custom_call_target="tpu_custom_call" | custom-call | tf_op jit(solution)/shard_map/next_errors/pallas_call | solution.py:905
  381.0 3.9 weight_update.1
  384.9 1.3 fusion.28
  (136 shorter events, 22.1 us)
Async XLA Ops:
  7.2 5.7 %copy-start.15 = (f32[2,24,16]{1,2,0:T(8,128)S(1)}, f32[2,24,16]{1,2,0:T(8,128)}, u32[]{:S(2)}) copy-start(f32[2,24,16]{1,2,0:T(8,128)} %param.37) | copy-start | bytes 9220
  7.2 6.0 %copy-start.1 = (f32[24,5376]{1,0:T(8,128)S(1)}, f32[24,5376]{1,0:T(8,128)}, u32[]{:S(2)}) copy-start(f32[24,5376]{1,0:T(8,128)} %w_cond.1) | copy-start | bytes 1548292
  7.2 84.6 %all-gather.3.cloned.1.call-start = ((), (), s32[]{:S(2)}) async-start(), calls=%async_computation.6 | async-start | bytes 7299072 | tf_op jit(solution)/shard_map/all_gather | solution.py:1020
  40.9 3.1 copy-start.17
  40.9 3.2 copy-start.11
  41.9 3.4 collective-permute-start
  44.0 54.3 %collective-permute-start.1 = (f32[2,1344]{1,0:T(2,128)S(1)}, f32[2,1344]{1,0:T(2,128)S(1)}, u32[]{:S(2)}, u32[]{:S(2)}) collective-permute-start(f32[2,1344]{1,0:T(2,128)S(1)} %copy-done.17), channel_id=1, source_target_pairs={{0,1},{1,0},{2,3},{3,2},{4,5},{5,4},{6,7},{7,6},{8,9},{9,8},{10,11... | collective-permute-start | bytes 32264 | tf_op jit(solution)/shard_map/ppermute | solution.py:975
  46.1 1.8 copy-start.3
  47.9 5.7 %copy-start.18 = (f32[16]{0:T(128)S(1)}, f32[16]{0:T(128)}, u32[]{:S(2)}) copy-start(f32[16]{0:T(128)} %param.30) | copy-start | bytes 196
  47.9 5.8 %copy-start.16 = (f32[16,256,16]{1,2,0:T(8,128)S(1)}, f32[16,256,16]{1,2,0:T(8,128)}, u32[]{:S(2)}) copy-start(f32[16,256,16]{1,2,0:T(8,128)} %param.32) | copy-start | bytes 786436
  49.9 14.4 %all-to-all-start.1 = ((f32[32,8,168]{2,1,0:T(8,128)}), f32[32,8,168]{2,1,0:T(8,128)S(1)}, u32[]{:S(2)}, u32[]{:S(2)}) async-start(f32[32,8,168]{2,1,0:T(8,128)} %fusion.6), calls=%async_computation.1 | async-start | bytes 524288 | tf_op jit(solution)/shard_map/all_to_all | solution.py:1058
  53.0 219.5 %all-gather.5.cloned.1.call-start = ((), (), s32[]{:S(2)}) async-start(), calls=%async_computation.7 | async-start | bytes 4386816 | tf_op jit(solution)/shard_map/all_gather | solution.py:1085
  98.3 0.6 copy-start.21
  216.4 56.1 %collective-permute-start.4 = (f32[1344,384]{1,0:T(8,128)}, f32[1344,384]{1,0:T(8,128)}, u32[]{:S(2)}, u32[]{:S(2)}) collective-permute-start(f32[1344,384]{1,0:T(8,128)} %get-tuple-element.132), channel_id=1, source_target_pairs={{0,1},{1,0},{2,3},{3,2},{4,5},{5,4},{6,7},{7,6},{8,9},{9,8},{10,11... | collective-permute-start | bytes 6193160 | tf_op jit(solution)/shard_map/ppermute | solution.py:975
  216.8 47.8 %copy-start.14 = (f32[2,1344,8]{1,2,0:T(8,128)S(1)}, f32[2,1344,8]{1,2,0:T(8,128)}, u32[]{:S(2)}) copy-start(f32[2,1344,8]{1,2,0:T(8,128)} %param.52) | copy-start | bytes 258052
  263.8 17.8 %collective-permute-start.2 = (f32[1344,384]{1,0:T(8,128)}, f32[1344,384]{1,0:T(8,128)}, u32[]{:S(2)}, u32[]{:S(2)}) collective-permute-start(f32[1344,384]{1,0:T(8,128)} %get-tuple-element.128), channel_id=1, source_target_pairs={{0,1},{1,0},{2,3},{3,2},{4,5},{5,4},{6,7},{7,6},{8,9},{9,8},{10,11... | collective-permute-start | bytes 6193160 | tf_op jit(solution)/shard_map/ppermute | solution.py:975
  264.1 8.5 %collective-permute-start.5 = (f32[960,384]{1,0:T(8,128)}, f32[960,384]{1,0:T(8,128)}, u32[]{:S(2)}, u32[]{:S(2)}) collective-permute-start(f32[960,384]{1,0:T(8,128)} %get-tuple-element.134), channel_id=1, source_target_pairs={{0,1},{1,0},{2,3},{3,2},{4,5},{5,4},{6,7},{7,6},{8,9},{9,8},{10,11... | collective-permute-start | bytes 4423688 | tf_op jit(solution)/shard_map/ppermute | solution.py:975
  264.4 17.2 %collective-permute-start.3 = (f32[960,384]{1,0:T(8,128)}, f32[960,384]{1,0:T(8,128)S(1)}, u32[]{:S(2)}, u32[]{:S(2)}) collective-permute-start(f32[960,384]{1,0:T(8,128)} %get-tuple-element.130), channel_id=1, source_target_pairs={{0,1},{1,0},{2,3},{3,2},{4,5},{5,4},{6,7},{7,6},{8,9},{9,8},{10,11... | collective-permute-start | bytes 4423688 | tf_op jit(solution)/shard_map/ppermute | solution.py:975
  266.1 15.5 %collective-permute-start.6 = (f32[64,384]{1,0:T(8,128)}, f32[64,384]{1,0:T(8,128)S(1)}, u32[]{:S(2)}, u32[]{:S(2)}) collective-permute-start(f32[64,384]{1,0:T(8,128)} %get-tuple-element.142), channel_id=1, source_target_pairs={{0,1},{1,0},{2,3},{3,2},{4,5},{5,4},{6,7},{7,6},{8,9},{9,8},{10,11... | collective-permute-start | bytes 294920 | tf_op jit(solution)/shard_map/ppermute | solution.py:975
  281.6 0.6 copy-start.12
  281.6 1.1 copy-start.5
  282.7 10.6 %copy-start.19 = (s32[256]{0:T(256)S(1)}, s32[256]{0:T(256)}, u32[]{:S(2)}) copy-start(s32[256]{0:T(256)} %param.31) | copy-start | bytes 3076
  289.4 17.7 %all-to-all-start.2 = ((f32[16,24,384]{2,1,0:T(8,128)}), f32[16,24,384]{2,1,0:T(8,128)S(1)}, u32[]{:S(2)}, u32[]{:S(2)}) async-start(f32[16,24,384]{2,1,0:T(8,128)} %get-tuple-element.143), calls=%async_computation.2 | async-start | bytes 1179648 | tf_op jit(solution)/shard_map/all_to_all | solution.py:979
  307.1 7.2 %copy-start.2 = (f32[16,24,384]{2,1,0:T(8,128)}, f32[16,24,384]{2,1,0:T(8,128)S(1)}, u32[]{:S(2)}) copy-start(f32[16,24,384]{2,1,0:T(8,128)S(1)} %all-to-all-done.2.refs_1_) | copy-start | bytes 1769476
  307.9 14.3 %all-to-all-start.3 = ((f32[16,8,384]{2,1,0:T(8,128)}), f32[16,8,384]{2,1,0:T(8,128)S(1)}, u32[]{:S(2)}, u32[]{:S(2)}) async-start(f32[16,8,384]{2,1,0:T(8,128)} %broadcast_in_dim.15), calls=%async_computation.3 | async-start | bytes 393216 | tf_op jit(solution)/shard_map/all_to_all | solution.py:979
  318.2 4.1 %collective-permute-start.7 = (f32[384,168]{1,0:T(8,128)}, f32[384,168]{1,0:T(8,128)S(1)}, u32[]{:S(2)}, u32[]{:S(2)}) collective-permute-start(f32[384,168]{1,0:T(8,128)} %get-tuple-element.150), channel_id=1, source_target_pairs={{0,1},{1,0},{2,3},{3,2},{4,5},{5,4},{6,7},{7,6},{8,9},{9,8},{10,11... | collective-permute-start | bytes 774152 | tf_op jit(solution)/shard_map/ppermute | solution.py:975
  320.9 1.4 copy-start.9
  320.9 1.4 collective-permute-start.8
  322.2 0.6 copy-start.13
  322.2 0.8 copy-start.10
  322.2 0.8 copy-start.4
  323.1 15.0 %copy-start.6 = (f32[648,384]{1,0:T(8,128)S(1)}, f32[648,384]{1,0:T(8,128)}, u32[]{:S(2)}) copy-start(f32[648,384]{1,0:T(8,128)} %get-tuple-element.156.time_own) | copy-start | bytes 2985988
  331.4 20.5 %all-to-all-start.4 = ((f32[16,24,384]{2,1,0:T(8,128)}), f32[16,24,384]{2,1,0:T(8,128)S(1)}, u32[]{:S(2)}, u32[]{:S(2)}) async-start(f32[16,24,384]{2,1,0:T(8,128)} %get-tuple-element.152), calls=%async_computation.4 | async-start | bytes 1179648 | tf_op jit(solution)/shard_map/all_to_all | solution.py:979
  338.1 25.7 %collective-permute-start.9 = (f32[648,384]{1,0:T(8,128)S(1)}, f32[648,384]{1,0:T(8,128)S(1)}, u32[]{:S(2)}, u32[]{:S(2)}) collective-permute-start(f32[648,384]{1,0:T(8,128)S(1)} %copy-done.6), channel_id=1, source_target_pairs={{0,1},{1,0},{2,3},{3,2},{4,5},{5,4},{6,7},{7,6},{8,9},{9,8},{10,11... | collective-permute-start | bytes 2985992 | tf_op jit(solution)/shard_map/ppermute | solution.py:975
  351.9 17.5 %copy-start = (f32[16,24,384]{2,1,0:T(8,128)}, f32[16,24,384]{2,1,0:T(8,128)S(1)}, u32[]{:S(2)}) copy-start(f32[16,24,384]{2,1,0:T(8,128)S(1)} %all-to-all-done.4.cond_own) | copy-start | bytes 1769476
  352.7 12.8 %all-to-all-start.5 = ((f32[16,8,384]{2,1,0:T(8,128)}), f32[16,8,384]{2,1,0:T(8,128)S(1)}, u32[]{:S(2)}, u32[]{:S(2)}) async-start(f32[16,8,384]{2,1,0:T(8,128)} %broadcast_in_dim.16), calls=%async_computation.5 | async-start | bytes 393216 | tf_op jit(solution)/shard_map/all_to_all | solution.py:979
  359.2 21.2 %collective-permute-start.11 = (f32[16,16,384]{2,1,0:T(8,128)}, f32[16,16,384]{2,1,0:T(8,128)}, u32[]{:S(2)}, u32[]{:S(2)}) collective-permute-start(f32[16,16,384]{2,1,0:T(8,128)} %slice.148), channel_id=1, source_target_pairs={{0,1},{1,0},{2,3},{3,2},{4,5},{5,4},{6,7},{7,6},{8,9},{9,8},{10,11... | collective-permute-start | bytes 1179656 | tf_op jit(solution)/shard_map/ppermute | solution.py:975
  363.8 1.0 copy-start.7
  365.5 0.7 copy-start.8
  369.4 11.0 %collective-permute-start.10 = (f32[1,128]{1,0:T(1,128)}, f32[1,128]{1,0:T(1,128)S(1)}, u32[]{:S(2)}, u32[]{:S(2)}) collective-permute-start(f32[1,128]{1,0:T(1,128)} %get-tuple-element.157.parts), channel_id=1, source_target_pairs={{0,1},{1,0},{2,3},{3,2},{4,5},{5,4},{6,7},{7,6},{8,9},{9,8},{10,11... | collective-permute-start | bytes 1544 | tf_op jit(solution)/shard_map/ppermute | solution.py:975
  380.4 0.5 copy-start.20
Sparse Core Ops, SparseCore 0:
  11.5 80.2 all-gather.2
  138.0 72.2 all-gather.4

commit v3 on v2

--- a/solution.py
+++ b/solution.py
@@ -18,6 +18,9 @@
 L = 2
 TOK = 256
 RANK = 8
+GROUP = 2
+AHEAD, MLP_AHEAD, BACK_AHEAD = 2, 2, 3
+LAG = 1
 
 norm_eps = 1e-06
 ortho_eps = 1e-06
@@ -117,115 +120,173 @@
     return jnp.where(mask, values, jnp.zeros_like(values))
 
 
-def layer_forward(x, mod, own, other, wqkv, wo, bqkv, bfc1, bproj, bfc2, put):
-    normed, inv_a = normalize(x)
+def gelu_parts(pre):
+    squared = pre * pre
+    coef = np.float32(np.sqrt(2.0 / np.pi))
+    tanh = jnp.tanh(pre * (coef + np.float32(coef * 0.044715) * squared))
+    half = 0.5 * (1.0 + tanh)
+    slope = half + (0.5 * pre) * (1.0 - tanh * tanh) * (
+        coef + np.float32(3.0 * 0.044715 * coef) * squared
+    )
+    return (pre * half).astype(bf16), slope
+
+
+def ahead_of(products, depth):
+    waiting = [next(products) for _ in range(depth)]
+    while waiting:
+        ready = waiting.pop(0)
+        following = next(products, None)
+        if following is not None:
+            waiting.append(following)
+        yield ready
+
+
+def run_steps(chains, lag):
+    waits = [lag * i for i in range(len(chains))]
+    live = dict(enumerate(chains))
+    while live:
+        for i in list(live):
+            if waits[i] > 0:
+                waits[i] -= 1
+            elif next(live[i], 1) is not None:
+                del live[i]
+
+
+def pair_span(pair):
+    return slice(pair * 2 * HD, (pair + 1) * 2 * HD)
+
+
+def layer_forward(x, mod, own, other, wqkv, wo, bqkv, bfc1, bproj, bfc2, put, result):
+    normed, _ = normalize(x)
     input_a = (normed * (1.0 + mod(1)) + mod(0)).astype(bf16)
-    qkv = (dot(input_a, wqkv[...]) + bqkv).astype(bf16)
-    query = qkv[:, :D] * jnp.asarray(HD**-0.5, bf16)
-    keyed = qkv[:, D : 2 * D]
-    valued = qkv[:, 2 * D :]
     put("input_a", input_a)
-    put("query", query)
-    put("keyed", keyed)
-    put("valued", valued)
+    yield
+    thirds = []
+    for part in range(3):
+        span = slice(part * D, (part + 1) * D)
+        value = (dot(input_a, wqkv[:, span]) + bqkv[:, span]).astype(bf16)
+        if part == 0:
+            value = value * jnp.asarray(HD**-0.5, bf16)
+        put(("query", "keyed", "valued")[part], value)
+        thirds.append(value)
+        yield
+    query, keyed, valued = thirds
+    scored = ahead_of(
+        (dot(keep(query[:, pair_span(pair)], head_mask(which)), keyed[:, pair_span(pair)], NT)
+         for pair in range(HEADS // 2) for which in range(2)), AHEAD
+    )
     pieces = []
     for pair in range(HEADS // 2):
-        span = slice(pair * 2 * HD, (pair + 1) * 2 * HD)
-        q_pair, k_pair, v_pair = query[:, span], keyed[:, span], valued[:, span]
         total = None
         for which in range(2):
-            mask = head_mask(which)
-            scores = dot(keep(q_pair, mask), k_pair, NT)
+            scores = next(scored)
+            yield
             expo = jnp.exp(scores - jnp.max(scores, -1, keepdims=True))
             probs = expo * (1.0 / jnp.sum(expo, -1, keepdims=True))
             put("probs", probs, 2 * pair + which)
-            mixed = dot(probs.astype(bf16), keep(v_pair, mask))
+            yield
+            mixed = dot(probs.astype(bf16), keep(valued[:, pair_span(pair)], head_mask(which)))
             total = mixed if total is None else total + mixed
         pieces.append(total.astype(bf16))
     mixed = jnp.concatenate(pieces, 1)
     put("mixed", mixed)
+    yield
     branch_a = dot(mixed, wo[...], NT) + bproj
     put("branch_a", branch_a)
     middle = x + mod(2) * branch_a
     put("middle", middle)
-    normed_m, inv_m = normalize(middle)
+    yield
+    normed_m, _ = normalize(middle)
     input_m = (normed_m * (1.0 + mod(4)) + mod(3)).astype(bf16)
     put("input_m", input_m)
+    yield
     branch_m = bfc2
     for side, weights in enumerate((own, other)):
         pre = dot(input_m, weights[:, :HMLP]) + bfc1[:, side * HMLP : (side + 1) * HMLP]
-        squared = pre * pre
-        coef = np.float32(np.sqrt(2.0 / np.pi))
-        tanh = jnp.tanh(pre * (coef + np.float32(coef * 0.044715) * squared))
-        half = 0.5 * (1.0 + tanh)
-        acted = (pre * half).astype(bf16)
-        slope = half + (0.5 * pre) * (1.0 - tanh * tanh) * (
-            coef + np.float32(3.0 * 0.044715 * coef) * squared
-        )
+        yield
+        acted, slope = gelu_parts(pre)
         put("acted", acted, side)
         put("slope", slope, side)
+        yield
         branch_m = branch_m + dot(acted, weights[:, OFF_W2 : OFF_W2 + HMLP], NT)
+        yield
     put("branch_m", branch_m)
-    return middle + mod(5) * branch_m
-
-
-def layer_backward(grad, x, mod, own, other, wqkv, wo, take, rows, stash, mods_out, bias):
+    result.append(middle + mod(5) * branch_m)
+
+
+def layer_backward(grad, x, mod, own, other, wqkv, wo, take, rows, stash, mods_out, bias, result):
     branch_m = take("branch_m")
     mods_out(5, token_sum(grad * branch_m))
     grad_branch_m = (grad * mod(5)).astype(bf16)
     bias("fc2", 0, grad_branch_m)
     stash["dym"][rows, :] = grad_branch_m
-    middle = take("middle")
-    normed_m, inv_m = normalize(middle)
+    yield
     grad_input = None
+    acting = ahead_of(
+        (dot(grad_branch_m, weights[:, OFF_W2 : OFF_W2 + HMLP]) for weights in (own, other)), MLP_AHEAD
+    )
     for side, weights in enumerate((own, other)):
         span = slice(side * HMLP, (side + 1) * HMLP)
-        grad_acted = dot(grad_branch_m, weights[:, OFF_W2 : OFF_W2 + HMLP])
+        grad_acted = next(acting)
+        yield
         grad_pre = (grad_acted * take("slope", side)).astype(bf16)
         stash["dg"][rows, span] = grad_pre
         bias("fc1", side * HMLP, grad_pre)
+        yield
         part = dot(grad_pre, weights[:, :HMLP], NT)
         grad_input = part if grad_input is None else grad_input + part
+        yield
+    middle = take("middle")
+    normed_m, inv_m = normalize(middle)
     mods_out(3, token_sum(grad_input))
     mods_out(4, token_sum(grad_input * normed_m))
     grad_middle = grad + norm_back(grad_input * (1.0 + mod(4)), normed_m, inv_m)
+    yield
     branch_a = take("branch_a")
     mods_out(2, token_sum(grad_middle * branch_a))
     grad_branch_a = (grad_middle * mod(2)).astype(bf16)
     bias("proj", 0, grad_branch_a)
     stash["dya"][rows, :] = grad_branch_a
+    yield
     grad_mixed = dot(grad_branch_a, wo[...]).astype(bf16)
+    yield
     query, keyed, valued = take("query"), take("keyed"), take("valued")
+    scored = ahead_of(
+        (dot(keep(grad_mixed[:, pair_span(pair)], head_mask(which)), valued[:, pair_span(pair)], NT)
+         for pair in range(HEADS // 2) for which in range(2)), BACK_AHEAD
+    )
     grads_q, grads_k, grads_v = [], [], []
     for pair in range(HEADS // 2):
-        span = slice(pair * 2 * HD, (pair + 1) * 2 * HD)
-        q_pair, k_pair, v_pair = query[:, span], keyed[:, span], valued[:, span]
-        g_pair = grad_mixed[:, span]
+        q_pair, k_pair = query[:, pair_span(pair)], keyed[:, pair_span(pair)]
         grad_q = grad_k = grad_v = None
         for which in range(2):
             mask = head_mask(which)
+            grad_probs = next(scored)
+            yield
             probs = take("probs", 2 * pair + which)
-            g_head = keep(g_pair, mask)
-            grad_probs = dot(g_head, v_pair, NT)
             row_dot = jnp.sum(grad_probs * probs, -1, keepdims=True)
             grad_scores = (probs * (grad_probs - row_dot)).astype(bf16)
+            yield
             part_q = dot(grad_scores, keep(k_pair, mask))
             part_k = dot(grad_scores, keep(q_pair, mask), TN)
-            part_v = dot(probs.astype(bf16), g_head, TN)
+            part_v = dot(probs.astype(bf16), keep(grad_mixed[:, pair_span(pair)], mask), TN)
             grad_q = part_q if grad_q is None else grad_q + part_q
             grad_k = part_k if grad_k is None else grad_k + part_k
             grad_v = part_v if grad_v is None else grad_v + part_v
         grads_q.append((grad_q * HD**-0.5).astype(bf16))
         grads_k.append(grad_k.astype(bf16))
         grads_v.append(grad_v.astype(bf16))
+    yield
     grad_qkv = jnp.concatenate(grads_q + grads_k + grads_v, 1)
     stash["dqkv"][rows, :] = grad_qkv
     bias("qkv", 0, grad_qkv)
+    yield
     grad_input_a = dot(grad_qkv, wqkv[...], NT)
+    yield
     normed, inv_a = normalize(x)
     mods_out(0, token_sum(grad_input_a))
     mods_out(1, token_sum(grad_input_a * normed))
-    return grad_middle + norm_back(grad_input_a * (1.0 + mod(1)), normed, inv_a)
+    result.append(grad_middle + norm_back(grad_input_a * (1.0 + mod(1)), normed, inv_a))
 
 
 def weight_grads(input_a, input_m, mixed, acted, stash, cols, rows_out):
@@ -262,20 +323,25 @@
     named = dict(query=query, keyed=keyed, valued=valued, mixed=mixed, branch_a=branch_a,
                  middle=middle, branch_m=branch_m, input_a=input_a, input_m=input_m)
 
-    def put(name, value, index=None):
-        if name == "probs":
-            probs[0, index] = value
-        elif name == "acted":
-            acted[0, :, index * HMLP : (index + 1) * HMLP] = value
-        elif name == "slope":
-            slope[0, :, index * HMLP : (index + 1) * HMLP] = value
-        else:
-            named[name][0] = value
-
-    x = dot(xt[0], wpatch[0], TN) + vector(b_rep, START_PATCH) + pos[...]
-    x0[0] = x
-    x2[0] = layer_forward(x, lambda j: mods[0, j : j + 1, :], own, other, wqkv, wo, bqkv[...],
-                          bfc1[...], vector(b_rep, 0), vector(b_rep, START_FC2), put)
+    def chain(i):
+        def put(name, value, index=None):
+            if name == "probs":
+                probs[i, index] = value
+            elif name == "acted":
+                acted[i, :, index * HMLP : (index + 1) * HMLP] = value
+            elif name == "slope":
+                slope[i, :, index * HMLP : (index + 1) * HMLP] = value
+            else:
+                named[name][i] = value
+
+        x = dot(xt[i], wpatch[0], TN) + vector(b_rep, START_PATCH) + pos[...]
+        x0[i] = x
+        result = []
+        yield from layer_forward(x, lambda j: mods[i, j : j + 1, :], own, other, wqkv, wo, bqkv[...],
+                                 bfc1[...], vector(b_rep, 0), vector(b_rep, START_FC2), put, result)
+        x2[i] = result[0]
+
+    run_steps([chain(i) for i in range(xt.shape[0])], LAG)
 
 
 def diagonal(count):
@@ -313,59 +379,71 @@
         dbhead[...] = jnp.zeros_like(dbhead)
         loss[...] = jnp.zeros_like(loss)
 
-    rows = pl.ds(pl.multiple_of(step * TOK, TOK), TOK)
     stacked = dict(mixed=mixed, input_a=input_a, input_m=input_m)
     single = dict(query=query, keyed=keyed, valued=valued, branch_a=branch_a, middle=middle,
                   branch_m=branch_m)
-
-    def put(name, value, index=None):
-        if name == "probs":
-            probs[index] = value
-        elif name == "acted":
-            acted[rows, index * HMLP : (index + 1) * HMLP] = value
-        elif name == "slope":
-            slope[:, index * HMLP : (index + 1) * HMLP] = value
-        elif name in stacked:
-            stacked[name][rows, :] = value
-        else:
-            single[name][...] = value
-
-    def take(name, index=None):
-        if name == "probs":
-            return probs[index]
-        if name == "slope":
-            return slope[:, index * HMLP : (index + 1) * HMLP]
-        return single[name][...]
-
-    def mod(j):
-        return mods[0, 6 + j : 7 + j, :]
-
-    x = layer_forward(x2[0], mod, own, other, wqkv, wo, bqkv[...], bfc1[...], vector(b_rep, D),
-                      vector(b_rep, START_FC2 + D), put)
-    normed, inv_std = normalize(x)
-    input_f = (normed * (1.0 + mod(7)) + mod(6)).astype(bf16)
-    bhead = jnp.sum(
-        jnp.where(diagonal(PV), b_rep[:, START_HEAD : START_HEAD + PV], 0.0), 1, keepdims=True
-    )
-    miss = dot(whead[0], input_f, NT) + bhead - targets[0]
-    loss[...] += jnp.sum(miss * miss, 0, keepdims=True)
-    grad_pred = (2.0 * miss).astype(bf16)
-    dhead[...] += dot(grad_pred, input_f)
-    dbhead[...] += jnp.sum(grad_pred.astype(f32), 1, keepdims=True)
-    grad_input = dot(grad_pred, whead[0], TN)
-    dmods[0, 6:7, :] = token_sum(grad_input)
-    dmods[0, 7:8, :] = token_sum(grad_input * normed)
-    grad = norm_back(grad_input * (1.0 + mod(7)), normed, inv_std)
-
-    def mods_out(j, value):
-        dmods[0, j : j + 1, :] = value
-
-    def bias(name, start, value):
-        at = BIAS[name] + start
-        dbias[:, at : at + value.shape[1]] += token_sum(value.astype(f32))
-
     stash = dict(dqkv=s_dqkv, dg=s_dg, dya=s_dya, dym=s_dym)
-    dx[0] = layer_backward(grad, x2[0], mod, own, other, wqkv, wo, take, rows, stash, mods_out, bias)
+    group = x2.shape[0]
+
+    def chain(i):
+        rows = pl.ds(pl.multiple_of((step * group + i) * TOK, TOK), TOK)
+
+        def put(name, value, index=None):
+            if name == "probs":
+                probs[i, index] = value
+            elif name == "acted":
+                acted[rows, index * HMLP : (index + 1) * HMLP] = value
+            elif name == "slope":
+                slope[i, :, index * HMLP : (index + 1) * HMLP] = value
+            elif name in stacked:
+                stacked[name][rows, :] = value
+            else:
+                single[name][i] = value
+
+        def take(name, index=None):
+            if name == "probs":
+                return probs[i, index]
+            if name == "slope":
+                return slope[i, :, index * HMLP : (index + 1) * HMLP]
+            return single[name][i]
+
+        def mod(j):
+            return mods[i, 6 + j : 7 + j, :]
+
+        def mods_out(j, value):
+            dmods[i, j : j + 1, :] = value
+
+        def bias(name, start, value):
+            at = BIAS[name] + start
+            dbias[:, at : at + value.shape[1]] += token_sum(value.astype(f32))
+
+        result = []
+        yield from layer_forward(x2[i], mod, own, other, wqkv, wo, bqkv[...], bfc1[...], vector(b_rep, D),
+                                 vector(b_rep, START_FC2 + D), put, result)
+        yield
+        normed, inv_std = normalize(result[0])
+        input_f = (normed * (1.0 + mod(7)) + mod(6)).astype(bf16)
+        bhead = jnp.sum(
+            jnp.where(diagonal(PV), b_rep[:, START_HEAD : START_HEAD + PV], 0.0), 1, keepdims=True
+        )
+        yield
+        miss = dot(whead[0], input_f, NT) + bhead - targets[i]
+        loss[...] += jnp.sum(miss * miss, 0, keepdims=True)
+        grad_pred = (2.0 * miss).astype(bf16)
+        yield
+        dhead[...] += dot(grad_pred, input_f)
+        dbhead[...] += jnp.sum(grad_pred.astype(f32), 1, keepdims=True)
+        grad_input = dot(grad_pred, whead[0], TN)
+        yield
+        mods_out(6, token_sum(grad_input))
+        mods_out(7, token_sum(grad_input * normed))
+        grad = norm_back(grad_input * (1.0 + mod(7)), normed, inv_std)
+        result = []
+        yield from layer_backward(grad, x2[i], mod, own, other, wqkv, wo, take, rows, stash, mods_out, bias,
+                                  result)
+        dx[i] = result[0]
+
+    run_steps([chain(i) for i in range(group)], LAG)
 
     @pl.when(step == pl.num_programs(0) - 1)
     def _():
@@ -409,8 +487,10 @@
         dbias[:, at : at + value.shape[1]] += token_sum(value.astype(f32))
 
     stash = dict(dqkv=s_dqkv, dg=s_dg, dya=s_dya, dym=s_dym)
-    grad = layer_backward(dx[0], x0[0], lambda j: mods[0, j : j + 1, :], own, other, wqkv, wo,
-                          take, rows, stash, mods_out, bias)
+    result = []
+    run_steps([layer_backward(dx[0], x0[0], lambda j: mods[0, j : j + 1, :], own, other, wqkv, wo,
+                              take, rows, stash, mods_out, bias, result)], 0)
+    (grad,) = result
     grad = grad.astype(bf16)
     pay_own[PAY_PATCH : PAY_PATCH + PV, :] += dot(xt[0], grad)
     pay_own[PAY_BPATCH : PAY_BPATCH + 1, :] += token_sum(grad.astype(f32))
@@ -441,9 +521,9 @@
             out[PAY_BCOL + 8 :, :] = jnp.zeros((PAY_ROWS - PAY_BCOL - 8, D), f32)
 
 
-def per_latent(*shape):
+def per_latent(*shape, group=1):
     zeros = (0,) * len(shape)
-    return pl.BlockSpec((1,) + shape, lambda n: (n,) + zeros)
+    return pl.BlockSpec((group,) + shape, lambda n: (n,) + zeros)
 
 
 def fixed(*shape):
@@ -487,10 +567,10 @@
     outs = [("x0", (TOK, D), f32)] + SAVED + [("x2", (TOK, D), f32)]
     return pl.pallas_call(
         forward_kernel,
-        grid=(count,),
-        in_specs=[per_latent(PV, TOK), per_latent(14, D),
+        grid=(count // GROUP,),
+        in_specs=[per_latent(PV, TOK, group=GROUP), per_latent(14, D, group=GROUP),
                   pl.BlockSpec((1, PV, D), lambda n: (0, 0, 0)), fixed(TOK, D)] + weight_specs(0),
-        out_specs=[per_latent(*shape) for _, shape, _ in outs],
+        out_specs=[per_latent(*shape, group=GROUP) for _, shape, _ in outs],
         out_shape=[jax.ShapeDtypeStruct((count,) + shape, kind) for _, shape, kind in outs],
         scratch_shapes=WEIGHT_SCRATCH,
         compiler_params=params(),
@@ -502,21 +582,21 @@
 def run_middle(x2, mods, weights, full_io, targets):
     count = x2.shape[0]
     rows = count * TOK
-    outs = [((count, TOK, D), per_latent(TOK, D)), ((count, 8, D), per_latent(8, D))]
+    outs = [((count, TOK, D), per_latent(TOK, D, group=GROUP)), ((count, 8, D), per_latent(8, D, group=GROUP))]
     outs += [(shape, fixed(*shape)) for shape in GRAD_SHAPES]
     outs += [(shape, fixed(*shape)) for shape in ((1, BIAS_WIDTH), (PV, D), (PV, 1), (1, TOK))]
     return pl.pallas_call(
         middle_kernel,
-        grid=(count,),
-        in_specs=[per_latent(TOK, D), per_latent(14, D)] + weight_specs(1)
-        + [pl.BlockSpec((1, PV, D), lambda n: (1, 0, 0)), per_latent(PV, TOK)],
+        grid=(count // GROUP,),
+        in_specs=[per_latent(TOK, D, group=GROUP), per_latent(14, D, group=GROUP)] + weight_specs(1)
+        + [pl.BlockSpec((1, PV, D), lambda n: (1, 0, 0)), per_latent(PV, TOK, group=GROUP)],
         out_specs=[spec for _, spec in outs],
         out_shape=[jax.ShapeDtypeStruct(shape, f32) for shape, _ in outs],
         scratch_shapes=WEIGHT_SCRATCH
-        + [pltpu.VMEM((TOK, D), bf16)] * 3
-        + [pltpu.VMEM((HEADS, TOK, TOK), f32), pltpu.VMEM((rows, D), bf16),
-           pltpu.VMEM((TOK, D), f32), pltpu.VMEM((TOK, D), f32), pltpu.VMEM((rows, MLP), bf16),
-           pltpu.VMEM((TOK, MLP), f32), pltpu.VMEM((TOK, D), f32),
+        + [pltpu.VMEM((GROUP, TOK, D), bf16)] * 3
+        + [pltpu.VMEM((GROUP, HEADS, TOK, TOK), f32), pltpu.VMEM((rows, D), bf16),
+           pltpu.VMEM((GROUP, TOK, D), f32), pltpu.VMEM((GROUP, TOK, D), f32), pltpu.VMEM((rows, MLP), bf16),
+           pltpu.VMEM((GROUP, TOK, MLP), f32), pltpu.VMEM((GROUP, TOK, D), f32),
            pltpu.VMEM((rows, D), bf16), pltpu.VMEM((rows, D), bf16)]
         + stash_scratch(count),
         compiler_params=params(),

time: 399 us -> 369 us (0.925)
  Pallas kernels: 206 us -> 175 us
    pallas_call x2, Pallas kernels: 117 us -> 90.7 us  [the longest x1 60.9 us: run_middle(): pl.pallas_call(middle_kernel, grid=(count // GROUP,), in_specs=[per_laten...]
    pallas_call x1, Pallas kernels: 47 us -> 42.9 us  [run_last(): pl.pallas_call(last_kernel, grid=(count,), in_specs=[per_latent(TOK, D),...]
  transfers between devices with their start and end apart: 19 -> 19, of which waited for: 8 -> 8; matrix products, arithmetic and copies ran while one was open for 10% -> 10% of each run, Pallas kernels for 38% -> 35%
where the time goes in v3:
time: 369 us; the launch traced here: 363 us
  Pallas kernels  175 us (47%)
  waiting for transfers between devices  65.4 us (18%)
  starting transfers between devices  36.3 us (10%)
  local copies, waits for them, and re-layouts  32.9 us (9%)
  blocking collectives  23.6 us (6%)
  between operations  14.9 us (4%)
  other arithmetic  10.3 us (3%)
  matrix products  4.18 us (1%)
    pallas_call x1, Pallas kernels, run_middle(): pl.pallas_call(middle_kernel, grid=(count // GROUP,), in_specs=[per_laten...  60.9 us
    pallas_call x1, Pallas kernels, run_last(): pl.pallas_call(last_kernel, grid=(count,), in_specs=[per_latent(TOK, D),...  42.9 us
    pallas_call x1, Pallas kernels, run_forward(): pl.pallas_call(forward_kernel, grid=(count // GROUP,), in_specs=[per_late...  29.8 us
    all_gather x1, waiting for transfers between devices, on_device(): full = lax.all_gather(shard, ('dp', 'tensor'))  26.5 us
    all_to_all x4, waiting for transfers between devices, trade(): return lax.all_to_all(chunks, 'dp', 0, 0, tiled=True)  24 us
    all_to_all x1, blocking collectives, trade(): return lax.all_to_all(chunks, 'dp', 0, 0, tiled=True)  23.6 us
    all_to_all x4, starting transfers between devices, trade(): return lax.all_to_all(chunks, 'dp', 0, 0, tiled=True)  22 us
    ppermute x12, starting transfers between devices, swap(): return lax.ppermute(values, 'tensor', [(0, 1), (1, 0)])  10.6 us
  transfers between devices with their start and end apart: 19, of which 8 were waited for; matrix products, arithmetic and copies ran while one was open for 10% of the time, Pallas kernels for 35%

profile of v3, /device:TPU:1, one launch (start us, length us, event | category | flops | bytes accessed | tf_op | source)
XLA Modules:
  0.0 363.0 jit_solution(126150557397902923)
XLA Ops:
  7.3 1.0 convert.35
  8.3 0.9 bitcast_convert_fusion.1
  9.4 0.8 concatenate.25
  10.8 0.8 convert_element_type.74
  11.7 1.2 fusion.1
  13.2 1.1 reshape.287
  16.0 0.9 reduce.6
  17.4 23.6 %all_to_all.37 = bf16[16,2,7648]{2,1,0:T(2,128)(2,1)S(1)} all-to-all(bf16[16,2,7648]{2,1,0:T(2,128)(2,1)S(1)} %reshape.324), channel_id=1, replica_groups=mesh['dp'=16,'tensor'=2] {'dp'}, dimensions={0} | all-to-all | bytes 978944 | tf_op jit(solution)/shard_map/all_to_all | solution.py:1059
  41.9 2.1 collective-permute-start
  44.5 0.8 collective-permute-done
  46.9 1.0 multiply_convert_fusion.1
  47.9 1.1 multiply_convert_fusion
  49.0 0.9 fusion.6
  49.9 3.1 all-to-all-start.1
  53.6 1.7 dynamic-slice_bitcast_fusion.1
  55.6 0.8 reshape.294.wpatch.whead
  56.4 7.9 %all-to-all-done.1 = f32[32,8,168]{2,1,0:T(8,128)S(1)} async-done(((f32[32,8,168]{2,1,0:T(8,128)}), f32[32,8,168]{2,1,0:T(8,128)S(1)}, u32[]{:S(2)}, u32[]{:S(2)}) %all-to-all-start.1) | async-done | bytes 172064 | tf_op jit(solution)/shard_map/all_to_all | solution.py:1138
  65.3 26.5 %all-gather.3.cloned.1.call-done = bf16[32,24,4608]{2,1,0:T(8,128)(2,1)} async-done(((bf16[1,24,4608]{2,1,0:T(8,128)(2,1)}), bf16[32,24,4608]{2,1,0:T(8,128)(2,1)}) %all-gather.3.cloned.1.call-update) | async-done | bytes 7077904 | tf_op jit(solution)/shard_map/all_gather | solution.py:1100
  91.9 6.5 %constant_dynamic-slice_fusion.5 = (bf16[16,1,24,4608]{3,2,1,0:T(8,128)(2,1)}, bf16[16,1,24,4608]{3,2,1,0:T(8,128)(2,1)}) fusion(bf16[16,2,24,4608]{3,2,1,0:T(8,128)(2,1)} %bitcast.106, s32[]{:T(128)S(6)} %select_n.44, s32[]{:T(128)S(6)} %select_n.22), kind=kLoop, calls=%fused_computation.56 | loop fusion | bytes 14155784 | tf_op jit(solution)/shard_map/dynamic_slice | solution.py:1161
  98.9 29.8 %forward_first.1 = (f32[8,256,384]{2,1,0:T(8,128)}, bf16[8,256,384]{2,1,0:T(8,128)(2,1)}, bf16[8,256,384]{2,1,0:T(8,128)(2,1)}, bf16[8,256,384]{2,1,0:T(8,128)(2...) custom-call(bf16[8,16,256]{2,1,0:T(8,128)(2,1)} %get-tuple-element.2, ...), custom_call_target="tpu_custom_call" | custom-call | flops 8000000000 | bytes 48000000 | tf_op jit(solution)/shard_map/forward_first/pallas_call | solution.py:568
  129.5 60.9 %layer_second.1 = (f32[8,256,384]{2,1,0:T(8,128)}, f32[8,8,384]{2,1,0:T(8,128)}, f32[1344,384]{1,0:T(8,128)}, f32[1344,384]{1,0:T(8,128)}, f32[960,384]{1,0:T(8,...) custom-call(f32[8,256,384]{2,1,0:T(8,128)} %get-tuple-element.107.x2, ...), custom_call_target="tpu_custom_call" | custom-call | flops 25600000000 | bytes 24000000 | tf_op jit(solution)/shard_map/layer_second/pallas_call | solution.py:588
  190.7 42.9 %backward_first.1 = (f32[8,14,384]{2,1,0:T(8,128)}, f32[1344,384]{1,0:T(8,128)}, f32[1344,384]{1,0:T(8,128)}, f32[960,384]{1,0:T(8,128)}, f32[960,384]{1,0:T(8,1...) custom-call(f32[8,256,384]{2,1,0:T(8,128)} %get-tuple-element.108.dx, f32[8,256,384]{2,1,0:T(8,128)} %get-tuple-element.109.x0, ...), custom_call_target="tpu_custom_call" | custom-call | flops 17600000000 | bytes 64000000 | tf_op jit(solution)/shard_map/backward_first/pallas_call | solution.py:614
  236.2 1.3 constant_dynamic-slice_fusion.4.refs_10_
  237.5 4.9 %collective-permute-done.5.refs_5_ = f32[960,384]{1,0:T(8,128)} collective-permute-done((f32[960,384]{1,0:T(8,128)}, f32[960,384]{1,0:T(8,128)}, u32[]{:S(2)}, u32[]{:S(2)}) %collective-permute-start.5) | collective-permute-done | bytes 1474592 | tf_op jit(solution)/shard_map/ppermute | solution.py:1055
  242.4 9.0 %left_second.1 = (f32[1344,384]{1,0:T(8,128)}, f32[960,384]{1,0:T(8,128)}, f32[8,384]{1,0:T(8,128)}, f32[8,1152]{1,0:T(8,128)}, f32[8,384]{1,0:T(8,128)}, /*index=5*/f32[16,8,384]{2,1,0:T(8,128)}) custom-call(f32[2,1344,384]{2,1,0:T(8,128)} %bitcast.104, f32[1344,384]{1,0:T(8,128)} %get-tuple-element.131.refs_1_, ...), custom_call_target="tpu_custom_call" | custom-call | tf_op jit(solution)/shard_map/left_second/pallas_call | solution.py:767
  252.6 6.7 %left_first.1 = (f32[1344,384]{1,0:T(8,128)}, f32[960,384]{1,0:T(8,128)}, f32[2,16,384]{2,1,0:T(8,128)}, f32[16,24,384]{2,1,0:T(8,128)}) custom-call(f32[2,1344,384]{2,1,0:T(8,128)} %bitcast.105, f32[1344,384]{1,0:T(8,128)} %get-tuple-element.127.own_col, f32[1344,384]{1,0:T(8,128)} %collective-permute-done.2.got_col, f32[2,960,384]{2,1,0:T(8,128)} %err_row.1, ...), custom_call_target="tpu_custom_call" | custom-call | tf_op jit(solution)/shard_map/left_first/pallas_call | solution.py:785
  259.3 3.8 %all-to-all-start.2 = ((f32[16,24,384]{2,1,0:T(8,128)}), f32[16,24,384]{2,1,0:T(8,128)S(1)}, u32[]{:S(2)}, u32[]{:S(2)}) async-start(f32[16,24,384]{2,1,0:T(8,128)} %get-tuple-element.143), calls=%async_computation.2 | async-start | bytes 1179648 | tf_op jit(solution)/shard_map/all_to_all | solution.py:1059
  264.1 1.6 dynamic-slice_bitcast_fusion.refs_4_
  267.0 9.9 %all-to-all-done.2.refs_1_ = f32[16,24,384]{2,1,0:T(8,128)S(1)} async-done(((f32[16,24,384]{2,1,0:T(8,128)}), f32[16,24,384]{2,1,0:T(8,128)S(1)}, u32[]{:S(2)}, u32[]{:S(2)}) %all-to-all-start.2) | async-done | bytes 589856 | tf_op jit(solution)/shard_map/all_to_all | solution.py:1059
  277.7 5.8 %all-to-all-start.3 = ((f32[16,8,384]{2,1,0:T(8,128)}), f32[16,8,384]{2,1,0:T(8,128)S(1)}, u32[]{:S(2)}, u32[]{:S(2)}) async-start(f32[16,8,384]{2,1,0:T(8,128)} %broadcast_in_dim.15), calls=%async_computation.3 | async-start | bytes 393216 | tf_op jit(solution)/shard_map/all_to_all | solution.py:1059
  284.2 3.8 %modulation_gradients.1 = (f32[384,168]{1,0:T(8,128)}, f32[384,168]{1,0:T(8,128)}, f32[648,384]{1,0:T(8,128)}, f32[384,1000]{1,0:T(8,128)}) custom-call(s32[1]{0:T(128)} %bitcast.refs_0_.core, f32[16,24,384]{2,1,0:T(8,128)} %copy-done.2, bf16[128,384]{1,0:T(8,128)(2,1)} %get-tuple-element.220.refs_2_, bf16[128,256]{1,0:T(8,128)(2,1)} %fusion.18.refs_3_, ...), custom_call_target="tpu_custom_call" | custom-call | tf_op jit(solution)/shard_map/modulation_gradients/pallas_call | solution.py:833
  288.0 1.8 collective-permute-start.7
  289.7 0.9 constant_dynamic-slice_fusion.3.table_own
  290.7 1.3 collective-permute-done.8.table_got
  292.9 8.4 %right_factors.1 = (f32[16,24,384]{2,1,0:T(8,128)}, f32[2,8,384]{2,1,0:T(8,128)}, f32[2,8,1152]{2,1,0:T(8,128)}, f32[2,8,384]{2,1,0:T(8,128)}, f32[24,1000]{1,0:T(8,128)}) custom-call(f32[8,16,384]{2,1,0:T(8,128)} %bitcast.119, f32[1344,384]{1,0:T(8,128)} %get-tuple-element.144.mat_col0, f32[960,384]{1,0:T(8,128)} %get-tuple-element.145.mat_row0, ...), custom_call_target="tpu_custom_call" | custom-call | tf_op jit(solution)/shard_map/right_factors/pallas_call | solution.py:912
  301.2 6.6 %all-to-all-start.4 = ((f32[16,24,384]{2,1,0:T(8,128)}), f32[16,24,384]{2,1,0:T(8,128)S(1)}, u32[]{:S(2)}, u32[]{:S(2)}) async-start(f32[16,24,384]{2,1,0:T(8,128)} %get-tuple-element.152), calls=%async_computation.4 | async-start | bytes 1179648 | tf_op jit(solution)/shard_map/all_to_all | solution.py:1059
  308.4 13.3 %all-to-all-done.4.cond_own = f32[16,24,384]{2,1,0:T(8,128)S(1)} async-done(((f32[16,24,384]{2,1,0:T(8,128)}), f32[16,24,384]{2,1,0:T(8,128)S(1)}, u32[]{:S(2)}, u32[]{:S(2)}) %all-to-all-start.4) | async-done | bytes 589856 | tf_op jit(solution)/shard_map/all_to_all | solution.py:1059
  322.5 5.8 %all-to-all-start.5 = ((f32[16,8,384]{2,1,0:T(8,128)}), f32[16,8,384]{2,1,0:T(8,128)S(1)}, u32[]{:S(2)}, u32[]{:S(2)}) async-start(f32[16,8,384]{2,1,0:T(8,128)} %broadcast_in_dim.16), calls=%async_computation.5 | async-start | bytes 393216 | tf_op jit(solution)/shard_map/all_to_all | solution.py:1059
  328.2 0.8 slice.148
  329.0 1.8 collective-permute-start.11
  330.8 1.4 constant_dynamic-slice_fusion.left_io
  332.2 1.4 constant_dynamic-slice_fusion.2.left_col
  335.9 3.2 gradient_norm.1
  339.2 2.8 collective-permute-start.10
  342.0 1.4 constant_dynamic-slice_fusion.1.right_row
  343.4 6.8 %next_errors.1 = (f32[2,1344,384]{2,1,0:T(8,128)}, f32[2,960,384]{2,1,0:T(8,128)}, f32[2,16,384]{2,1,0:T(8,128)}) custom-call(f32[1344,384]{1,0:T(8,128)} %get-tuple-element.144.mat_col0, f32[960,384]{1,0:T(8,128)} %get-tuple-element.145.mat_row0, f32[1344,384]{1,0:T(8,128)} %get-tuple-element.146.mat_col1, f32[960,384]{1,0:T(8,128)} %get-tuple-element.147.mat_row1, ...), custom_call_target="tpu_custom_call" | custom-call | tf_op jit(solution)/shard_map/next_errors/pallas_call | solution.py:985
  350.8 3.9 %weight_update.1 = (f32[1,128]{1,0:T(1,128)}, f32[2,24,1344]{2,1,0:T(8,128)}, f32[2,24,960]{2,1,0:T(8,128)}, f32[24,5376]{1,0:T(8,128)}, f32[40,384]{1,0:T(8,128...) custom-call(s32[1]{0:T(128)} %bitcast.refs_0_.core, ...), custom_call_target="tpu_custom_call" | custom-call | tf_op jit(solution)/shard_map/weight_update/pallas_call | solution.py:1045
  354.7 1.3 fusion.28
  (136 shorter events, 22.0 us)
Async XLA Ops:
  7.2 5.7 %copy-start.15 = (f32[2,24,16]{1,2,0:T(8,128)S(1)}, f32[2,24,16]{1,2,0:T(8,128)}, u32[]{:S(2)}) copy-start(f32[2,24,16]{1,2,0:T(8,128)} %param.37) | copy-start | bytes 9220
  7.2 6.0 %copy-start.1 = (f32[24,5376]{1,0:T(8,128)S(1)}, f32[24,5376]{1,0:T(8,128)}, u32[]{:S(2)}) copy-start(f32[24,5376]{1,0:T(8,128)} %w_cond.1) | copy-start | bytes 1548292
  7.2 84.6 %all-gather.3.cloned.1.call-start = ((), (), s32[]{:S(2)}) async-start(), calls=%async_computation.6 | async-start | bytes 7299072 | tf_op jit(solution)/shard_map/all_gather | solution.py:1100
  40.9 3.1 copy-start.17
  40.9 3.2 copy-start.11
  41.9 3.4 collective-permute-start
  44.0 54.3 %collective-permute-start.1 = (f32[2,1344]{1,0:T(2,128)S(1)}, f32[2,1344]{1,0:T(2,128)S(1)}, u32[]{:S(2)}, u32[]{:S(2)}) collective-permute-start(f32[2,1344]{1,0:T(2,128)S(1)} %copy-done.17), channel_id=1, source_target_pairs={{0,1},{1,0},{2,3},{3,2},{4,5},{5,4},{6,7},{7,6},{8,9},{9,8},{10,11... | collective-permute-start | bytes 32264 | tf_op jit(solution)/shard_map/ppermute | solution.py:1055
  46.1 1.8 copy-start.3
  47.9 5.7 %copy-start.18 = (f32[16]{0:T(128)S(1)}, f32[16]{0:T(128)}, u32[]{:S(2)}) copy-start(f32[16]{0:T(128)} %param.30) | copy-start | bytes 196
  47.9 5.8 %copy-start.16 = (f32[16,256,16]{1,2,0:T(8,128)S(1)}, f32[16,256,16]{1,2,0:T(8,128)}, u32[]{:S(2)}) copy-start(f32[16,256,16]{1,2,0:T(8,128)} %param.32) | copy-start | bytes 786436
  49.9 14.4 %all-to-all-start.1 = ((f32[32,8,168]{2,1,0:T(8,128)}), f32[32,8,168]{2,1,0:T(8,128)S(1)}, u32[]{:S(2)}, u32[]{:S(2)}) async-start(f32[32,8,168]{2,1,0:T(8,128)} %fusion.6), calls=%async_computation.1 | async-start | bytes 524288 | tf_op jit(solution)/shard_map/all_to_all | solution.py:1138
  53.0 189.3 %all-gather.5.cloned.1.call-start = ((), (), s32[]{:S(2)}) async-start(), calls=%async_computation.7 | async-start | bytes 4386816 | tf_op jit(solution)/shard_map/all_gather | solution.py:1165
  98.3 0.6 copy-start.21
  190.4 52.0 %collective-permute-start.4 = (f32[1344,384]{1,0:T(8,128)}, f32[1344,384]{1,0:T(8,128)}, u32[]{:S(2)}, u32[]{:S(2)}) collective-permute-start(f32[1344,384]{1,0:T(8,128)} %get-tuple-element.132), channel_id=1, source_target_pairs={{0,1},{1,0},{2,3},{3,2},{4,5},{5,4},{6,7},{7,6},{8,9},{9,8},{10,11... | collective-permute-start | bytes 6193160 | tf_op jit(solution)/shard_map/ppermute | solution.py:1055
  190.7 43.8 %copy-start.14 = (f32[2,1344,8]{1,2,0:T(8,128)S(1)}, f32[2,1344,8]{1,2,0:T(8,128)}, u32[]{:S(2)}) copy-start(f32[2,1344,8]{1,2,0:T(8,128)} %param.52) | copy-start | bytes 258052
  233.6 17.8 %collective-permute-start.2 = (f32[1344,384]{1,0:T(8,128)}, f32[1344,384]{1,0:T(8,128)}, u32[]{:S(2)}, u32[]{:S(2)}) collective-permute-start(f32[1344,384]{1,0:T(8,128)} %get-tuple-element.128), channel_id=1, source_target_pairs={{0,1},{1,0},{2,3},{3,2},{4,5},{5,4},{6,7},{7,6},{8,9},{9,8},{10,11... | collective-permute-start | bytes 6193160 | tf_op jit(solution)/shard_map/ppermute | solution.py:1055
  233.9 8.4 %collective-permute-start.5 = (f32[960,384]{1,0:T(8,128)}, f32[960,384]{1,0:T(8,128)}, u32[]{:S(2)}, u32[]{:S(2)}) collective-permute-start(f32[960,384]{1,0:T(8,128)} %get-tuple-element.134), channel_id=1, source_target_pairs={{0,1},{1,0},{2,3},{3,2},{4,5},{5,4},{6,7},{7,6},{8,9},{9,8},{10,11... | collective-permute-start | bytes 4423688 | tf_op jit(solution)/shard_map/ppermute | solution.py:1055
  234.2 17.2 %collective-permute-start.3 = (f32[960,384]{1,0:T(8,128)}, f32[960,384]{1,0:T(8,128)S(1)}, u32[]{:S(2)}, u32[]{:S(2)}) collective-permute-start(f32[960,384]{1,0:T(8,128)} %get-tuple-element.130), channel_id=1, source_target_pairs={{0,1},{1,0},{2,3},{3,2},{4,5},{5,4},{6,7},{7,6},{8,9},{9,8},{10,11... | collective-permute-start | bytes 4423688 | tf_op jit(solution)/shard_map/ppermute | solution.py:1055
  235.9 15.5 %collective-permute-start.6 = (f32[64,384]{1,0:T(8,128)}, f32[64,384]{1,0:T(8,128)S(1)}, u32[]{:S(2)}, u32[]{:S(2)}) collective-permute-start(f32[64,384]{1,0:T(8,128)} %get-tuple-element.142), channel_id=1, source_target_pairs={{0,1},{1,0},{2,3},{3,2},{4,5},{5,4},{6,7},{7,6},{8,9},{9,8},{10,11... | collective-permute-start | bytes 294920 | tf_op jit(solution)/shard_map/ppermute | solution.py:1055
  251.4 0.6 copy-start.12
  251.5 1.1 copy-start.5
  252.6 10.5 %copy-start.19 = (s32[256]{0:T(256)S(1)}, s32[256]{0:T(256)}, u32[]{:S(2)}) copy-start(s32[256]{0:T(256)} %param.31) | copy-start | bytes 3076
  259.3 17.6 %all-to-all-start.2 = ((f32[16,24,384]{2,1,0:T(8,128)}), f32[16,24,384]{2,1,0:T(8,128)S(1)}, u32[]{:S(2)}, u32[]{:S(2)}) async-start(f32[16,24,384]{2,1,0:T(8,128)} %get-tuple-element.143), calls=%async_computation.2 | async-start | bytes 1179648 | tf_op jit(solution)/shard_map/all_to_all | solution.py:1059
  276.9 7.3 %copy-start.2 = (f32[16,24,384]{2,1,0:T(8,128)}, f32[16,24,384]{2,1,0:T(8,128)S(1)}, u32[]{:S(2)}) copy-start(f32[16,24,384]{2,1,0:T(8,128)S(1)} %all-to-all-done.2.refs_1_) | copy-start | bytes 1769476
  277.7 14.3 %all-to-all-start.3 = ((f32[16,8,384]{2,1,0:T(8,128)}), f32[16,8,384]{2,1,0:T(8,128)S(1)}, u32[]{:S(2)}, u32[]{:S(2)}) async-start(f32[16,8,384]{2,1,0:T(8,128)} %broadcast_in_dim.15), calls=%async_computation.3 | async-start | bytes 393216 | tf_op jit(solution)/shard_map/all_to_all | solution.py:1059
  288.0 4.1 %collective-permute-start.7 = (f32[384,168]{1,0:T(8,128)}, f32[384,168]{1,0:T(8,128)S(1)}, u32[]{:S(2)}, u32[]{:S(2)}) collective-permute-start(f32[384,168]{1,0:T(8,128)} %get-tuple-element.150), channel_id=1, source_target_pairs={{0,1},{1,0},{2,3},{3,2},{4,5},{5,4},{6,7},{7,6},{8,9},{9,8},{10,11... | collective-permute-start | bytes 774152 | tf_op jit(solution)/shard_map/ppermute | solution.py:1055
  290.6 1.4 copy-start.9
  290.6 1.4 collective-permute-start.8
  292.0 0.6 copy-start.13
  292.0 0.8 copy-start.10
  292.0 0.8 copy-start.4
  292.9 15.0 %copy-start.6 = (f32[648,384]{1,0:T(8,128)S(1)}, f32[648,384]{1,0:T(8,128)}, u32[]{:S(2)}) copy-start(f32[648,384]{1,0:T(8,128)} %get-tuple-element.156.time_own) | copy-start | bytes 2985988
  301.2 20.5 %all-to-all-start.4 = ((f32[16,24,384]{2,1,0:T(8,128)}), f32[16,24,384]{2,1,0:T(8,128)S(1)}, u32[]{:S(2)}, u32[]{:S(2)}) async-start(f32[16,24,384]{2,1,0:T(8,128)} %get-tuple-element.152), calls=%async_computation.4 | async-start | bytes 1179648 | tf_op jit(solution)/shard_map/all_to_all | solution.py:1059
  307.9 25.7 %collective-permute-start.9 = (f32[648,384]{1,0:T(8,128)S(1)}, f32[648,384]{1,0:T(8,128)S(1)}, u32[]{:S(2)}, u32[]{:S(2)}) collective-permute-start(f32[648,384]{1,0:T(8,128)S(1)} %copy-done.6), channel_id=1, source_target_pairs={{0,1},{1,0},{2,3},{3,2},{4,5},{5,4},{6,7},{7,6},{8,9},{9,8},{10,11... | collective-permute-start | bytes 2985992 | tf_op jit(solution)/shard_map/ppermute | solution.py:1055
  321.7 17.5 %copy-start = (f32[16,24,384]{2,1,0:T(8,128)}, f32[16,24,384]{2,1,0:T(8,128)S(1)}, u32[]{:S(2)}) copy-start(f32[16,24,384]{2,1,0:T(8,128)S(1)} %all-to-all-done.4.cond_own) | copy-start | bytes 1769476
  322.5 12.8 %all-to-all-start.5 = ((f32[16,8,384]{2,1,0:T(8,128)}), f32[16,8,384]{2,1,0:T(8,128)S(1)}, u32[]{:S(2)}, u32[]{:S(2)}) async-start(f32[16,8,384]{2,1,0:T(8,128)} %broadcast_in_dim.16), calls=%async_computation.5 | async-start | bytes 393216 | tf_op jit(solution)/shard_map/all_to_all | solution.py:1059
  329.0 21.2 %collective-permute-start.11 = (f32[16,16,384]{2,1,0:T(8,128)}, f32[16,16,384]{2,1,0:T(8,128)}, u32[]{:S(2)}, u32[]{:S(2)}) collective-permute-start(f32[16,16,384]{2,1,0:T(8,128)} %slice.148), channel_id=1, source_target_pairs={{0,1},{1,0},{2,3},{3,2},{4,5},{5,4},{6,7},{7,6},{8,9},{9,8},{10,11... | collective-permute-start | bytes 1179656 | tf_op jit(solution)/shard_map/ppermute | solution.py:1055
  333.6 1.0 copy-start.7
  335.3 0.7 copy-start.8
  339.2 11.0 %collective-permute-start.10 = (f32[1,128]{1,0:T(1,128)}, f32[1,128]{1,0:T(1,128)S(1)}, u32[]{:S(2)}, u32[]{:S(2)}) collective-permute-start(f32[1,128]{1,0:T(1,128)} %get-tuple-element.157.parts), channel_id=1, source_target_pairs={{0,1},{1,0},{2,3},{3,2},{4,5},{5,4},{6,7},{7,6},{8,9},{9,8},{10,11... | collective-permute-start | bytes 1544 | tf_op jit(solution)/shard_map/ppermute | solution.py:1055
  350.2 0.5 copy-start.20
Sparse Core Ops, SparseCore 0:
  11.5 80.2 all-gather.2
  129.6 72.4 all-gather.4

commit v4 on v3

--- a/solution.py
+++ b/solution.py
@@ -214,7 +214,7 @@
     result.append(middle + mod(5) * branch_m)
 
 
-def layer_backward(grad, x, mod, own, other, wqkv, wo, take, rows, stash, mods_out, bias, result):
+def layer_backward(grad, x, mod, own, other, wqkv, wo, take, rows, stash, mods_out, bias, result, inputs=None):
     branch_m = take("branch_m")
     mods_out(5, token_sum(grad * branch_m))
     grad_branch_m = (grad * mod(5)).astype(bf16)
@@ -238,6 +238,8 @@
         yield
     middle = take("middle")
     normed_m, inv_m = normalize(middle)
+    if inputs is not None:
+        inputs[1][rows, :] = (normed_m * (1.0 + mod(4)) + mod(3)).astype(bf16)
     mods_out(3, token_sum(grad_input))
     mods_out(4, token_sum(grad_input * normed_m))
     grad_middle = grad + norm_back(grad_input * (1.0 + mod(4)), normed_m, inv_m)
@@ -284,25 +286,54 @@
     grad_input_a = dot(grad_qkv, wqkv[...], NT)
     yield
     normed, inv_a = normalize(x)
+    if inputs is not None:
+        inputs[0][rows, :] = (normed * (1.0 + mod(1)) + mod(0)).astype(bf16)
     mods_out(0, token_sum(grad_input_a))
     mods_out(1, token_sum(grad_input_a * normed))
     result.append(grad_middle + norm_back(grad_input_a * (1.0 + mod(1)), normed, inv_a))
 
 
-def weight_grads(input_a, input_m, mixed, acted, stash, cols, rows_out):
+def weight_grads(input_a, input_m, mixed, acted, stash, places, outs, sems, fills):
+    def add(side, start, value):
+        rows = slice(start, start + value.shape[0])
+        places[side][rows, :] = value if side else places[side][rows, :] + value
+
+    for copy in fills:
+        copy.wait()
+    copies = []
+
+    def send(side, start, stop):
+        rows = pl.ds(start, stop - start)
+        copy = pltpu.make_async_copy(places[side].at[rows, :], outs[side].at[rows, :], sems.at[len(copies)])
+        copy.start()
+        copies.append(copy)
+
     for part in range(3):
         piece = dot(stash["dqkv"][:, part * D : (part + 1) * D], input_a[...], TN)
-        for side, out in enumerate(cols):
+        for side in range(2):
             for head in range(HEADS // 2):
                 start = side * HALF + head * HD
                 place = (3 * head + part) * HD
-                out[place : place + HD, :] = piece[start : start + HD, :]
-    for side, out in enumerate(cols):
-        out[QKV_S:, :] = dot(stash["dg"][:, side * HMLP : (side + 1) * HMLP], input_m[...], TN)
+                add(side, place, piece[start : start + HD, :])
+    for side in (1, 0):
+        send(side, 0, QKV_S)
+    for side in (1, 0):
+        add(side, QKV_S, dot(stash["dg"][:, side * HMLP : (side + 1) * HMLP], input_m[...], TN))
+        send(side, QKV_S, COL_S)
+    for side in (1, 0):
+        add(side, COL_S + HALF, dot(acted[:, side * HMLP : (side + 1) * HMLP], stash["dym"][...], TN))
+        send(side, COL_S + HALF, BOTH)
     piece = dot(mixed[...], stash["dya"][...], TN)
-    for side, out in enumerate(rows_out):
-        out[:HALF, :] = piece[side * HALF : (side + 1) * HALF, :]
-        out[HALF:, :] = dot(acted[:, side * HMLP : (side + 1) * HMLP], stash["dym"][...], TN)
+    for side in (1, 0):
+        add(side, COL_S, piece[side * HALF : (side + 1) * HALF, :])
+        send(side, COL_S, COL_S + HALF)
+    for copy in copies:
+        copy.wait()
+
+
+def error_fills(layer, err_col, err_row, place, sems):
+    return [pltpu.make_async_copy(err_col.at[layer], place.at[pl.ds(0, COL_S), :], sems.at[0]),
+            pltpu.make_async_copy(err_row.at[layer], place.at[pl.ds(COL_S, ROW_S), :], sems.at[1])]
 
 
 BIAS = {"qkv": 0, "fc1": 3 * D, "proj": 3 * D + MLP, "fc2": 4 * D + MLP}
@@ -314,17 +345,19 @@
 
 
 def forward_kernel(xt, mods, wpatch, pos, own, other, bcol_own, bcol_other, b_rep,
-                   x0, query, keyed, valued, probs, branch_a, middle, slope, branch_m, mixed, acted,
-                   input_a, input_m, x2, wqkv, wo, bqkv, bfc1):
+                   query, keyed, valued, probs, branch_a, middle, slope, branch_m, mixed, acted,
+                   x2, wqkv, wo, bqkv, bfc1):
     @pl.when(pl.program_id(0) == 0)
     def _():
         assemble(0, own, other, bcol_own, bcol_other, wqkv, wo, bqkv, bfc1)
 
     named = dict(query=query, keyed=keyed, valued=valued, mixed=mixed, branch_a=branch_a,
-                 middle=middle, branch_m=branch_m, input_a=input_a, input_m=input_m)
+                 middle=middle, branch_m=branch_m)
 
     def chain(i):
         def put(name, value, index=None):
+            if name in ("input_a", "input_m"):
+                return
             if name == "probs":
                 probs[i, index] = value
             elif name == "acted":
@@ -335,7 +368,6 @@
                 named[name][i] = value
 
         x = dot(xt[i], wpatch[0], TN) + vector(b_rep, START_PATCH) + pos[...]
-        x0[i] = x
         result = []
         yield from layer_forward(x, lambda j: mods[i, j : j + 1, :], own, other, wqkv, wo, bqkv[...],
                                  bfc1[...], vector(b_rep, 0), vector(b_rep, START_FC2), put, result)
@@ -365,14 +397,18 @@
         out[at : at + 1, :] = line[:, row * D : (row + 1) * D]
 
 
-def middle_kernel(x2, mods, own, other, bcol_own, bcol_other, b_rep, whead, targets,
-                  dx, dmods, col_own, col_other, row_own, row_other, dbias, dhead, dbhead, loss,
+def middle_kernel(x2, mods, own, other, bcol_own, bcol_other, b_rep, whead, targets, err_col, err_row,
+                  dx, dmods, grad_own, grad_other, dbias, dhead, dbhead, loss,
                   wqkv, wo, bqkv, bfc1, query, keyed, valued, probs, mixed, branch_a, middle, acted,
-                  slope, branch_m, input_a, input_m, s_dqkv, s_dg, s_dya, s_dym):
+                  slope, branch_m, input_a, input_m, s_dqkv, s_dg, s_dya, s_dym, place_own, place_other,
+                  out_sems, fill_sems):
     step = pl.program_id(0)
+    fills = error_fills(1, err_col, err_row, place_own, fill_sems)
 
     @pl.when(step == 0)
     def _():
+        for copy in fills:
+            copy.start()
         assemble(1, own, other, bcol_own, bcol_other, wqkv, wo, bqkv, bfc1)
         dbias[...] = jnp.zeros_like(dbias)
         dhead[...] = jnp.zeros_like(dhead)
@@ -447,25 +483,27 @@
 
     @pl.when(step == pl.num_programs(0) - 1)
     def _():
-        weight_grads(input_a, input_m, mixed, acted, stash, (col_own, col_other), (row_own, row_other))
-
-
-def last_kernel(dx, x0, mods, own, other, bcol_own, bcol_other, b_rep, xt,
-                dbias1, dhead, dbhead, loss, dmods1,
-                query, keyed, valued, probs, branch_a, middle, slope, branch_m, mixed, acted, input_a, input_m,
-                dmods, col_own, col_other, row_own, row_other, pay_own, pay_other,
+        weight_grads(input_a, input_m, mixed, acted, stash, (place_own, place_other),
+                     (grad_own, grad_other), out_sems, fills)
+
+
+def last_kernel(dx, mods, own, other, bcol_own, bcol_other, b_rep, xt, wpatch, pos,
+                dbias1, dhead, dbhead, loss, dmods1, err_col, err_row,
+                query, keyed, valued, probs, branch_a, middle, slope, branch_m, mixed, acted,
+                dmods, grad_own, grad_other, pay_own, pay_other,
                 wqkv, wo, bqkv, bfc1, a_input_a, a_input_m, a_mixed, a_acted, s_dqkv, s_dg, s_dya, s_dym,
-                dbias, sems):
+                dbias, sems, place_own, place_other, out_sems, fill_sems):
     step = pl.program_id(0)
-    pairs = ((input_a, a_input_a), (input_m, a_input_m), (mixed, a_mixed), (acted, a_acted))
+    pairs = ((mixed, a_mixed), (acted, a_acted))
     copies = [pltpu.make_async_copy(src, dst, sems.at[i]) for i, (src, dst) in enumerate(pairs)]
+    fills = error_fills(0, err_col, err_row, place_own, fill_sems)
 
     @pl.when(step == 0)
     def _():
         assemble(0, own, other, bcol_own, bcol_other, wqkv, wo, bqkv, bfc1)
         dbias[...] = jnp.zeros_like(dbias)
         pay_own[...] = jnp.zeros_like(pay_own)
-        for copy in copies:
+        for copy in copies + fills:
             copy.start()
 
     rows = pl.ds(pl.multiple_of(step * TOK, TOK), TOK)
@@ -488,8 +526,9 @@
 
     stash = dict(dqkv=s_dqkv, dg=s_dg, dya=s_dya, dym=s_dym)
     result = []
-    run_steps([layer_backward(dx[0], x0[0], lambda j: mods[0, j : j + 1, :], own, other, wqkv, wo,
-                              take, rows, stash, mods_out, bias, result)], 0)
+    x = dot(xt[0], wpatch[0], TN) + vector(b_rep, START_PATCH) + pos[...]
+    run_steps([layer_backward(dx[0], x, lambda j: mods[0, j : j + 1, :], own, other, wqkv, wo,
+                              take, rows, stash, mods_out, bias, result, (a_input_a, a_input_m))], 0)
     (grad,) = result
     grad = grad.astype(bf16)
     pay_own[PAY_PATCH : PAY_PATCH + PV, :] += dot(xt[0], grad)
@@ -503,8 +542,8 @@
     def _():
         for copy in copies:
             copy.wait()
-        weight_grads(a_input_a, a_input_m, a_mixed, a_acted, stash,
-                     (col_own, col_other), (row_own, row_other))
+        weight_grads(a_input_a, a_input_m, a_mixed, a_acted, stash, (place_own, place_other),
+                     (grad_own, grad_other), out_sems, fills)
         pay_own[PAY_HEAD : PAY_HEAD + PV, :] = dhead[...]
         for layer, values in enumerate((dbias, dbias1)):
             pay_own[PAY_PROJ + layer : PAY_PROJ + layer + 1, :] = values[:, BIAS["proj"] : BIAS["proj"] + D]
@@ -539,9 +578,10 @@
     ("query", (TOK, D), bf16), ("keyed", (TOK, D), bf16), ("valued", (TOK, D), bf16),
     ("probs", (HEADS, TOK, TOK), f32), ("branch_a", (TOK, D), f32), ("middle", (TOK, D), f32),
     ("slope", (TOK, MLP), f32), ("branch_m", (TOK, D), f32), ("mixed", (TOK, D), bf16),
-    ("acted", (TOK, MLP), bf16), ("input_a", (TOK, D), bf16), ("input_m", (TOK, D), bf16),
+    ("acted", (TOK, MLP), bf16),
 ]
-GRAD_SHAPES = [(COL_S, D), (COL_S, D), (ROW_S, D), (ROW_S, D)]
+BOTH = COL_S + ROW_S
+GRAD_SHAPES = [(BOTH, D), (BOTH, D)]
 WEIGHT_SCRATCH = [pltpu.VMEM((D, 3 * D), bf16), pltpu.VMEM((D, D), bf16),
                   pltpu.VMEM((1, 3 * D), f32), pltpu.VMEM((1, MLP), f32)]
 
@@ -557,6 +597,10 @@
             pltpu.VMEM((rows, D), bf16), pltpu.VMEM((rows, D), bf16)]
 
 
+def place_scratch():
+    return [pltpu.VMEM(shape, f32) for shape in GRAD_SHAPES] + [pltpu.SemaphoreType.DMA((8,)), pltpu.SemaphoreType.DMA((2,))]
+
+
 def cost(flops, nbytes, count):
     return pl.CostEstimate(flops=int(flops * count), bytes_accessed=int(nbytes * count),
                            transcendentals=int(2e6 * count))
@@ -564,7 +608,7 @@
 
 def run_forward(xt, mods, full_io, pos, weights):
     count = xt.shape[0]
-    outs = [("x0", (TOK, D), f32)] + SAVED + [("x2", (TOK, D), f32)]
+    outs = SAVED + [("x2", (TOK, D), f32)]
     return pl.pallas_call(
         forward_kernel,
         grid=(count // GROUP,),
@@ -579,17 +623,18 @@
     )(xt, mods, full_io, pos, *weights)
 
 
-def run_middle(x2, mods, weights, full_io, targets):
+def run_middle(x2, mods, weights, full_io, targets, err_col, err_row):
     count = x2.shape[0]
     rows = count * TOK
     outs = [((count, TOK, D), per_latent(TOK, D, group=GROUP)), ((count, 8, D), per_latent(8, D, group=GROUP))]
-    outs += [(shape, fixed(*shape)) for shape in GRAD_SHAPES]
+    outs += [(shape, pl.BlockSpec(memory_space=pl.ANY)) for shape in GRAD_SHAPES]
     outs += [(shape, fixed(*shape)) for shape in ((1, BIAS_WIDTH), (PV, D), (PV, 1), (1, TOK))]
     return pl.pallas_call(
         middle_kernel,
         grid=(count // GROUP,),
         in_specs=[per_latent(TOK, D, group=GROUP), per_latent(14, D, group=GROUP)] + weight_specs(1)
-        + [pl.BlockSpec((1, PV, D), lambda n: (1, 0, 0)), per_latent(PV, TOK, group=GROUP)],
+        + [pl.BlockSpec((1, PV, D), lambda n: (1, 0, 0)), per_latent(PV, TOK, group=GROUP)]
+        + [pl.BlockSpec(memory_space=pl.ANY)] * 2,
         out_specs=[spec for _, spec in outs],
         out_shape=[jax.ShapeDtypeStruct(shape, f32) for shape, _ in outs],
         scratch_shapes=WEIGHT_SCRATCH
@@ -598,35 +643,38 @@
            pltpu.VMEM((GROUP, TOK, D), f32), pltpu.VMEM((GROUP, TOK, D), f32), pltpu.VMEM((rows, MLP), bf16),
            pltpu.VMEM((GROUP, TOK, MLP), f32), pltpu.VMEM((GROUP, TOK, D), f32),
            pltpu.VMEM((rows, D), bf16), pltpu.VMEM((rows, D), bf16)]
-        + stash_scratch(count),
+        + stash_scratch(count) + place_scratch(),
         compiler_params=params(),
         cost_estimate=cost(3.2e9, 3e6, count),
         name="layer_second",
-    )(x2, mods, *weights, full_io, targets)
-
-
-def run_last(dx, x0, mods, weights, xt, smalls, dmods1, saved):
+    )(x2, mods, *weights, full_io, targets, err_col, err_row)
+
+
+def run_last(dx, mods, weights, xt, full_io, pos, smalls, dmods1, err_col, err_row, saved):
     count = dx.shape[0]
     rows = count * TOK
     outs = [((count, 14, D), per_latent(14, D))]
-    outs += [(shape, fixed(*shape)) for shape in GRAD_SHAPES]
+    outs += [(shape, pl.BlockSpec(memory_space=pl.ANY)) for shape in GRAD_SHAPES]
     outs += [(shape, fixed(*shape)) for shape in ((PAY_ROWS, D), (PAY_ROWS, D))]
     return pl.pallas_call(
         last_kernel,
         grid=(count,),
-        in_specs=[per_latent(TOK, D), per_latent(TOK, D), per_latent(14, D)] + weight_specs(0)
-        + [per_latent(PV, TOK)]
+        in_specs=[per_latent(TOK, D), per_latent(14, D)] + weight_specs(0)
+        + [per_latent(PV, TOK), pl.BlockSpec((1, PV, D), lambda n: (0, 0, 0)), fixed(TOK, D)]
         + [fixed(*shape) for shape in ((1, BIAS_WIDTH), (PV, D), (PV, 1), (1, TOK))] + [per_latent(8, D)]
-        + [per_latent(*shape) for _, shape, _ in SAVED[:-4]] + [pl.BlockSpec(memory_space=pl.ANY)] * 4,
+        + [pl.BlockSpec(memory_space=pl.ANY)] * 2
+        + [per_latent(*shape) for _, shape, _ in SAVED[:-2]] + [pl.BlockSpec(memory_space=pl.ANY)] * 2,
         out_specs=[spec for _, spec in outs],
         out_shape=[jax.ShapeDtypeStruct(shape, f32) for shape, _ in outs],
         scratch_shapes=WEIGHT_SCRATCH
         + [pltpu.VMEM((rows, D), bf16)] * 3 + [pltpu.VMEM((rows, MLP), bf16)]
-        + stash_scratch(count) + [pltpu.VMEM((1, BIAS_WIDTH), f32), pltpu.SemaphoreType.DMA((4,))],
+        + stash_scratch(count) + [pltpu.VMEM((1, BIAS_WIDTH), f32), pltpu.SemaphoreType.DMA((2,))]
+        + place_scratch(),
         compiler_params=params(),
         cost_estimate=cost(2.2e9, 8e6, count),
         name="backward_first",
-    )(dx, x0, mods, *weights, xt, *smalls, dmods1, *saved[:-4], *[v.reshape(rows, -1) for v in saved[-4:]])
+    )(dx, mods, *weights, xt, full_io, pos, *smalls, dmods1, err_col, err_row,
+      *saved[:-2], *[v.reshape(rows, -1) for v in saved[-2:]])
 
 
 PACK = 128
@@ -659,141 +707,134 @@
     )
 
 
-PROJECT_STEPS = 2
-WIDE_BLOCK = COL_S // PROJECT_STEPS
-TALL_BLOCK = ROW_S // PROJECT_STEPS
-
-
-def project_step(err_col, own_col, got_col, err_row, own_row, got_row, fac_col, fac_row,
-                 mat_col, mat_row, left_col, left_row):
-    step = pl.program_id(0)
-    matrix = err_col[0] + (own_col[...] + got_col[...])
-    mat_col[...] = matrix
-    part = narrow_dot(fac_col[0], matrix, NN)
-    matrix = err_row[0] + (own_row[...] + got_row[...])
-    mat_row[...] = matrix
-    side = narrow_dot(fac_row[0], matrix, NT)
-
-    @pl.when(step == 0)
-    def _():
-        left_col[...] = part
-        left_row[...] = jnp.zeros_like(left_row)
-        left_row[:, :TALL_BLOCK] = side
-
-    @pl.when(step == 1)
-    def _():
-        left_col[...] += part
-        left_row[:, TALL_BLOCK:ROW_S] = side
-
-
-def project_second_kernel(block, err_col, own_col, got_col, err_row, own_row, got_row, fac_col, fac_row,
-                          dmods, full_cond, cond_own,
-                          mat_col, mat_row, left_col, left_row, grad_cond, cols_sent):
-    project_step(err_col, own_col, got_col, err_row, own_row, got_row, fac_col, fac_row,
-                 mat_col, mat_row, left_col, left_row)
-
-    @pl.when(pl.program_id(0) == 0)
-    def _():
-        n_dp, count = cols_sent.shape[0], cols_sent.shape[1]
-        line = jnp.concatenate([dmods[:, j, :] for j in range(14)], 1)
-        grad_act = dot(line.astype(bf16), full_cond[...], NT)
-        cond = cond_own[...]
-        gate = 1.0 / (1.0 + jnp.exp(-cond))
-        grad_cond[...] = grad_act * (gate * (1.0 + cond * (1.0 - gate)))
-        for j in range(n_dp):
-            cols_sent[j] = jnp.concatenate(
-                [line[:, j * block : (j + 1) * block], jnp.zeros((count, D - block), f32)], 1
-            )
-
-
-def packed_slots():
-    return ["row0", "row1", "col0", "col1", "io0", "io1", "row0", "row1", "row0", "row1"]
-
-
-def project_first_kernel(err_col, own_col, got_col, err_row, own_row, got_row, fac_col, fac_row,
-                         left_col1, left_row1, grad_cond, cols_sent, pay_own, pay_got, err_io, fac_io,
-                         mat_col, mat_row, mat_io, sent, left_col, left_row):
-    project_step(err_col, own_col, got_col, err_row, own_row, got_row, fac_col, fac_row,
-                 mat_col, mat_row, left_col, left_row)
-
-    @pl.when(pl.program_id(0) == PROJECT_STEPS - 1)
-    def _():
-        n_dp, count = cols_sent.shape[0], cols_sent.shape[1]
-        share = PACK // n_dp
-        pay = pay_own[...] + pay_got[...]
-        left_io = []
-        for index in range(2):
-            matrix = pay[index * PV : (index + 1) * PV] + err_io[index]
-            mat_io[index] = matrix
-            left_io.append(dot_full(fac_io[index], matrix))
-        sent[:, :count, :] = jnp.broadcast_to(grad_cond[...][None], (n_dp, count, D))
-        sent[:, count : 2 * count, :] = cols_sent[...]
-        sent[:, 2 * count :, :] = jnp.zeros((n_dp, share, D), f32)
-        tall = (left_row, left_row1)
-        for column in range(RANK):
-            pick = slice(column, column + 1)
-            lines = [tall[i % 2][pick, (i // 2) * D : (i // 2 + 1) * D] for i in (0, 1)]
-            lines += [left_col[pick, :], left_col1[pick, :], left_io[0][pick], left_io[1][pick]]
-            lines += [tall[i % 2][pick, (i // 2) * D : (i // 2 + 1) * D] for i in (2, 3, 4, 5)]
-            for extra in range(6):
-                at = column * 6 + extra
-                if at < SMALL_ROWS:
-                    lines.append(pay[PAY_PROJ + at : PAY_PROJ + at + 1])
-            for slot, line in enumerate(lines):
-                at = column * 16 + slot
-                place = 2 * count + at % share
-                sent[at // share, place : place + 1, :] = line
-
-
-def project_specs(layer):
-    col_block = pl.BlockSpec((WIDE_BLOCK, D), lambda n: (n, 0))
-    row_block = pl.BlockSpec((TALL_BLOCK, D), lambda n: (n, 0))
-    ins = [pl.BlockSpec((1, WIDE_BLOCK, D), lambda n: (layer, n, 0)), col_block, col_block,
-           pl.BlockSpec((1, TALL_BLOCK, D), lambda n: (layer, n, 0)), row_block, row_block,
-           pl.BlockSpec((1, RANK, WIDE_BLOCK), lambda n: (n, 0, 0)),
-           pl.BlockSpec((1, RANK, D), lambda n: (layer, 0, 0))]
-    return ins, [col_block, row_block]
-
-
-def steps_of(fac_col):
-    return fac_col.reshape(RANK, PROJECT_STEPS, WIDE_BLOCK).transpose(1, 0, 2)
-
-
-def run_project_second(err_col, grads, err_row, fac_col, fac_row, dmods, full_cond, cond_own, n_dp):
-    own_col, got_col, own_row, got_row = grads
+CHUNKS = [(448 * k, 448) for k in range(3)] + [(COL_S + 480 * k, 480) for k in range(2)]
+
+
+def layer_chunks(layer, err_col, err_row):
+    for at, size in CHUNKS:
+        ref, start = (err_col, at) if at < COL_S else (err_row, at - COL_S)
+        yield ref.at[layer, pl.ds(start, size), :], pl.ds(at, size)
+
+
+def project(layer, own, got, fac_col, fac_row, mat, left_col, left_row, v_own, v_got, sems, out_sems):
+    loads, stores = [], []
+    for k, (at, size) in enumerate(CHUNKS):
+        rows = pl.ds(at, size)
+        loads.append([pltpu.make_async_copy(src.at[rows, :], dst.at[rows, :], sems.at[2 * k + i])
+                      for i, (src, dst) in enumerate(((own, v_own), (got, v_got)))])
+        stores.append(pltpu.make_async_copy(v_own.at[rows, :], mat.at[rows, :], out_sems.at[k]))
+        for copy in loads[-1]:
+            copy.start()
+    left_row[...] = jnp.zeros_like(left_row)
+    total = None
+    for (at, size), copies, store in zip(CHUNKS, loads, stores):
+        for copy in copies:
+            copy.wait()
+        matrix = v_own[at : at + size, :] + v_got[at : at + size, :]
+        v_own[at : at + size, :] = matrix
+        store.start()
+        if at < COL_S:
+            part = narrow_dot(fac_col[layer][:, at : at + size], matrix, NN)
+            total = part if total is None else total + part
+        else:
+            left_row[:, at - COL_S : at - COL_S + size] = narrow_dot(fac_row[layer], matrix, NT)
+    left_col[...] = total
+    for store in stores:
+        store.wait()
+
+
+ANY = pl.BlockSpec(memory_space=pl.ANY)
+VMEM = pl.BlockSpec(memory_space=pltpu.VMEM)
+SMEM = pl.BlockSpec(memory_space=pltpu.SMEM)
+PROJECT_SCRATCH = [pltpu.VMEM((BOTH, D), f32)] * 2 + [
+    pltpu.SemaphoreType.DMA((2 * len(CHUNKS),)), pltpu.SemaphoreType.DMA((len(CHUNKS),))]
+
+
+def large():
+    return pltpu.CompilerParams(vmem_limit_bytes=62 * 2**20)
+
+
+def shapes_of(shapes):
+    return [jax.ShapeDtypeStruct(shape, f32) for shape in shapes]
+
+
+def run_project_second(own, got, fac_col, fac_row):
+    return pl.pallas_call(
+        lambda *refs: project(1, *refs),
+        in_specs=[ANY] * 2 + [VMEM] * 2,
+        out_specs=[ANY, VMEM, VMEM],
+        out_shape=shapes_of([(BOTH, D), (RANK, D), (RANK, WIDE)]),
+        scratch_shapes=PROJECT_SCRATCH,
+        compiler_params=large(),
+        cost_estimate=pl.CostEstimate(flops=int(1e9), bytes_accessed=int(1.5e7), transcendentals=0),
+        name="left_second",
+    )(own, got, fac_col, fac_row)
+
+
+def exchange_kernel(block, place, dmods, full_cond, cond, sent):
+    n_dp = sent.shape[0]
     count = dmods.shape[0]
-    ins, outs = project_specs(1)
-    extra = [(RANK, D), (RANK, WIDE), (count, D), (n_dp, count, D)]
+    line = jnp.concatenate([dmods[:, j, :] for j in range(14)], 1)
+    grad_act = dot(line.astype(bf16), full_cond[...], NT)
+    cond_own = cond[pl.ds(pl.multiple_of(place[0] * count, count), count), :]
+    gate = 1.0 / (1.0 + jnp.exp(-cond_own))
+    grad_cond = grad_act * (gate * (1.0 + cond_own * (1.0 - gate)))
+    sent[:, :count, :] = jnp.broadcast_to(grad_cond[None], (n_dp, count, D))
+    for j in range(n_dp):
+        sent[j, count:, :] = jnp.concatenate(
+            [line[:, j * block : (j + 1) * block], jnp.zeros((count, D - block), f32)], 1
+        )
+
+
+def run_exchange(n_dp, place, dmods, full_cond, cond):
     return pl.pallas_call(
-        lambda *refs: project_second_kernel(N_MODS // n_dp, *refs),
-        grid=(PROJECT_STEPS,),
-        in_specs=ins + [fixed(count, 14, D), fixed(D, N_MODS), fixed(count, D)],
-        out_specs=outs + [fixed(*shape) for shape in extra],
-        out_shape=[jax.ShapeDtypeStruct(shape, f32) for shape in [(COL_S, D), (ROW_S, D)] + extra],
-        compiler_params=params(),
-        name="left_second",
-    )(err_col, own_col, got_col, err_row, own_row, got_row, steps_of(fac_col[1]), fac_row,
-      dmods, full_cond, cond_own)
-
-
-def run_project_first(err_col, grads, err_row, fac_col, fac_row, left_col1, left_row1, grad_cond, cols_sent,
+        lambda *refs: exchange_kernel(N_MODS // n_dp, *refs),
+        in_specs=[SMEM, VMEM, VMEM, VMEM],
+        out_shape=jax.ShapeDtypeStruct((n_dp, 2 * dmods.shape[0], D), f32),
+        compiler_params=large(),
+        name="modulation_rows",
+    )(place, dmods, full_cond, cond)
+
+
+def project_first_kernel(own, got, fac_col, fac_row,
+                         left_col1, left_row1, pay_own, pay_got, err_io, fac_io,
+                         mat, mat_io, sent, left_col, left_row, *scratch):
+    project(0, own, got, fac_col, fac_row, mat, left_col, left_row, *scratch)
+    share = sent.shape[1]
+    pay = pay_own[...] + pay_got[...]
+    left_io = []
+    for index in range(2):
+        matrix = pay[index * PV : (index + 1) * PV] + err_io[index]
+        mat_io[index] = matrix
+        left_io.append(dot_full(fac_io[index], matrix))
+    sent[...] = jnp.zeros_like(sent)
+    tall = (left_row, left_row1)
+    for column in range(RANK):
+        pick = slice(column, column + 1)
+        lines = [tall[i % 2][pick, (i // 2) * D : (i // 2 + 1) * D] for i in (0, 1)]
+        lines += [left_col[pick, :], left_col1[pick, :], left_io[0][pick], left_io[1][pick]]
+        lines += [tall[i % 2][pick, (i // 2) * D : (i // 2 + 1) * D] for i in (2, 3, 4, 5)]
+        for extra in range(6):
+            at = column * 6 + extra
+            if at < SMALL_ROWS:
+                lines.append(pay[PAY_PROJ + at : PAY_PROJ + at + 1])
+        for slot, line in enumerate(lines):
+            at = column * 16 + slot
+            sent[at // share, at % share : at % share + 1, :] = line
+
+
+def run_project_first(n_dp, own, got, fac_col, fac_row, left_col1, left_row1,
                       pay_own, pay_got, err_io, fac_io):
-    own_col, got_col, own_row, got_row = grads
-    n_dp, count = cols_sent.shape[:2]
-    ins, outs = project_specs(0)
-    extra = [(2, PV, D), (n_dp, 2 * count + PACK // n_dp, D)]
     return pl.pallas_call(
         project_first_kernel,
-        grid=(PROJECT_STEPS,),
-        in_specs=ins + [fixed(RANK, D), fixed(RANK, WIDE), fixed(count, D), fixed(n_dp, count, D),
-                        fixed(PAY_ROWS, D), fixed(PAY_ROWS, D), fixed(2, PV, D), fixed(2, RANK, PV)],
-        out_specs=outs + [fixed(*shape) for shape in extra],
-        out_shape=[jax.ShapeDtypeStruct(shape, f32) for shape in [(COL_S, D), (ROW_S, D)] + extra],
-        scratch_shapes=[pltpu.VMEM((RANK, D), f32), pltpu.VMEM((RANK, WIDE), f32)],
-        compiler_params=params(),
+        in_specs=[ANY] * 2 + [VMEM] * 8,
+        out_specs=[ANY, VMEM, VMEM],
+        out_shape=shapes_of([(BOTH, D), (2, PV, D), (n_dp, PACK // n_dp, D)]),
+        scratch_shapes=[pltpu.VMEM((RANK, D), f32), pltpu.VMEM((RANK, WIDE), f32)] + PROJECT_SCRATCH,
+        compiler_params=large(),
+        cost_estimate=pl.CostEstimate(flops=int(1e9), bytes_accessed=int(1.5e7), transcendentals=0),
         name="left_first",
-    )(err_col, own_col, got_col, err_row, own_row, got_row, steps_of(fac_col[0]), fac_row,
-      left_col1, left_row1, grad_cond, cols_sent, pay_own, pay_got, err_io, fac_io)
+    )(own, got, fac_col, fac_row, left_col1, left_row1, pay_own, pay_got, err_io, fac_io)
 
 
 TIME_ROWS = FREQ + D + 8
@@ -802,7 +843,7 @@
 def modulation_kernel(block, core, got, act_half, features, first, first_act, full_time, labels,
                       cond_mine, cond_their, time_part, table_part):
     n_dp = got.shape[0]
-    count = (got.shape[1] - PACK // n_dp) // 2
+    count = got.shape[1] // 2
     half = block // 2
     grad_cond = got[:, :count, :].reshape(n_dp * count, D)
     cols = got[:, count : 2 * count, :].reshape(n_dp * count, D)
@@ -871,11 +912,47 @@
     return jnp.sum(values * values, keepdims=True)
 
 
-def right_kernel(packed, mat_col0, mat_row0, mat_col1, mat_row1, mat_io, cond_own, cond_got, table_own, table_got,
-                 sent, left_col, left_row, left_io, table_share, flat):
+def rows_kernel(cond_own, cond_got, table_own, table_got, sent, table_share, sums):
+    cond_grad = cond_own[...] + cond_got[...]
+    table = table_own[...] + table_got[...]
+    table_share[...] = table
+    sums[...] = jnp.concatenate([total_squares(cond_grad), total_squares(table), jnp.zeros((1, D - 2), f32)], 1)
+    n_dp = sent.shape[0]
+    rows, half = D // n_dp, cond_grad.shape[1]
+    top = cond_top(rows)
+    for j in range(n_dp):
+        piece = cond_grad[j * rows : (j + 1) * rows]
+        sent[j, : min(top, rows), :half] = piece[:top]
+        if rows > top:
+            sent[j, : rows - top, half : 2 * half] = piece[top:]
+
+
+def run_rows(n_dp, cond_own, cond_got, table_own, table_got):
+    return pl.pallas_call(
+        rows_kernel,
+        out_shape=shapes_of([(n_dp, cond_top(D // n_dp), D), table_own.shape, (1, D)]),
+        compiler_params=large(),
+        name="modulation_sums",
+    )(cond_own, cond_got, table_own, table_got)
+
+
+def mat_loads(mats, places, sems):
+    return [[pltpu.make_async_copy(mat.at[pl.ds(at, size), :], place.at[pl.ds(at, size), :],
+                                   sems.at[layer * len(CHUNKS) + k]) for k, (at, size) in enumerate(CHUNKS)]
+            for layer, (mat, place) in enumerate(zip(mats, places))]
+
+
+def right_kernel(packed, mat0, mat1, mat_io, sums, sent, left_col, left_row, left_io, flat, v0, v1, sems):
+    loads = mat_loads((mat0, mat1), (v0, v1), sems)
+    for copies in loads:
+        for copy in copies:
+            copy.start()
     ortho(packed, left_col, left_row, left_io)
-    for layer, (col, row) in enumerate(((mat_col0, mat_row0), (mat_col1, mat_row1))):
-        right = narrow_dot(left_col[layer], col[...], NT)
+    for copies in loads:
+        for copy in copies:
+            copy.wait()
+    for layer, mat in enumerate((v0, v1)):
+        right = narrow_dot(left_col[layer], mat[:COL_S, :], NT)
         for piece in range(4):
             wide = min(D, COL_S - piece * D)
             at = layer * COL_ROWS + piece * RANK
@@ -883,39 +960,25 @@
                 flat[at : at + RANK, :] = jnp.zeros((RANK, D), f32)
             flat[at : at + RANK, :wide] = right[:, piece * D : piece * D + wide]
         at = ROW_AT + layer * RANK
-        flat[at : at + RANK, :] = narrow_dot(left_row[layer][:, :ROW_S], row[...], NN)
+        flat[at : at + RANK, :] = narrow_dot(left_row[layer][:, :ROW_S], mat[COL_S:, :], NN)
         at = IO_AT + layer * RANK
         flat[at : at + RANK, :] = jnp.zeros((RANK, D), f32)
         flat[at : at + RANK, :PV] = dot_full(left_io[layer], mat_io[layer], NT)
-    cond_grad = cond_own[...] + cond_got[...]
-    table = table_own[...] + table_got[...]
-    table_share[...] = table
     flat[EXTRA_AT:, :] = jnp.zeros((PACK - EXTRA_AT, D), f32)
-    flat[EXTRA_AT : EXTRA_AT + 1, :] = jnp.concatenate(
-        [total_squares(cond_grad), total_squares(table), jnp.zeros((1, D - 2), f32)], 1
-    )
-    n_dp = sent.shape[0]
-    share = PACK // n_dp
-    rows, half = D // n_dp, cond_grad.shape[1]
-    top = cond_top(rows)
-    sent[:, :share, :] = flat[...].reshape(n_dp, share, D)
-    for j in range(n_dp):
-        piece = cond_grad[j * rows : (j + 1) * rows]
-        sent[j, share : share + min(top, rows), :half] = piece[:top]
-        if rows > top:
-            sent[j, share : share + rows - top, half : 2 * half] = piece[top:]
-
-
-def run_right(n_dp, packed, mats, mat_io, cond_own, cond_got, table_own, table_got):
-    shapes = [(n_dp, PACK // n_dp + cond_top(D // n_dp), D), (L, RANK, D), (L, RANK, WIDE), (2, RANK, D),
-              table_own.shape]
+    flat[EXTRA_AT : EXTRA_AT + 1, :] = sums[...]
+    sent[...] = flat[...].reshape(sent.shape)
+
+
+def run_right(n_dp, packed, mats, mat_io, sums):
     return pl.pallas_call(
         right_kernel,
-        out_shape=[jax.ShapeDtypeStruct(shape, f32) for shape in shapes],
-        scratch_shapes=[pltpu.VMEM((PACK, D), f32)],
-        compiler_params=pltpu.CompilerParams(vmem_limit_bytes=62 * 2**20),
+        in_specs=[VMEM, ANY, ANY, VMEM, VMEM],
+        out_shape=shapes_of([(n_dp, PACK // n_dp, D), (L, RANK, D), (L, RANK, WIDE), (2, RANK, D)]),
+        scratch_shapes=[pltpu.VMEM((PACK, D), f32), pltpu.VMEM((BOTH, D), f32), pltpu.VMEM((BOTH, D), f32),
+                        pltpu.SemaphoreType.DMA((L * len(CHUNKS),))],
+        compiler_params=large(),
         name="right_factors",
-    )(packed, *mats, mat_io, cond_own, cond_got, table_own, table_got)
+    )(packed, *mats, mat_io, sums)
 
 
 def norm_kernel(packed, left_packed, left_col, left_row, left_io, time_own, time_got,
@@ -971,28 +1034,48 @@
     )(packed, left_packed, *lefts, time_own, time_got)
 
 
-def error_kernel(mat_col0, mat_row0, mat_col1, mat_row1, mat_io, left_col, left_row, left_io,
-                 right_col, right_row, right_io, err_col, err_row, err_io):
-    for layer, (col, row) in enumerate(((mat_col0, mat_row0), (mat_col1, mat_row1))):
-        @pl.when(pl.program_id(0) == layer)
-        def _():
-            err_col[0] = col[...] - outer(right_col[layer], left_col[layer])
-            err_row[0] = row[...] - outer(left_row[layer][:, :ROW_S], right_row[layer])
-            err_io[layer] = mat_io[layer] - outer(right_io[layer], left_io[layer])
+def error_kernel(mat0, mat1, mat_io, left_col, left_row, left_io, right_col, right_row, right_io,
+                 err_col, err_row, err_io, v0, v1, sems, out_sems):
+    loads = mat_loads((mat0, mat1), (v0, v1), sems)
+    for copies in loads:
+        for copy in copies:
+            copy.start()
+    stores = []
+    for layer, place in enumerate((v0, v1)):
+        for k, ((at, size), (target, rows)) in enumerate(zip(CHUNKS, layer_chunks(layer, err_col, err_row))):
+            if at < COL_S:
+                approx = outer(right_col[layer][:, at : at + size], left_col[layer])
+            else:
+                approx = outer(left_row[layer][:, at - COL_S : at - COL_S + size], right_row[layer])
+            loads[layer][k].wait()
+            place[at : at + size, :] = place[at : at + size, :] - approx
+            store = pltpu.make_async_copy(place.at[rows, :], target, out_sems.at[layer * len(CHUNKS) + k])
+            store.start()
+            stores.append(store)
+        err_io[layer] = mat_io[layer] - outer(right_io[layer], left_io[layer])
+    for store in stores:
+        store.wait()
 
 
 def run_error(mats, mat_io, lefts, rights):
     return pl.pallas_call(
         error_kernel,
-        grid=(L,),
-        in_specs=[fixed(*v.shape) for v in (*mats, mat_io, *lefts, *rights)],
-        out_specs=[pl.BlockSpec((1, COL_S, D), lambda n: (n, 0, 0)),
-                   pl.BlockSpec((1, ROW_S, D), lambda n: (n, 0, 0)), fixed(2, PV, D)],
-        out_shape=[jax.ShapeDtypeStruct((L, COL_S, D), f32), jax.ShapeDtypeStruct((L, ROW_S, D), f32),
-                   jax.ShapeDtypeStruct((2, PV, D), f32)],
-        compiler_params=params(),
+        in_specs=[ANY, ANY] + [VMEM] * 7,
+        out_specs=[ANY, ANY, VMEM],
+        out_shape=shapes_of([(L, COL_S, D), (L, ROW_S, D), (2, PV, D)]),
+        scratch_shapes=[pltpu.VMEM((BOTH, D), f32), pltpu.VMEM((BOTH, D), f32),
+                        pltpu.SemaphoreType.DMA((L * len(CHUNKS),)), pltpu.SemaphoreType.DMA((L * len(CHUNKS),))],
+        compiler_params=large(),
         name="next_errors",
     )(*mats, mat_io, *lefts, *rights)
+
+
+def own_columns(values, first, count):
+    across = lax.broadcasted_iota(jnp.int32, (count, D), 1)
+    down = lax.broadcasted_iota(jnp.int32, (count, D), 0)
+    pick = (across == down + first).astype(f32).astype(bf16)
+    high, mid, low = split3(values)
+    return dot(high, pick, NT) + (dot(mid, pick, NT) + dot(low, pick, NT))
 
 
 def update_kernel(core, parts, parts_got, left_col, right_col, right_row, left_row, right_io, left_io,
@@ -1009,22 +1092,23 @@
         moved = momentum_decay * momentum + scaling * gradient
         return weight - learn_rate * moved, moved
 
+    n_dp = cond_own.shape[0]
+    rows = w_cond.shape[0]
+    at = core[1] * rows
     for layer in range(L):
         n_col[layer], v_col[layer] = advance(
-            w_col[layer], m_col[layer], outer(left_col[layer], right_col[layer]))
+            w_col[layer], m_col[layer], outer(own_columns(left_col[layer], at, rows), right_col[layer]))
         n_row[layer], v_row[layer] = advance(
-            w_row[layer], m_row[layer], outer(right_row[layer], left_row[layer][:, :ROW_S]))
+            w_row[layer], m_row[layer],
+            outer(own_columns(right_row[layer], at, rows), left_row[layer][:, :ROW_S]))
         n_io[layer], v_io[layer] = advance(
-            w_io[layer], m_io[layer], outer(right_io[layer], left_io[layer]))
-    n_dp = cond_own.shape[0]
-    rows = w_cond.shape[0]
+            w_io[layer], m_io[layer], outer(right_io[layer], own_columns(left_io[layer], at, rows)))
     half = N_MODS // n_dp // 2
     top = cond_top(rows)
-    share = cond_own.shape[1] - top
     is_first = core[0] == 0
     pieces = []
     for j in range(n_dp):
-        mine, theirs = cond_own[j, share:, :], cond_got[j]
+        mine, theirs = cond_own[j], cond_got[j]
         for pair in ((mine, theirs), (theirs, mine)):
             block = jnp.where(is_first, pair[0], pair[1])
             if rows > top:
@@ -1078,7 +1162,7 @@
     n_dp = lax.axis_size("dp")
     index_dp = lax.axis_index("dp")
     index_t = lax.axis_index("tensor")
-    core = index_t.astype(jnp.int32).reshape(1)
+    core = jnp.stack([index_t, index_dp]).astype(jnp.int32)
     first_core = index_t == 0
     n_all = labels.shape[0]
     per_dp = latents.shape[0]
@@ -1147,7 +1231,6 @@
 
     halves_of = [half_of(v) for v in (cond_act, features, first, first_act)]
     labels_half = half_of(labels)[:, None]
-    cond_own = lax.dynamic_slice_in_dim(cond, (index_dp * 2 + index_t) * count, count, 0)
 
     def mine_of(values):
         return lax.dynamic_slice_in_dim(values, index_t * count, count, 0)
@@ -1160,53 +1243,52 @@
     own = lax.dynamic_slice_in_dim(full, index_t, 1, 1).reshape(D, L * GATH)
     other = lax.dynamic_slice_in_dim(full, 1 - index_t, 1, 1).reshape(D, L * GATH)
     weights = (own, other, b_col, swap(b_col), b_line)
-    x0, *saved, x2 = run_forward(xt, mods, full_io, jnp.asarray(position_table()), weights)
+    pos = jnp.asarray(position_table())
+    *saved, x2 = run_forward(xt, mods, full_io, pos, weights)
     x2, late_cond = lax.optimization_barrier((x2, w_cond))
     full_cond = lax.all_gather(late_cond.astype(bf16), "dp", axis=0, tiled=True)
-    dx, dmods1, col_own1, col_oth1, row_own1, row_oth1, *smalls = run_middle(
-        x2, mods, weights, full_io, flip(mine_of(targets))
-    )
-    grads1 = (col_own1, swap(col_oth1), row_own1, swap(row_oth1))
-    dmods, col_own0, col_oth0, row_own0, row_oth0, pay_own, pay_oth = run_last(
-        dx, x0, mods, weights, xt, smalls, dmods1, saved
-    )
-    grads0 = (col_own0, swap(col_oth0), row_own0, swap(row_oth0))
-    pay_got = swap(pay_oth)
-
     err_col_t, err_io_t = flip(err_col), flip(err_io)
+    dx, dmods1, own1, oth1, *smalls = run_middle(
+        x2, mods, weights, full_io, flip(mine_of(targets)), err_col_t, err_row
+    )
+    got1 = swap(oth1)
+    dmods, own0, oth0, pay_own, pay_oth = run_last(
+        dx, mods, weights, xt, full_io, pos, smalls, dmods1, err_col_t, err_row, saved
+    )
+    got0, pay_got = swap(oth0), swap(pay_oth)
+
+    place = (index_dp * 2 + index_t).astype(jnp.int32).reshape(1)
+    rows_got = trade(run_exchange(n_dp, place, dmods, full_cond, cond))
     fac_col_t, fac_row_t, fac_io_t = flip(fac_col), flip(fac_row), flip(fac_io)
-    mat_col1, mat_row1, left_col1, left_row1, grad_cond, cols_sent = run_project_second(
-        err_col_t, grads1, err_row, fac_col_t, fac_row_t, dmods, full_cond, cond_own, n_dp
-    )
-    mat_col0, mat_row0, mat_io, sent = run_project_first(
-        err_col_t, grads0, err_row, fac_col_t, fac_row_t, left_col1, left_row1, grad_cond, cols_sent,
+    mat1, left_col1, left_row1 = run_project_second(own1, got1, fac_col_t, fac_row_t)
+    mat0, mat_io, sent = run_project_first(
+        n_dp, own0, got0, fac_col_t, fac_row_t, left_col1, left_row1,
         pay_own, pay_got, err_io_t, fac_io_t
     )
-    mats = (mat_col0, mat_row0, mat_col1, mat_row1)
-    got = trade(sent)
-    left_packed = spread(jnp.sum(got[:, 2 * count :], 0)).reshape(RANK, 16, D)
-
-    cond_mine, cond_their, time_own, table_part = run_modulation(core, got, *halves_of, full_time, labels_half)
+    mats = (mat0, mat1)
+    rows_got, sent = lax.optimization_barrier((rows_got, sent))
+    share = jnp.sum(trade(sent), 0)
+
+    cond_mine, cond_their, time_own, table_part = run_modulation(core, rows_got, *halves_of, full_time, labels_half)
+    share, cond_mine, cond_their, time_own, table_part = lax.optimization_barrier(
+        (share, cond_mine, cond_their, time_own, table_part)
+    )
+    left_packed = spread(share).reshape(RANK, 16, D)
     cond_got, time_got = swap(cond_their), swap(time_own)
     table_own = lax.dynamic_slice_in_dim(table_part, index_dp * rows, rows, 0)
-    table_got = swap(table_own)
-
-    sent, left_col, left_row, left_io, table_share = run_right(
-        n_dp, left_packed, mats, mat_io, cond_mine, cond_got, table_own, table_got
-    )
-    share = PACK // n_dp
-    got = trade(sent)
-    packed = spread(jnp.sum(got[:, :share], 0)).reshape(PACK, D)
-    cond_rows_got = swap(got[:, share:])
+    cond_sent, table_share, sums = run_rows(n_dp, cond_mine, cond_got, table_own, swap(table_own))
+    cond_rows = trade(cond_sent)
+
+    sent, left_col, left_row, left_io = run_right(n_dp, left_packed, mats, mat_io, sums)
+    cond_rows, sent = lax.optimization_barrier((cond_rows, sent))
+    packed = spread(jnp.sum(trade(sent), 0)).reshape(PACK, D)
+    cond_rows_got = swap(cond_rows)
     lefts = (left_col, left_row, left_io)
     right_col, right_row, right_io, parts, brep_grad, bcol_grad = run_norm(
         packed, left_packed, lefts, time_own, time_got
     )
     parts_got = swap(parts)
     next_err_col, next_err_row, next_err_io = run_error(mats, mat_io, lefts, (right_col, right_row, right_io))
-
-    def mine_cols(values):
-        return lax.dynamic_slice_in_dim(values, index_dp * rows, rows, 2)
 
     time_at = index_dp * time_rows
     time_grad = (
@@ -1217,8 +1299,8 @@
     momenta = (mom_col, flip(mom_row), mom_cond, mom_time, flip(mom_io), mom_table.T, mom_bcol, mom_brep[None])
     scalars, *new = run_update(
         core,
-        (parts, parts_got, mine_cols(left_col), right_col, mine_cols(right_row), left_row, right_io,
-         mine_cols(left_io), got, cond_rows_got, time_grad, table_share, bcol_grad, brep_grad),
+        (parts, parts_got, left_col, right_col, right_row, left_row, right_io, left_io,
+         cond_rows, cond_rows_got, time_grad, table_share, bcol_grad, brep_grad),
         olds, momenta,
     )
 

time: 369 us -> 360 us (0.976)
  waiting for transfers between devices: 65.4 us -> 45.2 us
  blocking collectives: 23.6 us -> 35.9 us
  local copies, waits for them, and re-layouts: 32.9 us -> 24.9 us
    all_to_all x4 -> x5, waiting for transfers between devices: 24 us -> 9.98 us  [trade(): return lax.all_to_all(chunks, 'dp', 0, 0, tiled=True)]
    all_to_all x1 -> x2, blocking collectives: 23.6 us -> 35.9 us  [trade(): return lax.all_to_all(chunks, 'dp', 0, 0, tiled=True)]
    dynamic_slice x4 -> x0, local copies, waits for them, and re-layouts: 5.46 us -> none  [the longest x3 4.16 us: mine_cols(): return lax.dynamic_slice_in_dim(values, index_dp * rows, rows, 2)]
    ppermute x12 -> x10, waiting for transfers between devices: 7.02 us -> 1.57 us  [swap(): return lax.ppermute(values, 'tensor', [(0, 1), (1, 0)])]
    all_to_all x4 -> x5, starting transfers between devices: 22 us -> 26.3 us  [trade(): return lax.all_to_all(chunks, 'dp', 0, 0, tiled=True)]
    pallas_call x4 -> x6, Pallas kernels: 30.9 us -> 34.3 us  [the longest x1 7.38 us: run_right(): pl.pallas_call(right_kernel, in_specs=[VMEM, ANY, ANY, VMEM, VMEM], out_s...]
    ppermute x12 -> x10, starting transfers between devices: 10.6 us -> 7.97 us  [swap(): return lax.ppermute(values, 'tensor', [(0, 1), (1, 0)])]
  transfers between devices with their start and end apart: 19 -> 18, of which waited for: 8 -> 8; matrix products, arithmetic and copies ran while one was open for 10% -> 9% of each run, Pallas kernels for 35% -> 41%
where the time goes in v4:
time: 360 us; the launch traced here: 354 us
  Pallas kernels  178 us (49%)
  waiting for transfers between devices  45.2 us (13%)
  starting transfers between devices  38.4 us (11%)
  blocking collectives  35.9 us (10%)
  local copies, waits for them, and re-layouts  24.9 us (7%)
  between operations  15 us (4%)
  other arithmetic  12.5 us (3%)
  matrix products  4.14 us (1%)
    pallas_call x1, Pallas kernels, run_middle(): pl.pallas_call(middle_kernel, grid=(count // GROUP,), in_specs=[per_laten...  59.5 us
    pallas_call x1, Pallas kernels, run_last(): pl.pallas_call(last_kernel, grid=(count,), in_specs=[per_latent(TOK, D),...  43.4 us
    all_to_all x2, blocking collectives, trade(): return lax.all_to_all(chunks, 'dp', 0, 0, tiled=True)  35.9 us
    pallas_call x1, Pallas kernels, run_forward(): pl.pallas_call(forward_kernel, grid=(count // GROUP,), in_specs=[per_late...  28.8 us
    all_to_all x5, starting transfers between devices, trade(): return lax.all_to_all(chunks, 'dp', 0, 0, tiled=True)  26.3 us
    all_gather x1, waiting for transfers between devices, on_device(): full = lax.all_gather(shard, ('dp', 'tensor'))  25.3 us
    all_to_all x5, waiting for transfers between devices, trade(): return lax.all_to_all(chunks, 'dp', 0, 0, tiled=True)  9.98 us
    all_to_all x1, waiting for transfers between devices, on_device(): mods = lax.all_to_all(mods, ('dp', 'tensor'), 0, 0, tiled=True)  8.31 us
  transfers between devices with their start and end apart: 18, of which 8 were waited for; matrix products, arithmetic and copies ran while one was open for 9% of the time, Pallas kernels for 41%

profile of v4, /device:TPU:1, one launch (start us, length us, event | category | flops | bytes accessed | tf_op | source)
XLA Modules:
  0.0 353.7 jit_solution(7675600719034113361)
XLA Ops:
  7.2 1.0 convert.35
  8.2 0.9 bitcast_convert_fusion.1
  9.3 0.8 concatenate.25
  10.8 0.8 convert_element_type.74
  11.6 1.2 fusion.1
  13.8 1.1 convert_element_type.79
  14.9 1.1 reshape.281
  17.7 0.9 reduce.6
  19.1 23.9 %all_to_all.47 = bf16[16,2,7648]{2,1,0:T(2,128)(2,1)S(1)} all-to-all(bf16[16,2,7648]{2,1,0:T(2,128)(2,1)S(1)} %reshape.316), channel_id=1, replica_groups=mesh['dp'=16,'tensor'=2] {'dp'}, dimensions={0} | all-to-all | bytes 978944 | tf_op jit(solution)/shard_map/all_to_all | solution.py:1143
  42.9 0.7 reshape.317
  43.9 0.8 collective-permute-start
  47.6 0.9 multiply_convert_fusion.1
  48.6 1.1 multiply_convert_fusion
  49.7 0.9 fusion.6
  50.6 3.9 %all-to-all-start.1 = ((f32[32,8,168]{2,1,0:T(8,128)}), f32[32,8,168]{2,1,0:T(8,128)S(1)}, u32[]{:S(2)}, u32[]{:S(2)}) async-start(f32[32,8,168]{2,1,0:T(8,128)} %fusion.6), calls=%async_computation.1 | async-start | bytes 524288 | tf_op jit(solution)/shard_map/all_to_all | solution.py:1222
  55.8 0.8 reshape.288.wpatch.whead
  56.6 8.3 %all-to-all-done.1 = f32[32,8,168]{2,1,0:T(8,128)S(1)} async-done(((f32[32,8,168]{2,1,0:T(8,128)}), f32[32,8,168]{2,1,0:T(8,128)S(1)}, u32[]{:S(2)}, u32[]{:S(2)}) %all-to-all-start.1) | async-done | bytes 172064 | tf_op jit(solution)/shard_map/all_to_all | solution.py:1222
  66.0 25.3 %all-gather.3.cloned.1.call-done = bf16[32,24,4608]{2,1,0:T(8,128)(2,1)} async-done(((bf16[1,24,4608]{2,1,0:T(8,128)(2,1)}), bf16[32,24,4608]{2,1,0:T(8,128)(2,1)}) %all-gather.3.cloned.1.call-update) | async-done | bytes 7077904 | tf_op jit(solution)/shard_map/all_gather | solution.py:1184
  91.2 6.6 %constant_dynamic-slice_fusion.1 = (bf16[16,1,24,4608]{3,2,1,0:T(8,128)(2,1)}, bf16[16,1,24,4608]{3,2,1,0:T(8,128)(2,1)}) fusion(bf16[16,2,24,4608]{3,2,1,0:T(8,128)(2,1)} %bitcast.104, s32[]{:T(128)S(6)} %select_n.38, s32[]{:T(128)S(6)} %select_n.36), kind=kLoop, calls=%fused_computation.49 | loop fusion | bytes 14155784 | tf_op jit(solution)/shard_map/dynamic_slice | solution.py:1244
  98.4 28.8 %forward_first.1 = (bf16[8,256,384]{2,1,0:T(8,128)(2,1)}, bf16[8,256,384]{2,1,0:T(8,128)(2,1)}, bf16[8,256,384]{2,1,0:T(8,128)(2,1)}, f32[8,6,256,256]{3,2,1,0:T...) custom-call(bf16[8,16,256]{2,1,0:T(8,128)(2,1)} %get-tuple-element.2, ...), custom_call_target="tpu_custom_call" | custom-call | flops 8000000000 | bytes 48000000 | tf_op jit(solution)/shard_map/forward_first/pallas_call | solution.py:612
  128.0 59.5 %layer_second.1 = (f32[8,256,384]{2,1,0:T(8,128)}, f32[8,8,384]{2,1,0:T(8,128)}, f32[2304,384]{1,0:T(8,128)}, f32[2304,384]{1,0:T(8,128)}, f32[1,3456]{1,0:T(1,1...) custom-call(f32[8,256,384]{2,1,0:T(8,128)} %get-tuple-element.107.x2, ...), custom_call_target="tpu_custom_call" | custom-call | flops 25600000000 | bytes 24000000 | tf_op jit(solution)/shard_map/layer_second/pallas_call | solution.py:632
  187.8 43.4 %backward_first.1 = (f32[8,14,384]{2,1,0:T(8,128)}, f32[2304,384]{1,0:T(8,128)}, f32[2304,384]{1,0:T(8,128)}, f32[64,384]{1,0:T(8,128)}, f32[64,384]{1,0:T(8,128)}) custom-call(f32[8,256,384]{2,1,0:T(8,128)} %get-tuple-element.108.dx, f32[8,14,384]{2,1,0:T(8,128)} %broadcast_add_fusion.mods, bf16[384,4608]{1,0:T(8,128)(2,1)} %bitcast.103, ...), custom_call_target="tpu_custom_call" | custom-call | flops 17600000000 | bytes 64000000 | tf_op jit(solution)/shard_map/backward_first/pallas_call | solution.py:659
  231.5 4.2 %modulation_rows.1 = f32[16,16,384]{2,1,0:T(8,128)} custom-call(s32[1]{0:T(128)} %bitcast.2.refs_0_, f32[8,14,384]{2,1,0:T(8,128)} %get-tuple-element.124.refs_1_, bf16[384,5376]{1,0:T(8,128)(2,1)} %all-gather.5.cloned.1.call-done.refs_2_, f32[256,384]{1,0:T(8,128)} %get-tuple-element.212.refs_3_), custom_call_target="tpu_custom_call" | custom-call | tf_op jit(solution)/shard_map/modulation_rows/pallas_call | solution.py:790
  235.7 3.9 %all-to-all-start.2 = ((f32[16,16,384]{2,1,0:T(8,128)}), f32[16,16,384]{2,1,0:T(8,128)S(1)}, u32[]{:S(2)}, u32[]{:S(2)}) async-start(f32[16,16,384]{2,1,0:T(8,128)} %modulation_rows.1), calls=%async_computation.2 | async-start | bytes 786432 | tf_op jit(solution)/shard_map/all_to_all | solution.py:1143
  241.9 6.4 %left_second.1 = (f32[2304,384]{1,0:T(8,128)}, f32[8,384]{1,0:T(8,128)}, f32[8,1152]{1,0:T(8,128)}) custom-call(f32[2304,384]{1,0:T(8,128)} %get-tuple-element.128.refs_0_, f32[2304,384]{1,0:T(8,128)} %collective-permute-done.3.refs_1_, f32[2,8,1344]{2,1,0:T(8,128)} %bitcast.125, f32[2,8,384]{2,1,0:T(8,128)} %bitcast.136), custom_call_target="tpu_custom_call" | custom-call | flops 1000000000 | bytes 15000000 | tf_op jit(solution)/shard_map/left_second/pallas_call | solution.py:762
  249.0 6.8 %left_first.1 = (f32[2304,384]{1,0:T(8,128)}, f32[2,16,384]{2,1,0:T(8,128)}, f32[16,8,384]{2,1,0:T(8,128)}) custom-call(f32[2304,384]{1,0:T(8,128)} %get-tuple-element.126.own, f32[2304,384]{1,0:T(8,128)} %collective-permute-done.2.got, f32[2,8,1344]{2,1,0:T(8,128)} %bitcast.126, f32[2,8,384]{2,1,0:T(8,128)} %bitcast.137, ...), custom_call_target="tpu_custom_call" | custom-call | flops 1000000000 | bytes 15000000 | tf_op jit(solution)/shard_map/left_first/pallas_call | solution.py:828
  255.8 6.6 %all-to-all-start.3 = ((f32[16,8,384]{2,1,0:T(8,128)}), f32[16,8,384]{2,1,0:T(8,128)S(1)}, u32[]{:S(2)}, u32[]{:S(2)}) async-start(f32[16,8,384]{2,1,0:T(8,128)} %get-tuple-element.135), calls=%async_computation.3 | async-start | bytes 393216 | tf_op jit(solution)/shard_map/all_to_all | solution.py:1143
  265.0 3.7 %modulation_gradients.1 = (f32[384,168]{1,0:T(8,128)}, f32[384,168]{1,0:T(8,128)}, f32[648,384]{1,0:T(8,128)}, f32[384,1000]{1,0:T(8,128)}) custom-call(s32[2]{0:T(128)} %pad_add_fusion.refs_0_.core, f32[16,16,384]{2,1,0:T(8,128)} %copy-done.3, bf16[128,384]{1,0:T(8,128)(2,1)} %get-tuple-element.218.refs_2_, bf16[128,256]{1,0:T(8,128)(2,1)} %fusion.18.refs_3_, ...), custom_call_target="tpu_custom_call" | custom-call | tf_op jit(solution)/shard_map/modulation_gradients/pallas_call | solution.py:874
  268.8 1.6 all-to-all-done.3
  271.1 4.7 %all-to-all-start.5 = ((f32[16,8,384]{2,1,0:T(8,128)}), f32[16,8,384]{2,1,0:T(8,128)S(1)}, u32[]{:S(2)}, u32[]{:S(2)}) async-start(f32[16,8,384]{2,1,0:T(8,128)} %broadcast_in_dim.15), calls=%async_computation.5 | async-start | bytes 393216 | tf_op jit(solution)/shard_map/all_to_all | solution.py:1143
  275.8 0.9 collective-permute-start.5
  276.8 0.9 constant_dynamic-slice_fusion.table_own
  277.8 1.3 collective-permute-done.6.table_got
  279.7 0.7 copy-done.7
  280.4 2.2 modulation_sums.1
  282.9 6.3 %all-to-all-start.4 = ((f32[16,16,384]{2,1,0:T(8,128)}), f32[16,16,384]{2,1,0:T(8,128)S(1)}, u32[]{:S(2)}, u32[]{:S(2)}) async-start(f32[16,16,384]{2,1,0:T(8,128)} %get-tuple-element.144), calls=%async_computation.4 | async-start | bytes 786432 | tf_op jit(solution)/shard_map/all_to_all | solution.py:1143
  289.7 7.4 %right_factors.1 = (f32[16,8,384]{2,1,0:T(8,128)}, f32[2,8,384]{2,1,0:T(8,128)}, f32[2,8,1152]{2,1,0:T(8,128)}, f32[2,8,384]{2,1,0:T(8,128)}) custom-call(f32[8,16,384]{2,1,0:T(8,128)} %bitcast.114, f32[2304,384]{1,0:T(8,128)} %get-tuple-element.146.mat0, f32[2304,384]{1,0:T(8,128)} %get-tuple-element.147.mat1, f32[2,16,384]{2,1,0:T(8,128)} %get-tuple-element.148.mat_io, ...), custom_call_target="tpu_custom_call" | custom-call | tf_op jit(solution)/shard_map/right_factors/pallas_call | solution.py:973
  297.1 2.7 all-to-all-done.4.cond_own
  299.8 12.0 %all_to_all.48 = f32[16,8,384]{2,1,0:T(8,128)S(1)} all-to-all(f32[16,8,384]{2,1,0:T(8,128)} %get-tuple-element.151), channel_id=1, replica_groups=mesh['dp'=16,'tensor'=2] {'dp'}, dimensions={0} | all-to-all | bytes 393216 | tf_op jit(solution)/shard_map/all_to_all | solution.py:1143
  312.6 4.7 %all-to-all-start.7 = ((f32[16,8,384]{2,1,0:T(8,128)}), f32[16,8,384]{2,1,0:T(8,128)S(1)}, u32[]{:S(2)}, u32[]{:S(2)}) async-start(f32[16,8,384]{2,1,0:T(8,128)} %broadcast_in_dim.16), calls=%async_computation.7 | async-start | bytes 393216 | tf_op jit(solution)/shard_map/all_to_all | solution.py:1143
  317.3 1.7 collective-permute-start.9
  319.0 5.3 %all-to-all-done.7 = f32[16,8,384]{2,1,0:T(8,128)S(1)} async-done(((f32[16,8,384]{2,1,0:T(8,128)}), f32[16,8,384]{2,1,0:T(8,128)S(1)}, u32[]{:S(2)}, u32[]{:S(2)}) %all-to-all-start.7) | async-done | bytes 196640 | tf_op jit(solution)/shard_map/all_to_all | solution.py:1143
  325.0 3.2 gradient_norm.1
  328.2 2.7 collective-permute-start.8
  330.9 1.5 dynamic-slice_add_fusion.time_grad
  332.3 7.3 %next_errors.1 = (f32[2,1344,384]{2,1,0:T(8,128)}, f32[2,960,384]{2,1,0:T(8,128)}, f32[2,16,384]{2,1,0:T(8,128)}) custom-call(f32[2304,384]{1,0:T(8,128)} %get-tuple-element.146.mat0, f32[2304,384]{1,0:T(8,128)} %get-tuple-element.147.mat1, f32[2,16,384]{2,1,0:T(8,128)} %get-tuple-element.148.mat_io, f32[2,8,384]{2,1,0:T(8,128)} %get-tuple-element.152.left_col, ...), custom_call_target="tpu_custom_call" | custom-call | tf_op jit(solution)/shard_map/next_errors/pallas_call | solution.py:1061
  340.4 4.9 %weight_update.1 = (f32[1,128]{1,0:T(1,128)}, f32[2,24,1344]{2,1,0:T(8,128)}, f32[2,24,960]{2,1,0:T(8,128)}, f32[24,5376]{1,0:T(8,128)}, f32[40,384]{1,0:T(8,128...) custom-call(s32[2]{0:T(128)} %pad_add_fusion.refs_0_.core, ...), custom_call_target="tpu_custom_call" | custom-call | tf_op jit(solution)/shard_map/weight_update/pallas_call | solution.py:1129
  345.3 1.3 fusion.27
  (132 shorter events, 21.1 us)
Async XLA Ops:
  7.2 84.1 %all-gather.3.cloned.1.call-start = ((), (), s32[]{:S(2)}) async-start(), calls=%async_computation.8 | async-start | bytes 7299072 | tf_op jit(solution)/shard_map/all_gather | solution.py:1184
  17.1 27.6 %copy-start.18 = (f32[2,1344]{1,0:T(2,128)S(1)}, f32[2,1344]{1,0:T(2,128)}, u32[]{:S(2)}) copy-start(f32[2,1344]{1,0:T(2,128)} %b_col.1) | copy-start | bytes 32260
  17.2 27.6 %copy-start.10 = (f32[8080]{0:T(1024)S(1)}, f32[8080]{0:T(1024)}, u32[]{:S(2)}) copy-start(f32[8080]{0:T(1024)} %param.40) | copy-start | bytes 96964
  43.9 2.1 collective-permute-start
  44.7 53.1 %collective-permute-start.1 = (f32[2,1344]{1,0:T(2,128)S(1)}, f32[2,1344]{1,0:T(2,128)S(1)}, u32[]{:S(2)}, u32[]{:S(2)}) collective-permute-start(f32[2,1344]{1,0:T(2,128)S(1)} %copy-done.18), channel_id=1, source_target_pairs={{0,1},{1,0},{2,3},{3,2},{4,5},{5,4},{6,7},{7,6},{8,9},{9,8},{10,11... | collective-permute-start | bytes 32264 | tf_op jit(solution)/shard_map/ppermute | solution.py:1139
  46.7 2.9 copy-start.1
  46.9 7.9 %copy-start.20 = (f32[16]{0:T(128)S(1)}, f32[16]{0:T(128)}, u32[]{:S(2)}) copy-start(f32[16]{0:T(128)} %param.30) | copy-start | bytes 196
  46.9 8.0 %copy-start.13 = (f32[16,256,16]{1,2,0:T(8,128)S(1)}, f32[16,256,16]{1,2,0:T(8,128)}, u32[]{:S(2)}) copy-start(f32[16,256,16]{1,2,0:T(8,128)} %param.32) | copy-start | bytes 786436
  46.9 8.0 %copy-start.14 = (f32[16,256,16]{1,2,0:T(8,128)S(1)}, f32[16,256,16]{1,2,0:T(8,128)}, u32[]{:S(2)}) copy-start(f32[16,256,16]{1,2,0:T(8,128)} %param.29) | copy-start | bytes 786436
  46.9 8.0 %copy-start.15 = (f32[16,256,16]{1,2,0:T(8,128)S(1)}, f32[16,256,16]{1,2,0:T(8,128)}, u32[]{:S(2)}) copy-start(f32[16,256,16]{1,2,0:T(8,128)} %param.28) | copy-start | bytes 786436
  48.6 1.1 copy-start.16
  50.6 14.3 %all-to-all-start.1 = ((f32[32,8,168]{2,1,0:T(8,128)}), f32[32,8,168]{2,1,0:T(8,128)S(1)}, u32[]{:S(2)}, u32[]{:S(2)}) async-start(f32[32,8,168]{2,1,0:T(8,128)} %fusion.6), calls=%async_computation.1 | async-start | bytes 524288 | tf_op jit(solution)/shard_map/all_to_all | solution.py:1222
  54.5 177.0 %all-gather.5.cloned.1.call-start = ((), (), s32[]{:S(2)}) async-start(), calls=%async_computation.9 | async-start | bytes 4386816 | tf_op jit(solution)/shard_map/all_gather | solution.py:1249
  97.8 0.6 copy-start.19
  98.4 28.8 %copy-start = (f32[24,5376]{1,0:T(8,128)S(1)}, f32[24,5376]{1,0:T(8,128)}, u32[]{:S(2)}) copy-start(f32[24,5376]{1,0:T(8,128)} %w_cond.1) | copy-start | bytes 1548292
  187.4 54.5 %collective-permute-start.3 = (f32[2304,384]{1,0:T(8,128)}, f32[2304,384]{1,0:T(8,128)}, u32[]{:S(2)}, u32[]{:S(2)}) collective-permute-start(f32[2304,384]{1,0:T(8,128)} %get-tuple-element.129), channel_id=1, source_target_pairs={{0,1},{1,0},{2,3},{3,2},{4,5},{5,4},{6,7},{7,6},{8,9},{9,8},{10,11... | collective-permute-start | bytes 10616840 | tf_op jit(solution)/shard_map/ppermute | solution.py:1139
  231.2 8.5 %copy-start.23 = (f32[64,384]{1,0:T(8,128)S(1)}, f32[64,384]{1,0:T(8,128)}, u32[]{:S(2)}) copy-start(f32[64,384]{1,0:T(8,128)} %get-tuple-element.133) | copy-start | bytes 294916
  231.2 9.7 %copy-start.21 = (s32[256]{0:T(256)S(1)}, s32[256]{0:T(256)}, u32[]{:S(2)}) copy-start(s32[256]{0:T(256)} %param.31) | copy-start | bytes 3076
  231.2 17.1 %collective-permute-start.2 = (f32[2304,384]{1,0:T(8,128)}, f32[2304,384]{1,0:T(8,128)}, u32[]{:S(2)}, u32[]{:S(2)}) collective-permute-start(f32[2304,384]{1,0:T(8,128)} %get-tuple-element.127), channel_id=1, source_target_pairs={{0,1},{1,0},{2,3},{3,2},{4,5},{5,4},{6,7},{7,6},{8,9},{9,8},{10,11... | collective-permute-start | bytes 10616840 | tf_op jit(solution)/shard_map/ppermute | solution.py:1139
  235.7 20.0 %all-to-all-start.2 = ((f32[16,16,384]{2,1,0:T(8,128)}), f32[16,16,384]{2,1,0:T(8,128)S(1)}, u32[]{:S(2)}, u32[]{:S(2)}) async-start(f32[16,16,384]{2,1,0:T(8,128)} %modulation_rows.1), calls=%async_computation.2 | async-start | bytes 786432 | tf_op jit(solution)/shard_map/all_to_all | solution.py:1143
  239.7 8.7 %collective-permute-start.4 = (f32[64,384]{1,0:T(8,128)S(1)}, f32[64,384]{1,0:T(8,128)S(1)}, u32[]{:S(2)}, u32[]{:S(2)}) collective-permute-start(f32[64,384]{1,0:T(8,128)S(1)} %copy-done.23), channel_id=1, source_target_pairs={{0,1},{1,0},{2,3},{3,2},{4,5},{5,4},{6,7},{7,6},{8,9},{9,8},{10,11... | collective-permute-start | bytes 294920 | tf_op jit(solution)/shard_map/ppermute | solution.py:1139
  248.3 0.6 copy-start.11
  249.0 15.4 %copy-start.17 = (bf16[256,384]{1,0:T(8,128)(2,1)S(1)}, bf16[256,384]{1,0:T(8,128)(2,1)}, u32[]{:S(2)}) copy-start(bf16[256,384]{1,0:T(8,128)(2,1)} %copy-done.16) | copy-start | bytes 589828
  255.8 9.2 %copy-start.3 = (f32[16,16,384]{2,1,0:T(8,128)}, f32[16,16,384]{2,1,0:T(8,128)S(1)}, u32[]{:S(2)}) copy-start(f32[16,16,384]{2,1,0:T(8,128)S(1)} %all-to-all-done.2.refs_1_) | copy-start | bytes 1179652
  255.8 14.6 %all-to-all-start.3 = ((f32[16,8,384]{2,1,0:T(8,128)}), f32[16,8,384]{2,1,0:T(8,128)S(1)}, u32[]{:S(2)}, u32[]{:S(2)}) async-start(f32[16,8,384]{2,1,0:T(8,128)} %get-tuple-element.135), calls=%async_computation.3 | async-start | bytes 393216 | tf_op jit(solution)/shard_map/all_to_all | solution.py:1143
  271.1 11.8 %all-to-all-start.5 = ((f32[16,8,384]{2,1,0:T(8,128)}), f32[16,8,384]{2,1,0:T(8,128)S(1)}, u32[]{:S(2)}, u32[]{:S(2)}) async-start(f32[16,8,384]{2,1,0:T(8,128)} %broadcast_in_dim.15), calls=%async_computation.5 | async-start | bytes 393216 | tf_op jit(solution)/shard_map/all_to_all | solution.py:1143
  275.8 3.2 collective-permute-start.5
  277.7 1.4 copy-start.9
  277.7 1.4 collective-permute-start.6
  279.0 0.6 copy-start.12
  279.7 0.7 copy-start.7
  282.9 6.8 %copy-start.2 = (f32[16,8,384]{2,1,0:T(8,128)}, f32[16,8,384]{2,1,0:T(8,128)S(1)}, u32[]{:S(2)}) copy-start(f32[16,8,384]{2,1,0:T(8,128)S(1)} %all-to-all-done.5) | copy-start | bytes 589828
  282.9 16.9 %all-to-all-start.4 = ((f32[16,16,384]{2,1,0:T(8,128)}), f32[16,16,384]{2,1,0:T(8,128)S(1)}, u32[]{:S(2)}, u32[]{:S(2)}) async-start(f32[16,16,384]{2,1,0:T(8,128)} %get-tuple-element.144), calls=%async_computation.4 | async-start | bytes 786432 | tf_op jit(solution)/shard_map/all_to_all | solution.py:1143
  289.2 29.8 %collective-permute-start.7 = (f32[648,384]{1,0:T(8,128)}, f32[648,384]{1,0:T(8,128)S(1)}, u32[]{:S(2)}, u32[]{:S(2)}) collective-permute-start(f32[648,384]{1,0:T(8,128)} %get-tuple-element.155.time_own), channel_id=1, source_target_pairs={{0,1},{1,0},{2,3},{3,2},{4,5},{5,4},{6,7},{7,6},{8,9},{9,8},{10,11... | collective-permute-start | bytes 2985992 | tf_op jit(solution)/shard_map/ppermute | solution.py:1139
  299.8 39.9 %copy-start.4 = (f32[16,16,384]{2,1,0:T(8,128)}, f32[16,16,384]{2,1,0:T(8,128)S(1)}, u32[]{:S(2)}) copy-start(f32[16,16,384]{2,1,0:T(8,128)S(1)} %all-to-all-done.4.cond_own) | copy-start | bytes 1179652
  312.6 11.7 %all-to-all-start.7 = ((f32[16,8,384]{2,1,0:T(8,128)}), f32[16,8,384]{2,1,0:T(8,128)S(1)}, u32[]{:S(2)}, u32[]{:S(2)}) async-start(f32[16,8,384]{2,1,0:T(8,128)} %broadcast_in_dim.16), calls=%async_computation.7 | async-start | bytes 393216 | tf_op jit(solution)/shard_map/all_to_all | solution.py:1143
  317.3 22.4 %collective-permute-start.9 = (f32[16,16,384]{2,1,0:T(8,128)S(1)}, f32[16,16,384]{2,1,0:T(8,128)S(1)}, u32[]{:S(2)}, u32[]{:S(2)}) collective-permute-start(f32[16,16,384]{2,1,0:T(8,128)S(1)} %all-to-all-done.4.cond_own), channel_id=1, source_target_pairs={{0,1},{1,0},{2,3},{3,2},{4,5},{5,4},{6,7},{7,6},{8,9},{9,8},{10,11... | collective-permute-start | bytes 1179656 | tf_op jit(solution)/shard_map/ppermute | solution.py:1139
  319.0 5.3 %copy-start.5 = (f32[648,384]{1,0:T(8,128)}, f32[648,384]{1,0:T(8,128)S(1)}, u32[]{:S(2)}) copy-start(f32[648,384]{1,0:T(8,128)S(1)} %collective-permute-done.7.time_got) | copy-start | bytes 2985988
  324.3 0.7 copy-start.6
  328.2 11.5 %collective-permute-start.8 = (f32[1,128]{1,0:T(1,128)}, f32[1,128]{1,0:T(1,128)S(1)}, u32[]{:S(2)}, u32[]{:S(2)}) collective-permute-start(f32[1,128]{1,0:T(1,128)} %get-tuple-element.156.parts), channel_id=1, source_target_pairs={{0,1},{1,0},{2,3},{3,2},{4,5},{5,4},{6,7},{7,6},{8,9},{9,8},{10,11... | collective-permute-start | bytes 1544 | tf_op jit(solution)/shard_map/ppermute | solution.py:1139
  339.7 0.8 copy-start.8
  339.7 0.7 copy-start.22
Sparse Core Ops, SparseCore 0:
  11.5 79.7 all-gather.2
  128.1 72.2 all-gather.4

commit v5 on v4

--- a/solution.py
+++ b/solution.py
@@ -344,11 +344,18 @@
 SMALL_ROWS = PAY_BCOL + 8 - PAY_PROJ
 
 
-def forward_kernel(xt, mods, wpatch, pos, own, other, bcol_own, bcol_other, b_rep,
+def forward_kernel(core, full, xt, mods, wpatch, pos, own, other, bcol_own, bcol_other, b_rep,
                    query, keyed, valued, probs, branch_a, middle, slope, branch_m, mixed, acted,
-                   x2, wqkv, wo, bqkv, bfc1):
+                   x2, next_own, next_other, wqkv, wo, bqkv, bfc1, hold_own, hold_other, sems):
+    picks = [pltpu.make_async_copy(full.at[:, side, :, pl.ds(GATH, GATH)], hold, sems.at[i])
+             for i, (side, hold) in enumerate(((core[0], hold_own), (1 - core[0], hold_other)))]
+    leaves = [pltpu.make_async_copy(hold, out, sems.at[2 + i])
+              for i, (hold, out) in enumerate(((hold_own, next_own), (hold_other, next_other)))]
+
     @pl.when(pl.program_id(0) == 0)
     def _():
+        for copy in picks:
+            copy.start()
         assemble(0, own, other, bcol_own, bcol_other, wqkv, wo, bqkv, bfc1)
 
     named = dict(query=query, keyed=keyed, valued=valued, mixed=mixed, branch_a=branch_a,
@@ -374,6 +381,17 @@
         x2[i] = result[0]
 
     run_steps([chain(i) for i in range(xt.shape[0])], LAG)
+
+    @pl.when(pl.program_id(0) == 0)
+    def _():
+        for copy, leave in zip(picks, leaves):
+            copy.wait()
+            leave.start()
+
+    @pl.when(pl.program_id(0) == pl.num_programs(0) - 1)
+    def _():
+        for leave in leaves:
+            leave.wait()
 
 
 def diagonal(count):
@@ -586,9 +604,8 @@
                   pltpu.VMEM((1, 3 * D), f32), pltpu.VMEM((1, MLP), f32)]
 
 
-def weight_specs(layer):
-    half = pl.BlockSpec((D, GATH), lambda n: (0, layer), pipeline_mode=pl.Buffered(1))
-    return [half, half, fixed(L, COL_S), fixed(L, COL_S), fixed(1, NBR)]
+def weight_specs():
+    return [fixed(D, GATH), fixed(D, GATH), fixed(L, COL_S), fixed(L, COL_S), fixed(1, NBR)]
 
 
 def stash_scratch(count):
@@ -606,21 +623,24 @@
                            transcendentals=int(2e6 * count))
 
 
-def run_forward(xt, mods, full_io, pos, weights):
+def run_forward(core, full, xt, mods, full_io, pos, weights):
     count = xt.shape[0]
     outs = SAVED + [("x2", (TOK, D), f32)]
     return pl.pallas_call(
         forward_kernel,
         grid=(count // GROUP,),
-        in_specs=[per_latent(PV, TOK, group=GROUP), per_latent(14, D, group=GROUP),
-                  pl.BlockSpec((1, PV, D), lambda n: (0, 0, 0)), fixed(TOK, D)] + weight_specs(0),
-        out_specs=[per_latent(*shape, group=GROUP) for _, shape, _ in outs],
-        out_shape=[jax.ShapeDtypeStruct((count,) + shape, kind) for _, shape, kind in outs],
-        scratch_shapes=WEIGHT_SCRATCH,
+        in_specs=[pl.BlockSpec(memory_space=pltpu.SMEM), pl.BlockSpec(memory_space=pl.ANY), per_latent(PV, TOK, group=GROUP), per_latent(14, D, group=GROUP),
+                  pl.BlockSpec((1, PV, D), lambda n: (0, 0, 0)), fixed(TOK, D)] + weight_specs(),
+        out_specs=[per_latent(*shape, group=GROUP) for _, shape, _ in outs]
+        + [pl.BlockSpec(memory_space=pl.ANY)] * 2,
+        out_shape=[jax.ShapeDtypeStruct((count,) + shape, kind) for _, shape, kind in outs]
+        + [jax.ShapeDtypeStruct((full.shape[0], full.shape[2], GATH), bf16)] * 2,
+        scratch_shapes=WEIGHT_SCRATCH + [pltpu.VMEM((full.shape[0], full.shape[2], GATH), bf16)] * 2
+        + [pltpu.SemaphoreType.DMA((4,))],
         compiler_params=params(),
         cost_estimate=cost(1.0e9, 6e6, count),
         name="forward_first",
-    )(xt, mods, full_io, pos, *weights)
+    )(core, full, xt, mods, full_io, pos, *weights)
 
 
 def run_middle(x2, mods, weights, full_io, targets, err_col, err_row):
@@ -632,7 +652,7 @@
     return pl.pallas_call(
         middle_kernel,
         grid=(count // GROUP,),
-        in_specs=[per_latent(TOK, D, group=GROUP), per_latent(14, D, group=GROUP)] + weight_specs(1)
+        in_specs=[per_latent(TOK, D, group=GROUP), per_latent(14, D, group=GROUP)] + weight_specs()
         + [pl.BlockSpec((1, PV, D), lambda n: (1, 0, 0)), per_latent(PV, TOK, group=GROUP)]
         + [pl.BlockSpec(memory_space=pl.ANY)] * 2,
         out_specs=[spec for _, spec in outs],
@@ -659,7 +679,7 @@
     return pl.pallas_call(
         last_kernel,
         grid=(count,),
-        in_specs=[per_latent(TOK, D), per_latent(14, D)] + weight_specs(0)
+        in_specs=[per_latent(TOK, D), per_latent(14, D)] + weight_specs()
         + [per_latent(PV, TOK), pl.BlockSpec((1, PV, D), lambda n: (0, 0, 0)), fixed(TOK, D)]
         + [fixed(*shape) for shape in ((1, BIAS_WIDTH), (PV, D), (PV, 1), (1, TOK))] + [per_latent(8, D)]
         + [pl.BlockSpec(memory_space=pl.ANY)] * 2
@@ -1082,11 +1102,12 @@
                   cond_own, cond_got, time_grad, table_grad, bcol_grad, brep_grad,
                   w_col, w_row, w_cond, w_time, w_io, w_table, b_col, b_rep,
                   m_col, m_row, m_cond, m_time, m_io, m_table, m_bcol, m_brep,
-                  scalars, n_col, n_row, n_cond, n_time, n_io, n_table, n_bcol, n_brep,
+                  loss, clip, n_col, n_row, n_cond, n_time, n_io, n_table, n_bcol, n_brep,
                   v_col, v_row, v_cond, v_time, v_io, v_table, v_bcol, v_brep):
     clip_norm = jnp.sqrt(parts[:, 0:1] + parts_got[:, 0:1] + parts[:, 1:2])
     scaling = jnp.minimum(1.0, clip_limit / clip_norm)
-    scalars[...] = jnp.concatenate([parts[:, 2:3], clip_norm, jnp.zeros((1, 126), f32)], 1)
+    loss[...] = parts[:, 2:3]
+    clip[...] = clip_norm
 
     def advance(weight, momentum, gradient):
         moved = momentum_decay * momentum + scaling * gradient
@@ -1125,7 +1146,7 @@
 
 def run_update(core, grads, weights, momenta):
     vmem = pl.BlockSpec(memory_space=pltpu.VMEM)
-    shapes = [(1, 128)] + [v.shape for v in weights] * 2
+    shapes = [(1, 1), (1, 1)] + [v.shape for v in weights] * 2
     return pl.pallas_call(
         update_kernel,
         in_specs=[pl.BlockSpec(memory_space=pltpu.SMEM)] + [vmem] * (len(grads) + 2 * len(weights)),
@@ -1222,15 +1243,17 @@
     mods = lax.all_to_all(mods, ("dp", "tensor"), 0, 0, tiled=True)
     mods = mods.transpose(1, 0, 2).reshape(count, N_MODS)
     mods = (mods + b_rep[START_COND:START_FIRST]).reshape(count, 14, D)
-    full, mods = lax.optimization_barrier((full, mods))
-    full = full.reshape(n_dp, 2, rows, L * GATH)
-
     def half_of(values):
         split = values.reshape((n_dp, 2, count) + values.shape[1:])
         return lax.dynamic_slice_in_dim(split, index_t, 1, 1).reshape((n_dp * count,) + values.shape[1:])
 
     halves_of = [half_of(v) for v in (cond_act, features, first, first_act)]
     labels_half = half_of(labels)[:, None]
+    place = (index_dp * 2 + index_t).astype(jnp.int32).reshape(1)
+    full, mods, halves_of, labels_half, core, place = lax.optimization_barrier(
+        (full, mods, halves_of, labels_half, core, place)
+    )
+    full = full.reshape(n_dp, 2, rows, L * GATH)
 
     def mine_of(values):
         return lax.dynamic_slice_in_dim(values, index_t * count, count, 0)
@@ -1240,16 +1263,19 @@
         (1.0 - steps_own) * flip(mine_of(latents)) + steps_own * flip(mine_of(gauss_noise))
     ).astype(bf16)
     b_line = b_rep[None]
-    own = lax.dynamic_slice_in_dim(full, index_t, 1, 1).reshape(D, L * GATH)
-    other = lax.dynamic_slice_in_dim(full, 1 - index_t, 1, 1).reshape(D, L * GATH)
-    weights = (own, other, b_col, swap(b_col), b_line)
+    first_layer = full[:, :, :, :GATH]
+    own = lax.dynamic_slice_in_dim(first_layer, index_t, 1, 1).reshape(D, GATH)
+    other = lax.dynamic_slice_in_dim(first_layer, 1 - index_t, 1, 1).reshape(D, GATH)
+    biases = (b_col, swap(b_col), b_line)
+    weights = (own, other, *biases)
     pos = jnp.asarray(position_table())
-    *saved, x2 = run_forward(xt, mods, full_io, pos, weights)
+    *saved, x2, own1, other1 = run_forward(core, full, xt, mods, full_io, pos, weights)
+    weights1 = (own1.reshape(D, GATH), other1.reshape(D, GATH), *biases)
     x2, late_cond = lax.optimization_barrier((x2, w_cond))
     full_cond = lax.all_gather(late_cond.astype(bf16), "dp", axis=0, tiled=True)
     err_col_t, err_io_t = flip(err_col), flip(err_io)
     dx, dmods1, own1, oth1, *smalls = run_middle(
-        x2, mods, weights, full_io, flip(mine_of(targets)), err_col_t, err_row
+        x2, mods, weights1, full_io, flip(mine_of(targets)), err_col_t, err_row
     )
     got1 = swap(oth1)
     dmods, own0, oth0, pay_own, pay_oth = run_last(
@@ -1257,7 +1283,6 @@
     )
     got0, pay_got = swap(oth0), swap(pay_oth)
 
-    place = (index_dp * 2 + index_t).astype(jnp.int32).reshape(1)
     rows_got = trade(run_exchange(n_dp, place, dmods, full_cond, cond))
     fac_col_t, fac_row_t, fac_io_t = flip(fac_col), flip(fac_row), flip(fac_io)
     mat1, left_col1, left_row1 = run_project_second(own1, got1, fac_col_t, fac_row_t)
@@ -1280,7 +1305,12 @@
     cond_rows = trade(cond_sent)
 
     sent, left_col, left_row, left_io = run_right(n_dp, left_packed, mats, mat_io, sums)
-    cond_rows, sent = lax.optimization_barrier((cond_rows, sent))
+    time_at = index_dp * time_rows
+    time_grad = (
+        lax.dynamic_slice_in_dim(time_own, time_at, time_rows, 0)
+        + lax.dynamic_slice_in_dim(time_got, time_at, time_rows, 0)
+    )
+    cond_rows, sent, time_grad = lax.optimization_barrier((cond_rows, sent, time_grad))
     packed = spread(jnp.sum(trade(sent), 0)).reshape(PACK, D)
     cond_rows_got = swap(cond_rows)
     lefts = (left_col, left_row, left_io)
@@ -1290,14 +1320,9 @@
     parts_got = swap(parts)
     next_err_col, next_err_row, next_err_io = run_error(mats, mat_io, lefts, (right_col, right_row, right_io))
 
-    time_at = index_dp * time_rows
-    time_grad = (
-        lax.dynamic_slice_in_dim(time_own, time_at, time_rows, 0)
-        + lax.dynamic_slice_in_dim(time_got, time_at, time_rows, 0)
-    )
     olds = (w_col, flip(w_row), w_cond, w_time, flip(w_io), class_table.T, b_col, b_line)
     momenta = (mom_col, flip(mom_row), mom_cond, mom_time, flip(mom_io), mom_table.T, mom_bcol, mom_brep[None])
-    scalars, *new = run_update(
+    loss, clip_norm, *new = run_update(
         core,
         (parts, parts_got, left_col, right_col, right_row, left_row, right_io, left_io,
          cond_rows, cond_rows_got, time_grad, table_share, bcol_grad, brep_grad),
@@ -1308,7 +1333,7 @@
         return (col, flip(row), cond, time, flip(io), table.T, bcol, brep[0])
 
     return (
-        scalars[0, 0], scalars[0, 1], *outward(*new[:8]), *outward(*new[8:]),
+        loss.reshape(()), clip_norm.reshape(()), *outward(*new[:8]), *outward(*new[8:]),
         flip(next_err_col), next_err_row, flip(next_err_io), flip(right_col), flip(right_row), flip(right_io),
     )
 

time: 360 us -> 352 us (0.978)
  blocking collectives: 35.9 us -> 11.6 us
  waiting for transfers between devices: 45.2 us -> 58.1 us
  starting transfers between devices: 38.4 us -> 45 us
  local copies, waits for them, and re-layouts: 24.9 us -> 20.3 us
    all_to_all x2 -> x1, blocking collectives: 35.9 us -> 11.6 us  [trade(): return lax.all_to_all(chunks, 'dp', 0, 0, tiled=True)]
    all_to_all x5 -> x6, waiting for transfers between devices: 9.98 us -> 26.8 us  [trade(): return lax.all_to_all(chunks, 'dp', 0, 0, tiled=True)]
    dynamic_slice x1, local copies, waits for them, and re-layouts: 6.58 us -> 2.06 us  [on_device(): lax.dynamic_slice_in_dim(first_layer, 1 - index_t, 1, 1).reshape(D, GATH)]
    all_to_all x5 -> x6, starting transfers between devices: 26.3 us -> 30.7 us  [trade(): return lax.all_to_all(chunks, 'dp', 0, 0, tiled=True)]
  transfers between devices with their start and end apart: 18 -> 19, of which waited for: 8 -> 8; matrix products, arithmetic and copies ran while one was open for 9% -> 8% of each run, Pallas kernels for 41% -> 42%
where the time goes in v5:
time: 352 us; the launch traced here: 345 us
  Pallas kernels  179 us (51%)
  waiting for transfers between devices  58.1 us (17%)
  starting transfers between devices  45 us (13%)
  local copies, waits for them, and re-layouts  20.3 us (6%)
  between operations  15 us (4%)
  other arithmetic  12.5 us (4%)
  blocking collectives  11.6 us (3%)
    pallas_call x1, Pallas kernels, run_middle(): pl.pallas_call(middle_kernel, grid=(count // GROUP,), in_specs=[per_laten...  59.4 us
    pallas_call x1, Pallas kernels, run_last(): pl.pallas_call(last_kernel, grid=(count,), in_specs=[per_latent(TOK, D),...  43.4 us
    all_to_all x6, starting transfers between devices, trade(): return lax.all_to_all(chunks, 'dp', 0, 0, tiled=True)  30.7 us
    pallas_call x1, Pallas kernels, run_forward(): pl.pallas_call(forward_kernel, grid=(count // GROUP,), in_specs=[pl.Block...  30.1 us
    all_to_all x6, waiting for transfers between devices, trade(): return lax.all_to_all(chunks, 'dp', 0, 0, tiled=True)  26.8 us
    all_gather x1, waiting for transfers between devices, on_device(): full = lax.all_gather(shard, ('dp', 'tensor'))  24 us
    all_to_all x1, blocking collectives, trade(): return lax.all_to_all(chunks, 'dp', 0, 0, tiled=True)  11.6 us
    ppermute x10, starting transfers between devices, swap(): return lax.ppermute(values, 'tensor', [(0, 1), (1, 0)])  10.4 us
  transfers between devices with their start and end apart: 19, of which 8 were waited for; matrix products, arithmetic and copies ran while one was open for 8% of the time, Pallas kernels for 42%

profile of v5, /device:TPU:1, one launch (start us, length us, event | category | flops | bytes accessed | tf_op | source)
XLA Modules:
  0.0 345.1 jit_solution(13542226060895265161)
XLA Ops:
  7.2 1.0 convert.35
  8.2 0.9 bitcast_convert_fusion.1
  10.8 0.8 convert_element_type.72
  11.6 1.2 fusion.1
  13.8 1.1 convert_element_type.77
  14.9 1.1 reshape.292
  17.7 0.9 reduce.6
  18.6 1.3 reshape.332
  19.9 7.4 %all-to-all-start = ((bf16[16,2,7648]{2,1,0:T(2,128)(2,1)}), bf16[16,2,7648]{2,1,0:T(2,128)(2,1)S(1)}, u32[]{:S(2)}, u32[]{:S(2)}) async-start(bf16[16,2,7648]{2,1,0:T(2,128)(2,1)} %reshape.332), calls=%async_computation | async-start | bytes 983040 | tf_op jit(solution)/shard_map/all_to_all | solution.py:1164
  27.3 1.0 collective-permute-start.1
  28.4 14.1 %all-to-all-done = bf16[16,2,7648]{2,1,0:T(2,128)(2,1)S(1)} async-done(((bf16[16,2,7648]{2,1,0:T(2,128)(2,1)}), bf16[16,2,7648]{2,1,0:T(2,128)(2,1)S(1)}, u32[]{:S(2)}, u32[]{:S(2)}) %all-to-all-start) | async-done | bytes 489504 | tf_op jit(solution)/shard_map/all_to_all | solution.py:1164
  43.4 1.7 collective-permute-start
  49.1 1.1 multiply_convert_fusion
  50.2 0.9 fusion.6
  51.1 3.6 %all-to-all-start.1 = ((f32[32,8,168]{2,1,0:T(8,128)}), f32[32,8,168]{2,1,0:T(8,128)S(1)}, u32[]{:S(2)}, u32[]{:S(2)}) async-start(f32[32,8,168]{2,1,0:T(8,128)} %fusion.6), calls=%async_computation.1 | async-start | bytes 524288 | tf_op jit(solution)/shard_map/all_to_all | solution.py:1243
  55.3 0.8 reshape.309.wpatch.whead
  58.7 6.3 %all-to-all-done.1 = f32[32,8,168]{2,1,0:T(8,128)S(1)} async-done(((f32[32,8,168]{2,1,0:T(8,128)}), f32[32,8,168]{2,1,0:T(8,128)S(1)}, u32[]{:S(2)}, u32[]{:S(2)}) %all-to-all-start.1) | async-done | bytes 172064 | tf_op jit(solution)/shard_map/all_to_all | solution.py:1243
  66.1 24.0 %all-gather.3.cloned.1.call-done = bf16[32,24,4608]{2,1,0:T(8,128)(2,1)} async-done(((bf16[1,24,4608]{2,1,0:T(8,128)(2,1)}), bf16[32,24,4608]{2,1,0:T(8,128)(2,1)}) %all-gather.3.cloned.1.call-update) | async-done | bytes 7077904 | tf_op jit(solution)/shard_map/all_gather | solution.py:1205
  90.1 2.2 slice.120
  92.3 2.1 constant_dynamic-slice_fusion.1
  95.0 30.1 %forward_first.1 = (bf16[8,256,384]{2,1,0:T(8,128)(2,1)}, bf16[8,256,384]{2,1,0:T(8,128)(2,1)}, bf16[8,256,384]{2,1,0:T(8,128)(2,1)}, f32[8,6,256,256]{3,2,1,0:T...) custom-call(s32[2]{0:T(128)} %pad_add_fusion.core.refs_0_, ...), custom_call_target="tpu_custom_call" | custom-call | flops 8000000000 | bytes 48000000 | tf_op jit(solution)/shard_map/forward_first/pallas_call | solution.py:629
  125.8 59.4 %layer_second.1 = (f32[8,256,384]{2,1,0:T(8,128)}, f32[8,8,384]{2,1,0:T(8,128)}, f32[2304,384]{1,0:T(8,128)}, f32[2304,384]{1,0:T(8,128)}, f32[1,3456]{1,0:T(1,1...) custom-call(f32[8,256,384]{2,1,0:T(8,128)} %get-tuple-element.120.x2, ...), custom_call_target="tpu_custom_call" | custom-call | flops 25600000000 | bytes 24000000 | tf_op jit(solution)/shard_map/layer_second/pallas_call | solution.py:652
  185.6 43.4 %backward_first.1 = (f32[8,14,384]{2,1,0:T(8,128)}, f32[2304,384]{1,0:T(8,128)}, f32[2304,384]{1,0:T(8,128)}, f32[64,384]{1,0:T(8,128)}, f32[64,384]{1,0:T(8,128)}) custom-call(f32[8,256,384]{2,1,0:T(8,128)} %get-tuple-element.123.dx, f32[8,14,384]{2,1,0:T(8,128)} %broadcast_add_fusion.mods, bf16[384,2304]{1,0:T(8,128)(2,1)} %bitcast.107, ...), custom_call_target="tpu_custom_call" | custom-call | flops 17600000000 | bytes 64000000 | tf_op jit(solution)/shard_map/backward_first/pallas_call | solution.py:679
  229.3 4.2 %modulation_rows.1 = f32[16,16,384]{2,1,0:T(8,128)} custom-call(s32[1]{0:T(128)} %bitcast.21.refs_0_, f32[8,14,384]{2,1,0:T(8,128)} %get-tuple-element.139.refs_1_, bf16[384,5376]{1,0:T(8,128)(2,1)} %all-gather.5.cloned.1.call-done.refs_2_, f32[256,384]{1,0:T(8,128)} %get-tuple-element.232.refs_3_), custom_call_target="tpu_custom_call" | custom-call | tf_op jit(solution)/shard_map/modulation_rows/pallas_call | solution.py:810
  233.5 3.9 %all-to-all-start.2 = ((f32[16,16,384]{2,1,0:T(8,128)}), f32[16,16,384]{2,1,0:T(8,128)S(1)}, u32[]{:S(2)}, u32[]{:S(2)}) async-start(f32[16,16,384]{2,1,0:T(8,128)} %modulation_rows.1), calls=%async_computation.2 | async-start | bytes 786432 | tf_op jit(solution)/shard_map/all_to_all | solution.py:1164
  238.0 6.4 %left_second.1 = (f32[2304,384]{1,0:T(8,128)}, f32[8,384]{1,0:T(8,128)}, f32[8,1152]{1,0:T(8,128)}) custom-call(f32[2304,384]{1,0:T(8,128)} %get-tuple-element.143.refs_0_, f32[2304,384]{1,0:T(8,128)} %collective-permute-done.3.refs_1_, f32[2,8,1344]{2,1,0:T(8,128)} %bitcast.118, f32[2,8,384]{2,1,0:T(8,128)} %bitcast.129), custom_call_target="tpu_custom_call" | custom-call | flops 1000000000 | bytes 15000000 | tf_op jit(solution)/shard_map/left_second/pallas_call | solution.py:782
  245.0 6.8 %left_first.1 = (f32[2304,384]{1,0:T(8,128)}, f32[2,16,384]{2,1,0:T(8,128)}, f32[16,8,384]{2,1,0:T(8,128)}) custom-call(f32[2304,384]{1,0:T(8,128)} %get-tuple-element.141.own, f32[2304,384]{1,0:T(8,128)} %collective-permute-done.2.got, f32[2,8,1344]{2,1,0:T(8,128)} %bitcast.119, f32[2,8,384]{2,1,0:T(8,128)} %bitcast.130, ...), custom_call_target="tpu_custom_call" | custom-call | flops 1000000000 | bytes 15000000 | tf_op jit(solution)/shard_map/left_first/pallas_call | solution.py:848
  251.8 6.6 %all-to-all-start.3 = ((f32[16,8,384]{2,1,0:T(8,128)}), f32[16,8,384]{2,1,0:T(8,128)S(1)}, u32[]{:S(2)}, u32[]{:S(2)}) async-start(f32[16,8,384]{2,1,0:T(8,128)} %get-tuple-element.150), calls=%async_computation.3 | async-start | bytes 393216 | tf_op jit(solution)/shard_map/all_to_all | solution.py:1164
  259.2 3.7 %modulation_gradients.1 = (f32[384,168]{1,0:T(8,128)}, f32[384,168]{1,0:T(8,128)}, f32[648,384]{1,0:T(8,128)}, f32[384,1000]{1,0:T(8,128)}) custom-call(s32[2]{0:T(128)} %pad_add_fusion.core.refs_0_, f32[16,16,384]{2,1,0:T(8,128)} %copy-done.3, bf16[128,384]{1,0:T(8,128)(2,1)} %get-tuple-element.152.refs_2_, bf16[128,256]{1,0:T(8,128)(2,1)} %fusion.18.refs_3_, ...), custom_call_target="tpu_custom_call" | custom-call | tf_op jit(solution)/shard_map/modulation_gradients/pallas_call | solution.py:894
  263.0 3.4 all-to-all-done.3
  266.4 1.7 collective-permute-start.7
  268.9 3.5 %all-to-all-start.5 = ((f32[16,8,384]{2,1,0:T(8,128)}), f32[16,8,384]{2,1,0:T(8,128)S(1)}, u32[]{:S(2)}, u32[]{:S(2)}) async-start(f32[16,8,384]{2,1,0:T(8,128)} %broadcast_in_dim.15), calls=%async_computation.5 | async-start | bytes 393216 | tf_op jit(solution)/shard_map/all_to_all | solution.py:1164
  272.5 0.9 constant_dynamic-slice_fusion.table_own
  273.9 0.9 collective-permute-done.6.table_got
  276.3 2.2 modulation_sums.1
  278.4 2.2 all-to-all-done.5
  280.6 4.2 %all-to-all-start.4 = ((f32[16,16,384]{2,1,0:T(8,128)}), f32[16,16,384]{2,1,0:T(8,128)S(1)}, u32[]{:S(2)}, u32[]{:S(2)}) async-start(f32[16,16,384]{2,1,0:T(8,128)} %get-tuple-element.164), calls=%async_computation.4 | async-start | bytes 786432 | tf_op jit(solution)/shard_map/all_to_all | solution.py:1164
  284.8 7.4 %right_factors.1 = (f32[16,8,384]{2,1,0:T(8,128)}, f32[2,8,384]{2,1,0:T(8,128)}, f32[2,8,1152]{2,1,0:T(8,128)}, f32[2,8,384]{2,1,0:T(8,128)}) custom-call(f32[8,16,384]{2,1,0:T(8,128)} %bitcast.108, f32[2304,384]{1,0:T(8,128)} %get-tuple-element.166.mat0, f32[2304,384]{1,0:T(8,128)} %get-tuple-element.167.mat1, f32[2,16,384]{2,1,0:T(8,128)} %get-tuple-element.168.mat_io, ...), custom_call_target="tpu_custom_call" | custom-call | tf_op jit(solution)/shard_map/right_factors/pallas_call | solution.py:993
  292.3 1.5 dynamic-slice_add_fusion.time_grad
  293.8 1.6 all-to-all-done.4.cond_own
  295.4 5.1 %all-to-all-start.6 = ((f32[16,8,384]{2,1,0:T(8,128)}), f32[16,8,384]{2,1,0:T(8,128)S(1)}, u32[]{:S(2)}, u32[]{:S(2)}) async-start(f32[16,8,384]{2,1,0:T(8,128)} %get-tuple-element.172), calls=%async_computation.6 | async-start | bytes 393216 | tf_op jit(solution)/shard_map/all_to_all | solution.py:1164
  300.5 1.6 collective-permute-start.9
  302.1 5.4 %all-to-all-done.6 = f32[16,8,384]{2,1,0:T(8,128)S(1)} async-done(((f32[16,8,384]{2,1,0:T(8,128)}), f32[16,8,384]{2,1,0:T(8,128)S(1)}, u32[]{:S(2)}, u32[]{:S(2)}) %all-to-all-start.6) | async-done | bytes 196640 | tf_op jit(solution)/shard_map/all_to_all | solution.py:1164
  307.6 11.6 %all_to_all.47 = f32[16,8,384]{2,1,0:T(8,128)} all-to-all(f32[16,8,384]{2,1,0:T(8,128)S(1)} %broadcast_in_dim.16), channel_id=1, replica_groups=mesh['dp'=16,'tensor'=2] {'dp'}, dimensions={0} | all-to-all | bytes 393216 | tf_op jit(solution)/shard_map/all_to_all | solution.py:1164
  319.2 3.2 gradient_norm.1
  322.4 2.5 collective-permute-start.8
  325.0 7.3 %next_errors.1 = (f32[2,1344,384]{2,1,0:T(8,128)}, f32[2,960,384]{2,1,0:T(8,128)}, f32[2,16,384]{2,1,0:T(8,128)}) custom-call(f32[2304,384]{1,0:T(8,128)} %get-tuple-element.166.mat0, f32[2304,384]{1,0:T(8,128)} %get-tuple-element.167.mat1, f32[2,16,384]{2,1,0:T(8,128)} %get-tuple-element.168.mat_io, f32[2,8,384]{2,1,0:T(8,128)} %get-tuple-element.173.left_col, ...), custom_call_target="tpu_custom_call" | custom-call | tf_op jit(solution)/shard_map/next_errors/pallas_call | solution.py:1081
  333.1 4.8 %weight_update.1 = (f32[1,1]{1,0:T(1,128)}, f32[1,1]{1,0:T(1,128)}, f32[2,24,1344]{2,1,0:T(8,128)}, f32[2,24,960]{2,1,0:T(8,128)}, f32[24,5376]{1,0:T(8,128)}, /...) custom-call(s32[2]{0:T(128)} %pad_add_fusion.core.refs_0_, ...), custom_call_target="tpu_custom_call" | custom-call | tf_op jit(solution)/shard_map/weight_update/pallas_call | solution.py:1150
  (128 shorter events, 20.7 us)
Async XLA Ops:
  7.2 82.9 %all-gather.3.cloned.1.call-start = ((), (), s32[]{:S(2)}) async-start(), calls=%async_computation.8 | async-start | bytes 7299072 | tf_op jit(solution)/shard_map/all_gather | solution.py:1205
  14.9 12.5 %copy-start.15 = (f32[2,1344]{1,0:T(2,128)S(1)}, f32[2,1344]{1,0:T(2,128)}, u32[]{:S(2)}) copy-start(f32[2,1344]{1,0:T(2,128)} %b_col.1) | copy-start | bytes 32260
  14.9 13.5 %copy-start.9 = (f32[8080]{0:T(1024)S(1)}, f32[8080]{0:T(1024)}, u32[]{:S(2)}) copy-start(f32[8080]{0:T(1024)} %param.40) | copy-start | bytes 96964
  18.6 27.2 %copy-start.17 = (s32[256]{0:T(256)S(1)}, s32[256]{0:T(256)}, u32[]{:S(2)}) copy-start(s32[256]{0:T(256)} %param.31) | copy-start | bytes 3076
  18.6 27.5 %copy-start.16 = (f32[16]{0:T(128)S(1)}, f32[16]{0:T(128)}, u32[]{:S(2)}) copy-start(f32[16]{0:T(128)} %param.30) | copy-start | bytes 196
  18.6 27.5 %copy-start.12 = (f32[16,256,16]{1,2,0:T(8,128)S(1)}, f32[16,256,16]{1,2,0:T(8,128)}, u32[]{:S(2)}) copy-start(f32[16,256,16]{1,2,0:T(8,128)} %param.32) | copy-start | bytes 786436
  18.6 27.5 %copy-start.13 = (f32[16,256,16]{1,2,0:T(8,128)S(1)}, f32[16,256,16]{1,2,0:T(8,128)}, u32[]{:S(2)}) copy-start(f32[16,256,16]{1,2,0:T(8,128)} %param.29) | copy-start | bytes 786436
  18.6 27.5 %copy-start.14 = (f32[16,256,16]{1,2,0:T(8,128)S(1)}, f32[16,256,16]{1,2,0:T(8,128)}, u32[]{:S(2)}) copy-start(f32[16,256,16]{1,2,0:T(8,128)} %param.28) | copy-start | bytes 786436
  19.9 22.6 %all-to-all-start = ((bf16[16,2,7648]{2,1,0:T(2,128)(2,1)}), bf16[16,2,7648]{2,1,0:T(2,128)(2,1)S(1)}, u32[]{:S(2)}, u32[]{:S(2)}) async-start(bf16[16,2,7648]{2,1,0:T(2,128)(2,1)} %reshape.332), calls=%async_computation | async-start | bytes 983040 | tf_op jit(solution)/shard_map/all_to_all | solution.py:1164
  27.3 67.0 %collective-permute-start.1 = (f32[2,1344]{1,0:T(2,128)S(1)}, f32[2,1344]{1,0:T(2,128)S(1)}, u32[]{:S(2)}, u32[]{:S(2)}) collective-permute-start(f32[2,1344]{1,0:T(2,128)S(1)} %copy-done.15), channel_id=1, source_target_pairs={{0,1},{1,0},{2,3},{3,2},{4,5},{5,4},{6,7},{7,6},{8,9},{9,8},{10,11... | collective-permute-start | bytes 32264 | tf_op jit(solution)/shard_map/ppermute | solution.py:1160
  43.4 3.8 %collective-permute-start = (bf16[16,11264]{1,0:T(8,128)(2,1)S(1)}, bf16[16,11264]{1,0:T(8,128)(2,1)S(1)}, u32[]{:S(2)}, u32[]{:S(2)}) collective-permute-start(bf16[16,11264]{1,0:T(8,128)(2,1)S(1)} %get-tuple-element.211), channel_id=1, source_target_pairs={{0,1},{1,0},{2,3},{3,2},{4,5},{5,4},{6,7},{7,6},{8,9},{9,8},{10,11... | collective-permute-start | bytes 1081352 | tf_op jit(solution)/shard_map/ppermute | solution.py:1160
  48.0 2.2 copy-start.1
  51.1 13.9 %all-to-all-start.1 = ((f32[32,8,168]{2,1,0:T(8,128)}), f32[32,8,168]{2,1,0:T(8,128)S(1)}, u32[]{:S(2)}, u32[]{:S(2)}) async-start(f32[32,8,168]{2,1,0:T(8,128)} %fusion.6), calls=%async_computation.1 | async-start | bytes 524288 | tf_op jit(solution)/shard_map/all_to_all | solution.py:1243
  54.8 174.5 %all-gather.5.cloned.1.call-start = ((), (), s32[]{:S(2)}) async-start(), calls=%async_computation.9 | async-start | bytes 4386816 | tf_op jit(solution)/shard_map/all_gather | solution.py:1275
  94.4 0.6 copy-start.20
  95.0 30.1 %copy-start = (f32[24,5376]{1,0:T(8,128)S(1)}, f32[24,5376]{1,0:T(8,128)}, u32[]{:S(2)}) copy-start(f32[24,5376]{1,0:T(8,128)} %w_cond.1) | copy-start | bytes 1548292
  185.2 52.8 %collective-permute-start.3 = (f32[2304,384]{1,0:T(8,128)}, f32[2304,384]{1,0:T(8,128)}, u32[]{:S(2)}, u32[]{:S(2)}) collective-permute-start(f32[2304,384]{1,0:T(8,128)} %get-tuple-element.144), channel_id=1, source_target_pairs={{0,1},{1,0},{2,3},{3,2},{4,5},{5,4},{6,7},{7,6},{8,9},{9,8},{10,11... | collective-permute-start | bytes 10616840 | tf_op jit(solution)/shard_map/ppermute | solution.py:1160
  229.0 8.4 %copy-start.19 = (f32[64,384]{1,0:T(8,128)S(1)}, f32[64,384]{1,0:T(8,128)}, u32[]{:S(2)}) copy-start(f32[64,384]{1,0:T(8,128)} %get-tuple-element.148) | copy-start | bytes 294916
  229.0 15.4 %collective-permute-start.2 = (f32[2304,384]{1,0:T(8,128)}, f32[2304,384]{1,0:T(8,128)}, u32[]{:S(2)}, u32[]{:S(2)}) collective-permute-start(f32[2304,384]{1,0:T(8,128)} %get-tuple-element.142), channel_id=1, source_target_pairs={{0,1},{1,0},{2,3},{3,2},{4,5},{5,4},{6,7},{7,6},{8,9},{9,8},{10,11... | collective-permute-start | bytes 10616840 | tf_op jit(solution)/shard_map/ppermute | solution.py:1160
  233.5 18.3 %all-to-all-start.2 = ((f32[16,16,384]{2,1,0:T(8,128)}), f32[16,16,384]{2,1,0:T(8,128)S(1)}, u32[]{:S(2)}, u32[]{:S(2)}) async-start(f32[16,16,384]{2,1,0:T(8,128)} %modulation_rows.1), calls=%async_computation.2 | async-start | bytes 786432 | tf_op jit(solution)/shard_map/all_to_all | solution.py:1164
  237.4 7.0 %collective-permute-start.4 = (f32[64,384]{1,0:T(8,128)S(1)}, f32[64,384]{1,0:T(8,128)S(1)}, u32[]{:S(2)}, u32[]{:S(2)}) collective-permute-start(f32[64,384]{1,0:T(8,128)S(1)} %copy-done.19), channel_id=1, source_target_pairs={{0,1},{1,0},{2,3},{3,2},{4,5},{5,4},{6,7},{7,6},{8,9},{9,8},{10,11... | collective-permute-start | bytes 294920 | tf_op jit(solution)/shard_map/ppermute | solution.py:1160
  244.4 0.6 copy-start.10
  251.8 7.4 %copy-start.3 = (f32[16,16,384]{2,1,0:T(8,128)}, f32[16,16,384]{2,1,0:T(8,128)S(1)}, u32[]{:S(2)}) copy-start(f32[16,16,384]{2,1,0:T(8,128)S(1)} %all-to-all-done.2.refs_1_) | copy-start | bytes 1179652
  251.8 14.6 %all-to-all-start.3 = ((f32[16,8,384]{2,1,0:T(8,128)}), f32[16,8,384]{2,1,0:T(8,128)S(1)}, u32[]{:S(2)}, u32[]{:S(2)}) async-start(f32[16,8,384]{2,1,0:T(8,128)} %get-tuple-element.150), calls=%async_computation.3 | async-start | bytes 393216 | tf_op jit(solution)/shard_map/all_to_all | solution.py:1164
  266.4 25.8 %collective-permute-start.7 = (f32[648,384]{1,0:T(8,128)}, f32[648,384]{1,0:T(8,128)S(1)}, u32[]{:S(2)}, u32[]{:S(2)}) collective-permute-start(f32[648,384]{1,0:T(8,128)} %get-tuple-element.171.time_own), channel_id=1, source_target_pairs={{0,1},{1,0},{2,3},{3,2},{4,5},{5,4},{6,7},{7,6},{8,9},{9,8},{10,11... | collective-permute-start | bytes 2985992 | tf_op jit(solution)/shard_map/ppermute | solution.py:1160
  268.9 11.8 %all-to-all-start.5 = ((f32[16,8,384]{2,1,0:T(8,128)}), f32[16,8,384]{2,1,0:T(8,128)S(1)}, u32[]{:S(2)}, u32[]{:S(2)}) async-start(f32[16,8,384]{2,1,0:T(8,128)} %broadcast_in_dim.15), calls=%async_computation.5 | async-start | bytes 393216 | tf_op jit(solution)/shard_map/all_to_all | solution.py:1164
  272.4 2.5 collective-permute-start.5
  273.4 1.5 copy-start.8
  273.4 1.5 collective-permute-start.6
  274.9 0.6 copy-start.11
  275.5 0.7 copy-start.6
  280.6 4.2 %copy-start.2 = (f32[16,8,384]{2,1,0:T(8,128)}, f32[16,8,384]{2,1,0:T(8,128)S(1)}, u32[]{:S(2)}) copy-start(f32[16,8,384]{2,1,0:T(8,128)S(1)} %all-to-all-done.5) | copy-start | bytes 589828
  280.6 14.8 %all-to-all-start.4 = ((f32[16,16,384]{2,1,0:T(8,128)}), f32[16,16,384]{2,1,0:T(8,128)S(1)}, u32[]{:S(2)}, u32[]{:S(2)}) async-start(f32[16,16,384]{2,1,0:T(8,128)} %get-tuple-element.164), calls=%async_computation.4 | async-start | bytes 786432 | tf_op jit(solution)/shard_map/all_to_all | solution.py:1164
  292.2 27.0 %copy-start.5 = (f32[648,384]{1,0:T(8,128)}, f32[648,384]{1,0:T(8,128)S(1)}, u32[]{:S(2)}) copy-start(f32[648,384]{1,0:T(8,128)S(1)} %collective-permute-done.7.time_got) | copy-start | bytes 2985988
  295.4 36.9 %copy-start.4 = (f32[16,16,384]{2,1,0:T(8,128)}, f32[16,16,384]{2,1,0:T(8,128)S(1)}, u32[]{:S(2)}) copy-start(f32[16,16,384]{2,1,0:T(8,128)S(1)} %all-to-all-done.4.cond_own) | copy-start | bytes 1179652
  295.4 12.1 %all-to-all-start.6 = ((f32[16,8,384]{2,1,0:T(8,128)}), f32[16,8,384]{2,1,0:T(8,128)S(1)}, u32[]{:S(2)}, u32[]{:S(2)}) async-start(f32[16,8,384]{2,1,0:T(8,128)} %get-tuple-element.172), calls=%async_computation.6 | async-start | bytes 393216 | tf_op jit(solution)/shard_map/all_to_all | solution.py:1164
  300.5 31.8 %collective-permute-start.9 = (f32[16,16,384]{2,1,0:T(8,128)S(1)}, f32[16,16,384]{2,1,0:T(8,128)S(1)}, u32[]{:S(2)}, u32[]{:S(2)}) collective-permute-start(f32[16,16,384]{2,1,0:T(8,128)S(1)} %all-to-all-done.4.cond_own), channel_id=1, source_target_pairs={{0,1},{1,0},{2,3},{3,2},{4,5},{5,4},{6,7},{7,6},{8,9},{9,8},{10,11... | collective-permute-start | bytes 1179656 | tf_op jit(solution)/shard_map/ppermute | solution.py:1160
  322.4 9.9 %collective-permute-start.8 = (f32[1,128]{1,0:T(1,128)}, f32[1,128]{1,0:T(1,128)S(1)}, u32[]{:S(2)}, u32[]{:S(2)}) collective-permute-start(f32[1,128]{1,0:T(1,128)} %get-tuple-element.176.parts), channel_id=1, source_target_pairs={{0,1},{1,0},{2,3},{3,2},{4,5},{5,4},{6,7},{7,6},{8,9},{9,8},{10,11... | collective-permute-start | bytes 1544 | tf_op jit(solution)/shard_map/ppermute | solution.py:1160
  332.4 0.8 copy-start.7
  332.4 0.7 copy-start.18
Sparse Core Ops, SparseCore 0:
  11.5 78.5 all-gather.2
  125.9 72.1 all-gather.4

commit v6 on v5

--- a/solution.py
+++ b/solution.py
@@ -736,7 +736,7 @@
         yield ref.at[layer, pl.ds(start, size), :], pl.ds(at, size)
 
 
-def project(layer, own, got, fac_col, fac_row, mat, left_col, left_row, v_own, v_got, sems, out_sems):
+def begin_project(own, got, mat, v_own, v_got, sems, out_sems):
     loads, stores = [], []
     for k, (at, size) in enumerate(CHUNKS):
         rows = pl.ds(at, size)
@@ -745,6 +745,10 @@
         stores.append(pltpu.make_async_copy(v_own.at[rows, :], mat.at[rows, :], out_sems.at[k]))
         for copy in loads[-1]:
             copy.start()
+    return loads, stores
+
+
+def project(layer, loads, stores, fac_col, fac_row, left_col, left_row, v_own, v_got):
     left_row[...] = jnp.zeros_like(left_row)
     total = None
     for (at, size), copies, store in zip(CHUNKS, loads, stores):
@@ -759,8 +763,6 @@
         else:
             left_row[:, at - COL_S : at - COL_S + size] = narrow_dot(fac_row[layer], matrix, NT)
     left_col[...] = total
-    for store in stores:
-        store.wait()
 
 
 ANY = pl.BlockSpec(memory_space=pl.ANY)
@@ -776,19 +778,6 @@
 
 def shapes_of(shapes):
     return [jax.ShapeDtypeStruct(shape, f32) for shape in shapes]
-
-
-def run_project_second(own, got, fac_col, fac_row):
-    return pl.pallas_call(
-        lambda *refs: project(1, *refs),
-        in_specs=[ANY] * 2 + [VMEM] * 2,
-        out_specs=[ANY, VMEM, VMEM],
-        out_shape=shapes_of([(BOTH, D), (RANK, D), (RANK, WIDE)]),
-        scratch_shapes=PROJECT_SCRATCH,
-        compiler_params=large(),
-        cost_estimate=pl.CostEstimate(flops=int(1e9), bytes_accessed=int(1.5e7), transcendentals=0),
-        name="left_second",
-    )(own, got, fac_col, fac_row)
 
 
 def exchange_kernel(block, place, dmods, full_cond, cond, sent):
@@ -816,10 +805,13 @@
     )(place, dmods, full_cond, cond)
 
 
-def project_first_kernel(own, got, fac_col, fac_row,
-                         left_col1, left_row1, pay_own, pay_got, err_io, fac_io,
-                         mat, mat_io, sent, left_col, left_row, *scratch):
-    project(0, own, got, fac_col, fac_row, mat, left_col, left_row, *scratch)
+def project_kernel(own1, got1, own0, got0, fac_col, fac_row, pay_own, pay_got, err_io, fac_io,
+                   mat1, mat0, mat_io, sent, left_col1, left_row1, left_col, left_row,
+                   v_own1, v_got1, sems1, out_sems1, v_own0, v_got0, sems0, out_sems0):
+    loads1, stores1 = begin_project(own1, got1, mat1, v_own1, v_got1, sems1, out_sems1)
+    loads0, stores0 = begin_project(own0, got0, mat0, v_own0, v_got0, sems0, out_sems0)
+    project(1, loads1, stores1, fac_col, fac_row, left_col1, left_row1, v_own1, v_got1)
+    project(0, loads0, stores0, fac_col, fac_row, left_col, left_row, v_own0, v_got0)
     share = sent.shape[1]
     pay = pay_own[...] + pay_got[...]
     left_io = []
@@ -841,20 +833,21 @@
         for slot, line in enumerate(lines):
             at = column * 16 + slot
             sent[at // share, at % share : at % share + 1, :] = line
-
-
-def run_project_first(n_dp, own, got, fac_col, fac_row, left_col1, left_row1,
-                      pay_own, pay_got, err_io, fac_io):
+    for store in stores1 + stores0:
+        store.wait()
+
+
+def run_project(n_dp, own1, got1, own0, got0, fac_col, fac_row, pay_own, pay_got, err_io, fac_io):
     return pl.pallas_call(
-        project_first_kernel,
-        in_specs=[ANY] * 2 + [VMEM] * 8,
-        out_specs=[ANY, VMEM, VMEM],
-        out_shape=shapes_of([(BOTH, D), (2, PV, D), (n_dp, PACK // n_dp, D)]),
-        scratch_shapes=[pltpu.VMEM((RANK, D), f32), pltpu.VMEM((RANK, WIDE), f32)] + PROJECT_SCRATCH,
+        project_kernel,
+        in_specs=[ANY] * 4 + [VMEM] * 6,
+        out_specs=[ANY, ANY, VMEM, VMEM],
+        out_shape=shapes_of([(BOTH, D), (BOTH, D), (2, PV, D), (n_dp, PACK // n_dp, D)]),
+        scratch_shapes=[pltpu.VMEM((RANK, D), f32), pltpu.VMEM((RANK, WIDE), f32)] * 2 + PROJECT_SCRATCH * 2,
         compiler_params=large(),
         cost_estimate=pl.CostEstimate(flops=int(1e9), bytes_accessed=int(1.5e7), transcendentals=0),
-        name="left_first",
-    )(own, got, fac_col, fac_row, left_col1, left_row1, pay_own, pay_got, err_io, fac_io)
+        name="left_factors",
+    )(own1, got1, own0, got0, fac_col, fac_row, pay_own, pay_got, err_io, fac_io)
 
 
 TIME_ROWS = FREQ + D + 8
@@ -1054,12 +1047,8 @@
     )(packed, left_packed, *lefts, time_own, time_got)
 
 
-def error_kernel(mat0, mat1, mat_io, left_col, left_row, left_io, right_col, right_row, right_io,
-                 err_col, err_row, err_io, v0, v1, sems, out_sems):
-    loads = mat_loads((mat0, mat1), (v0, v1), sems)
-    for copies in loads:
-        for copy in copies:
-            copy.start()
+def next_errors(loads, mat_io, left_col, left_row, left_io, right_col, right_row, right_io,
+                err_col, err_row, err_io, v0, v1, out_sems):
     stores = []
     for layer, place in enumerate((v0, v1)):
         for k, ((at, size), (target, rows)) in enumerate(zip(CHUNKS, layer_chunks(layer, err_col, err_row))):
@@ -1073,21 +1062,7 @@
             store.start()
             stores.append(store)
         err_io[layer] = mat_io[layer] - outer(right_io[layer], left_io[layer])
-    for store in stores:
-        store.wait()
-
-
-def run_error(mats, mat_io, lefts, rights):
-    return pl.pallas_call(
-        error_kernel,
-        in_specs=[ANY, ANY] + [VMEM] * 7,
-        out_specs=[ANY, ANY, VMEM],
-        out_shape=shapes_of([(L, COL_S, D), (L, ROW_S, D), (2, PV, D)]),
-        scratch_shapes=[pltpu.VMEM((BOTH, D), f32), pltpu.VMEM((BOTH, D), f32),
-                        pltpu.SemaphoreType.DMA((L * len(CHUNKS),)), pltpu.SemaphoreType.DMA((L * len(CHUNKS),))],
-        compiler_params=large(),
-        name="next_errors",
-    )(*mats, mat_io, *lefts, *rights)
+    return stores
 
 
 def own_columns(values, first, count):
@@ -1144,16 +1119,33 @@
     n_brep[...], v_brep[...] = advance(b_rep[...], m_brep[...], brep_grad[...])
 
 
-def run_update(core, grads, weights, momenta):
-    vmem = pl.BlockSpec(memory_space=pltpu.VMEM)
+def final_kernel(*refs):
+    head, (mat0, mat1, mat_io) = refs[:31], refs[31:34]
+    news, (err_col, err_row, err_io, v0, v1, sems, out_sems) = refs[34:52], refs[52:]
+    loads = mat_loads((mat0, mat1), (v0, v1), sems)
+    for copies in loads:
+        for copy in copies:
+            copy.start()
+    left_col, right_col, right_row, left_row, right_io, left_io = head[3:9]
+    stores = next_errors(loads, mat_io, left_col, left_row, left_io, right_col, right_row, right_io,
+                         err_col, err_row, err_io, v0, v1, out_sems)
+    update_kernel(*head, *news)
+    for store in stores:
+        store.wait()
+
+
+def run_final(core, grads, weights, momenta, mats, mat_io):
     shapes = [(1, 1), (1, 1)] + [v.shape for v in weights] * 2
     return pl.pallas_call(
-        update_kernel,
-        in_specs=[pl.BlockSpec(memory_space=pltpu.SMEM)] + [vmem] * (len(grads) + 2 * len(weights)),
-        out_shape=[jax.ShapeDtypeStruct(shape, f32) for shape in shapes],
+        final_kernel,
+        in_specs=[SMEM] + [VMEM] * (len(grads) + 2 * len(weights)) + [ANY, ANY, VMEM],
+        out_specs=[VMEM] * len(shapes) + [ANY, ANY, VMEM],
+        out_shape=shapes_of(shapes + [(L, COL_S, D), (L, ROW_S, D), (2, PV, D)]),
+        scratch_shapes=[pltpu.VMEM((BOTH, D), f32), pltpu.VMEM((BOTH, D), f32),
+                        pltpu.SemaphoreType.DMA((L * len(CHUNKS),)), pltpu.SemaphoreType.DMA((L * len(CHUNKS),))],
         compiler_params=pltpu.CompilerParams(vmem_limit_bytes=62 * 2**20),
-        name="weight_update",
-    )(core, *grads, *weights, *momenta)
+        name="errors_and_update",
+    )(core, *grads, *weights, *momenta, *mats, mat_io)
 
 
 def swap(values):
@@ -1285,10 +1277,8 @@
 
     rows_got = trade(run_exchange(n_dp, place, dmods, full_cond, cond))
     fac_col_t, fac_row_t, fac_io_t = flip(fac_col), flip(fac_row), flip(fac_io)
-    mat1, left_col1, left_row1 = run_project_second(own1, got1, fac_col_t, fac_row_t)
-    mat0, mat_io, sent = run_project_first(
-        n_dp, own0, got0, fac_col_t, fac_row_t, left_col1, left_row1,
-        pay_own, pay_got, err_io_t, fac_io_t
+    mat1, mat0, mat_io, sent = run_project(
+        n_dp, own1, got1, own0, got0, fac_col_t, fac_row_t, pay_own, pay_got, err_io_t, fac_io_t
     )
     mats = (mat0, mat1)
     rows_got, sent = lax.optimization_barrier((rows_got, sent))
@@ -1318,15 +1308,14 @@
         packed, left_packed, lefts, time_own, time_got
     )
     parts_got = swap(parts)
-    next_err_col, next_err_row, next_err_io = run_error(mats, mat_io, lefts, (right_col, right_row, right_io))
 
     olds = (w_col, flip(w_row), w_cond, w_time, flip(w_io), class_table.T, b_col, b_line)
     momenta = (mom_col, flip(mom_row), mom_cond, mom_time, flip(mom_io), mom_table.T, mom_bcol, mom_brep[None])
-    loss, clip_norm, *new = run_update(
+    loss, clip_norm, *new, next_err_col, next_err_row, next_err_io = run_final(
         core,
         (parts, parts_got, left_col, right_col, right_row, left_row, right_io, left_io,
          cond_rows, cond_rows_got, time_grad, table_share, bcol_grad, brep_grad),
-        olds, momenta,
+        olds, momenta, mats, mat_io,
     )
 
     def outward(col, row, cond, time, io, table, bcol, brep):

time: 352 us -> 350 us (level)
  Pallas kernels: 179 us -> 175 us
    pallas_call x4 -> x2, Pallas kernels: 25.3 us -> 21.5 us  [the longest x1 10.8 us: run_project(): pl.pallas_call(project_kernel, in_specs=[ANY] * 4 + [VMEM] * 6, out_specs...]
  transfers between devices with their start and end apart: 19 -> 19, of which waited for: 8 -> 11; matrix products, arithmetic and copies ran while one was open for 8% -> 9% of each run, Pallas kernels for 42% -> 39%
where the time goes in v6:
time: 350 us; the launch traced here: 343 us
  Pallas kernels  175 us (50%)
  waiting for transfers between devices  60.6 us (17%)
  starting transfers between devices  44.5 us (13%)
  local copies, waits for them, and re-layouts  19.9 us (6%)
  between operations  15 us (4%)
  other arithmetic  12.6 us (4%)
  blocking collectives  11.6 us (3%)
    pallas_call x1, Pallas kernels, run_middle(): pl.pallas_call(middle_kernel, grid=(count // GROUP,), in_specs=[per_laten...  59.4 us
    pallas_call x1, Pallas kernels, run_last(): pl.pallas_call(last_kernel, grid=(count,), in_specs=[per_latent(TOK, D),...  43.5 us
    pallas_call x1, Pallas kernels, run_forward(): pl.pallas_call(forward_kernel, grid=(count // GROUP,), in_specs=[pl.Block...  30.1 us
    all_to_all x6, starting transfers between devices, trade(): return lax.all_to_all(chunks, 'dp', 0, 0, tiled=True)  29.5 us
    all_to_all x6, waiting for transfers between devices, trade(): return lax.all_to_all(chunks, 'dp', 0, 0, tiled=True)  26.1 us
    all_gather x1, waiting for transfers between devices, on_device(): full = lax.all_gather(shard, ('dp', 'tensor'))  24 us
    all_to_all x1, blocking collectives, trade(): return lax.all_to_all(chunks, 'dp', 0, 0, tiled=True)  11.6 us
    ppermute x10, starting transfers between devices, swap(): return lax.ppermute(values, 'tensor', [(0, 1), (1, 0)])  11.1 us
  transfers between devices with their start and end apart: 19, of which 11 were waited for; matrix products, arithmetic and copies ran while one was open for 9% of the time, Pallas kernels for 39%

profile of v6, /device:TPU:1, one launch (start us, length us, event | category | flops | bytes accessed | tf_op | source)
XLA Modules:
  0.0 342.8 jit_solution(17203373051668593912)
XLA Ops:
  7.2 1.0 convert.35
  8.2 0.9 bitcast_convert_fusion.1
  10.8 0.8 convert_element_type.72
  11.6 1.2 fusion.1
  13.8 1.1 convert_element_type.77
  14.9 1.1 reshape.292
  17.7 0.9 reduce.6
  18.6 1.3 reshape.332
  19.9 7.4 %all-to-all-start = ((bf16[16,2,7648]{2,1,0:T(2,128)(2,1)}), bf16[16,2,7648]{2,1,0:T(2,128)(2,1)S(1)}, u32[]{:S(2)}, u32[]{:S(2)}) async-start(bf16[16,2,7648]{2,1,0:T(2,128)(2,1)} %reshape.332), calls=%async_computation | async-start | bytes 983040 | tf_op jit(solution)/shard_map/all_to_all | solution.py:1156
  27.3 1.0 collective-permute-start.1
  28.4 14.1 %all-to-all-done = bf16[16,2,7648]{2,1,0:T(2,128)(2,1)S(1)} async-done(((bf16[16,2,7648]{2,1,0:T(2,128)(2,1)}), bf16[16,2,7648]{2,1,0:T(2,128)(2,1)S(1)}, u32[]{:S(2)}, u32[]{:S(2)}) %all-to-all-start) | async-done | bytes 489504 | tf_op jit(solution)/shard_map/all_to_all | solution.py:1156
  43.4 1.7 collective-permute-start
  49.1 1.1 multiply_convert_fusion
  50.2 0.9 fusion.6
  51.1 3.6 %all-to-all-start.1 = ((f32[32,8,168]{2,1,0:T(8,128)}), f32[32,8,168]{2,1,0:T(8,128)S(1)}, u32[]{:S(2)}, u32[]{:S(2)}) async-start(f32[32,8,168]{2,1,0:T(8,128)} %fusion.6), calls=%async_computation.1 | async-start | bytes 524288 | tf_op jit(solution)/shard_map/all_to_all | solution.py:1235
  55.4 0.8 reshape.309.wpatch.whead
  58.7 6.3 %all-to-all-done.1 = f32[32,8,168]{2,1,0:T(8,128)S(1)} async-done(((f32[32,8,168]{2,1,0:T(8,128)}), f32[32,8,168]{2,1,0:T(8,128)S(1)}, u32[]{:S(2)}, u32[]{:S(2)}) %all-to-all-start.1) | async-done | bytes 172064 | tf_op jit(solution)/shard_map/all_to_all | solution.py:1235
  66.1 24.0 %all-gather.3.cloned.1.call-done = bf16[32,24,4608]{2,1,0:T(8,128)(2,1)} async-done(((bf16[1,24,4608]{2,1,0:T(8,128)(2,1)}), bf16[32,24,4608]{2,1,0:T(8,128)(2,1)}) %all-gather.3.cloned.1.call-update) | async-done | bytes 7077904 | tf_op jit(solution)/shard_map/all_gather | solution.py:1197
  90.0 2.2 slice.120
  92.3 2.0 constant_dynamic-slice_fusion.1
  94.9 30.1 %forward_first.1 = (bf16[8,256,384]{2,1,0:T(8,128)(2,1)}, bf16[8,256,384]{2,1,0:T(8,128)(2,1)}, bf16[8,256,384]{2,1,0:T(8,128)(2,1)}, f32[8,6,256,256]{3,2,1,0:T...) custom-call(s32[2]{0:T(128)} %pad_add_fusion.core.refs_0_, ...), custom_call_target="tpu_custom_call" | custom-call | flops 8000000000 | bytes 48000000 | tf_op jit(solution)/shard_map/forward_first/pallas_call | solution.py:629
  125.8 59.4 %layer_second.1 = (f32[8,256,384]{2,1,0:T(8,128)}, f32[8,8,384]{2,1,0:T(8,128)}, f32[2304,384]{1,0:T(8,128)}, f32[2304,384]{1,0:T(8,128)}, f32[1,3456]{1,0:T(1,1...) custom-call(f32[8,256,384]{2,1,0:T(8,128)} %get-tuple-element.118.x2, ...), custom_call_target="tpu_custom_call" | custom-call | flops 25600000000 | bytes 24000000 | tf_op jit(solution)/shard_map/layer_second/pallas_call | solution.py:652
  185.2 43.5 %backward_first.1 = (f32[8,14,384]{2,1,0:T(8,128)}, f32[2304,384]{1,0:T(8,128)}, f32[2304,384]{1,0:T(8,128)}, f32[64,384]{1,0:T(8,128)}, f32[64,384]{1,0:T(8,128)}) custom-call(f32[8,256,384]{2,1,0:T(8,128)} %get-tuple-element.121.dx, f32[8,14,384]{2,1,0:T(8,128)} %broadcast_add_fusion.mods, bf16[384,2304]{1,0:T(8,128)(2,1)} %bitcast.107, ...), custom_call_target="tpu_custom_call" | custom-call | flops 17600000000 | bytes 64000000 | tf_op jit(solution)/shard_map/backward_first/pallas_call | solution.py:679
  229.3 4.2 %modulation_rows.1 = f32[16,16,384]{2,1,0:T(8,128)} custom-call(s32[1]{0:T(128)} %bitcast.21.refs_0_, f32[8,14,384]{2,1,0:T(8,128)} %get-tuple-element.137.refs_1_, bf16[384,5376]{1,0:T(8,128)(2,1)} %all-gather.5.cloned.1.call-done.refs_2_, f32[256,384]{1,0:T(8,128)} %get-tuple-element.228.refs_3_), custom_call_target="tpu_custom_call" | custom-call | tf_op jit(solution)/shard_map/modulation_rows/pallas_call | solution.py:799
  233.5 3.9 %all-to-all-start.2 = ((f32[16,16,384]{2,1,0:T(8,128)}), f32[16,16,384]{2,1,0:T(8,128)S(1)}, u32[]{:S(2)}, u32[]{:S(2)}) async-start(f32[16,16,384]{2,1,0:T(8,128)} %modulation_rows.1), calls=%async_computation.2 | async-start | bytes 786432 | tf_op jit(solution)/shard_map/all_to_all | solution.py:1156
  238.0 2.2 collective-permute-done.4.pay_got
  240.8 10.8 %left_factors.1 = (f32[2304,384]{1,0:T(8,128)}, f32[2304,384]{1,0:T(8,128)}, f32[2,16,384]{2,1,0:T(8,128)}, f32[16,8,384]{2,1,0:T(8,128)}) custom-call(f32[2304,384]{1,0:T(8,128)} %get-tuple-element.139.own1, f32[2304,384]{1,0:T(8,128)} %collective-permute-done.2.got1, f32[2304,384]{1,0:T(8,128)} %get-tuple-element.141.own0, ...), custom_call_target="tpu_custom_call" | custom-call | flops 1000000000 | bytes 15000000 | tf_op jit(solution)/shard_map/left_factors/pallas_call | solution.py:841
  251.6 5.4 %all-to-all-start.3 = ((f32[16,8,384]{2,1,0:T(8,128)}), f32[16,8,384]{2,1,0:T(8,128)S(1)}, u32[]{:S(2)}, u32[]{:S(2)}) async-start(f32[16,8,384]{2,1,0:T(8,128)} %get-tuple-element.146), calls=%async_computation.3 | async-start | bytes 393216 | tf_op jit(solution)/shard_map/all_to_all | solution.py:1156
  257.8 3.7 %modulation_gradients.1 = (f32[384,168]{1,0:T(8,128)}, f32[384,168]{1,0:T(8,128)}, f32[648,384]{1,0:T(8,128)}, f32[384,1000]{1,0:T(8,128)}) custom-call(s32[2]{0:T(128)} %pad_add_fusion.core.refs_0_, f32[16,16,384]{2,1,0:T(8,128)} %copy-done.4, bf16[128,384]{1,0:T(8,128)(2,1)} %get-tuple-element.148.refs_2_, bf16[128,256]{1,0:T(8,128)(2,1)} %fusion.18.refs_3_, ...), custom_call_target="tpu_custom_call" | custom-call | tf_op jit(solution)/shard_map/modulation_gradients/pallas_call | solution.py:887
  261.6 2.8 all-to-all-done.3
  264.4 2.4 collective-permute-start.7
  267.4 3.5 %all-to-all-start.5 = ((f32[16,8,384]{2,1,0:T(8,128)}), f32[16,8,384]{2,1,0:T(8,128)S(1)}, u32[]{:S(2)}, u32[]{:S(2)}) async-start(f32[16,8,384]{2,1,0:T(8,128)} %broadcast_in_dim.15), calls=%async_computation.5 | async-start | bytes 393216 | tf_op jit(solution)/shard_map/all_to_all | solution.py:1156
  271.1 0.9 constant_dynamic-slice_fusion.table_own
  272.5 0.9 collective-permute-done.6.table_got
  274.9 2.2 modulation_sums.1
  277.0 2.2 all-to-all-done.5
  279.2 4.2 %all-to-all-start.4 = ((f32[16,16,384]{2,1,0:T(8,128)}), f32[16,16,384]{2,1,0:T(8,128)S(1)}, u32[]{:S(2)}, u32[]{:S(2)}) async-start(f32[16,16,384]{2,1,0:T(8,128)} %get-tuple-element.160), calls=%async_computation.4 | async-start | bytes 786432 | tf_op jit(solution)/shard_map/all_to_all | solution.py:1156
  283.4 7.4 %right_factors.1 = (f32[16,8,384]{2,1,0:T(8,128)}, f32[2,8,384]{2,1,0:T(8,128)}, f32[2,8,1152]{2,1,0:T(8,128)}, f32[2,8,384]{2,1,0:T(8,128)}) custom-call(f32[8,16,384]{2,1,0:T(8,128)} %bitcast.108, f32[2304,384]{1,0:T(8,128)} %get-tuple-element.162.mat0.refs_31_, f32[2304,384]{1,0:T(8,128)} %get-tuple-element.163.mat1.refs_32_, ...), custom_call_target="tpu_custom_call" | custom-call | tf_op jit(solution)/shard_map/right_factors/pallas_call | solution.py:986
  290.9 1.5 dynamic-slice_add_fusion.refs_11_
  292.4 1.6 all-to-all-done.4.refs_9_
  294.0 5.1 %all-to-all-start.6 = ((f32[16,8,384]{2,1,0:T(8,128)}), f32[16,8,384]{2,1,0:T(8,128)S(1)}, u32[]{:S(2)}, u32[]{:S(2)}) async-start(f32[16,8,384]{2,1,0:T(8,128)} %get-tuple-element.168), calls=%async_computation.6 | async-start | bytes 393216 | tf_op jit(solution)/shard_map/all_to_all | solution.py:1156
  299.1 1.6 collective-permute-start.9
  300.7 5.4 %all-to-all-done.6 = f32[16,8,384]{2,1,0:T(8,128)S(1)} async-done(((f32[16,8,384]{2,1,0:T(8,128)}), f32[16,8,384]{2,1,0:T(8,128)S(1)}, u32[]{:S(2)}, u32[]{:S(2)}) %all-to-all-start.6) | async-done | bytes 196640 | tf_op jit(solution)/shard_map/all_to_all | solution.py:1156
  306.2 11.6 %all_to_all.47 = f32[16,8,384]{2,1,0:T(8,128)} all-to-all(f32[16,8,384]{2,1,0:T(8,128)S(1)} %broadcast_in_dim.16), channel_id=1, replica_groups=mesh['dp'=16,'tensor'=2] {'dp'}, dimensions={0} | all-to-all | bytes 393216 | tf_op jit(solution)/shard_map/all_to_all | solution.py:1156
  317.8 3.2 gradient_norm.1
  321.0 2.5 collective-permute-start.8
  323.6 0.9 collective-permute-done.8.refs_2_
  325.0 10.7 %errors_and_update.1 = (f32[1,1]{1,0:T(1,128)}, f32[1,1]{1,0:T(1,128)}, f32[2,24,1344]{2,1,0:T(8,128)}, f32[2,24,960]{2,1,0:T(8,128)}, f32[24,5376]{1,0:T(8,128)...) custom-call(s32[2]{0:T(128)} %pad_add_fusion.core.refs_0_, ...), custom_call_target="tpu_custom_call" | custom-call | tf_op jit(solution)/shard_map/errors_and_update/pallas_call | solution.py:1139
  (126 shorter events, 20.4 us)
Async XLA Ops:
  7.2 82.9 %all-gather.3.cloned.1.call-start = ((), (), s32[]{:S(2)}) async-start(), calls=%async_computation.8 | async-start | bytes 7299072 | tf_op jit(solution)/shard_map/all_gather | solution.py:1197
  14.9 12.5 %copy-start.15 = (f32[2,1344]{1,0:T(2,128)S(1)}, f32[2,1344]{1,0:T(2,128)}, u32[]{:S(2)}) copy-start(f32[2,1344]{1,0:T(2,128)} %refs_21_.1) | copy-start | bytes 32260
  14.9 13.5 %copy-start.9 = (f32[8080]{0:T(1024)S(1)}, f32[8080]{0:T(1024)}, u32[]{:S(2)}) copy-start(f32[8080]{0:T(1024)} %param.40) | copy-start | bytes 96964
  18.6 27.2 %copy-start.17 = (s32[256]{0:T(256)S(1)}, s32[256]{0:T(256)}, u32[]{:S(2)}) copy-start(s32[256]{0:T(256)} %param.31) | copy-start | bytes 3076
  18.6 27.5 %copy-start.16 = (f32[16]{0:T(128)S(1)}, f32[16]{0:T(128)}, u32[]{:S(2)}) copy-start(f32[16]{0:T(128)} %param.30) | copy-start | bytes 196
  18.6 27.6 %copy-start.12 = (f32[16,256,16]{1,2,0:T(8,128)S(1)}, f32[16,256,16]{1,2,0:T(8,128)}, u32[]{:S(2)}) copy-start(f32[16,256,16]{1,2,0:T(8,128)} %param.32) | copy-start | bytes 786436
  18.6 27.5 %copy-start.13 = (f32[16,256,16]{1,2,0:T(8,128)S(1)}, f32[16,256,16]{1,2,0:T(8,128)}, u32[]{:S(2)}) copy-start(f32[16,256,16]{1,2,0:T(8,128)} %param.29) | copy-start | bytes 786436
  18.6 27.5 %copy-start.14 = (f32[16,256,16]{1,2,0:T(8,128)S(1)}, f32[16,256,16]{1,2,0:T(8,128)}, u32[]{:S(2)}) copy-start(f32[16,256,16]{1,2,0:T(8,128)} %param.28) | copy-start | bytes 786436
  19.9 22.6 %all-to-all-start = ((bf16[16,2,7648]{2,1,0:T(2,128)(2,1)}), bf16[16,2,7648]{2,1,0:T(2,128)(2,1)S(1)}, u32[]{:S(2)}, u32[]{:S(2)}) async-start(bf16[16,2,7648]{2,1,0:T(2,128)(2,1)} %reshape.332), calls=%async_computation | async-start | bytes 983040 | tf_op jit(solution)/shard_map/all_to_all | solution.py:1156
  27.3 67.0 %collective-permute-start.1 = (f32[2,1344]{1,0:T(2,128)S(1)}, f32[2,1344]{1,0:T(2,128)S(1)}, u32[]{:S(2)}, u32[]{:S(2)}) collective-permute-start(f32[2,1344]{1,0:T(2,128)S(1)} %copy-done.15), channel_id=1, source_target_pairs={{0,1},{1,0},{2,3},{3,2},{4,5},{5,4},{6,7},{7,6},{8,9},{9,8},{10,11... | collective-permute-start | bytes 32264 | tf_op jit(solution)/shard_map/ppermute | solution.py:1152
  43.4 3.8 %collective-permute-start = (bf16[16,11264]{1,0:T(8,128)(2,1)S(1)}, bf16[16,11264]{1,0:T(8,128)(2,1)S(1)}, u32[]{:S(2)}, u32[]{:S(2)}) collective-permute-start(bf16[16,11264]{1,0:T(8,128)(2,1)S(1)} %get-tuple-element.207), channel_id=1, source_target_pairs={{0,1},{1,0},{2,3},{3,2},{4,5},{5,4},{6,7},{7,6},{8,9},{9,8},{10,11... | collective-permute-start | bytes 1081352 | tf_op jit(solution)/shard_map/ppermute | solution.py:1152
  48.0 2.2 copy-start.1
  51.1 13.9 %all-to-all-start.1 = ((f32[32,8,168]{2,1,0:T(8,128)}), f32[32,8,168]{2,1,0:T(8,128)S(1)}, u32[]{:S(2)}, u32[]{:S(2)}) async-start(f32[32,8,168]{2,1,0:T(8,128)} %fusion.6), calls=%async_computation.1 | async-start | bytes 524288 | tf_op jit(solution)/shard_map/all_to_all | solution.py:1235
  54.8 174.5 %all-gather.5.cloned.1.call-start = ((), (), s32[]{:S(2)}) async-start(), calls=%async_computation.9 | async-start | bytes 4386816 | tf_op jit(solution)/shard_map/all_gather | solution.py:1267
  94.3 0.6 copy-start.20
  94.9 30.1 %copy-start = (f32[24,5376]{1,0:T(8,128)S(1)}, f32[24,5376]{1,0:T(8,128)}, u32[]{:S(2)}) copy-start(f32[24,5376]{1,0:T(8,128)} %refs_17_.1) | copy-start | bytes 1548292
  228.7 8.7 %copy-start.19 = (f32[64,384]{1,0:T(8,128)S(1)}, f32[64,384]{1,0:T(8,128)}, u32[]{:S(2)}) copy-start(f32[64,384]{1,0:T(8,128)} %get-tuple-element.144) | copy-start | bytes 294916
  228.7 11.5 %collective-permute-start.3 = (f32[2304,384]{1,0:T(8,128)}, f32[2304,384]{1,0:T(8,128)}, u32[]{:S(2)}, u32[]{:S(2)}) collective-permute-start(f32[2304,384]{1,0:T(8,128)} %get-tuple-element.142), channel_id=1, source_target_pairs={{0,1},{1,0},{2,3},{3,2},{4,5},{5,4},{6,7},{7,6},{8,9},{9,8},{10,11... | collective-permute-start | bytes 10616840 | tf_op jit(solution)/shard_map/ppermute | solution.py:1152
  229.0 11.4 %collective-permute-start.2 = (f32[2304,384]{1,0:T(8,128)}, f32[2304,384]{1,0:T(8,128)}, u32[]{:S(2)}, u32[]{:S(2)}) collective-permute-start(f32[2304,384]{1,0:T(8,128)} %get-tuple-element.140), channel_id=1, source_target_pairs={{0,1},{1,0},{2,3},{3,2},{4,5},{5,4},{6,7},{7,6},{8,9},{9,8},{10,11... | collective-permute-start | bytes 10616840 | tf_op jit(solution)/shard_map/ppermute | solution.py:1152
  233.5 18.1 %all-to-all-start.2 = ((f32[16,16,384]{2,1,0:T(8,128)}), f32[16,16,384]{2,1,0:T(8,128)S(1)}, u32[]{:S(2)}, u32[]{:S(2)}) async-start(f32[16,16,384]{2,1,0:T(8,128)} %modulation_rows.1), calls=%async_computation.2 | async-start | bytes 786432 | tf_op jit(solution)/shard_map/all_to_all | solution.py:1156
  237.4 2.8 collective-permute-start.4
  240.2 0.6 copy-start.10
  251.6 6.2 %copy-start.4 = (f32[16,16,384]{2,1,0:T(8,128)}, f32[16,16,384]{2,1,0:T(8,128)S(1)}, u32[]{:S(2)}) copy-start(f32[16,16,384]{2,1,0:T(8,128)S(1)} %all-to-all-done.2.refs_1_) | copy-start | bytes 1179652
  251.6 12.7 %all-to-all-start.3 = ((f32[16,8,384]{2,1,0:T(8,128)}), f32[16,8,384]{2,1,0:T(8,128)S(1)}, u32[]{:S(2)}, u32[]{:S(2)}) async-start(f32[16,8,384]{2,1,0:T(8,128)} %get-tuple-element.146), calls=%async_computation.3 | async-start | bytes 393216 | tf_op jit(solution)/shard_map/all_to_all | solution.py:1156
  264.4 26.5 %collective-permute-start.7 = (f32[648,384]{1,0:T(8,128)}, f32[648,384]{1,0:T(8,128)S(1)}, u32[]{:S(2)}, u32[]{:S(2)}) collective-permute-start(f32[648,384]{1,0:T(8,128)} %get-tuple-element.167.time_own), channel_id=1, source_target_pairs={{0,1},{1,0},{2,3},{3,2},{4,5},{5,4},{6,7},{7,6},{8,9},{9,8},{10,11... | collective-permute-start | bytes 2985992 | tf_op jit(solution)/shard_map/ppermute | solution.py:1152
  267.4 11.8 %all-to-all-start.5 = ((f32[16,8,384]{2,1,0:T(8,128)}), f32[16,8,384]{2,1,0:T(8,128)S(1)}, u32[]{:S(2)}, u32[]{:S(2)}) async-start(f32[16,8,384]{2,1,0:T(8,128)} %broadcast_in_dim.15), calls=%async_computation.5 | async-start | bytes 393216 | tf_op jit(solution)/shard_map/all_to_all | solution.py:1156
  271.0 2.5 collective-permute-start.5
  272.0 1.5 copy-start.8
  272.0 1.5 collective-permute-start.6
  273.5 0.6 copy-start.11
  274.1 0.7 copy-start.7
  279.2 4.2 %copy-start.2 = (f32[16,8,384]{2,1,0:T(8,128)}, f32[16,8,384]{2,1,0:T(8,128)S(1)}, u32[]{:S(2)}) copy-start(f32[16,8,384]{2,1,0:T(8,128)S(1)} %all-to-all-done.5) | copy-start | bytes 589828
  279.2 14.8 %all-to-all-start.4 = ((f32[16,16,384]{2,1,0:T(8,128)}), f32[16,16,384]{2,1,0:T(8,128)S(1)}, u32[]{:S(2)}, u32[]{:S(2)}) async-start(f32[16,16,384]{2,1,0:T(8,128)} %get-tuple-element.160), calls=%async_computation.4 | async-start | bytes 786432 | tf_op jit(solution)/shard_map/all_to_all | solution.py:1156
  290.8 27.0 %copy-start.5 = (f32[648,384]{1,0:T(8,128)}, f32[648,384]{1,0:T(8,128)S(1)}, u32[]{:S(2)}) copy-start(f32[648,384]{1,0:T(8,128)S(1)} %collective-permute-done.7.time_got) | copy-start | bytes 2985988
  294.0 30.4 %copy-start.3 = (f32[16,16,384]{2,1,0:T(8,128)}, f32[16,16,384]{2,1,0:T(8,128)S(1)}, u32[]{:S(2)}) copy-start(f32[16,16,384]{2,1,0:T(8,128)S(1)} %all-to-all-done.4.refs_9_) | copy-start | bytes 1179652
  294.0 12.1 %all-to-all-start.6 = ((f32[16,8,384]{2,1,0:T(8,128)}), f32[16,8,384]{2,1,0:T(8,128)S(1)}, u32[]{:S(2)}, u32[]{:S(2)}) async-start(f32[16,8,384]{2,1,0:T(8,128)} %get-tuple-element.168), calls=%async_computation.6 | async-start | bytes 393216 | tf_op jit(solution)/shard_map/all_to_all | solution.py:1156
  299.1 24.5 %collective-permute-start.9 = (f32[16,16,384]{2,1,0:T(8,128)S(1)}, f32[16,16,384]{2,1,0:T(8,128)S(1)}, u32[]{:S(2)}, u32[]{:S(2)}) collective-permute-start(f32[16,16,384]{2,1,0:T(8,128)S(1)} %all-to-all-done.4.refs_9_), channel_id=1, source_target_pairs={{0,1},{1,0},{2,3},{3,2},{4,5},{5,4},{6,7},{7,6},{8,9},{9,8},{10,11... | collective-permute-start | bytes 1179656 | tf_op jit(solution)/shard_map/ppermute | solution.py:1152
  321.0 3.4 collective-permute-start.8
  323.6 0.9 copy-start.6
  324.5 0.5 copy-start.18
Sparse Core Ops, SparseCore 0:
  11.5 78.5 all-gather.2
  125.9 72.4 all-gather.4

commit v7 on v6

--- a/solution.py
+++ b/solution.py
@@ -19,7 +19,7 @@
 TOK = 256
 RANK = 8
 GROUP = 2
-AHEAD, MLP_AHEAD, BACK_AHEAD = 2, 2, 3
+AHEAD, MLP_AHEAD, BACK_AHEAD = 2, 2, 6
 LAG = 1
 
 norm_eps = 1e-06

time: 350 us -> 350 us (level)
  no operation moved by 1% of the time
where the time goes in v7:
time: 350 us; the launch traced here: 343 us
  Pallas kernels  175 us (50%)
  waiting for transfers between devices  60.6 us (17%)
  starting transfers between devices  44.5 us (13%)
  local copies, waits for them, and re-layouts  19.9 us (6%)
  between operations  15 us (4%)
  other arithmetic  12.6 us (4%)
  blocking collectives  11.6 us (3%)
    pallas_call x1, Pallas kernels, run_middle(): pl.pallas_call(middle_kernel, grid=(count // GROUP,), in_specs=[per_laten...  59.4 us
    pallas_call x1, Pallas kernels, run_last(): pl.pallas_call(last_kernel, grid=(count,), in_specs=[per_latent(TOK, D),...  43.4 us
    pallas_call x1, Pallas kernels, run_forward(): pl.pallas_call(forward_kernel, grid=(count // GROUP,), in_specs=[pl.Block...  30.1 us
    all_to_all x6, starting transfers between devices, trade(): return lax.all_to_all(chunks, 'dp', 0, 0, tiled=True)  29.6 us
    all_to_all x6, waiting for transfers between devices, trade(): return lax.all_to_all(chunks, 'dp', 0, 0, tiled=True)  26.1 us
    all_gather x1, waiting for transfers between devices, on_device(): full = lax.all_gather(shard, ('dp', 'tensor'))  24 us
    all_to_all x1, blocking collectives, trade(): return lax.all_to_all(chunks, 'dp', 0, 0, tiled=True)  11.6 us
    ppermute x10, starting transfers between devices, swap(): return lax.ppermute(values, 'tensor', [(0, 1), (1, 0)])  11.1 us
  transfers between devices with their start and end apart: 19, of which 11 were waited for; matrix products, arithmetic and copies ran while one was open for 9% of the time, Pallas kernels for 39%

profile of v7, /device:TPU:1, one launch (start us, length us, event | category | flops | bytes accessed | tf_op | source)
XLA Modules:
  0.0 342.8 jit_solution(12788564736394561268)
XLA Ops:
  7.2 1.0 convert.35
  8.2 0.9 bitcast_convert_fusion.1
  10.8 0.8 convert_element_type.72
  11.6 1.2 fusion.1
  13.8 1.1 convert_element_type.77
  14.9 1.1 reshape.292
  17.7 0.9 reduce.6
  18.6 1.3 reshape.332
  19.9 7.4 %all-to-all-start = ((bf16[16,2,7648]{2,1,0:T(2,128)(2,1)}), bf16[16,2,7648]{2,1,0:T(2,128)(2,1)S(1)}, u32[]{:S(2)}, u32[]{:S(2)}) async-start(bf16[16,2,7648]{2,1,0:T(2,128)(2,1)} %reshape.332), calls=%async_computation | async-start | bytes 983040 | tf_op jit(solution)/shard_map/all_to_all | solution.py:1156
  27.3 1.0 collective-permute-start.1
  28.4 14.1 %all-to-all-done = bf16[16,2,7648]{2,1,0:T(2,128)(2,1)S(1)} async-done(((bf16[16,2,7648]{2,1,0:T(2,128)(2,1)}), bf16[16,2,7648]{2,1,0:T(2,128)(2,1)S(1)}, u32[]{:S(2)}, u32[]{:S(2)}) %all-to-all-start) | async-done | bytes 489504 | tf_op jit(solution)/shard_map/all_to_all | solution.py:1156
  43.4 1.7 collective-permute-start
  49.1 1.1 multiply_convert_fusion
  50.2 0.9 fusion.6
  51.1 3.6 %all-to-all-start.1 = ((f32[32,8,168]{2,1,0:T(8,128)}), f32[32,8,168]{2,1,0:T(8,128)S(1)}, u32[]{:S(2)}, u32[]{:S(2)}) async-start(f32[32,8,168]{2,1,0:T(8,128)} %fusion.6), calls=%async_computation.1 | async-start | bytes 524288 | tf_op jit(solution)/shard_map/all_to_all | solution.py:1235
  55.4 0.8 reshape.309.wpatch.whead
  58.7 6.3 %all-to-all-done.1 = f32[32,8,168]{2,1,0:T(8,128)S(1)} async-done(((f32[32,8,168]{2,1,0:T(8,128)}), f32[32,8,168]{2,1,0:T(8,128)S(1)}, u32[]{:S(2)}, u32[]{:S(2)}) %all-to-all-start.1) | async-done | bytes 172064 | tf_op jit(solution)/shard_map/all_to_all | solution.py:1235
  66.1 24.0 %all-gather.3.cloned.1.call-done = bf16[32,24,4608]{2,1,0:T(8,128)(2,1)} async-done(((bf16[1,24,4608]{2,1,0:T(8,128)(2,1)}), bf16[32,24,4608]{2,1,0:T(8,128)(2,1)}) %all-gather.3.cloned.1.call-update) | async-done | bytes 7077904 | tf_op jit(solution)/shard_map/all_gather | solution.py:1197
  90.0 2.2 slice.120
  92.3 2.0 constant_dynamic-slice_fusion.1
  94.9 30.1 %forward_first.1 = (bf16[8,256,384]{2,1,0:T(8,128)(2,1)}, bf16[8,256,384]{2,1,0:T(8,128)(2,1)}, bf16[8,256,384]{2,1,0:T(8,128)(2,1)}, f32[8,6,256,256]{3,2,1,0:T...) custom-call(s32[2]{0:T(128)} %pad_add_fusion.core.refs_0_, ...), custom_call_target="tpu_custom_call" | custom-call | flops 8000000000 | bytes 48000000 | tf_op jit(solution)/shard_map/forward_first/pallas_call | solution.py:629
  125.8 59.4 %layer_second.1 = (f32[8,256,384]{2,1,0:T(8,128)}, f32[8,8,384]{2,1,0:T(8,128)}, f32[2304,384]{1,0:T(8,128)}, f32[2304,384]{1,0:T(8,128)}, f32[1,3456]{1,0:T(1,1...) custom-call(f32[8,256,384]{2,1,0:T(8,128)} %get-tuple-element.118.x2, ...), custom_call_target="tpu_custom_call" | custom-call | flops 25600000000 | bytes 24000000 | tf_op jit(solution)/shard_map/layer_second/pallas_call | solution.py:652
  185.2 43.4 %backward_first.1 = (f32[8,14,384]{2,1,0:T(8,128)}, f32[2304,384]{1,0:T(8,128)}, f32[2304,384]{1,0:T(8,128)}, f32[64,384]{1,0:T(8,128)}, f32[64,384]{1,0:T(8,128)}) custom-call(f32[8,256,384]{2,1,0:T(8,128)} %get-tuple-element.121.dx, f32[8,14,384]{2,1,0:T(8,128)} %broadcast_add_fusion.mods, bf16[384,2304]{1,0:T(8,128)(2,1)} %bitcast.107, ...), custom_call_target="tpu_custom_call" | custom-call | flops 17600000000 | bytes 64000000 | tf_op jit(solution)/shard_map/backward_first/pallas_call | solution.py:679
  229.2 4.2 %modulation_rows.1 = f32[16,16,384]{2,1,0:T(8,128)} custom-call(s32[1]{0:T(128)} %bitcast.21.refs_0_, f32[8,14,384]{2,1,0:T(8,128)} %get-tuple-element.137.refs_1_, bf16[384,5376]{1,0:T(8,128)(2,1)} %all-gather.5.cloned.1.call-done.refs_2_, f32[256,384]{1,0:T(8,128)} %get-tuple-element.228.refs_3_), custom_call_target="tpu_custom_call" | custom-call | tf_op jit(solution)/shard_map/modulation_rows/pallas_call | solution.py:799
  233.4 3.9 %all-to-all-start.2 = ((f32[16,16,384]{2,1,0:T(8,128)}), f32[16,16,384]{2,1,0:T(8,128)S(1)}, u32[]{:S(2)}, u32[]{:S(2)}) async-start(f32[16,16,384]{2,1,0:T(8,128)} %modulation_rows.1), calls=%async_computation.2 | async-start | bytes 786432 | tf_op jit(solution)/shard_map/all_to_all | solution.py:1156
  238.0 2.1 collective-permute-done.4.pay_got
  240.7 10.8 %left_factors.1 = (f32[2304,384]{1,0:T(8,128)}, f32[2304,384]{1,0:T(8,128)}, f32[2,16,384]{2,1,0:T(8,128)}, f32[16,8,384]{2,1,0:T(8,128)}) custom-call(f32[2304,384]{1,0:T(8,128)} %get-tuple-element.139.own1, f32[2304,384]{1,0:T(8,128)} %collective-permute-done.2.got1, f32[2304,384]{1,0:T(8,128)} %get-tuple-element.141.own0, ...), custom_call_target="tpu_custom_call" | custom-call | flops 1000000000 | bytes 15000000 | tf_op jit(solution)/shard_map/left_factors/pallas_call | solution.py:841
  251.6 5.4 %all-to-all-start.3 = ((f32[16,8,384]{2,1,0:T(8,128)}), f32[16,8,384]{2,1,0:T(8,128)S(1)}, u32[]{:S(2)}, u32[]{:S(2)}) async-start(f32[16,8,384]{2,1,0:T(8,128)} %get-tuple-element.146), calls=%async_computation.3 | async-start | bytes 393216 | tf_op jit(solution)/shard_map/all_to_all | solution.py:1156
  257.8 3.7 %modulation_gradients.1 = (f32[384,168]{1,0:T(8,128)}, f32[384,168]{1,0:T(8,128)}, f32[648,384]{1,0:T(8,128)}, f32[384,1000]{1,0:T(8,128)}) custom-call(s32[2]{0:T(128)} %pad_add_fusion.core.refs_0_, f32[16,16,384]{2,1,0:T(8,128)} %copy-done.4, bf16[128,384]{1,0:T(8,128)(2,1)} %get-tuple-element.148.refs_2_, bf16[128,256]{1,0:T(8,128)(2,1)} %fusion.18.refs_3_, ...), custom_call_target="tpu_custom_call" | custom-call | tf_op jit(solution)/shard_map/modulation_gradients/pallas_call | solution.py:887
  261.5 2.8 all-to-all-done.3
  264.3 2.4 collective-permute-start.7
  267.4 3.5 %all-to-all-start.5 = ((f32[16,8,384]{2,1,0:T(8,128)}), f32[16,8,384]{2,1,0:T(8,128)S(1)}, u32[]{:S(2)}, u32[]{:S(2)}) async-start(f32[16,8,384]{2,1,0:T(8,128)} %broadcast_in_dim.15), calls=%async_computation.5 | async-start | bytes 393216 | tf_op jit(solution)/shard_map/all_to_all | solution.py:1156
  271.0 0.9 constant_dynamic-slice_fusion.table_own
  272.5 0.9 collective-permute-done.6.table_got
  274.8 2.2 modulation_sums.1
  276.9 2.2 all-to-all-done.5
  279.2 4.2 %all-to-all-start.4 = ((f32[16,16,384]{2,1,0:T(8,128)}), f32[16,16,384]{2,1,0:T(8,128)S(1)}, u32[]{:S(2)}, u32[]{:S(2)}) async-start(f32[16,16,384]{2,1,0:T(8,128)} %get-tuple-element.160), calls=%async_computation.4 | async-start | bytes 786432 | tf_op jit(solution)/shard_map/all_to_all | solution.py:1156
  283.4 7.4 %right_factors.1 = (f32[16,8,384]{2,1,0:T(8,128)}, f32[2,8,384]{2,1,0:T(8,128)}, f32[2,8,1152]{2,1,0:T(8,128)}, f32[2,8,384]{2,1,0:T(8,128)}) custom-call(f32[8,16,384]{2,1,0:T(8,128)} %bitcast.108, f32[2304,384]{1,0:T(8,128)} %get-tuple-element.162.mat0.refs_31_, f32[2304,384]{1,0:T(8,128)} %get-tuple-element.163.mat1.refs_32_, ...), custom_call_target="tpu_custom_call" | custom-call | tf_op jit(solution)/shard_map/right_factors/pallas_call | solution.py:986
  290.8 1.5 dynamic-slice_add_fusion.refs_11_
  292.3 1.6 all-to-all-done.4.refs_9_
  294.0 5.1 %all-to-all-start.6 = ((f32[16,8,384]{2,1,0:T(8,128)}), f32[16,8,384]{2,1,0:T(8,128)S(1)}, u32[]{:S(2)}, u32[]{:S(2)}) async-start(f32[16,8,384]{2,1,0:T(8,128)} %get-tuple-element.168), calls=%async_computation.6 | async-start | bytes 393216 | tf_op jit(solution)/shard_map/all_to_all | solution.py:1156
  299.0 1.6 collective-permute-start.9
  300.6 5.4 %all-to-all-done.6 = f32[16,8,384]{2,1,0:T(8,128)S(1)} async-done(((f32[16,8,384]{2,1,0:T(8,128)}), f32[16,8,384]{2,1,0:T(8,128)S(1)}, u32[]{:S(2)}, u32[]{:S(2)}) %all-to-all-start.6) | async-done | bytes 196640 | tf_op jit(solution)/shard_map/all_to_all | solution.py:1156
  306.1 11.6 %all_to_all.47 = f32[16,8,384]{2,1,0:T(8,128)} all-to-all(f32[16,8,384]{2,1,0:T(8,128)S(1)} %broadcast_in_dim.16), channel_id=1, replica_groups=mesh['dp'=16,'tensor'=2] {'dp'}, dimensions={0} | all-to-all | bytes 393216 | tf_op jit(solution)/shard_map/all_to_all | solution.py:1156
  317.7 3.2 gradient_norm.1
  321.0 2.5 collective-permute-start.8
  323.5 0.9 collective-permute-done.8.refs_2_
  324.9 10.7 %errors_and_update.1 = (f32[1,1]{1,0:T(1,128)}, f32[1,1]{1,0:T(1,128)}, f32[2,24,1344]{2,1,0:T(8,128)}, f32[2,24,960]{2,1,0:T(8,128)}, f32[24,5376]{1,0:T(8,128)...) custom-call(s32[2]{0:T(128)} %pad_add_fusion.core.refs_0_, ...), custom_call_target="tpu_custom_call" | custom-call | tf_op jit(solution)/shard_map/errors_and_update/pallas_call | solution.py:1139
  (126 shorter events, 20.4 us)
Async XLA Ops:
  7.2 82.9 %all-gather.3.cloned.1.call-start = ((), (), s32[]{:S(2)}) async-start(), calls=%async_computation.8 | async-start | bytes 7299072 | tf_op jit(solution)/shard_map/all_gather | solution.py:1197
  14.9 12.5 %copy-start.15 = (f32[2,1344]{1,0:T(2,128)S(1)}, f32[2,1344]{1,0:T(2,128)}, u32[]{:S(2)}) copy-start(f32[2,1344]{1,0:T(2,128)} %refs_21_.1) | copy-start | bytes 32260
  14.9 13.5 %copy-start.9 = (f32[8080]{0:T(1024)S(1)}, f32[8080]{0:T(1024)}, u32[]{:S(2)}) copy-start(f32[8080]{0:T(1024)} %param.40) | copy-start | bytes 96964
  18.6 27.2 %copy-start.17 = (s32[256]{0:T(256)S(1)}, s32[256]{0:T(256)}, u32[]{:S(2)}) copy-start(s32[256]{0:T(256)} %param.31) | copy-start | bytes 3076
  18.6 27.5 %copy-start.16 = (f32[16]{0:T(128)S(1)}, f32[16]{0:T(128)}, u32[]{:S(2)}) copy-start(f32[16]{0:T(128)} %param.30) | copy-start | bytes 196
  18.6 27.6 %copy-start.12 = (f32[16,256,16]{1,2,0:T(8,128)S(1)}, f32[16,256,16]{1,2,0:T(8,128)}, u32[]{:S(2)}) copy-start(f32[16,256,16]{1,2,0:T(8,128)} %param.32) | copy-start | bytes 786436
  18.6 27.5 %copy-start.13 = (f32[16,256,16]{1,2,0:T(8,128)S(1)}, f32[16,256,16]{1,2,0:T(8,128)}, u32[]{:S(2)}) copy-start(f32[16,256,16]{1,2,0:T(8,128)} %param.29) | copy-start | bytes 786436
  18.6 27.5 %copy-start.14 = (f32[16,256,16]{1,2,0:T(8,128)S(1)}, f32[16,256,16]{1,2,0:T(8,128)}, u32[]{:S(2)}) copy-start(f32[16,256,16]{1,2,0:T(8,128)} %param.28) | copy-start | bytes 786436
  19.9 22.6 %all-to-all-start = ((bf16[16,2,7648]{2,1,0:T(2,128)(2,1)}), bf16[16,2,7648]{2,1,0:T(2,128)(2,1)S(1)}, u32[]{:S(2)}, u32[]{:S(2)}) async-start(bf16[16,2,7648]{2,1,0:T(2,128)(2,1)} %reshape.332), calls=%async_computation | async-start | bytes 983040 | tf_op jit(solution)/shard_map/all_to_all | solution.py:1156
  27.3 67.0 %collective-permute-start.1 = (f32[2,1344]{1,0:T(2,128)S(1)}, f32[2,1344]{1,0:T(2,128)S(1)}, u32[]{:S(2)}, u32[]{:S(2)}) collective-permute-start(f32[2,1344]{1,0:T(2,128)S(1)} %copy-done.15), channel_id=1, source_target_pairs={{0,1},{1,0},{2,3},{3,2},{4,5},{5,4},{6,7},{7,6},{8,9},{9,8},{10,11... | collective-permute-start | bytes 32264 | tf_op jit(solution)/shard_map/ppermute | solution.py:1152
  43.4 3.8 %collective-permute-start = (bf16[16,11264]{1,0:T(8,128)(2,1)S(1)}, bf16[16,11264]{1,0:T(8,128)(2,1)S(1)}, u32[]{:S(2)}, u32[]{:S(2)}) collective-permute-start(bf16[16,11264]{1,0:T(8,128)(2,1)S(1)} %get-tuple-element.207), channel_id=1, source_target_pairs={{0,1},{1,0},{2,3},{3,2},{4,5},{5,4},{6,7},{7,6},{8,9},{9,8},{10,11... | collective-permute-start | bytes 1081352 | tf_op jit(solution)/shard_map/ppermute | solution.py:1152
  48.0 2.2 copy-start.1
  51.1 13.9 %all-to-all-start.1 = ((f32[32,8,168]{2,1,0:T(8,128)}), f32[32,8,168]{2,1,0:T(8,128)S(1)}, u32[]{:S(2)}, u32[]{:S(2)}) async-start(f32[32,8,168]{2,1,0:T(8,128)} %fusion.6), calls=%async_computation.1 | async-start | bytes 524288 | tf_op jit(solution)/shard_map/all_to_all | solution.py:1235
  54.8 174.4 %all-gather.5.cloned.1.call-start = ((), (), s32[]{:S(2)}) async-start(), calls=%async_computation.9 | async-start | bytes 4386816 | tf_op jit(solution)/shard_map/all_gather | solution.py:1267
  94.3 0.6 copy-start.20
  94.9 30.1 %copy-start = (f32[24,5376]{1,0:T(8,128)S(1)}, f32[24,5376]{1,0:T(8,128)}, u32[]{:S(2)}) copy-start(f32[24,5376]{1,0:T(8,128)} %refs_17_.1) | copy-start | bytes 1548292
  228.6 8.8 %copy-start.19 = (f32[64,384]{1,0:T(8,128)S(1)}, f32[64,384]{1,0:T(8,128)}, u32[]{:S(2)}) copy-start(f32[64,384]{1,0:T(8,128)} %get-tuple-element.144) | copy-start | bytes 294916
  228.6 11.5 %collective-permute-start.3 = (f32[2304,384]{1,0:T(8,128)}, f32[2304,384]{1,0:T(8,128)}, u32[]{:S(2)}, u32[]{:S(2)}) collective-permute-start(f32[2304,384]{1,0:T(8,128)} %get-tuple-element.142), channel_id=1, source_target_pairs={{0,1},{1,0},{2,3},{3,2},{4,5},{5,4},{6,7},{7,6},{8,9},{9,8},{10,11... | collective-permute-start | bytes 10616840 | tf_op jit(solution)/shard_map/ppermute | solution.py:1152
  228.9 11.4 %collective-permute-start.2 = (f32[2304,384]{1,0:T(8,128)}, f32[2304,384]{1,0:T(8,128)}, u32[]{:S(2)}, u32[]{:S(2)}) collective-permute-start(f32[2304,384]{1,0:T(8,128)} %get-tuple-element.140), channel_id=1, source_target_pairs={{0,1},{1,0},{2,3},{3,2},{4,5},{5,4},{6,7},{7,6},{8,9},{9,8},{10,11... | collective-permute-start | bytes 10616840 | tf_op jit(solution)/shard_map/ppermute | solution.py:1152
  233.4 18.1 %all-to-all-start.2 = ((f32[16,16,384]{2,1,0:T(8,128)}), f32[16,16,384]{2,1,0:T(8,128)S(1)}, u32[]{:S(2)}, u32[]{:S(2)}) async-start(f32[16,16,384]{2,1,0:T(8,128)} %modulation_rows.1), calls=%async_computation.2 | async-start | bytes 786432 | tf_op jit(solution)/shard_map/all_to_all | solution.py:1156
  237.4 2.7 collective-permute-start.4
  240.1 0.6 copy-start.10
  251.5 6.2 %copy-start.4 = (f32[16,16,384]{2,1,0:T(8,128)}, f32[16,16,384]{2,1,0:T(8,128)S(1)}, u32[]{:S(2)}) copy-start(f32[16,16,384]{2,1,0:T(8,128)S(1)} %all-to-all-done.2.refs_1_) | copy-start | bytes 1179652
  251.6 12.7 %all-to-all-start.3 = ((f32[16,8,384]{2,1,0:T(8,128)}), f32[16,8,384]{2,1,0:T(8,128)S(1)}, u32[]{:S(2)}, u32[]{:S(2)}) async-start(f32[16,8,384]{2,1,0:T(8,128)} %get-tuple-element.146), calls=%async_computation.3 | async-start | bytes 393216 | tf_op jit(solution)/shard_map/all_to_all | solution.py:1156
  264.3 26.5 %collective-permute-start.7 = (f32[648,384]{1,0:T(8,128)}, f32[648,384]{1,0:T(8,128)S(1)}, u32[]{:S(2)}, u32[]{:S(2)}) collective-permute-start(f32[648,384]{1,0:T(8,128)} %get-tuple-element.167.time_own), channel_id=1, source_target_pairs={{0,1},{1,0},{2,3},{3,2},{4,5},{5,4},{6,7},{7,6},{8,9},{9,8},{10,11... | collective-permute-start | bytes 2985992 | tf_op jit(solution)/shard_map/ppermute | solution.py:1152
  267.4 11.8 %all-to-all-start.5 = ((f32[16,8,384]{2,1,0:T(8,128)}), f32[16,8,384]{2,1,0:T(8,128)S(1)}, u32[]{:S(2)}, u32[]{:S(2)}) async-start(f32[16,8,384]{2,1,0:T(8,128)} %broadcast_in_dim.15), calls=%async_computation.5 | async-start | bytes 393216 | tf_op jit(solution)/shard_map/all_to_all | solution.py:1156
  270.9 2.5 collective-permute-start.5
  271.9 1.5 copy-start.8
  271.9 1.5 collective-permute-start.6
  273.4 0.6 copy-start.11
  274.0 0.7 copy-start.7
  279.1 4.2 %copy-start.2 = (f32[16,8,384]{2,1,0:T(8,128)}, f32[16,8,384]{2,1,0:T(8,128)S(1)}, u32[]{:S(2)}) copy-start(f32[16,8,384]{2,1,0:T(8,128)S(1)} %all-to-all-done.5) | copy-start | bytes 589828
  279.2 14.8 %all-to-all-start.4 = ((f32[16,16,384]{2,1,0:T(8,128)}), f32[16,16,384]{2,1,0:T(8,128)S(1)}, u32[]{:S(2)}, u32[]{:S(2)}) async-start(f32[16,16,384]{2,1,0:T(8,128)} %get-tuple-element.160), calls=%async_computation.4 | async-start | bytes 786432 | tf_op jit(solution)/shard_map/all_to_all | solution.py:1156
  290.8 27.0 %copy-start.5 = (f32[648,384]{1,0:T(8,128)}, f32[648,384]{1,0:T(8,128)S(1)}, u32[]{:S(2)}) copy-start(f32[648,384]{1,0:T(8,128)S(1)} %collective-permute-done.7.time_got) | copy-start | bytes 2985988
  294.0 30.4 %copy-start.3 = (f32[16,16,384]{2,1,0:T(8,128)}, f32[16,16,384]{2,1,0:T(8,128)S(1)}, u32[]{:S(2)}) copy-start(f32[16,16,384]{2,1,0:T(8,128)S(1)} %all-to-all-done.4.refs_9_) | copy-start | bytes 1179652
  294.0 12.1 %all-to-all-start.6 = ((f32[16,8,384]{2,1,0:T(8,128)}), f32[16,8,384]{2,1,0:T(8,128)S(1)}, u32[]{:S(2)}, u32[]{:S(2)}) async-start(f32[16,8,384]{2,1,0:T(8,128)} %get-tuple-element.168), calls=%async_computation.6 | async-start | bytes 393216 | tf_op jit(solution)/shard_map/all_to_all | solution.py:1156
  299.0 24.5 %collective-permute-start.9 = (f32[16,16,384]{2,1,0:T(8,128)S(1)}, f32[16,16,384]{2,1,0:T(8,128)S(1)}, u32[]{:S(2)}, u32[]{:S(2)}) collective-permute-start(f32[16,16,384]{2,1,0:T(8,128)S(1)} %all-to-all-done.4.refs_9_), channel_id=1, source_target_pairs={{0,1},{1,0},{2,3},{3,2},{4,5},{5,4},{6,7},{7,6},{8,9},{9,8},{10,11... | collective-permute-start | bytes 1179656 | tf_op jit(solution)/shard_map/ppermute | solution.py:1152
  321.0 3.4 collective-permute-start.8
  323.5 0.9 copy-start.6
  324.4 0.5 copy-start.18
Sparse Core Ops, SparseCore 0:
  11.5 78.5 all-gather.2
  125.9 72.4 all-gather.4
